TPU v7x, 32 devices: a whole 2x2x4 slice. The times are simulated.
32 devices in a mesh: groups: 2 (over x), wide: 16 (over z, y, core).
Axes of the slice: x: 2, y: 2, z: 4, core: 2. Of those that a mesh axis runs over, the one named last changes fastest.
Arguments:
- gamma: bfloat16 [4, 11008, 512], P('groups', 'wide'), parts along dimension 0, may hold values from -6 to 6
- coefficients: bfloat16 [6144, 11008], P('wide'), may hold values from -0.0546875 to 0.0546875
- owners: int32 [2048, 1], P('wide'), may hold values from 0 to 15; in each aligned block of 128 rows (0 to 127, 128 to 255, ...) at most 16 rows name the same one
Outputs:
- owned_blocks: bfloat16 [16, 16, 32, 6, 512], P('wide', None, 'groups'), parts along dimension 2
- owned_ids: int32 [16, 32, 16], P('wide', 'groups'), parts along dimension 1
There are 2 independent parts, one for each index of `groups`. A program takes and returns all parts, laid end to end along the dimension named above; an argument that names none is the same for every part. Nothing has to cross between parts.
Inputs may be any that keep to these rules, and one draw needn't show every extreme that they name: `owners`: among the 128 blocks of one source device (aligned blocks of rows), no owner is named more than 16 times, a bound that some block reaches; every owner owns some block.
All inputs are finite; a program needn't handle non-finite values.
Results may differ from a plain program's by a relative error of at most 0.001.
Values may be sent and summed in bfloat16 or wider, within the bound.
No kernel may reach another device: no remote copies, remote signals or barrier semaphores. Data moves between devices by JAX's collectives and lax.ppermute only.
A program may use at most 128 MiB of HBM per device.

v0:
```python
import jax
import jax.numpy as jnp
from jax import lax
from jax.sharding import PartitionSpec as P


def transform(left, gamma):
    return jnp.einsum(
        "ra,ian->irn",
        left,
        lax.all_gather(gamma, "wide", axis=1, tiled=True),
        preferred_element_type=jnp.float32,
    )


def local(gamma, coefficients, owners):
    count = lax.axis_size("wide")
    blocks_here = owners.shape[0]
    slots = max(2, 2 * blocks_here // count)
    block_rows = coefficients.shape[0] // blocks_here
    naux = gamma.shape[2]
    norb = gamma.shape[0]
    owner_col = owners[:, 0]
    same = owner_col[:, None] == owner_col[None, :]
    lower = jnp.arange(blocks_here)[:, None] > jnp.arange(blocks_here)[None, :]
    rank = jnp.sum((same & lower).astype(jnp.int32), axis=1)
    target = owner_col * slots + rank
    select = jnp.arange(count * slots, dtype=jnp.int32)[:, None] == target[None, :]
    global_ids = lax.axis_index("wide") * blocks_here + jnp.arange(blocks_here, dtype=jnp.int32)
    labels = jnp.sum(jnp.where(select, global_ids[None, :] + 1, 0), axis=1) - 1
    labels = labels.reshape(count, slots)
    select_mat = select.astype(jnp.bfloat16)
    result = transform(coefficients, gamma).astype(jnp.bfloat16)
    items = result.reshape(norb, blocks_here, block_rows, naux).transpose(1, 0, 2, 3)
    items = items.reshape(blocks_here, norb * block_rows * naux)
    outgoing = jnp.dot(select_mat, items, preferred_element_type=jnp.float32).astype(jnp.bfloat16)
    outgoing = outgoing.reshape(count, slots, norb * block_rows, naux)
    placed, arrived_ids = (
        lax.all_to_all(outgoing, "wide", split_axis=0, concat_axis=0, tiled=True),
        lax.all_to_all(labels, "wide", split_axis=0, concat_axis=0, tiled=True),
    )
    return (placed[None], arrived_ids[None])


def solution(mesh):
    placed = (P("groups", "wide", None), P("wide", None), P("wide", None))
    return jax.shard_map(
        local,
        mesh=mesh,
        in_specs=placed,
        out_specs=(P("wide", None, "groups", None, None), P("wide", "groups", None)),
        check_vma=False,
    )
```

profile of v0, /device:TPU:13, one launch (start us, length us, event | category | flops | bytes accessed | tf_op | source)
XLA Modules:
  0.0 201.5 jit_solution(10846760997665330605)
XLA Ops:
  7.2 0.0 all-gather.2.cloned.1.call-start
  7.2 0.7 all-gather.2.cloned.1.call-update
  7.9 0.9 convert_reduce_fusion
  8.8 0.7 add_add_fusion
  9.5 0.1 select_reduce_fusion
  9.6 0.7 sub.7
  10.3 6.6 %all-to-all-start.1 = ((s32[16,1,16]{2,1,0:T(1,128)}), s32[16,1,16]{2,1,0:T(1,128)S(1)}, u32[]{:S(2)}, u32[]{:S(2)}) async-start(s32[16,1,16]{2,1,0:T(1,128)} %sub.7), calls=%async_computation.1 | async-start | bytes 16384 | tf_op jit(solution)/shard_map/all_to_all | solution.py:40
  16.9 110.4 %all-gather.2.cloned.1.call-done = bf16[2,11008,512]{2,1,0:T(8,128)(2,1)} async-done(((bf16[2,688,512]{2,1,0:T(8,128)(2,1)}), bf16[2,11008,512]{2,1,0:T(8,128)(2,1)}) %all-gather.2.cloned.1.call-update) | async-done | bytes 22544400 | tf_op jit(solution)/shard_map/all_gather | solution.py:11
  127.3 15.7 %fusion.5 = bf16[2,384,512]{2,1,0:T(8,128)(2,1)S(1)} fusion(bf16[2,11008,512]{2,1,0:T(8,128)(2,1)} %all-gather.2.cloned.1.call-done, bf16[384,11008]{1,0:T(8,128)(2,1)} %param.4), kind=kOutput, calls=%fused_computation.4 | convolution fusion | flops 8657436672 | bytes 31784960 | tf_op jit(solution)/shard_map/ra,ian->irn/dot_general | solution.py:8
  143.0 0.8 copy.12
  143.8 0.8 copy.13
  144.6 1.7 convolution_convert_fusion
  146.3 3.4 %reshape.47 = bf16[16,16,6,512]{3,2,1,0:T(8,128)(2,1)S(1)} reshape(bf16[256,3072]{1,0:T(8,128)(2,1)} %convolution_convert_fusion) | data formatting | bytes 3145728 | tf_op jit(solution)/shard_map/reshape | solution.py:37
  149.8 1.8 copy.14
  151.5 0.0 all-to-all-done.1
  151.5 5.2 %all-to-all-start = ((bf16[16,16,6,512]{3,1,2,0:T(8,128)(2,1)}), bf16[16,16,6,512]{3,1,2,0:T(8,128)(2,1)S(1)}, u32[]{:S(2)}, u32[]{:S(2)}) async-start(bf16[16,16,6,512]{3,1,2,0:T(8,128)(2,1)} %copy.14), calls=%async_computation | async-start | bytes 3145728 | tf_op jit(solution)/shard_map/all_to_all | solution.py:39
  156.7 36.2 %all-to-all-done = bf16[16,16,6,512]{3,1,2,0:T(8,128)(2,1)S(1)} async-done(((bf16[16,16,6,512]{3,1,2,0:T(8,128)(2,1)}), bf16[16,16,6,512]{3,1,2,0:T(8,128)(2,1)S(1)}, u32[]{:S(2)}, u32[]{:S(2)}) %all-to-all-start) | async-done | bytes 1572896 | tf_op jit(solution)/shard_map/all_to_all | solution.py:39
  192.9 1.1 copy.17
  194.0 0.6 copy.18
  (1 shorter events, 0.0 us)
Async XLA Ops:
  7.2 120.1 %all-gather.2.cloned.1.call-start = ((), (), s32[]{:S(2)}) async-start(), calls=%async_computation.2 | async-start | bytes 23953408 | tf_op jit(solution)/shard_map/all_gather | solution.py:11
  10.3 141.2 %all-to-all-start.1 = ((s32[16,1,16]{2,1,0:T(1,128)}), s32[16,1,16]{2,1,0:T(1,128)S(1)}, u32[]{:S(2)}, u32[]{:S(2)}) async-start(s32[16,1,16]{2,1,0:T(1,128)} %sub.7), calls=%async_computation.1 | async-start | bytes 16384 | tf_op jit(solution)/shard_map/all_to_all | solution.py:40
  151.5 41.4 %all-to-all-start = ((bf16[16,16,6,512]{3,1,2,0:T(8,128)(2,1)}), bf16[16,16,6,512]{3,1,2,0:T(8,128)(2,1)S(1)}, u32[]{:S(2)}, u32[]{:S(2)}) async-start(bf16[16,16,6,512]{3,1,2,0:T(8,128)(2,1)} %copy.14), calls=%async_computation | async-start | bytes 3145728 | tf_op jit(solution)/shard_map/all_to_all | solution.py:39
Sparse Core Ops, SparseCore 0:
  9.5 117.7 all-gather.1
where the time goes:
time: 202 us; the launch traced here: 201 us
  waiting for transfers between devices  147 us (73%)
  matrix products  17.4 us (9%)
  between operations  14.1 us (7%)
  starting transfers between devices  11.8 us (6%)
  local copies, waits for them, and re-layouts  9.2 us (5%)
    all_gather x1, waiting for transfers between devices, transform(): lax.all_gather(gamma, 'wide', axis=1, tiled=True)  110 us
    all_to_all x1, waiting for transfers between devices, local(): lax.all_to_all(outgoing, 'wide', split_axis=0, concat_axis=0, tiled=True)  36.2 us
    dot_general x1, matrix products, transform(): jnp.einsum('ra,ian->irn', left, lax.all_gather(gamma, 'wide', axis=1, til...  15.7 us
    all_to_all x1, starting transfers between devices, local(): lax.all_to_all(labels, 'wide', split_axis=0, concat_axis=0, tiled=True)  6.57 us
    all_to_all x1, starting transfers between devices, local(): lax.all_to_all(outgoing, 'wide', split_axis=0, concat_axis=0, tiled=True)  5.18 us
    reshape x2, local copies, waits for them, and re-layouts, local(): outgoing = outgoing.reshape(count, slots, norb * block_rows, naux)  5.17 us
  transfers between devices with their start and end apart: 3, of which 2 were waited for; matrix products, arithmetic and copies ran while one was open for 13% of the time, Pallas kernels for 0%

commit v1 on v0

v1 whole, which is shorter than its diff:
```python
import jax
import jax.numpy as jnp
from jax import lax
from jax.sharding import PartitionSpec as P


def local(gamma, coefficients, owners):
    count = lax.axis_size("wide")
    blocks_here = owners.shape[0]
    slots = max(2, 2 * blocks_here // count)
    rows = coefficients.shape[0]
    block_rows = rows // blocks_here
    norb, _, naux = gamma.shape
    parts = 2
    width = naux // parts

    gathered = [
        [
            lax.all_gather(
                gamma[i, :, j * width : (j + 1) * width], "wide", axis=0, tiled=True
            )
            for j in range(parts)
        ]
        for i in range(norb)
    ]

    owner_col = owners[:, 0]
    same = owner_col[:, None] == owner_col[None, :]
    lower = jnp.arange(blocks_here)[:, None] > jnp.arange(blocks_here)[None, :]
    rank = jnp.sum((same & lower).astype(jnp.int32), axis=1)
    target = owner_col * slots + rank
    select = jnp.arange(count * slots, dtype=jnp.int32)[:, None] == target[None, :]
    global_ids = lax.axis_index("wide") * blocks_here + jnp.arange(blocks_here, dtype=jnp.int32)
    labels = jnp.sum(jnp.where(select, global_ids[None, :] + 1, 0), axis=1) - 1
    labels = labels.reshape(count, slots)
    ids = lax.all_to_all(labels, "wide", split_axis=0, concat_axis=0, tiled=True)

    row_at = jnp.arange(rows, dtype=jnp.int32)
    out_at = jnp.arange(count * block_rows * slots, dtype=jnp.int32)
    row_key = jnp.repeat(target, block_rows) * block_rows + row_at % block_rows
    out_key = (
        out_at // (block_rows * slots) * slots + out_at % slots
    ) * block_rows + out_at // slots % block_rows
    place = (out_key[:, None] == row_key[None, :]).astype(jnp.bfloat16)

    arrived = []
    for i in range(norb):
        row = []
        for j in range(parts):
            back = jnp.dot(
                coefficients, gathered[i][j], preferred_element_type=jnp.float32
            ).astype(jnp.bfloat16)
            out = jnp.dot(place, back, preferred_element_type=jnp.float32)
            out = out.astype(jnp.bfloat16).reshape(count, block_rows, slots, width)
            row.append(
                lax.all_to_all(out, "wide", split_axis=0, concat_axis=0, tiled=True)
            )
        arrived.append(jnp.concatenate(row, axis=3))
    placed = jnp.stack(arrived, axis=1)
    placed = placed.reshape(count, norb * block_rows, slots, naux).transpose(0, 2, 1, 3)
    return placed[None], ids[None]


def solution(mesh):
    placed = (P("groups", "wide", None), P("wide", None), P("wide", None))
    return jax.shard_map(
        local,
        mesh=mesh,
        in_specs=placed,
        out_specs=(P("wide", None, "groups", None, None), P("wide", "groups", None)),
        check_vma=False,
    )
```

time: 202 us -> 306 us (1.51)
  waiting for transfers between devices: 147 us -> 221 us
  matrix products: 17.4 us -> 35.2 us
  starting transfers between devices: 11.8 us -> 25.4 us
  local copies, waits for them, and re-layouts: 9.2 us -> 5.29 us
    all_gather x1 -> x4, waiting for transfers between devices: 110 us -> 209 us  [local(): lax.all_gather(gamma[i, :, j * width:(j + 1) * width], 'wide', axis=0, ti...]
    all_to_all x1 -> x4, waiting for transfers between devices: 36.2 us -> 10.7 us  [local(): lax.all_to_all(out, 'wide', split_axis=0, concat_axis=0, tiled=True)]
    dot_general x2 -> x4, matrix products: 17.4 us -> 35.2 us  [local(): out = jnp.dot(place, back, preferred_element_type=jnp.float32)]
    all_to_all x1 -> x4, starting transfers between devices: 5.18 us -> 18.7 us  [local(): lax.all_to_all(out, 'wide', split_axis=0, concat_axis=0, tiled=True)]
    reshape x2 -> x0, local copies, waits for them, and re-layouts: 5.17 us -> none  [local(): outgoing = outgoing.reshape(count, slots, norb * block_rows, naux)]
  transfers between devices with their start and end apart: 3 -> 9, of which waited for: 2 -> 5; matrix products, arithmetic and copies ran while one was open for 13% -> 13% of each run, Pallas kernels for 0% -> 0%
where the time goes in v1:
time: 306 us; the launch traced here: 303 us
  waiting for transfers between devices  221 us (72%)
  matrix products  35.2 us (12%)
  starting transfers between devices  25.4 us (8%)
  between operations  13.8 us (5%)
  local copies, waits for them, and re-layouts  5.29 us (2%)
    all_gather x4, waiting for transfers between devices, local(): lax.all_gather(gamma[i, :, j * width:(j + 1) * width], 'wide', axis=0, ti...  209 us
    dot_general x4, matrix products, local(): out = jnp.dot(place, back, preferred_element_type=jnp.float32)  35.2 us
    all_to_all x4, starting transfers between devices, local(): lax.all_to_all(out, 'wide', split_axis=0, concat_axis=0, tiled=True)  18.7 us
    all_to_all x4, waiting for transfers between devices, local(): lax.all_to_all(out, 'wide', split_axis=0, concat_axis=0, tiled=True)  10.7 us
    all_to_all x1, starting transfers between devices, local(): lax.all_to_all(labels, 'wide', split_axis=0, concat_axis=0, tiled=True)  6.55 us
  transfers between devices with their start and end apart: 9, of which 5 were waited for; matrix products, arithmetic and copies ran while one was open for 13% of the time, Pallas kernels for 0%

profile of v1, /device:TPU:13, one launch (start us, length us, event | category | flops | bytes accessed | tf_op | source)
XLA Modules:
  0.0 303.0 jit_solution(709580480900747602)
XLA Ops:
  7.2 0.0 all-gather.9.cloned.1.call-start
  7.2 2.4 fusion.78
  9.6 0.0 all-gather.9.cloned.1.call-update
  9.7 0.0 all-gather.11.cloned.1.call-start
  9.7 0.7 all-gather.11.cloned.1.call-update
  10.4 0.0 all-gather.13.cloned.1.call-start
  10.5 0.7 all-gather.13.cloned.1.call-update
  11.1 0.0 all-gather.15.cloned.1.call-start
  11.2 0.5 all-gather.15.cloned.1.call-update
  11.7 0.9 convert_reduce_fusion
  12.6 0.7 broadcast_multiply_fusion
  13.3 0.1 select_reduce_fusion
  13.4 0.7 sub.19
  14.1 6.6 %all-to-all-start.4 = ((s32[16,1,16]{2,1,0:T(1,128)}), s32[16,1,16]{2,1,0:T(1,128)S(1)}, u32[]{:S(2)}, u32[]{:S(2)}) async-start(s32[16,1,16]{2,1,0:T(1,128)} %sub.19), calls=%async_computation.4 | async-start | bytes 16384 | tf_op jit(solution)/shard_map/all_to_all | solution.py:36
  20.7 0.1 broadcast_in_dim.28
  20.7 0.2 mul.57
  21.0 48.7 %all-gather.9.cloned.1.call-done = bf16[1,11008,256]{2,1,0:T(8,128)(2,1)} async-done(((bf16[1,688,256]{2,1,0:T(8,128)(2,1)}), bf16[1,11008,256]{2,1,0:T(8,128)(2,1)}) %all-gather.9.cloned.1.call-update) | async-done | bytes 5636112 | tf_op jit(solution)/shard_map/all_gather | solution.py:19
  69.7 8.8 %fusion.16 = bf16[768,256]{1,0:T(8,128)(2,1)} fusion(bf16[384,11008]{1,0:T(8,128)(2,1)} %param.4, bf16[1,11008,256]{2,1,0:T(8,128)(2,1)} %all-gather.9.cloned.1.call-done, s32[384]{0:T(512)S(1)} %fusion.74, s32[768]{0:T(1024)S(1)} %fusion.66), kind=kOutput, calls=%fused_computation.17 | convolution fusion | flops 2315845632 | bytes 14488064 | tf_op jit(solution)/shard_map/dot_general | solution.py:53
  78.5 0.0 all-to-all-done.4
  78.5 4.7 %all-to-all-start = ((bf16[16,3,16,256]{3,2,1,0:T(8,128)(2,1)}), bf16[16,3,16,256]{3,2,1,0:T(8,128)(2,1)S(1)}, u32[]{:S(2)}, u32[]{:S(2)}) async-start(bf16[16,3,16,256]{3,2,1,0:T(8,128)(2,1)} %bitcast.2), calls=%async_computation | async-start | bytes 786432 | tf_op jit(solution)/shard_map/all_to_all | solution.py:56
  83.2 53.4 %all-gather.11.cloned.1.call-done = bf16[1,11008,256]{2,1,0:T(8,128)(2,1)} async-done(((bf16[1,688,256]{2,1,0:T(8,128)(2,1)}), bf16[1,11008,256]{2,1,0:T(8,128)(2,1)}) %all-gather.11.cloned.1.call-update) | async-done | bytes 5636112 | tf_op jit(solution)/shard_map/all_gather | solution.py:19
  136.6 8.8 %fusion.19 = bf16[768,256]{1,0:T(8,128)(2,1)} fusion(bf16[384,11008]{1,0:T(8,128)(2,1)} %param.4, bf16[1,11008,256]{2,1,0:T(8,128)(2,1)} %all-gather.11.cloned.1.call-done, s32[384]{0:T(512)S(1)} %fusion.74, s32[768]{0:T(1024)S(1)} %fusion.66), kind=kOutput, calls=%fused_computation.18 | convolution fusion | flops 2315845632 | bytes 14488064 | tf_op jit(solution)/shard_map/dot_general | solution.py:53
  145.3 0.0 all-to-all-done
  145.4 4.7 %all-to-all-start.1 = ((bf16[16,3,16,256]{3,2,1,0:T(8,128)(2,1)}), bf16[16,3,16,256]{3,2,1,0:T(8,128)(2,1)S(1)}, u32[]{:S(2)}, u32[]{:S(2)}) async-start(bf16[16,3,16,256]{3,2,1,0:T(8,128)(2,1)} %bitcast.4), calls=%async_computation.1 | async-start | bytes 786432 | tf_op jit(solution)/shard_map/all_to_all | solution.py:56
  150.0 53.4 %all-gather.13.cloned.1.call-done = bf16[1,11008,256]{2,1,0:T(8,128)(2,1)} async-done(((bf16[1,688,256]{2,1,0:T(8,128)(2,1)}), bf16[1,11008,256]{2,1,0:T(8,128)(2,1)}) %all-gather.13.cloned.1.call-update) | async-done | bytes 5636112 | tf_op jit(solution)/shard_map/all_gather | solution.py:19
  203.4 8.8 %fusion.22 = bf16[768,256]{1,0:T(8,128)(2,1)} fusion(bf16[384,11008]{1,0:T(8,128)(2,1)} %param.4, bf16[1,11008,256]{2,1,0:T(8,128)(2,1)} %all-gather.13.cloned.1.call-done, s32[384]{0:T(512)S(1)} %fusion.74, s32[768]{0:T(1024)S(1)} %fusion.66), kind=kOutput, calls=%fused_computation.19 | convolution fusion | flops 2315845632 | bytes 14488064 | tf_op jit(solution)/shard_map/dot_general | solution.py:53
  212.2 0.0 all-to-all-done.1
  212.2 4.7 %all-to-all-start.2 = ((bf16[16,3,16,256]{3,2,1,0:T(8,128)(2,1)}), bf16[16,3,16,256]{3,2,1,0:T(8,128)(2,1)S(1)}, u32[]{:S(2)}, u32[]{:S(2)}) async-start(bf16[16,3,16,256]{3,2,1,0:T(8,128)(2,1)} %bitcast.7), calls=%async_computation.2 | async-start | bytes 786432 | tf_op jit(solution)/shard_map/all_to_all | solution.py:56
  216.9 53.2 %all-gather.15.cloned.1.call-done = bf16[1,11008,256]{2,1,0:T(8,128)(2,1)} async-done(((bf16[1,688,256]{2,1,0:T(8,128)(2,1)}), bf16[1,11008,256]{2,1,0:T(8,128)(2,1)}) %all-gather.15.cloned.1.call-update) | async-done | bytes 5636112 | tf_op jit(solution)/shard_map/all_gather | solution.py:19
  270.1 8.8 %fusion.25 = bf16[768,256]{1,0:T(8,128)(2,1)} fusion(bf16[384,11008]{1,0:T(8,128)(2,1)} %param.4, bf16[1,11008,256]{2,1,0:T(8,128)(2,1)} %all-gather.15.cloned.1.call-done, s32[384]{0:T(512)S(1)} %fusion.74, s32[768]{0:T(1024)S(1)} %fusion.66), kind=kOutput, calls=%fused_computation.20 | convolution fusion | flops 2315845632 | bytes 14488064 | tf_op jit(solution)/shard_map/dot_general | solution.py:53
  278.9 0.0 all-to-all-done.2
  278.9 4.7 %all-to-all-start.3 = ((bf16[16,3,16,256]{3,2,1,0:T(8,128)(2,1)}), bf16[16,3,16,256]{3,2,1,0:T(8,128)(2,1)S(1)}, u32[]{:S(2)}, u32[]{:S(2)}) async-start(bf16[16,3,16,256]{3,2,1,0:T(8,128)(2,1)} %bitcast.9), calls=%async_computation.3 | async-start | bytes 786432 | tf_op jit(solution)/shard_map/all_to_all | solution.py:56
  283.6 0.1 maximum_bitcast_fusion
  283.7 10.7 %all-to-all-done.3 = bf16[16,3,16,256]{3,2,1,0:T(8,128)(2,1)S(1)} async-done(((bf16[16,3,16,256]{3,2,1,0:T(8,128)(2,1)}), bf16[16,3,16,256]{3,2,1,0:T(8,128)(2,1)S(1)}, u32[]{:S(2)}, u32[]{:S(2)}) %all-to-all-start.3) | async-done | bytes 393248 | tf_op jit(solution)/shard_map/all_to_all | solution.py:56
  294.3 0.1 maximum_bitcast_fusion.1
  294.4 0.1 pad_maximum_fusion
  294.6 1.3 copy.8
  295.9 0.6 copy.10
  (3 shorter events, 0.0 us)
Async XLA Ops:
  7.2 62.6 %all-gather.9.cloned.1.call-start = ((), (), s32[]{:S(2)}) async-start(), calls=%async_computation.5 | async-start | bytes 5988352 | tf_op jit(solution)/shard_map/all_gather | solution.py:19
  9.7 126.9 %all-gather.11.cloned.1.call-start = ((), (), s32[]{:S(2)}) async-start(), calls=%async_computation.6 | async-start | bytes 5988352 | tf_op jit(solution)/shard_map/all_gather | solution.py:19
  10.4 193.0 %all-gather.13.cloned.1.call-start = ((), (), s32[]{:S(2)}) async-start(), calls=%async_computation.7 | async-start | bytes 5988352 | tf_op jit(solution)/shard_map/all_gather | solution.py:19
  11.1 258.9 %all-gather.15.cloned.1.call-start = ((), (), s32[]{:S(2)}) async-start(), calls=%async_computation.8 | async-start | bytes 5988352 | tf_op jit(solution)/shard_map/all_gather | solution.py:19
  14.1 64.4 %all-to-all-start.4 = ((s32[16,1,16]{2,1,0:T(1,128)}), s32[16,1,16]{2,1,0:T(1,128)S(1)}, u32[]{:S(2)}, u32[]{:S(2)}) async-start(s32[16,1,16]{2,1,0:T(1,128)} %sub.19), calls=%async_computation.4 | async-start | bytes 16384 | tf_op jit(solution)/shard_map/all_to_all | solution.py:36
  78.5 66.8 %all-to-all-start = ((bf16[16,3,16,256]{3,2,1,0:T(8,128)(2,1)}), bf16[16,3,16,256]{3,2,1,0:T(8,128)(2,1)S(1)}, u32[]{:S(2)}, u32[]{:S(2)}) async-start(bf16[16,3,16,256]{3,2,1,0:T(8,128)(2,1)} %bitcast.2), calls=%async_computation | async-start | bytes 786432 | tf_op jit(solution)/shard_map/all_to_all | solution.py:56
  145.4 66.9 %all-to-all-start.1 = ((bf16[16,3,16,256]{3,2,1,0:T(8,128)(2,1)}), bf16[16,3,16,256]{3,2,1,0:T(8,128)(2,1)S(1)}, u32[]{:S(2)}, u32[]{:S(2)}) async-start(bf16[16,3,16,256]{3,2,1,0:T(8,128)(2,1)} %bitcast.4), calls=%async_computation.1 | async-start | bytes 786432 | tf_op jit(solution)/shard_map/all_to_all | solution.py:56
  212.2 66.7 %all-to-all-start.2 = ((bf16[16,3,16,256]{3,2,1,0:T(8,128)(2,1)}), bf16[16,3,16,256]{3,2,1,0:T(8,128)(2,1)S(1)}, u32[]{:S(2)}, u32[]{:S(2)}) async-start(bf16[16,3,16,256]{3,2,1,0:T(8,128)(2,1)} %bitcast.7), calls=%async_computation.2 | async-start | bytes 786432 | tf_op jit(solution)/shard_map/all_to_all | solution.py:56
  278.9 15.5 %all-to-all-start.3 = ((bf16[16,3,16,256]{3,2,1,0:T(8,128)(2,1)}), bf16[16,3,16,256]{3,2,1,0:T(8,128)(2,1)S(1)}, u32[]{:S(2)}, u32[]{:S(2)}) async-start(bf16[16,3,16,256]{3,2,1,0:T(8,128)(2,1)} %bitcast.9), calls=%async_computation.3 | async-start | bytes 786432 | tf_op jit(solution)/shard_map/all_to_all | solution.py:56
Sparse Core Ops, SparseCore 0:
  10.9 58.8 all-gather.8
  72.0 64.5 all-gather.10
  138.8 64.5 all-gather.12
  205.5 64.4 all-gather.14

commit v2 on v1

v2 whole, which is shorter than its diff:
```python
import jax
import jax.numpy as jnp
from jax import lax
from jax.sharding import PartitionSpec as P

GRID_RING = [0, 1, 3, 5, 7, 6, 4, 2]
LAG = 3


def routing(owners, count, slots, block_rows):
    blocks_here = owners.shape[0]
    rows = blocks_here * block_rows
    owner_col = owners[:, 0]
    same = owner_col[:, None] == owner_col[None, :]
    lower = jnp.arange(blocks_here)[:, None] > jnp.arange(blocks_here)[None, :]
    rank = jnp.sum((same & lower).astype(jnp.int32), axis=1)
    target = owner_col * slots + rank
    select = jnp.arange(count * slots, dtype=jnp.int32)[:, None] == target[None, :]
    global_ids = lax.axis_index("wide") * blocks_here + jnp.arange(blocks_here, dtype=jnp.int32)
    labels = jnp.sum(jnp.where(select, global_ids[None, :] + 1, 0), axis=1) - 1
    row_at = jnp.arange(rows, dtype=jnp.int32)
    out_at = jnp.arange(count * block_rows * slots, dtype=jnp.int32)
    row_key = jnp.repeat(target, block_rows) * block_rows + row_at % block_rows
    out_key = (
        out_at // (block_rows * slots) * slots + out_at % slots
    ) * block_rows + out_at // slots % block_rows
    place = (out_key[:, None] == row_key[None, :]).astype(jnp.bfloat16)
    return labels.reshape(count, slots), place


def local(gamma, coefficients, owners):
    count = lax.axis_size("wide")
    blocks_here = owners.shape[0]
    slots = max(2, 2 * blocks_here // count)
    rows, nvirt = coefficients.shape
    block_rows = rows // blocks_here
    norb, depth, naux = gamma.shape
    chips = count // 2
    half = naux // 2

    labels, place = routing(owners, count, slots, block_rows)

    def send(i_back):
        out = jnp.dot(place, i_back, preferred_element_type=jnp.float32)
        out = out.astype(jnp.bfloat16).reshape(count, block_rows, slots, naux)
        return lax.all_to_all(out, "wide", split_axis=0, concat_axis=0, tiled=True)

    ids = lax.all_to_all(labels, "wide", split_axis=0, concat_axis=0, tiled=True)

    if chips != len(GRID_RING):
        gathered = lax.all_gather(gamma, "wide", axis=1, tiled=True)
        arrived = [
            send(
                jnp.dot(
                    coefficients, gathered[i], preferred_element_type=jnp.float32
                ).astype(jnp.bfloat16)
            )
            for i in range(norb)
        ]
        placed = jnp.concatenate(arrived, axis=1).transpose(0, 2, 1, 3)
        return placed[None], ids[None]

    ring = GRID_RING
    me = lax.axis_index("wide")
    core = me % 2
    ring_at = jnp.asarray(ring, jnp.int32)
    place_of = jnp.asarray([ring.index(c) for c in range(chips)], jnp.int32)
    here = place_of[me // 2]
    swap = [(d, d ^ 1) for d in range(count)]
    by_source = coefficients.reshape(rows, count, depth).transpose(1, 0, 2)

    def shift(step):
        return [
            (2 * ring[p] + k, 2 * ring[(p + step) % chips] + k)
            for p in range(chips)
            for k in range(2)
        ]

    pieces = {}
    total = {}
    for i in range(norb):
        for d in range(2):
            pieces[i, d] = [gamma[i, :, d * half : (d + 1) * half]]
            total[i, d] = jnp.zeros((rows, half), jnp.float32)
    for tick in range(chips - 1 + LAG * (norb - 1)):
        for i in range(norb):
            t = tick - LAG * i
            if not 0 <= t < chips - 1:
                continue
            for d in range(2):
                block = pieces[i, d][t]
                if i:
                    ahead = min(chips - 1, t + LAG)
                    block, pieces[i - 1, d][ahead] = lax.optimization_barrier(
                        (block, pieces[i - 1, d][ahead])
                    )
                pieces[i, d].append(lax.ppermute(block, "wide", shift(1 - 2 * d)))

    arrived = []
    for i in range(norb):
        outs = []
        for d in range(2):
            acc = None
            for t in range(chips):
                own = pieces[i, d][t]
                other = lax.ppermute(own, "wide", swap)
                chip = ring_at[(here - t * (1 - 2 * d)) % chips]
                for block, which in ((own, core), (other, 1 - core)):
                    left = lax.dynamic_index_in_dim(by_source, 2 * chip + which, 0, False)
                    term = jnp.dot(left, block, preferred_element_type=jnp.float32)
                    acc = term if acc is None else acc + term
            outs.append(acc.astype(jnp.bfloat16))
        arrived.append(send(jnp.concatenate(outs, axis=1)))
    placed = jnp.concatenate(arrived, axis=1).transpose(0, 2, 1, 3)
    return placed[None], ids[None]


def solution(mesh):
    placed = (P("groups", "wide", None), P("wide", None), P("wide", None))
    return jax.shard_map(
        local,
        mesh=mesh,
        in_specs=placed,
        out_specs=(P("wide", None, "groups", None, None), P("wide", "groups", None)),
        check_vma=False,
    )
```

time: 306 us -> 240 us (0.78)
  waiting for transfers between devices: 221 us -> 71.3 us
  starting transfers between devices: 25.4 us -> 76 us
  local copies, waits for them, and re-layouts: 5.29 us -> 19.5 us
  matrix products: 35.2 us -> 46.2 us
  between operations: 13.8 us -> 22.3 us
    all_gather x4 -> x0, waiting for transfers between devices: 209 us -> none  [local(): lax.all_gather(gamma[i, :, j * width:(j + 1) * width], 'wide', axis=0, ti...]
    ppermute x0 -> x60, starting transfers between devices: none -> 60.6 us  [the longest x32 38.6 us: local(): other = lax.ppermute(own, 'wide', swap)]
    ppermute x0 -> x60, waiting for transfers between devices: none -> 42 us  [the longest x28 41.9 us: local(): pieces[i, d].append(lax.ppermute(block, 'wide', shift(1 - 2 * d)))]
    all_to_all x4 -> x2, waiting for transfers between devices: 10.7 us -> 29.3 us  [send(): return lax.all_to_all(out, 'wide', split_axis=0, concat_axis=0, tiled=True)]
    unnamed x1 -> x8, local copies, waits for them, and re-layouts: 0.6 us -> 12.8 us
    dot_general x4 -> x66, matrix products: 35.2 us -> 46.2 us  [the longest x64 43.2 us: local(): term = jnp.dot(left, block, preferred_element_type=jnp.float32)]
    all_to_all x4 -> x2, starting transfers between devices: 18.7 us -> 9.39 us  [send(): return lax.all_to_all(out, 'wide', split_axis=0, concat_axis=0, tiled=True)]
    dynamic_slice x0 -> x2, local copies, waits for them, and re-layouts: none -> 3.26 us  [the longest x1 1.96 us: local(): chip = ring_at[(here - t * (1 - 2 * d)) % chips]]
  transfers between devices with their start and end apart: 9 -> 63, of which waited for: 5 -> 18; matrix products, arithmetic and copies ran while one was open for 13% -> 27% of each run, Pallas kernels for 0% -> 0%
where the time goes in v2:
time: 240 us; the launch traced here: 238 us
  starting transfers between devices  76 us (32%)
  waiting for transfers between devices  71.3 us (30%)
  matrix products  46.2 us (19%)
  between operations  22.3 us (9%)
  local copies, waits for them, and re-layouts  19.5 us (8%)
  other arithmetic  2.99 us (1%)
    dot_general x64, matrix products, local(): term = jnp.dot(left, block, preferred_element_type=jnp.float32)  43.2 us
    ppermute x28, waiting for transfers between devices, local(): pieces[i, d].append(lax.ppermute(block, 'wide', shift(1 - 2 * d)))  41.9 us
    ppermute x32, starting transfers between devices, local(): other = lax.ppermute(own, 'wide', swap)  38.6 us
    all_to_all x2, waiting for transfers between devices, send(): return lax.all_to_all(out, 'wide', split_axis=0, concat_axis=0, tiled=True)  29.3 us
    ppermute x28, starting transfers between devices, local(): pieces[i, d].append(lax.ppermute(block, 'wide', shift(1 - 2 * d)))  21.9 us
    unnamed x8, local copies, waits for them, and re-layouts  12.8 us
    all_to_all x2, starting transfers between devices, send(): return lax.all_to_all(out, 'wide', split_axis=0, concat_axis=0, tiled=True)  9.39 us
    all_to_all x1, starting transfers between devices, local(): lax.all_to_all(labels, 'wide', split_axis=0, concat_axis=0, tiled=True)  5.99 us
  transfers between devices with their start and end apart: 63, of which 18 were waited for; matrix products, arithmetic and copies ran while one was open for 27% of the time, Pallas kernels for 0%

profile of v2, /device:TPU:13, one launch (start us, length us, event | category | flops | bytes accessed | tf_op | source)
XLA Modules:
  0.0 238.2 jit_solution(53139500714450081)
XLA Ops:
  0.6 2.4 %slice_bitcast_fusion.3 = (bf16[688,256]{1,0:T(8,128)(2,1)}, bf16[688,256]{1,0:T(8,128)(2,1)}, bf16[688,256]{1,0:T(8,128)(2,1)}, bf16[688,256]{1,0:T(8,128)(2,1)}) fusion(bf16[2,688,512]{2,1,0:T(8,128)(2,1)} %param.5), kind=kLoop, calls=%fused_computation.236 | loop fusion | bytes 2818048 | tf_op jit(solution)/shard_map/squeeze | solution.py:83
  3.7 1.3 collective-permute-start.1
  8.4 6.0 %all-to-all-start.2 = ((s32[16,1,16]{2,1,0:T(1,128)}), s32[16,1,16]{2,1,0:T(1,128)S(1)}, u32[]{:S(2)}, u32[]{:S(2)}) async-start(s32[16,1,16]{2,1,0:T(1,128)} %sub.67), calls=%async_computation.2 | async-start | bytes 16384 | tf_op jit(solution)/shard_map/all_to_all | solution.py:48
  14.4 1.3 dynamic_slice.130
  26.7 2.0 fusion.300
  33.7 12.2 %copy.9 = bf16[384,11008]{0,1:T(8,128)(2,1)} copy(bf16[384,11008]{1,0:T(8,128)(2,1)} %param.6) | data formatting | bytes 16908288 | tf_op args[1]
  45.9 1.5 fusion.140
  47.4 1.5 fusion.138
  53.4 1.5 fusion.136
  55.4 1.6 fusion.134
  57.4 1.2 collective-permute-start.3
  58.6 1.6 convolution_add_fusion.31
  60.2 1.5 convolution_add_fusion.30
  62.5 1.6 convolution_add_fusion.24
  64.1 1.5 convolution_add_fusion.23
  66.0 1.6 convolution_add_fusion.17
  68.0 1.2 collective-permute-start.5
  69.7 2.4 collective-permute-done.24
  73.2 4.6 %collective-permute-done.5 = bf16[688,256]{1,0:T(8,128)(2,1)S(1)} collective-permute-done((bf16[688,256]{1,0:T(8,128)(2,1)S(1)}, bf16[688,256]{1,0:T(8,128)(2,1)S(1)}, u32[]{:S(2)}, u32[]{:S(2)}) %collective-permute-start.5) | collective-permute-done | bytes 352288 | tf_op jit(solution)/shard_map/ppermute | solution.py:97
  79.1 1.2 collective-permute-start.7
  80.9 1.8 collective-permute-start.27
  83.0 1.2 collective-permute-start.8
  84.8 4.4 %collective-permute-done.7 = bf16[688,256]{1,0:T(8,128)(2,1)S(1)} collective-permute-done((bf16[688,256]{1,0:T(8,128)(2,1)}, bf16[688,256]{1,0:T(8,128)(2,1)S(1)}, u32[]{:S(2)}, u32[]{:S(2)}) %collective-permute-start.7) | collective-permute-done | bytes 352288 | tf_op jit(solution)/shard_map/ppermute | solution.py:97
  89.3 1.2 collective-permute-start.4
  90.9 5.9 %collective-permute-done.8 = bf16[688,256]{1,0:T(8,128)(2,1)S(1)} collective-permute-done((bf16[688,256]{1,0:T(8,128)(2,1)S(1)}, bf16[688,256]{1,0:T(8,128)(2,1)S(1)}, u32[]{:S(2)}, u32[]{:S(2)}) %collective-permute-start.8) | collective-permute-done | bytes 352288 | tf_op jit(solution)/shard_map/ppermute | solution.py:97
  97.6 2.5 %collective-permute-done.29 = bf16[688,256]{1,0:T(8,128)(2,1)S(1)} collective-permute-done((bf16[688,256]{1,0:T(8,128)(2,1)S(1)}, bf16[688,256]{1,0:T(8,128)(2,1)S(1)}, u32[]{:S(2)}, u32[]{:S(2)}) %collective-permute-start.29) | collective-permute-done | bytes 352288 | tf_op jit(solution)/shard_map/ppermute | solution.py:97
  100.1 1.2 collective-permute-start.10
  102.0 1.2 collective-permute-start.11
  105.3 3.8 %collective-permute-done.10 = bf16[688,256]{1,0:T(8,128)(2,1)S(1)} collective-permute-done((bf16[688,256]{1,0:T(8,128)(2,1)S(1)}, bf16[688,256]{1,0:T(8,128)(2,1)S(1)}, u32[]{:S(2)}, u32[]{:S(2)}) %collective-permute-start.10) | collective-permute-done | bytes 352288 | tf_op jit(solution)/shard_map/ppermute | solution.py:97
  109.1 2.9 %collective-permute-start.30 = (bf16[688,256]{1,0:T(8,128)(2,1)S(1)}, bf16[688,256]{1,0:T(8,128)(2,1)S(1)}, u32[]{:S(2)}, u32[]{:S(2)}) collective-permute-start(bf16[688,256]{1,0:T(8,128)(2,1)S(1)} %collective-permute-done.29), channel_id=1, source_target_pairs={{0,1},{1,0},{2,3},{3,2},{4,5},{5,4},{6,7},{7,6},{8,9},{9,8},{10,11... | collective-permute-start | bytes 1056776 | tf_op jit(solution)/shard_map/ppermute | solution.py:106
  112.0 4.6 %collective-permute-done.11 = bf16[688,256]{1,0:T(8,128)(2,1)S(1)} collective-permute-done((bf16[688,256]{1,0:T(8,128)(2,1)S(1)}, bf16[688,256]{1,0:T(8,128)(2,1)S(1)}, u32[]{:S(2)}, u32[]{:S(2)}) %collective-permute-start.11) | collective-permute-done | bytes 352288 | tf_op jit(solution)/shard_map/ppermute | solution.py:97
  116.6 1.7 collective-permute-start.43
  118.3 1.4 collective-permute-start.13
  121.3 1.2 collective-permute-start.14
  124.7 2.1 collective-permute-start.12
  127.4 3.3 %collective-permute-start.33 = (bf16[688,256]{1,0:T(8,128)(2,1)S(1)}, bf16[688,256]{1,0:T(8,128)(2,1)S(1)}, u32[]{:S(2)}, u32[]{:S(2)}) collective-permute-start(bf16[688,256]{1,0:T(8,128)(2,1)S(1)} %collective-permute-done.32), channel_id=1, source_target_pairs={{0,1},{1,0},{2,3},{3,2},{4,5},{5,4},{6,7},{7,6},{8,9},{9,8},{10,11... | collective-permute-start | bytes 1056776 | tf_op jit(solution)/shard_map/ppermute | solution.py:106
  130.6 4.3 %collective-permute-done.14 = bf16[688,256]{1,0:T(8,128)(2,1)S(1)} collective-permute-done((bf16[688,256]{1,0:T(8,128)(2,1)S(1)}, bf16[688,256]{1,0:T(8,128)(2,1)S(1)}, u32[]{:S(2)}, u32[]{:S(2)}) %collective-permute-start.14) | collective-permute-done | bytes 352288 | tf_op jit(solution)/shard_map/ppermute | solution.py:97
  134.9 1.8 collective-permute-start.44
  143.1 2.6 %collective-permute-start.45 = (bf16[688,256]{1,0:T(8,128)(2,1)S(1)}, bf16[688,256]{1,0:T(8,128)(2,1)S(1)}, u32[]{:S(2)}, u32[]{:S(2)}) collective-permute-start(bf16[688,256]{1,0:T(8,128)(2,1)S(1)} %collective-permute-done.13), channel_id=1, source_target_pairs={{0,1},{1,0},{2,3},{3,2},{4,5},{5,4},{6,7},{7,6},{8,9},{9,8},{10,11... | collective-permute-start | bytes 1056776 | tf_op jit(solution)/shard_map/ppermute | solution.py:106
  146.1 3.4 %collective-permute-start.15 = (bf16[688,256]{1,0:T(8,128)(2,1)S(1)}, bf16[688,256]{1,0:T(8,128)(2,1)S(1)}, u32[]{:S(2)}, u32[]{:S(2)}) collective-permute-start(bf16[688,256]{1,0:T(8,128)(2,1)S(1)} %collective-permute-done.14), channel_id=1, source_target_pairs={{0,1},{1,0},{2,3},{3,2},{4,5},{5,4},{6,7},{7,6},{8,9},{9,8},{10,11... | collective-permute-start | bytes 1056776 | tf_op jit(solution)/shard_map/ppermute | solution.py:106
  149.6 3.3 %collective-permute-done.17 = bf16[688,256]{1,0:T(8,128)(2,1)S(1)} collective-permute-done((bf16[688,256]{1,0:T(8,128)(2,1)S(1)}, bf16[688,256]{1,0:T(8,128)(2,1)S(1)}, u32[]{:S(2)}, u32[]{:S(2)}) %collective-permute-start.17) | collective-permute-done | bytes 352288 | tf_op jit(solution)/shard_map/ppermute | solution.py:97
  152.8 2.3 collective-permute-start.36
  158.1 2.0 collective-permute-start.46
  161.5 2.1 collective-permute-done.18
  163.6 1.7 collective-permute-start.19
  165.4 2.7 %collective-permute-start.47 = (bf16[688,256]{1,0:T(8,128)(2,1)S(1)}, bf16[688,256]{1,0:T(8,128)(2,1)S(1)}, u32[]{:S(2)}, u32[]{:S(2)}) collective-permute-start(bf16[688,256]{1,0:T(8,128)(2,1)S(1)} %collective-permute-done.18), channel_id=1, source_target_pairs={{0,1},{1,0},{2,3},{3,2},{4,5},{5,4},{6,7},{7,6},{8,9},{9,8},{10,11... | collective-permute-start | bytes 1056776 | tf_op jit(solution)/shard_map/ppermute | solution.py:106
  169.9 1.3 collective-permute-done.19
  171.2 3.0 %collective-permute-start.20 = (bf16[688,256]{1,0:T(8,128)(2,1)S(1)}, bf16[688,256]{1,0:T(8,128)(2,1)S(1)}, u32[]{:S(2)}, u32[]{:S(2)}) collective-permute-start(bf16[688,256]{1,0:T(8,128)(2,1)S(1)} %collective-permute-done.17), channel_id=1, source_target_pairs={{0,1},{1,0},{2,3},{3,2},{4,5},{5,4},{6,7},{7,6},{8,9},{9,8},{10,11... | collective-permute-start | bytes 1056776 | tf_op jit(solution)/shard_map/ppermute | solution.py:106
  174.7 1.4 collective-permute-start.41
  176.9 1.3 collective-permute-start.58
  182.4 1.5 fusion.4
  183.9 2.1 collective-permute-done.49
  186.1 1.4 fusion.91
  188.4 4.4 %all-to-all-start = ((bf16[16,3,16,512]{3,2,1,0:T(8,128)(2,1)}), bf16[16,3,16,512]{3,2,1,0:T(8,128)(2,1)S(1)}, u32[]{:S(2)}, u32[]{:S(2)}) async-start(bf16[16,3,16,512]{3,2,1,0:T(8,128)(2,1)} %bitcast.52), calls=%async_computation | async-start | bytes 1572864 | tf_op jit(solution)/shard_map/all_to_all | solution.py:46
  192.9 1.6 fusion.16
  194.4 1.6 fusion.49
  196.0 1.6 fusion.10
  197.6 1.5 fusion.40
  199.1 1.5 fusion.41
  200.6 1.5 fusion.7
  202.1 10.0 %all-to-all-done = bf16[16,3,16,512]{3,2,1,0:T(8,128)(2,1)S(1)} async-done(((bf16[16,3,16,512]{3,2,1,0:T(8,128)(2,1)}), bf16[16,3,16,512]{3,2,1,0:T(8,128)(2,1)S(1)}, u32[]{:S(2)}, u32[]{:S(2)}) %all-to-all-start) | async-done | bytes 786464 | tf_op jit(solution)/shard_map/all_to_all | solution.py:46
  212.1 5.0 %all-to-all-start.1 = ((bf16[16,3,16,512]{3,2,1,0:T(8,128)(2,1)}), bf16[16,3,16,512]{3,2,1,0:T(8,128)(2,1)S(1)}, u32[]{:S(2)}, u32[]{:S(2)}) async-start(bf16[16,3,16,512]{3,2,1,0:T(8,128)(2,1)} %bitcast.53), calls=%async_computation.1 | async-start | bytes 1572864 | tf_op jit(solution)/shard_map/all_to_all | solution.py:46
  217.0 19.2 %all-to-all-done.1 = bf16[16,3,16,512]{3,2,1,0:T(8,128)(2,1)S(1)} async-done(((bf16[16,3,16,512]{3,2,1,0:T(8,128)(2,1)}), bf16[16,3,16,512]{3,2,1,0:T(8,128)(2,1)S(1)}, u32[]{:S(2)}, u32[]{:S(2)}) %all-to-all-start.1) | async-done | bytes 786464 | tf_op jit(solution)/shard_map/all_to_all | solution.py:46
  236.3 1.3 maximum_bitcast_fusion
  (149 shorter events, 38.7 us)
Async XLA Ops:
  3.0 53.9 %collective-permute-start = (bf16[688,256]{1,0:T(8,128)(2,1)}, bf16[688,256]{1,0:T(8,128)(2,1)}, u32[]{:S(2)}, u32[]{:S(2)}) collective-permute-start(bf16[688,256]{1,0:T(8,128)(2,1)} %get-tuple-element.60), channel_id=1, source_target_pairs={{0,1},{1,0},{2,3},{3,2},{4,5},{5,4},{6,7},{7,6},{8,9},{9,8},{10,11... | collective-permute-start | bytes 1056776 | tf_op jit(solution)/shard_map/ppermute | solution.py:106
  3.7 53.7 %collective-permute-start.1 = (bf16[688,256]{1,0:T(8,128)(2,1)}, bf16[688,256]{1,0:T(8,128)(2,1)S(1)}, u32[]{:S(2)}, u32[]{:S(2)}) collective-permute-start(bf16[688,256]{1,0:T(8,128)(2,1)} %get-tuple-element.60), channel_id=1, source_target_pairs={{0,2},{1,3},{2,6},{3,7},{6,10},{7,11},{10,14},{11,15},{14,12},{15,... | collective-permute-start | bytes 1056776 | tf_op jit(solution)/shard_map/ppermute | solution.py:97
  5.0 56.7 %collective-permute-start.21 = (bf16[688,256]{1,0:T(8,128)(2,1)}, bf16[688,256]{1,0:T(8,128)(2,1)}, u32[]{:S(2)}, u32[]{:S(2)}) collective-permute-start(bf16[688,256]{1,0:T(8,128)(2,1)} %get-tuple-element.63), channel_id=1, source_target_pairs={{0,1},{1,0},{2,3},{3,2},{4,5},{5,4},{6,7},{7,6},{8,9},{9,8},{10,11... | collective-permute-start | bytes 1056776 | tf_op jit(solution)/shard_map/ppermute | solution.py:106
  5.3 56.9 %collective-permute-start.22 = (bf16[688,256]{1,0:T(8,128)(2,1)}, bf16[688,256]{1,0:T(8,128)(2,1)S(1)}, u32[]{:S(2)}, u32[]{:S(2)}) collective-permute-start(bf16[688,256]{1,0:T(8,128)(2,1)} %get-tuple-element.63), channel_id=1, source_target_pairs={{0,4},{1,5},{2,0},{3,1},{6,2},{7,3},{10,6},{11,7},{14,10},{15,11},... | collective-permute-start | bytes 1056776 | tf_op jit(solution)/shard_map/ppermute | solution.py:97
  5.5 60.1 %collective-permute-start.42 = (bf16[688,256]{1,0:T(8,128)(2,1)}, bf16[688,256]{1,0:T(8,128)(2,1)}, u32[]{:S(2)}, u32[]{:S(2)}) collective-permute-start(bf16[688,256]{1,0:T(8,128)(2,1)} %get-tuple-element.31), channel_id=1, source_target_pairs={{0,1},{1,0},{2,3},{3,2},{4,5},{5,4},{6,7},{7,6},{8,9},{9,8},{10,11... | collective-permute-start | bytes 1056776 | tf_op jit(solution)/shard_map/ppermute | solution.py:106
  8.4 180.1 %all-to-all-start.2 = ((s32[16,1,16]{2,1,0:T(1,128)}), s32[16,1,16]{2,1,0:T(1,128)S(1)}, u32[]{:S(2)}, u32[]{:S(2)}) async-start(s32[16,1,16]{2,1,0:T(1,128)} %sub.67), calls=%async_computation.2 | async-start | bytes 16384 | tf_op jit(solution)/shard_map/all_to_all | solution.py:48
  57.0 10.5 %collective-permute-start.51 = (bf16[688,256]{1,0:T(8,128)(2,1)}, bf16[688,256]{1,0:T(8,128)(2,1)S(1)}, u32[]{:S(2)}, u32[]{:S(2)}) collective-permute-start(bf16[688,256]{1,0:T(8,128)(2,1)} %get-tuple-element.44), channel_id=1, source_target_pairs={{0,1},{1,0},{2,3},{3,2},{4,5},{5,4},{6,7},{7,6},{8,9},{9,8},{10,11... | collective-permute-start | bytes 1056776 | tf_op jit(solution)/shard_map/ppermute | solution.py:106
  57.4 10.6 %collective-permute-start.3 = (bf16[688,256]{1,0:T(8,128)(2,1)S(1)}, bf16[688,256]{1,0:T(8,128)(2,1)S(1)}, u32[]{:S(2)}, u32[]{:S(2)}) collective-permute-start(bf16[688,256]{1,0:T(8,128)(2,1)S(1)} %collective-permute-done.1), channel_id=1, source_target_pairs={{0,2},{1,3},{2,6},{3,7},{6,10},{7,11},{10,14},{11,15},{14,12},{15,... | collective-permute-start | bytes 1056776 | tf_op jit(solution)/shard_map/ppermute | solution.py:97
  60.2 22.5 %copy-start.2 = (bf16[688,256]{1,0:T(8,128)(2,1)S(1)}, bf16[688,256]{1,0:T(8,128)(2,1)}, u32[]{:S(2)}) copy-start(bf16[688,256]{1,0:T(8,128)(2,1)} %get-tuple-element.44) | copy-start | bytes 1056772
  61.7 11.0 %collective-permute-start.2 = (bf16[688,256]{1,0:T(8,128)(2,1)S(1)}, bf16[688,256]{1,0:T(8,128)(2,1)S(1)}, u32[]{:S(2)}, u32[]{:S(2)}) collective-permute-start(bf16[688,256]{1,0:T(8,128)(2,1)S(1)} %collective-permute-done.1), channel_id=1, source_target_pairs={{0,1},{1,0},{2,3},{3,2},{4,5},{5,4},{6,7},{7,6},{8,9},{9,8},{10,11... | collective-permute-start | bytes 1056776 | tf_op jit(solution)/shard_map/ppermute | solution.py:106
  62.2 9.8 %collective-permute-start.24 = (bf16[688,256]{1,0:T(8,128)(2,1)S(1)}, bf16[688,256]{1,0:T(8,128)(2,1)S(1)}, u32[]{:S(2)}, u32[]{:S(2)}) collective-permute-start(bf16[688,256]{1,0:T(8,128)(2,1)S(1)} %collective-permute-done.22), channel_id=1, source_target_pairs={{0,4},{1,5},{2,0},{3,1},{6,2},{7,3},{10,6},{11,7},{14,10},{15,11},... | collective-permute-start | bytes 1056776 | tf_op jit(solution)/shard_map/ppermute | solution.py:97
  65.6 13.2 %collective-permute-start.23 = (bf16[688,256]{1,0:T(8,128)(2,1)S(1)}, bf16[688,256]{1,0:T(8,128)(2,1)S(1)}, u32[]{:S(2)}, u32[]{:S(2)}) collective-permute-start(bf16[688,256]{1,0:T(8,128)(2,1)S(1)} %collective-permute-done.22), channel_id=1, source_target_pairs={{0,1},{1,0},{2,3},{3,2},{4,5},{5,4},{6,7},{7,6},{8,9},{9,8},{10,11... | collective-permute-start | bytes 1056776 | tf_op jit(solution)/shard_map/ppermute | solution.py:106
  68.0 9.7 %collective-permute-start.5 = (bf16[688,256]{1,0:T(8,128)(2,1)S(1)}, bf16[688,256]{1,0:T(8,128)(2,1)S(1)}, u32[]{:S(2)}, u32[]{:S(2)}) collective-permute-start(bf16[688,256]{1,0:T(8,128)(2,1)S(1)} %collective-permute-done.3), channel_id=1, source_target_pairs={{0,2},{1,3},{2,6},{3,7},{6,10},{7,11},{10,14},{11,15},{14,12},{15,... | collective-permute-start | bytes 1056776 | tf_op jit(solution)/shard_map/ppermute | solution.py:97
  72.0 8.9 %collective-permute-start.26 = (bf16[688,256]{1,0:T(8,128)(2,1)S(1)}, bf16[688,256]{1,0:T(8,128)(2,1)S(1)}, u32[]{:S(2)}, u32[]{:S(2)}) collective-permute-start(bf16[688,256]{1,0:T(8,128)(2,1)S(1)} %collective-permute-done.24), channel_id=1, source_target_pairs={{0,4},{1,5},{2,0},{3,1},{6,2},{7,3},{10,6},{11,7},{14,10},{15,11},... | collective-permute-start | bytes 1056776 | tf_op jit(solution)/shard_map/ppermute | solution.py:97
  77.7 6.4 %collective-permute-start.6 = (bf16[688,256]{1,0:T(8,128)(2,1)S(1)}, bf16[688,256]{1,0:T(8,128)(2,1)S(1)}, u32[]{:S(2)}, u32[]{:S(2)}) collective-permute-start(bf16[688,256]{1,0:T(8,128)(2,1)S(1)} %collective-permute-done.5), channel_id=1, source_target_pairs={{0,1},{1,0},{2,3},{3,2},{4,5},{5,4},{6,7},{7,6},{8,9},{9,8},{10,11... | collective-permute-start | bytes 1056776 | tf_op jit(solution)/shard_map/ppermute | solution.py:106
  79.1 10.1 %collective-permute-start.7 = (bf16[688,256]{1,0:T(8,128)(2,1)}, bf16[688,256]{1,0:T(8,128)(2,1)S(1)}, u32[]{:S(2)}, u32[]{:S(2)}) collective-permute-start(bf16[688,256]{1,0:T(8,128)(2,1)} %get-tuple-element.31), channel_id=1, source_target_pairs={{0,2},{1,3},{2,6},{3,7},{6,10},{7,11},{10,14},{11,15},{14,12},{15,... | collective-permute-start | bytes 1056776 | tf_op jit(solution)/shard_map/ppermute | solution.py:97
  80.9 20.3 %collective-permute-start.27 = (bf16[688,256]{1,0:T(8,128)(2,1)S(1)}, bf16[688,256]{1,0:T(8,128)(2,1)S(1)}, u32[]{:S(2)}, u32[]{:S(2)}) collective-permute-start(bf16[688,256]{1,0:T(8,128)(2,1)S(1)} %collective-permute-done.26), channel_id=1, source_target_pairs={{0,1},{1,0},{2,3},{3,2},{4,5},{5,4},{6,7},{7,6},{8,9},{9,8},{10,11... | collective-permute-start | bytes 1056776 | tf_op jit(solution)/shard_map/ppermute | solution.py:106
  82.7 14.9 %collective-permute-start.28 = (bf16[688,256]{1,0:T(8,128)(2,1)S(1)}, bf16[688,256]{1,0:T(8,128)(2,1)S(1)}, u32[]{:S(2)}, u32[]{:S(2)}) collective-permute-start(bf16[688,256]{1,0:T(8,128)(2,1)S(1)} %copy-done.2), channel_id=1, source_target_pairs={{0,4},{1,5},{2,0},{3,1},{6,2},{7,3},{10,6},{11,7},{14,10},{15,11},... | collective-permute-start | bytes 1056776 | tf_op jit(solution)/shard_map/ppermute | solution.py:97
  83.0 13.9 %collective-permute-start.8 = (bf16[688,256]{1,0:T(8,128)(2,1)S(1)}, bf16[688,256]{1,0:T(8,128)(2,1)S(1)}, u32[]{:S(2)}, u32[]{:S(2)}) collective-permute-start(bf16[688,256]{1,0:T(8,128)(2,1)S(1)} %collective-permute-done.5), channel_id=1, source_target_pairs={{0,2},{1,3},{2,6},{3,7},{6,10},{7,11},{10,14},{11,15},{14,12},{15,... | collective-permute-start | bytes 1056776 | tf_op jit(solution)/shard_map/ppermute | solution.py:97
  84.1 15.9 %collective-permute-start.29 = (bf16[688,256]{1,0:T(8,128)(2,1)S(1)}, bf16[688,256]{1,0:T(8,128)(2,1)S(1)}, u32[]{:S(2)}, u32[]{:S(2)}) collective-permute-start(bf16[688,256]{1,0:T(8,128)(2,1)S(1)} %collective-permute-done.26), channel_id=1, source_target_pairs={{0,4},{1,5},{2,0},{3,1},{6,2},{7,3},{10,6},{11,7},{14,10},{15,11},... | collective-permute-start | bytes 1056776 | tf_op jit(solution)/shard_map/ppermute | solution.py:97
  89.3 12.7 %collective-permute-start.4 = (bf16[688,256]{1,0:T(8,128)(2,1)S(1)}, bf16[688,256]{1,0:T(8,128)(2,1)S(1)}, u32[]{:S(2)}, u32[]{:S(2)}) collective-permute-start(bf16[688,256]{1,0:T(8,128)(2,1)S(1)} %collective-permute-done.3), channel_id=1, source_target_pairs={{0,1},{1,0},{2,3},{3,2},{4,5},{5,4},{6,7},{7,6},{8,9},{9,8},{10,11... | collective-permute-start | bytes 1056776 | tf_op jit(solution)/shard_map/ppermute | solution.py:106
  96.8 6.8 %collective-permute-start.25 = (bf16[688,256]{1,0:T(8,128)(2,1)S(1)}, bf16[688,256]{1,0:T(8,128)(2,1)S(1)}, u32[]{:S(2)}, u32[]{:S(2)}) collective-permute-start(bf16[688,256]{1,0:T(8,128)(2,1)S(1)} %collective-permute-done.24), channel_id=1, source_target_pairs={{0,1},{1,0},{2,3},{3,2},{4,5},{5,4},{6,7},{7,6},{8,9},{9,8},{10,11... | collective-permute-start | bytes 1056776 | tf_op jit(solution)/shard_map/ppermute | solution.py:106
  97.6 22.5 %collective-permute-start.9 = (bf16[688,256]{1,0:T(8,128)(2,1)S(1)}, bf16[688,256]{1,0:T(8,128)(2,1)S(1)}, u32[]{:S(2)}, u32[]{:S(2)}) collective-permute-start(bf16[688,256]{1,0:T(8,128)(2,1)S(1)} %collective-permute-done.8), channel_id=1, source_target_pairs={{0,1},{1,0},{2,3},{3,2},{4,5},{5,4},{6,7},{7,6},{8,9},{9,8},{10,11... | collective-permute-start | bytes 1056776 | tf_op jit(solution)/shard_map/ppermute | solution.py:106
  100.1 9.0 %collective-permute-start.10 = (bf16[688,256]{1,0:T(8,128)(2,1)S(1)}, bf16[688,256]{1,0:T(8,128)(2,1)S(1)}, u32[]{:S(2)}, u32[]{:S(2)}) collective-permute-start(bf16[688,256]{1,0:T(8,128)(2,1)S(1)} %collective-permute-done.7), channel_id=1, source_target_pairs={{0,2},{1,3},{2,6},{3,7},{6,10},{7,11},{10,14},{11,15},{14,12},{15,... | collective-permute-start | bytes 1056776 | tf_op jit(solution)/shard_map/ppermute | solution.py:97
  101.3 17.0 %collective-permute-start.31 = (bf16[688,256]{1,0:T(8,128)(2,1)S(1)}, bf16[688,256]{1,0:T(8,128)(2,1)S(1)}, u32[]{:S(2)}, u32[]{:S(2)}) collective-permute-start(bf16[688,256]{1,0:T(8,128)(2,1)S(1)} %collective-permute-done.28), channel_id=1, source_target_pairs={{0,4},{1,5},{2,0},{3,1},{6,2},{7,3},{10,6},{11,7},{14,10},{15,11},... | collective-permute-start | bytes 1056776 | tf_op jit(solution)/shard_map/ppermute | solution.py:97
  102.0 14.6 %collective-permute-start.11 = (bf16[688,256]{1,0:T(8,128)(2,1)S(1)}, bf16[688,256]{1,0:T(8,128)(2,1)S(1)}, u32[]{:S(2)}, u32[]{:S(2)}) collective-permute-start(bf16[688,256]{1,0:T(8,128)(2,1)S(1)} %collective-permute-done.8), channel_id=1, source_target_pairs={{0,2},{1,3},{2,6},{3,7},{6,10},{7,11},{10,14},{11,15},{14,12},{15,... | collective-permute-start | bytes 1056776 | tf_op jit(solution)/shard_map/ppermute | solution.py:97
  103.7 14.7 %collective-permute-start.32 = (bf16[688,256]{1,0:T(8,128)(2,1)S(1)}, bf16[688,256]{1,0:T(8,128)(2,1)S(1)}, u32[]{:S(2)}, u32[]{:S(2)}) collective-permute-start(bf16[688,256]{1,0:T(8,128)(2,1)S(1)} %collective-permute-done.29), channel_id=1, source_target_pairs={{0,4},{1,5},{2,0},{3,1},{6,2},{7,3},{10,6},{11,7},{14,10},{15,11},... | collective-permute-start | bytes 1056776 | tf_op jit(solution)/shard_map/ppermute | solution.py:97
  109.1 12.3 %collective-permute-start.30 = (bf16[688,256]{1,0:T(8,128)(2,1)S(1)}, bf16[688,256]{1,0:T(8,128)(2,1)S(1)}, u32[]{:S(2)}, u32[]{:S(2)}) collective-permute-start(bf16[688,256]{1,0:T(8,128)(2,1)S(1)} %collective-permute-done.29), channel_id=1, source_target_pairs={{0,1},{1,0},{2,3},{3,2},{4,5},{5,4},{6,7},{7,6},{8,9},{9,8},{10,11... | collective-permute-start | bytes 1056776 | tf_op jit(solution)/shard_map/ppermute | solution.py:106
  116.6 6.8 %collective-permute-start.43 = (bf16[688,256]{1,0:T(8,128)(2,1)S(1)}, bf16[688,256]{1,0:T(8,128)(2,1)S(1)}, u32[]{:S(2)}, u32[]{:S(2)}) collective-permute-start(bf16[688,256]{1,0:T(8,128)(2,1)S(1)} %collective-permute-done.7), channel_id=1, source_target_pairs={{0,1},{1,0},{2,3},{3,2},{4,5},{5,4},{6,7},{7,6},{8,9},{9,8},{10,11... | collective-permute-start | bytes 1056776 | tf_op jit(solution)/shard_map/ppermute | solution.py:106
  118.3 6.4 %collective-permute-start.52 = (bf16[688,256]{1,0:T(8,128)(2,1)S(1)}, bf16[688,256]{1,0:T(8,128)(2,1)S(1)}, u32[]{:S(2)}, u32[]{:S(2)}) collective-permute-start(bf16[688,256]{1,0:T(8,128)(2,1)S(1)} %collective-permute-done.28), channel_id=1, source_target_pairs={{0,1},{1,0},{2,3},{3,2},{4,5},{5,4},{6,7},{7,6},{8,9},{9,8},{10,11... | collective-permute-start | bytes 1056776 | tf_op jit(solution)/shard_map/ppermute | solution.py:106
  118.3 9.1 %collective-permute-start.13 = (bf16[688,256]{1,0:T(8,128)(2,1)S(1)}, bf16[688,256]{1,0:T(8,128)(2,1)S(1)}, u32[]{:S(2)}, u32[]{:S(2)}) collective-permute-start(bf16[688,256]{1,0:T(8,128)(2,1)S(1)} %collective-permute-done.10), channel_id=1, source_target_pairs={{0,2},{1,3},{2,6},{3,7},{6,10},{7,11},{10,14},{11,15},{14,12},{15,... | collective-permute-start | bytes 1056776 | tf_op jit(solution)/shard_map/ppermute | solution.py:97
  120.1 16.6 %collective-permute-start.34 = (bf16[688,256]{1,0:T(8,128)(2,1)S(1)}, bf16[688,256]{1,0:T(8,128)(2,1)S(1)}, u32[]{:S(2)}, u32[]{:S(2)}) collective-permute-start(bf16[688,256]{1,0:T(8,128)(2,1)S(1)} %collective-permute-done.31), channel_id=1, source_target_pairs={{0,4},{1,5},{2,0},{3,1},{6,2},{7,3},{10,6},{11,7},{14,10},{15,11},... | collective-permute-start | bytes 1056776 | tf_op jit(solution)/shard_map/ppermute | solution.py:97
  121.3 13.6 %collective-permute-start.14 = (bf16[688,256]{1,0:T(8,128)(2,1)S(1)}, bf16[688,256]{1,0:T(8,128)(2,1)S(1)}, u32[]{:S(2)}, u32[]{:S(2)}) collective-permute-start(bf16[688,256]{1,0:T(8,128)(2,1)S(1)} %collective-permute-done.11), channel_id=1, source_target_pairs={{0,2},{1,3},{2,6},{3,7},{6,10},{7,11},{10,14},{11,15},{14,12},{15,... | collective-permute-start | bytes 1056776 | tf_op jit(solution)/shard_map/ppermute | solution.py:97
  123.4 13.6 %collective-permute-start.35 = (bf16[688,256]{1,0:T(8,128)(2,1)S(1)}, bf16[688,256]{1,0:T(8,128)(2,1)S(1)}, u32[]{:S(2)}, u32[]{:S(2)}) collective-permute-start(bf16[688,256]{1,0:T(8,128)(2,1)S(1)} %collective-permute-done.32), channel_id=1, source_target_pairs={{0,4},{1,5},{2,0},{3,1},{6,2},{7,3},{10,6},{11,7},{14,10},{15,11},... | collective-permute-start | bytes 1056776 | tf_op jit(solution)/shard_map/ppermute | solution.py:97
  124.7 13.7 %collective-permute-start.12 = (bf16[688,256]{1,0:T(8,128)(2,1)S(1)}, bf16[688,256]{1,0:T(8,128)(2,1)S(1)}, u32[]{:S(2)}, u32[]{:S(2)}) collective-permute-start(bf16[688,256]{1,0:T(8,128)(2,1)S(1)} %collective-permute-done.11), channel_id=1, source_target_pairs={{0,1},{1,0},{2,3},{3,2},{4,5},{5,4},{6,7},{7,6},{8,9},{9,8},{10,11... | collective-permute-start | bytes 1056776 | tf_op jit(solution)/shard_map/ppermute | solution.py:106
  127.4 12.4 %collective-permute-start.33 = (bf16[688,256]{1,0:T(8,128)(2,1)S(1)}, bf16[688,256]{1,0:T(8,128)(2,1)S(1)}, u32[]{:S(2)}, u32[]{:S(2)}) collective-permute-start(bf16[688,256]{1,0:T(8,128)(2,1)S(1)} %collective-permute-done.32), channel_id=1, source_target_pairs={{0,1},{1,0},{2,3},{3,2},{4,5},{5,4},{6,7},{7,6},{8,9},{9,8},{10,11... | collective-permute-start | bytes 1056776 | tf_op jit(solution)/shard_map/ppermute | solution.py:106
  134.9 6.8 %collective-permute-start.44 = (bf16[688,256]{1,0:T(8,128)(2,1)S(1)}, bf16[688,256]{1,0:T(8,128)(2,1)S(1)}, u32[]{:S(2)}, u32[]{:S(2)}) collective-permute-start(bf16[688,256]{1,0:T(8,128)(2,1)S(1)} %collective-permute-done.10), channel_id=1, source_target_pairs={{0,1},{1,0},{2,3},{3,2},{4,5},{5,4},{6,7},{7,6},{8,9},{9,8},{10,11... | collective-permute-start | bytes 1056776 | tf_op jit(solution)/shard_map/ppermute | solution.py:106
  136.7 6.3 %collective-permute-start.53 = (bf16[688,256]{1,0:T(8,128)(2,1)S(1)}, bf16[688,256]{1,0:T(8,128)(2,1)S(1)}, u32[]{:S(2)}, u32[]{:S(2)}) collective-permute-start(bf16[688,256]{1,0:T(8,128)(2,1)S(1)} %collective-permute-done.31), channel_id=1, source_target_pairs={{0,1},{1,0},{2,3},{3,2},{4,5},{5,4},{6,7},{7,6},{8,9},{9,8},{10,11... | collective-permute-start | bytes 1056776 | tf_op jit(solution)/shard_map/ppermute | solution.py:106
  137.0 9.1 %collective-permute-start.16 = (bf16[688,256]{1,0:T(8,128)(2,1)S(1)}, bf16[688,256]{1,0:T(8,128)(2,1)S(1)}, u32[]{:S(2)}, u32[]{:S(2)}) collective-permute-start(bf16[688,256]{1,0:T(8,128)(2,1)S(1)} %collective-permute-done.13), channel_id=1, source_target_pairs={{0,2},{1,3},{2,6},{3,7},{6,10},{7,11},{10,14},{11,15},{14,12},{15,... | collective-permute-start | bytes 1056776 | tf_op jit(solution)/shard_map/ppermute | solution.py:97
  138.4 16.8 %collective-permute-start.37 = (bf16[688,256]{1,0:T(8,128)(2,1)S(1)}, bf16[688,256]{1,0:T(8,128)(2,1)S(1)}, u32[]{:S(2)}, u32[]{:S(2)}) collective-permute-start(bf16[688,256]{1,0:T(8,128)(2,1)S(1)} %collective-permute-done.34), channel_id=1, source_target_pairs={{0,4},{1,5},{2,0},{3,1},{6,2},{7,3},{10,6},{11,7},{14,10},{15,11},... | collective-permute-start | bytes 1056776 | tf_op jit(solution)/shard_map/ppermute | solution.py:97
  139.8 13.1 %collective-permute-start.17 = (bf16[688,256]{1,0:T(8,128)(2,1)S(1)}, bf16[688,256]{1,0:T(8,128)(2,1)S(1)}, u32[]{:S(2)}, u32[]{:S(2)}) collective-permute-start(bf16[688,256]{1,0:T(8,128)(2,1)S(1)} %collective-permute-done.14), channel_id=1, source_target_pairs={{0,2},{1,3},{2,6},{3,7},{6,10},{7,11},{10,14},{11,15},{14,12},{15,... | collective-permute-start | bytes 1056776 | tf_op jit(solution)/shard_map/ppermute | solution.py:97
  141.7 13.5 %collective-permute-start.38 = (bf16[688,256]{1,0:T(8,128)(2,1)S(1)}, bf16[688,256]{1,0:T(8,128)(2,1)S(1)}, u32[]{:S(2)}, u32[]{:S(2)}) collective-permute-start(bf16[688,256]{1,0:T(8,128)(2,1)S(1)} %collective-permute-done.35), channel_id=1, source_target_pairs={{0,4},{1,5},{2,0},{3,1},{6,2},{7,3},{10,6},{11,7},{14,10},{15,11},... | collective-permute-start | bytes 1056776 | tf_op jit(solution)/shard_map/ppermute | solution.py:97
  143.1 13.6 %collective-permute-start.45 = (bf16[688,256]{1,0:T(8,128)(2,1)S(1)}, bf16[688,256]{1,0:T(8,128)(2,1)S(1)}, u32[]{:S(2)}, u32[]{:S(2)}) collective-permute-start(bf16[688,256]{1,0:T(8,128)(2,1)S(1)} %collective-permute-done.13), channel_id=1, source_target_pairs={{0,1},{1,0},{2,3},{3,2},{4,5},{5,4},{6,7},{7,6},{8,9},{9,8},{10,11... | collective-permute-start | bytes 1056776 | tf_op jit(solution)/shard_map/ppermute | solution.py:106
  146.1 14.4 %collective-permute-start.15 = (bf16[688,256]{1,0:T(8,128)(2,1)S(1)}, bf16[688,256]{1,0:T(8,128)(2,1)S(1)}, u32[]{:S(2)}, u32[]{:S(2)}) collective-permute-start(bf16[688,256]{1,0:T(8,128)(2,1)S(1)} %collective-permute-done.14), channel_id=1, source_target_pairs={{0,1},{1,0},{2,3},{3,2},{4,5},{5,4},{6,7},{7,6},{8,9},{9,8},{10,11... | collective-permute-start | bytes 1056776 | tf_op jit(solution)/shard_map/ppermute | solution.py:106
  152.8 8.2 %collective-permute-start.36 = (bf16[688,256]{1,0:T(8,128)(2,1)S(1)}, bf16[688,256]{1,0:T(8,128)(2,1)S(1)}, u32[]{:S(2)}, u32[]{:S(2)}) collective-permute-start(bf16[688,256]{1,0:T(8,128)(2,1)S(1)} %collective-permute-done.35), channel_id=1, source_target_pairs={{0,1},{1,0},{2,3},{3,2},{4,5},{5,4},{6,7},{7,6},{8,9},{9,8},{10,11... | collective-permute-start | bytes 1056776 | tf_op jit(solution)/shard_map/ppermute | solution.py:106
  155.2 2.9 %collective-permute-start.54 = (bf16[688,256]{1,0:T(8,128)(2,1)S(1)}, bf16[688,256]{1,0:T(8,128)(2,1)S(1)}, u32[]{:S(2)}, u32[]{:S(2)}) collective-permute-start(bf16[688,256]{1,0:T(8,128)(2,1)S(1)} %collective-permute-done.34), channel_id=1, source_target_pairs={{0,1},{1,0},{2,3},{3,2},{4,5},{5,4},{6,7},{7,6},{8,9},{9,8},{10,11... | collective-permute-start | bytes 1056776 | tf_op jit(solution)/shard_map/ppermute | solution.py:106
  155.2 8.4 %collective-permute-start.18 = (bf16[688,256]{1,0:T(8,128)(2,1)S(1)}, bf16[688,256]{1,0:T(8,128)(2,1)S(1)}, u32[]{:S(2)}, u32[]{:S(2)}) collective-permute-start(bf16[688,256]{1,0:T(8,128)(2,1)S(1)} %collective-permute-done.16), channel_id=1, source_target_pairs={{0,2},{1,3},{2,6},{3,7},{6,10},{7,11},{10,14},{11,15},{14,12},{15,... | collective-permute-start | bytes 1056776 | tf_op jit(solution)/shard_map/ppermute | solution.py:97
  156.7 8.8 %collective-permute-start.39 = (bf16[688,256]{1,0:T(8,128)(2,1)S(1)}, bf16[688,256]{1,0:T(8,128)(2,1)S(1)}, u32[]{:S(2)}, u32[]{:S(2)}) collective-permute-start(bf16[688,256]{1,0:T(8,128)(2,1)S(1)} %collective-permute-done.37), channel_id=1, source_target_pairs={{0,4},{1,5},{2,0},{3,1},{6,2},{7,3},{10,6},{11,7},{14,10},{15,11},... | collective-permute-start | bytes 1056776 | tf_op jit(solution)/shard_map/ppermute | solution.py:97
  158.1 10.5 %collective-permute-start.46 = (bf16[688,256]{1,0:T(8,128)(2,1)S(1)}, bf16[688,256]{1,0:T(8,128)(2,1)S(1)}, u32[]{:S(2)}, u32[]{:S(2)}) collective-permute-start(bf16[688,256]{1,0:T(8,128)(2,1)S(1)} %collective-permute-done.16), channel_id=1, source_target_pairs={{0,1},{1,0},{2,3},{3,2},{4,5},{5,4},{6,7},{7,6},{8,9},{9,8},{10,11... | collective-permute-start | bytes 1056776 | tf_op jit(solution)/shard_map/ppermute | solution.py:106
  160.5 9.0 %collective-permute-start.55 = (bf16[688,256]{1,0:T(8,128)(2,1)S(1)}, bf16[688,256]{1,0:T(8,128)(2,1)S(1)}, u32[]{:S(2)}, u32[]{:S(2)}) collective-permute-start(bf16[688,256]{1,0:T(8,128)(2,1)S(1)} %collective-permute-done.37), channel_id=1, source_target_pairs={{0,1},{1,0},{2,3},{3,2},{4,5},{5,4},{6,7},{7,6},{8,9},{9,8},{10,11... | collective-permute-start | bytes 1056776 | tf_op jit(solution)/shard_map/ppermute | solution.py:106
  163.6 7.6 %collective-permute-start.19 = (bf16[688,256]{1,0:T(8,128)(2,1)S(1)}, bf16[688,256]{1,0:T(8,128)(2,1)S(1)}, u32[]{:S(2)}, u32[]{:S(2)}) collective-permute-start(bf16[688,256]{1,0:T(8,128)(2,1)S(1)} %collective-permute-done.18), channel_id=1, source_target_pairs={{0,2},{1,3},{2,6},{3,7},{6,10},{7,11},{10,14},{11,15},{14,12},{15,... | collective-permute-start | bytes 1056776 | tf_op jit(solution)/shard_map/ppermute | solution.py:97
  165.4 9.2 %collective-permute-start.40 = (bf16[688,256]{1,0:T(8,128)(2,1)S(1)}, bf16[688,256]{1,0:T(8,128)(2,1)S(1)}, u32[]{:S(2)}, u32[]{:S(2)}) collective-permute-start(bf16[688,256]{1,0:T(8,128)(2,1)S(1)} %collective-permute-done.39), channel_id=1, source_target_pairs={{0,4},{1,5},{2,0},{3,1},{6,2},{7,3},{10,6},{11,7},{14,10},{15,11},... | collective-permute-start | bytes 1056776 | tf_op jit(solution)/shard_map/ppermute | solution.py:97
  165.4 11.5 %collective-permute-start.47 = (bf16[688,256]{1,0:T(8,128)(2,1)S(1)}, bf16[688,256]{1,0:T(8,128)(2,1)S(1)}, u32[]{:S(2)}, u32[]{:S(2)}) collective-permute-start(bf16[688,256]{1,0:T(8,128)(2,1)S(1)} %collective-permute-done.18), channel_id=1, source_target_pairs={{0,1},{1,0},{2,3},{3,2},{4,5},{5,4},{6,7},{7,6},{8,9},{9,8},{10,11... | collective-permute-start | bytes 1056776 | tf_op jit(solution)/shard_map/ppermute | solution.py:106
  168.6 11.0 %collective-permute-start.56 = (bf16[688,256]{1,0:T(8,128)(2,1)S(1)}, bf16[688,256]{1,0:T(8,128)(2,1)S(1)}, u32[]{:S(2)}, u32[]{:S(2)}) collective-permute-start(bf16[688,256]{1,0:T(8,128)(2,1)S(1)} %collective-permute-done.39), channel_id=1, source_target_pairs={{0,1},{1,0},{2,3},{3,2},{4,5},{5,4},{6,7},{7,6},{8,9},{9,8},{10,11... | collective-permute-start | bytes 1056776 | tf_op jit(solution)/shard_map/ppermute | solution.py:106
  171.2 9.4 %collective-permute-start.20 = (bf16[688,256]{1,0:T(8,128)(2,1)S(1)}, bf16[688,256]{1,0:T(8,128)(2,1)S(1)}, u32[]{:S(2)}, u32[]{:S(2)}) collective-permute-start(bf16[688,256]{1,0:T(8,128)(2,1)S(1)} %collective-permute-done.17), channel_id=1, source_target_pairs={{0,1},{1,0},{2,3},{3,2},{4,5},{5,4},{6,7},{7,6},{8,9},{9,8},{10,11... | collective-permute-start | bytes 1056776 | tf_op jit(solution)/shard_map/ppermute | solution.py:106
  174.7 6.9 %collective-permute-start.41 = (bf16[688,256]{1,0:T(8,128)(2,1)S(1)}, bf16[688,256]{1,0:T(8,128)(2,1)S(1)}, u32[]{:S(2)}, u32[]{:S(2)}) collective-permute-start(bf16[688,256]{1,0:T(8,128)(2,1)S(1)} %collective-permute-done.38), channel_id=1, source_target_pairs={{0,1},{1,0},{2,3},{3,2},{4,5},{5,4},{6,7},{7,6},{8,9},{9,8},{10,11... | collective-permute-start | bytes 1056776 | tf_op jit(solution)/shard_map/ppermute | solution.py:106
  176.1 10.0 %collective-permute-start.49 = (bf16[688,256]{1,0:T(8,128)(2,1)S(1)}, bf16[688,256]{1,0:T(8,128)(2,1)}, u32[]{:S(2)}, u32[]{:S(2)}) collective-permute-start(bf16[688,256]{1,0:T(8,128)(2,1)S(1)} %collective-permute-done.19), channel_id=1, source_target_pairs={{0,2},{1,3},{2,6},{3,7},{6,10},{7,11},{10,14},{11,15},{14,12},{15,... | collective-permute-start | bytes 1056776 | tf_op jit(solution)/shard_map/ppermute | solution.py:97
  176.9 11.4 %collective-permute-start.58 = (bf16[688,256]{1,0:T(8,128)(2,1)S(1)}, bf16[688,256]{1,0:T(8,128)(2,1)}, u32[]{:S(2)}, u32[]{:S(2)}) collective-permute-start(bf16[688,256]{1,0:T(8,128)(2,1)S(1)} %collective-permute-done.40), channel_id=1, source_target_pairs={{0,4},{1,5},{2,0},{3,1},{6,2},{7,3},{10,6},{11,7},{14,10},{15,11},... | collective-permute-start | bytes 1056776 | tf_op jit(solution)/shard_map/ppermute | solution.py:97
  179.5 13.3 %collective-permute-start.48 = (bf16[688,256]{1,0:T(8,128)(2,1)S(1)}, bf16[688,256]{1,0:T(8,128)(2,1)}, u32[]{:S(2)}, u32[]{:S(2)}) collective-permute-start(bf16[688,256]{1,0:T(8,128)(2,1)S(1)} %collective-permute-done.19), channel_id=1, source_target_pairs={{0,1},{1,0},{2,3},{3,2},{4,5},{5,4},{6,7},{7,6},{8,9},{9,8},{10,11... | collective-permute-start | bytes 1056776 | tf_op jit(solution)/shard_map/ppermute | solution.py:106
  180.6 15.4 %collective-permute-start.57 = (bf16[688,256]{1,0:T(8,128)(2,1)S(1)}, bf16[688,256]{1,0:T(8,128)(2,1)}, u32[]{:S(2)}, u32[]{:S(2)}) collective-permute-start(bf16[688,256]{1,0:T(8,128)(2,1)S(1)} %collective-permute-done.40), channel_id=1, source_target_pairs={{0,1},{1,0},{2,3},{3,2},{4,5},{5,4},{6,7},{7,6},{8,9},{9,8},{10,11... | collective-permute-start | bytes 1056776 | tf_op jit(solution)/shard_map/ppermute | solution.py:106
  187.5 10.1 %collective-permute-start.50 = (bf16[688,256]{1,0:T(8,128)(2,1)}, bf16[688,256]{1,0:T(8,128)(2,1)S(1)}, u32[]{:S(2)}, u32[]{:S(2)}) collective-permute-start(bf16[688,256]{1,0:T(8,128)(2,1)} %collective-permute-done.49), channel_id=1, source_target_pairs={{0,1},{1,0},{2,3},{3,2},{4,5},{5,4},{6,7},{7,6},{8,9},{9,8},{10,11... | collective-permute-start | bytes 1056776 | tf_op jit(solution)/shard_map/ppermute | solution.py:106
  188.3 10.7 %collective-permute-start.59 = (bf16[688,256]{1,0:T(8,128)(2,1)}, bf16[688,256]{1,0:T(8,128)(2,1)S(1)}, u32[]{:S(2)}, u32[]{:S(2)}) collective-permute-start(bf16[688,256]{1,0:T(8,128)(2,1)} %collective-permute-done.58), channel_id=1, source_target_pairs={{0,1},{1,0},{2,3},{3,2},{4,5},{5,4},{6,7},{7,6},{8,9},{9,8},{10,11... | collective-permute-start | bytes 1056776 | tf_op jit(solution)/shard_map/ppermute | solution.py:106
  188.4 23.7 %all-to-all-start = ((bf16[16,3,16,512]{3,2,1,0:T(8,128)(2,1)}), bf16[16,3,16,512]{3,2,1,0:T(8,128)(2,1)S(1)}, u32[]{:S(2)}, u32[]{:S(2)}) async-start(bf16[16,3,16,512]{3,2,1,0:T(8,128)(2,1)} %bitcast.52), calls=%async_computation | async-start | bytes 1572864 | tf_op jit(solution)/shard_map/all_to_all | solution.py:46
  212.1 24.2 %all-to-all-start.1 = ((bf16[16,3,16,512]{3,2,1,0:T(8,128)(2,1)}), bf16[16,3,16,512]{3,2,1,0:T(8,128)(2,1)S(1)}, u32[]{:S(2)}, u32[]{:S(2)}) async-start(bf16[16,3,16,512]{3,2,1,0:T(8,128)(2,1)} %bitcast.53), calls=%async_computation.1 | async-start | bytes 1572864 | tf_op jit(solution)/shard_map/all_to_all | solution.py:46
  (2 other events, 24.4 us)

commit v3 on v0

v3 whole, which is shorter than its diff:
```python
import math

import jax
import jax.numpy as jnp
from jax import lax
from jax.experimental import pallas as pl
from jax.experimental.pallas import tpu as pltpu
from jax.sharding import PartitionSpec as P

GRID_CHIPS = 8
HALVES = 2
BEHIND = (0, 0, 0, 0, 2, 4, 6)


def ring_chip(at):
    at = at % GRID_CHIPS
    back = 2 * ((GRID_CHIPS - at) % GRID_CHIPS)
    up = 2 * at - 1
    if isinstance(at, int):
        return up if 1 <= at <= GRID_CHIPS // 2 else back
    return jnp.where((at >= 1) & (at <= GRID_CHIPS // 2), up, back)


def ring_place(chip):
    z, y = chip // 2, chip % 2
    return jnp.where(y == 1, 1 + z, (GRID_CHIPS - z) % GRID_CHIPS)


def routing(owners, count, slots, block_rows):
    blocks_here = owners.shape[0]
    rows = blocks_here * block_rows
    owner_col = owners[:, 0]
    same = owner_col[:, None] == owner_col[None, :]
    lower = jnp.arange(blocks_here)[:, None] > jnp.arange(blocks_here)[None, :]
    rank = jnp.sum((same & lower).astype(jnp.int32), axis=1)
    target = owner_col * slots + rank
    select = jnp.arange(count * slots, dtype=jnp.int32)[:, None] == target[None, :]
    global_ids = lax.axis_index("wide") * blocks_here + jnp.arange(blocks_here, dtype=jnp.int32)
    labels = jnp.sum(jnp.where(select, global_ids[None, :] + 1, 0), axis=1) - 1
    row_at = jnp.arange(rows, dtype=jnp.int32)
    out_at = jnp.arange(count * block_rows * slots, dtype=jnp.int32)
    row_key = jnp.repeat(target, block_rows) * block_rows + row_at % block_rows
    out_key = (
        out_at // (block_rows * slots) * slots + out_at % slots
    ) * block_rows + out_at // slots % block_rows
    place = (out_key[:, None] == row_key[None, :]).astype(jnp.bfloat16)
    return labels.reshape(count, slots), place


def finish_kernel(place_ref, *refs):
    out_ref = refs[-1]
    mine, theirs = refs[: len(refs) // 2], refs[len(refs) // 2 : -1]
    count, planes, slots, naux = out_ref.shape
    norb = len(mine) // HALVES
    width = naux // HALVES
    for at in range(norb * HALVES):
        i, j = at // HALVES, at % HALVES
        back = (mine[at][...] + theirs[at][...]).astype(jnp.bfloat16)
        out = jnp.dot(place_ref[...], back, preferred_element_type=jnp.float32)
        out = out.astype(jnp.bfloat16).reshape(count, planes // norb, slots, width)
        out_ref[:, pl.ds(i * (planes // norb), planes // norb), :, pl.ds(j * width, width)] = out


def finish(place, mine, theirs, shape):
    return pl.pallas_call(
        finish_kernel,
        out_shape=jax.ShapeDtypeStruct(shape, jnp.bfloat16),
        in_specs=[pl.BlockSpec(memory_space=pltpu.VMEM)] * (1 + len(mine) + len(theirs)),
        out_specs=pl.BlockSpec(memory_space=pltpu.VMEM),
        compiler_params=pltpu.CompilerParams(vmem_limit_bytes=20 << 20),
        cost_estimate=pl.CostEstimate(
            flops=2 * math.prod(shape) * place.shape[1],
            bytes_accessed=2 * math.prod(shape),
            transcendentals=0,
        ),
    )(place, *mine, *theirs)


def spread_kernel(core_ref, c_ref, kept_ref, given_ref):
    chips, _, depth = kept_ref.shape
    second = core_ref[0] == 1
    for chip in range(chips):
        even = c_ref[:, 2 * chip * depth : (2 * chip + 1) * depth]
        odd = c_ref[:, (2 * chip + 1) * depth : (2 * chip + 2) * depth]
        kept_ref[chip] = jnp.where(second, odd, even)
        given_ref[chip] = jnp.where(second, even, odd)


def spread(coefficients, core):
    rows, nvirt = coefficients.shape
    depth = nvirt // (2 * GRID_CHIPS)
    step = 48
    part = pl.BlockSpec((GRID_CHIPS, step, depth), lambda at: (0, at, 0))
    shape = jax.ShapeDtypeStruct((GRID_CHIPS, rows, depth), coefficients.dtype)
    return pl.pallas_call(
        spread_kernel,
        grid=(rows // step,),
        out_shape=(shape, shape),
        in_specs=[
            pl.BlockSpec(memory_space=pltpu.SMEM),
            pl.BlockSpec((step, nvirt), lambda at: (at, 0)),
        ],
        out_specs=(part, part),
        compiler_params=pltpu.CompilerParams(vmem_limit_bytes=16 << 20),
        cost_estimate=pl.CostEstimate(
            flops=0, bytes_accessed=4 * rows * nvirt, transcendentals=0
        ),
    )(core, coefficients)


def after(value, event):
    return lax.optimization_barrier((value, event))[0]


def ring_products(gamma, coefficients):
    count = lax.axis_size("wide")
    rows = coefficients.shape[0]
    norb, depth, naux = gamma.shape
    width = naux // HALVES
    me = lax.axis_index("wide")
    core = me % 2
    here = ring_place(me // 2)
    swap = [(d, d ^ 1) for d in range(count)]

    ways = (1, -1)
    streams = [(i, j) for i in range(norb) for j in range(HALVES)]
    piece = {(i, j): gamma[i, :, j * width : (j + 1) * width] for i, j in streams}
    shift = [
        [
            (2 * ring_chip(p) + k, 2 * ring_chip(p + way) + k)
            for p in range(GRID_CHIPS)
            for k in range(2)
        ]
        for way in ways
    ]
    mine = {s: jnp.zeros((rows, width), jnp.float32) for s in streams}
    theirs = {s: [jnp.zeros((rows, width), jnp.float32)] for s in streams}
    for t in range(GRID_CHIPS):
        arrived = dict(piece)
        if t + 1 < GRID_CHIPS:
            for s in streams:
                done = BEHIND[t]
                sent = after(piece[s], theirs[s][done]) if done else piece[s]
                piece[s] = lax.ppermute(sent, "wide", shift[s[0]])
        if t == 0:
            ready = after(coefficients, piece[streams[-1]])
            kept, given = spread(ready, core.reshape(1))
            taken = lax.ppermute(given, "wide", swap)
        for i, j in streams:
            chip = ring_chip(here - t * ways[i] + GRID_CHIPS)
            block = arrived[i, j]
            left = lax.dynamic_index_in_dim(taken, chip, 0, False)
            term = jnp.dot(left, block, preferred_element_type=jnp.float32)
            theirs[i, j].append(theirs[i, j][-1] + term)
            left = lax.dynamic_index_in_dim(kept, chip, 0, False)
            mine[i, j] += jnp.dot(left, block, preferred_element_type=jnp.float32)
        if t == 2:
            second = arrived[streams[0]]
    swapped = [lax.ppermute(theirs[s][-1], "wide", swap) for s in streams]
    return [mine[s] for s in streams], swapped, second


def local(gamma, coefficients, owners):
    count = lax.axis_size("wide")
    blocks_here = owners.shape[0]
    slots = max(2, 2 * blocks_here // count)
    block_rows = coefficients.shape[0] // blocks_here
    norb, depth, naux = gamma.shape
    shape = (count, norb * block_rows, slots, naux)

    labels, place = routing(owners, count, slots, block_rows)
    if count == 2 * GRID_CHIPS and norb == 2:
        mine, theirs, second = ring_products(gamma, coefficients)
        labels = after(labels, second)
        out = finish(place, mine, theirs, shape)
    else:
        gathered = lax.all_gather(gamma, "wide", axis=1, tiled=True)
        back = jnp.einsum(
            "ra,ian->irn", coefficients, gathered, preferred_element_type=jnp.float32
        ).astype(jnp.bfloat16)
        out = jnp.einsum("tr,irn->itn", place, back, preferred_element_type=jnp.float32)
        out = out.astype(jnp.bfloat16).reshape(norb, count, block_rows, slots, naux)
        out = out.transpose(1, 0, 2, 3, 4).reshape(shape)
    ids = lax.all_to_all(labels, "wide", split_axis=0, concat_axis=0, tiled=True)
    placed = lax.all_to_all(out, "wide", split_axis=0, concat_axis=0, tiled=True)
    return placed.transpose(0, 2, 1, 3)[None], ids[None]


def solution(mesh):
    placed = (P("groups", "wide", None), P("wide", None), P("wide", None))
    return jax.shard_map(
        local,
        mesh=mesh,
        in_specs=placed,
        out_specs=(P("wide", None, "groups", None, None), P("wide", "groups", None)),
        check_vma=False,
    )
```

time: 202 us -> 208 us (1.030)
  waiting for transfers between devices: 147 us -> 53.3 us
  matrix products: 17.4 us -> 70.9 us
  starting transfers between devices: 11.8 us -> 46.1 us
  Pallas kernels: 0 us -> 13.2 us
  between operations: 14.1 us -> 1.72 us
  local copies, waits for them, and re-layouts: 9.2 us -> 18.6 us
    all_gather x1 -> x0, waiting for transfers between devices: 110 us -> none  [transform(): lax.all_gather(gamma, 'wide', axis=1, tiled=True)]
    dot_general x2 -> x64, matrix products: 17.4 us -> 70.9 us  [the longest x32 46 us: ring_products(): term = jnp.dot(left, block, preferred_element_type=jnp.float32)]
    ppermute x0 -> x33, starting transfers between devices: none -> 34.4 us  [the longest x28 21.2 us: ring_products(): piece[s] = lax.ppermute(sent, 'wide', shift[s[0]])]
    ppermute x0 -> x33, waiting for transfers between devices: none -> 17.1 us  [the longest x28 17.1 us: ring_products(): piece[s] = lax.ppermute(sent, 'wide', shift[s[0]])]
    pallas_call x0 -> x2, Pallas kernels: none -> 13.2 us  [the longest x1 11.1 us: spread(): pl.pallas_call(spread_kernel, grid=(rows // step,), out_shape=(shape, sha...]
    unnamed x2 -> x18, local copies, waits for them, and re-layouts: 1.74 us -> 9.45 us
    pallas_call x0 -> x1, local copies, waits for them, and re-layouts: none -> 6.75 us  [spread(): pl.pallas_call(spread_kernel, grid=(rows // step,), out_shape=(shape, sha...]
    reshape x2 -> x0, local copies, waits for them, and re-layouts: 5.17 us -> none  [local(): outgoing = outgoing.reshape(count, slots, norb * block_rows, naux)]
  transfers between devices with their start and end apart: 3 -> 35, of which waited for: 2 -> 8; matrix products, arithmetic and copies ran while one was open for 13% -> 39% of each run, Pallas kernels for 0% -> 6%
where the time goes in v3:
time: 208 us; the launch traced here: 206 us
  matrix products  70.9 us (34%)
  waiting for transfers between devices  53.3 us (26%)
  starting transfers between devices  46.1 us (22%)
  local copies, waits for them, and re-layouts  18.6 us (9%)
  Pallas kernels  13.2 us (6%)
    dot_general x32, matrix products, ring_products(): term = jnp.dot(left, block, preferred_element_type=jnp.float32)  46 us
    all_to_all x1, waiting for transfers between devices, local(): lax.all_to_all(out, 'wide', split_axis=0, concat_axis=0, tiled=True)  36.2 us
    dot_general x32, matrix products, ring_products(): mine[i, j] += jnp.dot(left, block, preferred_element_type=jnp.float32)  24.9 us
    ppermute x28, starting transfers between devices, ring_products(): piece[s] = lax.ppermute(sent, 'wide', shift[s[0]])  21.2 us
    ppermute x28, waiting for transfers between devices, ring_products(): piece[s] = lax.ppermute(sent, 'wide', shift[s[0]])  17.1 us
    pallas_call x1, Pallas kernels, spread(): pl.pallas_call(spread_kernel, grid=(rows // step,), out_shape=(shape, sha...  11.1 us
    ppermute x4, starting transfers between devices, ring_products(): swapped = [lax.ppermute(theirs[s][-1], 'wide', swap) for s in streams]  9.87 us
    unnamed x18, local copies, waits for them, and re-layouts  9.45 us
  transfers between devices with their start and end apart: 35, of which 8 were waited for; matrix products, arithmetic and copies ran while one was open for 39% of the time, Pallas kernels for 6%

profile of v3, /device:TPU:13, one launch (start us, length us, event | category | flops | bytes accessed | tf_op | source)
XLA Modules:
  0.0 205.6 jit_solution(1746014825630735203)
XLA Ops:
  0.6 1.4 slice_bitcast_fusion
  2.0 1.3 collective-permute-start.1
  3.5 1.3 collective-permute-start.9
  8.1 4.2 %collective-permute-done = bf16[688,256]{1,0:T(8,128)(2,1)} collective-permute-done((bf16[688,256]{1,0:T(8,128)(2,1)S(1)}, bf16[688,256]{1,0:T(8,128)(2,1)}, u32[]{:S(2)}, u32[]{:S(2)}) %collective-permute-start) | collective-permute-done | bytes 352288 | tf_op jit(solution)/shard_map/ppermute | solution.py:144
  12.3 3.4 %copy-done.2 = bf16[384,11008]{1,0:T(8,128)(2,1)S(1)} copy-done((bf16[384,11008]{1,0:T(8,128)(2,1)S(1)}, bf16[384,11008]{1,0:T(8,128)(2,1)}, u32[]{:S(2)}) %copy-start.2) | copy-done | bytes 8454168
  15.7 11.1 %shard_map.50 = (bf16[8,384,688]{2,1,0:T(8,128)(2,1)S(1)}, bf16[8,384,688]{2,1,0:T(8,128)(2,1)S(1)}) custom-call(s32[1]{0:T(128)} %bitcast.1.core_ref, bf16[384,11008]{1,0:T(8,128)(2,1)S(1)} %copy-done.2), custom_call_target="tpu_custom_call" | custom-call | bytes 16908288 | tf_op jit(solution)/shard_map/pallas_call | solution.py:95
  26.8 2.1 %copy-done = bf16[8,384,688]{2,1,0:T(8,128)(2,1)} copy-done((bf16[8,384,688]{2,1,0:T(8,128)(2,1)}, bf16[8,384,688]{2,1,0:T(8,128)(2,1)S(1)}, u32[]{:S(2)}) %copy-start) | copy-done | bytes 4227096
  28.9 2.1 %copy-done.3 = bf16[8,384,688]{2,1,0:T(8,128)(2,1)} copy-done((bf16[8,384,688]{2,1,0:T(8,128)(2,1)}, bf16[8,384,688]{2,1,0:T(8,128)(2,1)S(1)}, u32[]{:S(2)}) %copy-start.3) | copy-done | bytes 4227096
  31.1 6.7 %copy.6 = bf16[8,384,688]{1,2,0:T(8,128)(2,1)} copy(bf16[8,384,688]{2,1,0:T(8,128)(2,1)} %copy-done.3) | data formatting | bytes 8454144 | tf_op jit(solution)/shard_map/pallas_call | solution.py:95
  37.8 3.3 %collective-permute-start.5 = (bf16[8,384,688]{1,2,0:T(8,128)(2,1)}, bf16[8,384,688]{1,2,0:T(8,128)(2,1)}, u32[]{:S(2)}, u32[]{:S(2)}) collective-permute-start(bf16[8,384,688]{1,2,0:T(8,128)(2,1)} %copy.6), channel_id=1, source_target_pairs={{0,1},{1,0},{2,3},{3,2},{4,5},{5,4},{6,7},{7,6},{8,9},{9,8},{10,11... | collective-permute-start | bytes 12681224 | tf_op jit(solution)/shard_map/ppermute | solution.py:148
  41.6 1.3 collective-permute-start.2
  42.9 1.3 collective-permute-start.10
  44.3 1.4 fusion.66
  45.7 1.4 fusion.64
  47.1 1.4 fusion.62
  48.5 1.5 convolution_add_fusion.35
  50.0 1.4 convolution_add_fusion.27
  51.4 2.1 %convolution_add_fusion.19 = f32[384,256]{1,0:T(8,128)} fusion(f32[384,256]{1,0:T(8,128)S(1)} %fusion.62, bf16[688,256]{1,0:T(8,128)(2,1)} %collective-permute-done.16, bf16[8,384,688]{2,1,0:T(8,128)(2,1)S(1)} %copy-done.1, s32[]{:T(128)S(6)} %select_n.464), kind=kOutput, calls=%fused_computation.31 | convolution fusion | flops 135364608 | bytes 1728516 | tf_op jit(solution)/shard_map/dot_general | solution.py:156
  53.8 2.1 %convolution_add_fusion.11 = f32[384,256]{1,0:T(8,128)} fusion(f32[384,256]{1,0:T(8,128)S(1)} %fusion.60, bf16[688,256]{1,0:T(8,128)(2,1)} %collective-permute-done, bf16[8,384,688]{2,1,0:T(8,128)(2,1)S(1)} %copy-done.1, s32[]{:T(128)S(6)} %select_n.464), kind=kOutput, calls=%fused_computation.19 | convolution fusion | flops 135364608 | bytes 1728516 | tf_op jit(solution)/shard_map/dot_general | solution.py:156
  55.8 6.0 %all-to-all-start.1 = ((s32[16,1,16]{2,1,0:T(1,128)}), s32[16,1,16]{2,1,0:T(1,128)S(1)}, u32[]{:S(2)}, u32[]{:S(2)}) async-start(s32[16,1,16]{2,1,0:T(1,128)} %bitcast.38), calls=%async_computation.1 | async-start | bytes 16384 | tf_op jit(solution)/shard_map/all_to_all | solution.py:184
  64.8 1.5 convolution_add_fusion.34
  66.3 1.5 convolution_add_fusion.26
  67.8 1.6 convolution_add_fusion.18
  69.4 1.5 convolution_add_fusion.10
  72.8 6.4 %collective-permute-done.11 = bf16[688,256]{1,0:T(8,128)(2,1)S(1)} collective-permute-done((bf16[688,256]{1,0:T(8,128)(2,1)}, bf16[688,256]{1,0:T(8,128)(2,1)S(1)}, u32[]{:S(2)}, u32[]{:S(2)}) %collective-permute-start.11) | collective-permute-done | bytes 352288 | tf_op jit(solution)/shard_map/ppermute | solution.py:144
  81.1 1.4 convolution_add_fusion.33
  83.6 1.5 fusion.106
  85.1 1.4 convolution_add_fusion.31
  87.9 1.5 fusion.104
  89.4 1.4 convolution_add_fusion.23
  90.8 3.4 %collective-permute-done.12 = bf16[688,256]{1,0:T(8,128)(2,1)S(1)} collective-permute-done((bf16[688,256]{1,0:T(8,128)(2,1)S(1)}, bf16[688,256]{1,0:T(8,128)(2,1)S(1)}, u32[]{:S(2)}, u32[]{:S(2)}) %collective-permute-start.12) | collective-permute-done | bytes 352288 | tf_op jit(solution)/shard_map/ppermute | solution.py:144
  95.4 1.5 fusion.92
  96.9 1.4 convolution_add_fusion.15
  98.7 1.5 fusion.90
  100.2 1.4 convolution_add_fusion.7
  102.2 1.5 convolution_add_fusion.30
  103.7 1.5 convolution_add_fusion.22
  105.2 1.5 convolution_add_fusion.14
  106.8 1.5 convolution_add_fusion.6
  108.3 1.4 convolution_add_fusion.29
  109.7 1.4 convolution_add_fusion.21
  111.1 1.4 convolution_add_fusion.13
  112.6 1.4 convolution_add_fusion.5
  117.0 1.4 fusion.96
  118.7 1.4 fusion.94
  120.5 1.4 fusion.82
  122.2 1.4 fusion.80
  123.6 1.4 fusion.16
  125.1 1.4 fusion.12
  126.5 1.4 fusion.8
  128.2 1.4 fusion.4
  134.0 1.9 collective-permute-done.8
  135.9 1.4 fusion.76
  137.3 1.4 fusion.3
  138.8 8.3 %collective-permute-start.29 = (f32[384,256]{1,0:T(8,128)S(1)}, f32[384,256]{1,0:T(8,128)S(1)}, u32[]{:S(2)}, u32[]{:S(2)}) collective-permute-start(f32[384,256]{1,0:T(8,128)S(1)} %fusion.3), channel_id=1, source_target_pairs={{0,1},{1,0},{2,3},{3,2},{4,5},{5,4},{6,7},{7,6},{8,9},{9,8},{10,11... | collective-permute-start | bytes 1179656 | tf_op jit(solution)/shard_map/ppermute | solution.py:159
  147.0 1.4 fusion.74
  148.5 1.4 fusion.2
  150.8 1.4 fusion.70
  152.2 1.4 fusion.1
  153.8 1.4 fusion.68
  155.2 1.4 fusion
  159.8 2.1 %shard_map.51 = bf16[16,6,16,512]{3,2,1,0:T(8,128)(2,1)} custom-call(bf16[768,384]{1,0:T(8,128)(2,1)S(1)} %compare_convert_fusion.place_ref, f32[384,256]{1,0:T(8,128)S(1)} %fusion.19.refs_0_, f32[384,256]{1,0:T(8,128)S(1)} %fusion.15.refs_1_, f32[384,256]{1,0:T(8,128)S(1)} %fusion.11.refs_2_, f32[384,256]{1,0:T(8,128)S(1)} %fusion.7.refs_3_, ...), custom_call_target="tpu_custom_call" | custom-call | flops 603979776 | bytes 1572864 | tf_op jit(solution)/shard_map/pallas_call | solution.py:65
  162.0 5.7 %all-to-all-start = ((bf16[16,6,16,512]{3,2,1,0:T(8,128)(2,1)}), bf16[16,6,16,512]{3,2,1,0:T(8,128)(2,1)S(1)}, u32[]{:S(2)}, u32[]{:S(2)}) async-start(bf16[16,6,16,512]{3,2,1,0:T(8,128)(2,1)} %shard_map.51), calls=%async_computation | async-start | bytes 3145728 | tf_op jit(solution)/shard_map/all_to_all | solution.py:185
  167.7 36.2 %all-to-all-done = bf16[16,6,16,512]{3,2,1,0:T(8,128)(2,1)S(1)} async-done(((bf16[16,6,16,512]{3,2,1,0:T(8,128)(2,1)}), bf16[16,6,16,512]{3,2,1,0:T(8,128)(2,1)S(1)}, u32[]{:S(2)}, u32[]{:S(2)}) %all-to-all-start) | async-done | bytes 1572896 | tf_op jit(solution)/shard_map/all_to_all | solution.py:185
  (103 shorter events, 29.6 us)
Async XLA Ops:
  2.0 39.5 %collective-permute-start.1 = (bf16[688,256]{1,0:T(8,128)(2,1)S(1)}, bf16[688,256]{1,0:T(8,128)(2,1)}, u32[]{:S(2)}, u32[]{:S(2)}) collective-permute-start(bf16[688,256]{1,0:T(8,128)(2,1)S(1)} %get-tuple-element.37), channel_id=1, source_target_pairs={{0,2},{1,3},{2,6},{3,7},{6,10},{7,11},{10,14},{11,15},{14,12},{15,... | collective-permute-start | bytes 1056776 | tf_op jit(solution)/shard_map/ppermute | solution.py:144
  3.4 8.9 %collective-permute-start = (bf16[688,256]{1,0:T(8,128)(2,1)S(1)}, bf16[688,256]{1,0:T(8,128)(2,1)}, u32[]{:S(2)}, u32[]{:S(2)}) collective-permute-start(bf16[688,256]{1,0:T(8,128)(2,1)S(1)} %get-tuple-element.38), channel_id=1, source_target_pairs={{0,4},{1,5},{2,0},{3,1},{6,2},{7,3},{10,6},{11,7},{14,10},{15,11},... | collective-permute-start | bytes 1056776 | tf_op jit(solution)/shard_map/ppermute | solution.py:144
  3.5 39.3 %collective-permute-start.9 = (bf16[688,256]{1,0:T(8,128)(2,1)S(1)}, bf16[688,256]{1,0:T(8,128)(2,1)}, u32[]{:S(2)}, u32[]{:S(2)}) collective-permute-start(bf16[688,256]{1,0:T(8,128)(2,1)S(1)} %get-tuple-element.39), channel_id=1, source_target_pairs={{0,2},{1,3},{2,6},{3,7},{6,10},{7,11},{10,14},{11,15},{14,12},{15,... | collective-permute-start | bytes 1056776 | tf_op jit(solution)/shard_map/ppermute | solution.py:144
  4.8 39.3 %collective-permute-start.16 = (bf16[688,256]{1,0:T(8,128)(2,1)S(1)}, bf16[688,256]{1,0:T(8,128)(2,1)}, u32[]{:S(2)}, u32[]{:S(2)}) collective-permute-start(bf16[688,256]{1,0:T(8,128)(2,1)S(1)} %get-tuple-element.36), channel_id=1, source_target_pairs={{0,4},{1,5},{2,0},{3,1},{6,2},{7,3},{10,6},{11,7},{14,10},{15,11},... | collective-permute-start | bytes 1056776 | tf_op jit(solution)/shard_map/ppermute | solution.py:144
  12.3 3.4 %copy-start.2 = (bf16[384,11008]{1,0:T(8,128)(2,1)S(1)}, bf16[384,11008]{1,0:T(8,128)(2,1)}, u32[]{:S(2)}) copy-start(bf16[384,11008]{1,0:T(8,128)(2,1)} %c_ref) | copy-start | bytes 25362436
  26.8 2.1 %copy-start = (bf16[8,384,688]{2,1,0:T(8,128)(2,1)}, bf16[8,384,688]{2,1,0:T(8,128)(2,1)S(1)}, u32[]{:S(2)}) copy-start(bf16[8,384,688]{2,1,0:T(8,128)(2,1)S(1)} %get-tuple-element.19) | copy-start | bytes 12681220
  28.9 2.1 %copy-start.3 = (bf16[8,384,688]{2,1,0:T(8,128)(2,1)}, bf16[8,384,688]{2,1,0:T(8,128)(2,1)S(1)}, u32[]{:S(2)}) copy-start(bf16[8,384,688]{2,1,0:T(8,128)(2,1)S(1)} %get-tuple-element.20) | copy-start | bytes 12681220
  31.1 13.3 %copy-start.4 = (bf16[2,688,512]{2,1,0:T(8,128)(2,1)S(1)}, bf16[2,688,512]{2,1,0:T(8,128)(2,1)}, u32[]{:S(2)}) copy-start(bf16[2,688,512]{2,1,0:T(8,128)(2,1)} %param.3) | copy-start | bytes 4227076
  37.8 12.2 %copy-start.1 = (bf16[8,384,688]{2,1,0:T(8,128)(2,1)S(1)}, bf16[8,384,688]{2,1,0:T(8,128)(2,1)}, u32[]{:S(2)}) copy-start(bf16[8,384,688]{2,1,0:T(8,128)(2,1)} %copy-done) | copy-start | bytes 12681220
  37.8 45.7 %collective-permute-start.5 = (bf16[8,384,688]{1,2,0:T(8,128)(2,1)}, bf16[8,384,688]{1,2,0:T(8,128)(2,1)}, u32[]{:S(2)}, u32[]{:S(2)}) collective-permute-start(bf16[8,384,688]{1,2,0:T(8,128)(2,1)} %copy.6), channel_id=1, source_target_pairs={{0,1},{1,0},{2,3},{3,2},{4,5},{5,4},{6,7},{7,6},{8,9},{9,8},{10,11... | collective-permute-start | bytes 12681224 | tf_op jit(solution)/shard_map/ppermute | solution.py:148
  41.3 23.2 %collective-permute-start.23 = (bf16[688,256]{1,0:T(8,128)(2,1)}, bf16[688,256]{1,0:T(8,128)(2,1)}, u32[]{:S(2)}, u32[]{:S(2)}) collective-permute-start(bf16[688,256]{1,0:T(8,128)(2,1)} %collective-permute-done), channel_id=1, source_target_pairs={{0,4},{1,5},{2,0},{3,1},{6,2},{7,3},{10,6},{11,7},{14,10},{15,11},... | collective-permute-start | bytes 1056776 | tf_op jit(solution)/shard_map/ppermute | solution.py:144
  41.6 14.3 %collective-permute-start.2 = (bf16[688,256]{1,0:T(8,128)(2,1)}, bf16[688,256]{1,0:T(8,128)(2,1)}, u32[]{:S(2)}, u32[]{:S(2)}) collective-permute-start(bf16[688,256]{1,0:T(8,128)(2,1)} %collective-permute-done.1), channel_id=1, source_target_pairs={{0,2},{1,3},{2,6},{3,7},{6,10},{7,11},{10,14},{11,15},{14,12},{15,... | collective-permute-start | bytes 1056776 | tf_op jit(solution)/shard_map/ppermute | solution.py:144
  42.9 20.2 %collective-permute-start.10 = (bf16[688,256]{1,0:T(8,128)(2,1)}, bf16[688,256]{1,0:T(8,128)(2,1)}, u32[]{:S(2)}, u32[]{:S(2)}) collective-permute-start(bf16[688,256]{1,0:T(8,128)(2,1)} %collective-permute-done.9), channel_id=1, source_target_pairs={{0,2},{1,3},{2,6},{3,7},{6,10},{7,11},{10,14},{11,15},{14,12},{15,... | collective-permute-start | bytes 1056776 | tf_op jit(solution)/shard_map/ppermute | solution.py:144
  44.2 20.1 %collective-permute-start.17 = (bf16[688,256]{1,0:T(8,128)(2,1)}, bf16[688,256]{1,0:T(8,128)(2,1)}, u32[]{:S(2)}, u32[]{:S(2)}) collective-permute-start(bf16[688,256]{1,0:T(8,128)(2,1)} %collective-permute-done.16), channel_id=1, source_target_pairs={{0,4},{1,5},{2,0},{3,1},{6,2},{7,3},{10,6},{11,7},{14,10},{15,11},... | collective-permute-start | bytes 1056776 | tf_op jit(solution)/shard_map/ppermute | solution.py:144
  50.0 32.5 %slice-start = ((s8[4718592]{0:T(1024)(128)(4,1)}), s8[524288]{0:T(1024)(128)(4,1)S(1)}, s32[]{:S(2)}) async-start(s8[4718592]{0:T(1024)(128)(4,1)} %bitcast.239), calls=%async_computation.2 | async-start | bytes 1048576
  55.8 106.1 %all-to-all-start.1 = ((s32[16,1,16]{2,1,0:T(1,128)}), s32[16,1,16]{2,1,0:T(1,128)S(1)}, u32[]{:S(2)}, u32[]{:S(2)}) async-start(s32[16,1,16]{2,1,0:T(1,128)} %bitcast.38), calls=%async_computation.1 | async-start | bytes 16384 | tf_op jit(solution)/shard_map/all_to_all | solution.py:184
  61.8 7.6 %copy-start.5 = (f32[384,256]{1,0:T(8,128)S(1)}, f32[384,256]{1,0:T(8,128)}, u32[]{:S(2)}) copy-start(f32[384,256]{1,0:T(8,128)} %convolution_add_fusion.11) | copy-start | bytes 1179652
  61.8 20.7 %slice-start.1 = ((s8[4718592]{0:T(1024)(128)(4,1)}), s8[4194304]{0:T(1024)(128)(4,1)S(1)}, s32[]{:S(2)}) async-start(s8[4718592]{0:T(1024)(128)(4,1)} %bitcast.239), calls=%async_computation.3 | async-start | bytes 8388608
  61.9 9.7 %collective-permute-start.3 = (bf16[688,256]{1,0:T(8,128)(2,1)}, bf16[688,256]{1,0:T(8,128)(2,1)S(1)}, u32[]{:S(2)}, u32[]{:S(2)}) collective-permute-start(bf16[688,256]{1,0:T(8,128)(2,1)} %collective-permute-done.2), channel_id=1, source_target_pairs={{0,2},{1,3},{2,6},{3,7},{6,10},{7,11},{10,14},{11,15},{14,12},{15,... | collective-permute-start | bytes 1056776 | tf_op jit(solution)/shard_map/ppermute | solution.py:144
  63.1 16.0 %collective-permute-start.11 = (bf16[688,256]{1,0:T(8,128)(2,1)}, bf16[688,256]{1,0:T(8,128)(2,1)S(1)}, u32[]{:S(2)}, u32[]{:S(2)}) collective-permute-start(bf16[688,256]{1,0:T(8,128)(2,1)} %collective-permute-done.10), channel_id=1, source_target_pairs={{0,2},{1,3},{2,6},{3,7},{6,10},{7,11},{10,14},{11,15},{14,12},{15,... | collective-permute-start | bytes 1056776 | tf_op jit(solution)/shard_map/ppermute | solution.py:144
  64.3 16.0 %collective-permute-start.18 = (bf16[688,256]{1,0:T(8,128)(2,1)}, bf16[688,256]{1,0:T(8,128)(2,1)S(1)}, u32[]{:S(2)}, u32[]{:S(2)}) collective-permute-start(bf16[688,256]{1,0:T(8,128)(2,1)} %collective-permute-done.17), channel_id=1, source_target_pairs={{0,4},{1,5},{2,0},{3,1},{6,2},{7,3},{10,6},{11,7},{14,10},{15,11},... | collective-permute-start | bytes 1056776 | tf_op jit(solution)/shard_map/ppermute | solution.py:144
  64.6 16.3 %collective-permute-start.24 = (bf16[688,256]{1,0:T(8,128)(2,1)}, bf16[688,256]{1,0:T(8,128)(2,1)S(1)}, u32[]{:S(2)}, u32[]{:S(2)}) collective-permute-start(bf16[688,256]{1,0:T(8,128)(2,1)} %collective-permute-done.23), channel_id=1, source_target_pairs={{0,4},{1,5},{2,0},{3,1},{6,2},{7,3},{10,6},{11,7},{14,10},{15,11},... | collective-permute-start | bytes 1056776 | tf_op jit(solution)/shard_map/ppermute | solution.py:144
  71.6 15.1 %collective-permute-start.4 = (bf16[688,256]{1,0:T(8,128)(2,1)S(1)}, bf16[688,256]{1,0:T(8,128)(2,1)S(1)}, u32[]{:S(2)}, u32[]{:S(2)}) collective-permute-start(bf16[688,256]{1,0:T(8,128)(2,1)S(1)} %collective-permute-done.3), channel_id=1, source_target_pairs={{0,2},{1,3},{2,6},{3,7},{6,10},{7,11},{10,14},{11,15},{14,12},{15,... | collective-permute-start | bytes 1056776 | tf_op jit(solution)/shard_map/ppermute | solution.py:144
  79.1 15.1 %collective-permute-start.12 = (bf16[688,256]{1,0:T(8,128)(2,1)S(1)}, bf16[688,256]{1,0:T(8,128)(2,1)S(1)}, u32[]{:S(2)}, u32[]{:S(2)}) collective-permute-start(bf16[688,256]{1,0:T(8,128)(2,1)S(1)} %collective-permute-done.11), channel_id=1, source_target_pairs={{0,2},{1,3},{2,6},{3,7},{6,10},{7,11},{10,14},{11,15},{14,12},{15,... | collective-permute-start | bytes 1056776 | tf_op jit(solution)/shard_map/ppermute | solution.py:144
  80.3 18.0 %collective-permute-start.19 = (bf16[688,256]{1,0:T(8,128)(2,1)S(1)}, bf16[688,256]{1,0:T(8,128)(2,1)S(1)}, u32[]{:S(2)}, u32[]{:S(2)}) collective-permute-start(bf16[688,256]{1,0:T(8,128)(2,1)S(1)} %collective-permute-done.18), channel_id=1, source_target_pairs={{0,4},{1,5},{2,0},{3,1},{6,2},{7,3},{10,6},{11,7},{14,10},{15,11},... | collective-permute-start | bytes 1056776 | tf_op jit(solution)/shard_map/ppermute | solution.py:144
  80.9 20.8 %collective-permute-start.25 = (bf16[688,256]{1,0:T(8,128)(2,1)S(1)}, bf16[688,256]{1,0:T(8,128)(2,1)S(1)}, u32[]{:S(2)}, u32[]{:S(2)}) collective-permute-start(bf16[688,256]{1,0:T(8,128)(2,1)S(1)} %collective-permute-done.24), channel_id=1, source_target_pairs={{0,4},{1,5},{2,0},{3,1},{6,2},{7,3},{10,6},{11,7},{14,10},{15,11},... | collective-permute-start | bytes 1056776 | tf_op jit(solution)/shard_map/ppermute | solution.py:144
  86.7 27.3 %collective-permute-start.6 = (bf16[688,256]{1,0:T(8,128)(2,1)S(1)}, bf16[688,256]{1,0:T(8,128)(2,1)S(1)}, u32[]{:S(2)}, u32[]{:S(2)}) collective-permute-start(bf16[688,256]{1,0:T(8,128)(2,1)S(1)} %collective-permute-done.4), channel_id=1, source_target_pairs={{0,2},{1,3},{2,6},{3,7},{6,10},{7,11},{10,14},{11,15},{14,12},{15,... | collective-permute-start | bytes 1056776 | tf_op jit(solution)/shard_map/ppermute | solution.py:144
  94.2 20.9 %collective-permute-start.13 = (bf16[688,256]{1,0:T(8,128)(2,1)S(1)}, bf16[688,256]{1,0:T(8,128)(2,1)S(1)}, u32[]{:S(2)}, u32[]{:S(2)}) collective-permute-start(bf16[688,256]{1,0:T(8,128)(2,1)S(1)} %collective-permute-done.12), channel_id=1, source_target_pairs={{0,2},{1,3},{2,6},{3,7},{6,10},{7,11},{10,14},{11,15},{14,12},{15,... | collective-permute-start | bytes 1056776 | tf_op jit(solution)/shard_map/ppermute | solution.py:144
  98.3 18.0 %collective-permute-start.20 = (bf16[688,256]{1,0:T(8,128)(2,1)S(1)}, bf16[688,256]{1,0:T(8,128)(2,1)S(1)}, u32[]{:S(2)}, u32[]{:S(2)}) collective-permute-start(bf16[688,256]{1,0:T(8,128)(2,1)S(1)} %collective-permute-done.19), channel_id=1, source_target_pairs={{0,4},{1,5},{2,0},{3,1},{6,2},{7,3},{10,6},{11,7},{14,10},{15,11},... | collective-permute-start | bytes 1056776 | tf_op jit(solution)/shard_map/ppermute | solution.py:144
  101.6 15.0 %collective-permute-start.26 = (bf16[688,256]{1,0:T(8,128)(2,1)S(1)}, bf16[688,256]{1,0:T(8,128)(2,1)S(1)}, u32[]{:S(2)}, u32[]{:S(2)}) collective-permute-start(bf16[688,256]{1,0:T(8,128)(2,1)S(1)} %collective-permute-done.25), channel_id=1, source_target_pairs={{0,4},{1,5},{2,0},{3,1},{6,2},{7,3},{10,6},{11,7},{14,10},{15,11},... | collective-permute-start | bytes 1056776 | tf_op jit(solution)/shard_map/ppermute | solution.py:144
  114.0 15.7 %collective-permute-start.7 = (bf16[688,256]{1,0:T(8,128)(2,1)S(1)}, bf16[688,256]{1,0:T(8,128)(2,1)S(1)}, u32[]{:S(2)}, u32[]{:S(2)}) collective-permute-start(bf16[688,256]{1,0:T(8,128)(2,1)S(1)} %collective-permute-done.6), channel_id=1, source_target_pairs={{0,2},{1,3},{2,6},{3,7},{6,10},{7,11},{10,14},{11,15},{14,12},{15,... | collective-permute-start | bytes 1056776 | tf_op jit(solution)/shard_map/ppermute | solution.py:144
  115.1 15.7 %collective-permute-start.14 = (bf16[688,256]{1,0:T(8,128)(2,1)S(1)}, bf16[688,256]{1,0:T(8,128)(2,1)S(1)}, u32[]{:S(2)}, u32[]{:S(2)}) collective-permute-start(bf16[688,256]{1,0:T(8,128)(2,1)S(1)} %collective-permute-done.13), channel_id=1, source_target_pairs={{0,2},{1,3},{2,6},{3,7},{6,10},{7,11},{10,14},{11,15},{14,12},{15,... | collective-permute-start | bytes 1056776 | tf_op jit(solution)/shard_map/ppermute | solution.py:144
  116.3 15.7 %collective-permute-start.21 = (bf16[688,256]{1,0:T(8,128)(2,1)S(1)}, bf16[688,256]{1,0:T(8,128)(2,1)S(1)}, u32[]{:S(2)}, u32[]{:S(2)}) collective-permute-start(bf16[688,256]{1,0:T(8,128)(2,1)S(1)} %collective-permute-done.20), channel_id=1, source_target_pairs={{0,4},{1,5},{2,0},{3,1},{6,2},{7,3},{10,6},{11,7},{14,10},{15,11},... | collective-permute-start | bytes 1056776 | tf_op jit(solution)/shard_map/ppermute | solution.py:144
  116.6 15.7 %collective-permute-start.27 = (bf16[688,256]{1,0:T(8,128)(2,1)S(1)}, bf16[688,256]{1,0:T(8,128)(2,1)S(1)}, u32[]{:S(2)}, u32[]{:S(2)}) collective-permute-start(bf16[688,256]{1,0:T(8,128)(2,1)S(1)} %collective-permute-done.26), channel_id=1, source_target_pairs={{0,4},{1,5},{2,0},{3,1},{6,2},{7,3},{10,6},{11,7},{14,10},{15,11},... | collective-permute-start | bytes 1056776 | tf_op jit(solution)/shard_map/ppermute | solution.py:144
  129.7 6.2 %collective-permute-start.8 = (bf16[688,256]{1,0:T(8,128)(2,1)S(1)}, bf16[688,256]{1,0:T(8,128)(2,1)S(1)}, u32[]{:S(2)}, u32[]{:S(2)}) collective-permute-start(bf16[688,256]{1,0:T(8,128)(2,1)S(1)} %collective-permute-done.7), channel_id=1, source_target_pairs={{0,2},{1,3},{2,6},{3,7},{6,10},{7,11},{10,14},{11,15},{14,12},{15,... | collective-permute-start | bytes 1056776 | tf_op jit(solution)/shard_map/ppermute | solution.py:144
  130.8 16.2 %collective-permute-start.15 = (bf16[688,256]{1,0:T(8,128)(2,1)S(1)}, bf16[688,256]{1,0:T(8,128)(2,1)S(1)}, u32[]{:S(2)}, u32[]{:S(2)}) collective-permute-start(bf16[688,256]{1,0:T(8,128)(2,1)S(1)} %collective-permute-done.14), channel_id=1, source_target_pairs={{0,2},{1,3},{2,6},{3,7},{6,10},{7,11},{10,14},{11,15},{14,12},{15,... | collective-permute-start | bytes 1056776 | tf_op jit(solution)/shard_map/ppermute | solution.py:144
  132.0 18.8 %collective-permute-start.22 = (bf16[688,256]{1,0:T(8,128)(2,1)S(1)}, bf16[688,256]{1,0:T(8,128)(2,1)S(1)}, u32[]{:S(2)}, u32[]{:S(2)}) collective-permute-start(bf16[688,256]{1,0:T(8,128)(2,1)S(1)} %collective-permute-done.21), channel_id=1, source_target_pairs={{0,4},{1,5},{2,0},{3,1},{6,2},{7,3},{10,6},{11,7},{14,10},{15,11},... | collective-permute-start | bytes 1056776 | tf_op jit(solution)/shard_map/ppermute | solution.py:144
  132.3 21.5 %collective-permute-start.28 = (bf16[688,256]{1,0:T(8,128)(2,1)S(1)}, bf16[688,256]{1,0:T(8,128)(2,1)S(1)}, u32[]{:S(2)}, u32[]{:S(2)}) collective-permute-start(bf16[688,256]{1,0:T(8,128)(2,1)S(1)} %collective-permute-done.27), channel_id=1, source_target_pairs={{0,4},{1,5},{2,0},{3,1},{6,2},{7,3},{10,6},{11,7},{14,10},{15,11},... | collective-permute-start | bytes 1056776 | tf_op jit(solution)/shard_map/ppermute | solution.py:144
  138.8 21.0 %collective-permute-start.29 = (f32[384,256]{1,0:T(8,128)S(1)}, f32[384,256]{1,0:T(8,128)S(1)}, u32[]{:S(2)}, u32[]{:S(2)}) collective-permute-start(f32[384,256]{1,0:T(8,128)S(1)} %fusion.3), channel_id=1, source_target_pairs={{0,1},{1,0},{2,3},{3,2},{4,5},{5,4},{6,7},{7,6},{8,9},{9,8},{10,11... | collective-permute-start | bytes 1179656 | tf_op jit(solution)/shard_map/ppermute | solution.py:159
  149.9 9.9 %collective-permute-start.30 = (f32[384,256]{1,0:T(8,128)S(1)}, f32[384,256]{1,0:T(8,128)S(1)}, u32[]{:S(2)}, u32[]{:S(2)}) collective-permute-start(f32[384,256]{1,0:T(8,128)S(1)} %fusion.2), channel_id=1, source_target_pairs={{0,1},{1,0},{2,3},{3,2},{4,5},{5,4},{6,7},{7,6},{8,9},{9,8},{10,11... | collective-permute-start | bytes 1179656 | tf_op jit(solution)/shard_map/ppermute | solution.py:159
  153.7 6.1 %collective-permute-start.31 = (f32[384,256]{1,0:T(8,128)S(1)}, f32[384,256]{1,0:T(8,128)S(1)}, u32[]{:S(2)}, u32[]{:S(2)}) collective-permute-start(f32[384,256]{1,0:T(8,128)S(1)} %fusion.1), channel_id=1, source_target_pairs={{0,1},{1,0},{2,3},{3,2},{4,5},{5,4},{6,7},{7,6},{8,9},{9,8},{10,11... | collective-permute-start | bytes 1179656 | tf_op jit(solution)/shard_map/ppermute | solution.py:159
  156.6 3.2 %collective-permute-start.32 = (f32[384,256]{1,0:T(8,128)S(1)}, f32[384,256]{1,0:T(8,128)S(1)}, u32[]{:S(2)}, u32[]{:S(2)}) collective-permute-start(f32[384,256]{1,0:T(8,128)S(1)} %fusion), channel_id=1, source_target_pairs={{0,1},{1,0},{2,3},{3,2},{4,5},{5,4},{6,7},{7,6},{8,9},{9,8},{10,11... | collective-permute-start | bytes 1179656 | tf_op jit(solution)/shard_map/ppermute | solution.py:159
  162.0 41.9 %all-to-all-start = ((bf16[16,6,16,512]{3,2,1,0:T(8,128)(2,1)}), bf16[16,6,16,512]{3,2,1,0:T(8,128)(2,1)S(1)}, u32[]{:S(2)}, u32[]{:S(2)}) async-start(bf16[16,6,16,512]{3,2,1,0:T(8,128)(2,1)} %shard_map.51), calls=%async_computation | async-start | bytes 3145728 | tf_op jit(solution)/shard_map/all_to_all | solution.py:185

commit v4 on v3

v4 whole, which is shorter than its diff:
```python
import functools
import math

import jax
import jax.numpy as jnp
from jax import lax
from jax.experimental import pallas as pl
from jax.experimental.pallas import tpu as pltpu
from jax.sharding import PartitionSpec as P

GRID_CHIPS = 8
HALVES = 2
WAYS = (1, -1)
LANES = 128
WINDOW = 896


def ring_chip(at):
    at = at % GRID_CHIPS
    back = 2 * ((GRID_CHIPS - at) % GRID_CHIPS)
    up = 2 * at - 1
    if isinstance(at, int):
        return up if 1 <= at <= GRID_CHIPS // 2 else back
    return jnp.where((at >= 1) & (at <= GRID_CHIPS // 2), up, back)


def ring_place(chip):
    z, y = chip // 2, chip % 2
    return jnp.where(y == 1, 1 + z, (GRID_CHIPS - z) % GRID_CHIPS)


def routing(owners, count, slots, block_rows):
    blocks_here = owners.shape[0]
    rows = blocks_here * block_rows
    owner_col = owners[:, 0]
    same = owner_col[:, None] == owner_col[None, :]
    lower = jnp.arange(blocks_here)[:, None] > jnp.arange(blocks_here)[None, :]
    rank = jnp.sum((same & lower).astype(jnp.int32), axis=1)
    target = owner_col * slots + rank
    select = jnp.arange(count * slots, dtype=jnp.int32)[:, None] == target[None, :]
    global_ids = lax.axis_index("wide") * blocks_here + jnp.arange(blocks_here, dtype=jnp.int32)
    labels = jnp.sum(jnp.where(select, global_ids[None, :] + 1, 0), axis=1) - 1
    row_at = jnp.arange(rows, dtype=jnp.int32)
    out_at = jnp.arange(count * block_rows * slots, dtype=jnp.int32)
    row_key = jnp.repeat(target, block_rows) * block_rows + row_at % block_rows
    out_key = (
        out_at // (block_rows * slots) * slots + out_at % slots
    ) * block_rows + out_at // slots % block_rows
    place = (out_key[:, None] == row_key[None, :]).astype(jnp.bfloat16)
    return labels.reshape(count, slots), place


def window_at(start, nvirt):
    return jnp.minimum(start // LANES * LANES, nvirt - WINDOW)


def step_kernel(t, own_hbm, other_hbm, *refs):
    norb = len(WAYS)
    pieces = refs[:norb]
    before, (mine_ref, theirs_ref, c_buf, g_buf, sems) = refs[norb:-5], refs[-5:]
    rows, nvirt = own_hbm.shape
    depth = pieces[0].shape[0]
    me = lax.axis_index("wide")
    core = lax.rem(me, 2)
    here = ring_place(lax.div(me, 2))
    shifts, copies = [], []
    for i in range(norb):
        chip = ring_chip(here - t * WAYS[i] + GRID_CHIPS)
        start = (2 * chip + core) * depth
        at = pl.multiple_of(window_at(start, nvirt), LANES)
        shifts.append(pl.multiple_of(start - at, 16))
        columns = pl.ds(at, WINDOW)
        copies.append(
            [
                pltpu.make_async_copy(
                    source.at[:, columns], c_buf.at[i, pl.ds(k * rows, rows)], sems.at[i, k]
                )
                for k, source in enumerate((own_hbm, other_hbm))
            ]
        )
        for copy in copies[i]:
            copy.start()
    for i in range(norb):
        g_buf[i] = jnp.zeros_like(g_buf[i])
        g_buf[i, pl.ds(shifts[i], depth), :] = pieces[i][...]
    for i in range(norb):
        for copy in copies[i]:
            copy.wait()
        term = jnp.dot(c_buf[i], g_buf[i], preferred_element_type=jnp.float32)
        if before:
            mine_ref[i] = before[0][i] + term[:rows]
            theirs_ref[i] = before[1][i] + term[rows:]
        else:
            mine_ref[i] = term[:rows]
            theirs_ref[i] = term[rows:]


def add_products(t, own, other, pieces, before):
    rows, nvirt = own.shape
    norb = len(pieces)
    depth, width = pieces[0].shape
    sums = jax.ShapeDtypeStruct((norb, rows, width), jnp.float32)
    vmem = pl.BlockSpec(memory_space=pltpu.VMEM)
    hbm = pl.BlockSpec(memory_space=pltpu.HBM)
    return pl.pallas_call(
        functools.partial(step_kernel, t),
        out_shape=(sums, sums),
        in_specs=[hbm, hbm] + [vmem] * (norb + len(before)),
        out_specs=(vmem, vmem),
        input_output_aliases={2 + norb + k: k for k in range(len(before))},
        scratch_shapes=[
            pltpu.VMEM((norb, 2 * rows, WINDOW), jnp.bfloat16),
            pltpu.VMEM((norb, WINDOW, width), jnp.bfloat16),
            pltpu.SemaphoreType.DMA((norb, 2)),
        ],
        compiler_params=pltpu.CompilerParams(vmem_limit_bytes=16 << 20),
        cost_estimate=pl.CostEstimate(
            flops=4 * norb * rows * WINDOW * width,
            bytes_accessed=4 * norb * rows * WINDOW,
            transcendentals=0,
        ),
    )(own, other, *pieces, *before)


def finish_kernel(place_ref, *refs):
    out_ref = refs[-1]
    mine, theirs = refs[:HALVES], refs[HALVES:-1]
    count, planes, slots, naux = out_ref.shape
    norb, _, width = mine[0].shape
    for i in range(norb):
        for j in range(HALVES):
            back = (mine[j][i] + theirs[j][i]).astype(jnp.bfloat16)
            out = jnp.dot(place_ref[...], back, preferred_element_type=jnp.float32)
            out = out.astype(jnp.bfloat16).reshape(count, planes // norb, slots, width)
            out_ref[
                :, pl.ds(i * (planes // norb), planes // norb), :, pl.ds(j * width, width)
            ] = out


def finish(place, mine, theirs, shape):
    return pl.pallas_call(
        finish_kernel,
        out_shape=jax.ShapeDtypeStruct(shape, jnp.bfloat16),
        in_specs=[pl.BlockSpec(memory_space=pltpu.VMEM)] * (1 + len(mine) + len(theirs)),
        out_specs=pl.BlockSpec(memory_space=pltpu.VMEM),
        compiler_params=pltpu.CompilerParams(vmem_limit_bytes=20 << 20),
        cost_estimate=pl.CostEstimate(
            flops=2 * math.prod(shape) * place.shape[1],
            bytes_accessed=2 * math.prod(shape),
            transcendentals=0,
        ),
    )(place, *mine, *theirs)


def ring_products(gamma, coefficients, early):
    count = lax.axis_size("wide")
    norb, depth, naux = gamma.shape
    width = naux // HALVES
    swap = [(d, d ^ 1) for d in range(count)]
    other = lax.ppermute(coefficients, "wide", swap)

    piece = [
        [gamma[i, :, j * width : (j + 1) * width] for i in range(norb)] for j in range(HALVES)
    ]
    shift = [
        [
            (2 * ring_chip(p) + k, 2 * ring_chip(p + way) + k)
            for p in range(GRID_CHIPS)
            for k in range(2)
        ]
        for way in WAYS
    ]
    sums = [()] * HALVES
    for t in range(GRID_CHIPS):
        for j in range(HALVES):
            arrived = list(piece[j])
            if t + 1 < GRID_CHIPS:
                for i in range(norb):
                    sent = arrived[i]
                    if t == 2 and i == j == 0:
                        sent, early = lax.optimization_barrier((sent, early))
                    if t >= 4:
                        sent, sums[j] = lax.optimization_barrier((sent, sums[j]))
                    piece[j][i] = lax.ppermute(sent, "wide", shift[i])
            sums[j] = add_products(t, coefficients, other, arrived, sums[j])
    mine = [sums[j][0] for j in range(HALVES)]
    theirs = [lax.ppermute(sums[j][1], "wide", swap) for j in range(HALVES)]
    return mine, theirs, early


def local(gamma, coefficients, owners):
    count = lax.axis_size("wide")
    blocks_here = owners.shape[0]
    slots = max(2, 2 * blocks_here // count)
    block_rows = coefficients.shape[0] // blocks_here
    norb, depth, naux = gamma.shape
    shape = (count, norb * block_rows, slots, naux)

    labels, place = routing(owners, count, slots, block_rows)
    ids = lax.all_to_all(labels, "wide", split_axis=0, concat_axis=0, tiled=True)
    if count == 2 * GRID_CHIPS and norb == len(WAYS):
        mine, theirs, (ids, place) = ring_products(gamma, coefficients, (ids, place))
        out = finish(place, mine, theirs, shape)
    else:
        gathered = lax.all_gather(gamma, "wide", axis=1, tiled=True)
        back = jnp.einsum(
            "ra,ian->irn", coefficients, gathered, preferred_element_type=jnp.float32
        ).astype(jnp.bfloat16)
        out = jnp.einsum("tr,irn->itn", place, back, preferred_element_type=jnp.float32)
        out = out.astype(jnp.bfloat16).reshape(norb, count, block_rows, slots, naux)
        out = out.transpose(1, 0, 2, 3, 4).reshape(shape)
    placed = lax.all_to_all(out, "wide", split_axis=0, concat_axis=0, tiled=True)
    return placed.transpose(0, 2, 1, 3)[None], ids[None]


def solution(mesh):
    placed = (P("groups", "wide", None), P("wide", None), P("wide", None))
    return jax.shard_map(
        local,
        mesh=mesh,
        in_specs=placed,
        out_specs=(P("wide", None, "groups", None, None), P("wide", "groups", None)),
        check_vma=False,
    )
```

time: 208 us -> 179 us (0.86)
  matrix products: 70.9 us -> 0 us
  Pallas kernels: 13.2 us -> 55.8 us
  waiting for transfers between devices: 53.3 us -> 71.7 us
  local copies, waits for them, and re-layouts: 18.6 us -> 7.52 us
  starting transfers between devices: 46.1 us -> 41.8 us
    dot_general x64 -> x0, matrix products: 70.9 us -> none  [the longest x32 46 us: ring_products(): term = jnp.dot(left, block, preferred_element_type=jnp.float32)]
    pallas_call x1 -> x16, Pallas kernels: 11.1 us -> 53.7 us  [add_products(): pl.pallas_call(functools.partial(step_kernel, t), out_shape=(sums, sums),...]
    ppermute x33 -> x31, waiting for transfers between devices: 17.1 us -> 34 us  [the longest x28 32.1 us: ring_products(): piece[j][i] = lax.ppermute(sent, 'wide', shift[i])]
    pallas_call x1 -> x0, local copies, waits for them, and re-layouts: 6.75 us -> none  [spread(): pl.pallas_call(spread_kernel, grid=(rows // step,), out_shape=(shape, sha...]
    ppermute x33 -> x31, starting transfers between devices: 34.4 us -> 28.9 us  [the longest x28 20.8 us: ring_products(): piece[j][i] = lax.ppermute(sent, 'wide', shift[i])]
    unnamed x18 -> x6, local copies, waits for them, and re-layouts: 9.45 us -> 5.15 us
  transfers between devices with their start and end apart: 35 -> 33, of which waited for: 8 -> 12; matrix products, arithmetic and copies ran while one was open for 39% -> 2% of each run, Pallas kernels for 6% -> 30%
where the time goes in v4:
time: 179 us; the launch traced here: 178 us
  waiting for transfers between devices  71.7 us (40%)
  Pallas kernels  55.8 us (31%)
  starting transfers between devices  41.8 us (23%)
  local copies, waits for them, and re-layouts  7.52 us (4%)
    pallas_call x16, Pallas kernels, add_products(): pl.pallas_call(functools.partial(step_kernel, t), out_shape=(sums, sums),...  53.7 us
    all_to_all x1, waiting for transfers between devices, local(): lax.all_to_all(out, 'wide', split_axis=0, concat_axis=0, tiled=True)  36.2 us
    ppermute x28, waiting for transfers between devices, ring_products(): piece[j][i] = lax.ppermute(sent, 'wide', shift[i])  32.1 us
    ppermute x28, starting transfers between devices, ring_products(): piece[j][i] = lax.ppermute(sent, 'wide', shift[i])  20.8 us
    all_to_all x1, starting transfers between devices, local(): lax.all_to_all(labels, 'wide', split_axis=0, concat_axis=0, tiled=True)  7.68 us
    ppermute x2, starting transfers between devices, ring_products(): theirs = [lax.ppermute(sums[j][1], 'wide', swap) for j in range(HALVES)]  7.34 us
    all_to_all x1, starting transfers between devices, local(): lax.all_to_all(out, 'wide', split_axis=0, concat_axis=0, tiled=True)  5.2 us
    unnamed x6, local copies, waits for them, and re-layouts  5.15 us
  transfers between devices with their start and end apart: 33, of which 12 were waited for; matrix products, arithmetic and copies ran while one was open for 2% of the time, Pallas kernels for 30%

profile of v4, /device:TPU:13, one launch (start us, length us, event | category | flops | bytes accessed | tf_op | source)
XLA Modules:
  0.0 178.1 jit_solution(12574392942764230727)
XLA Ops:
  0.6 0.7 collective-permute-start.2
  1.4 1.4 slice_bitcast_fusion
  2.8 1.3 collective-permute-start.15
  4.1 0.2 collective-permute-start.19
  4.3 1.3 collective-permute-start
  5.6 0.2 collective-permute-start.5
  5.8 0.2 convert_reduce_fusion
  6.1 6.6 %collective-permute-done.15.refs_0_ = bf16[688,256]{1,0:T(8,128)(2,1)S(1)} collective-permute-done((bf16[688,256]{1,0:T(8,128)(2,1)S(1)}, bf16[688,256]{1,0:T(8,128)(2,1)S(1)}, u32[]{:S(2)}, u32[]{:S(2)}) %collective-permute-start.15) | collective-permute-done | bytes 352288 | tf_op jit(solution)/shard_map/ppermute | solution.py:184
  12.7 1.3 collective-permute-start.16
  14.0 0.2 collective-permute-start.20
  14.2 0.7 sub.17
  14.8 7.7 %all-to-all-start = ((s32[16,1,16]{2,1,0:T(1,128)}), s32[16,1,16]{2,1,0:T(1,128)S(1)}, u32[]{:S(2)}, u32[]{:S(2)}) async-start(s32[16,1,16]{2,1,0:T(1,128)} %sub.17), calls=%async_computation | async-start | bytes 16384 | tf_op jit(solution)/shard_map/all_to_all | solution.py:200
  22.6 0.2 mul.58
  22.8 1.2 collective-permute-start.1
  24.1 0.3 collective-permute-start.6
  24.4 3.5 %collective-permute-done.16.refs_0_ = bf16[688,256]{1,0:T(8,128)(2,1)} collective-permute-done((bf16[688,256]{1,0:T(8,128)(2,1)S(1)}, bf16[688,256]{1,0:T(8,128)(2,1)}, u32[]{:S(2)}, u32[]{:S(2)}) %collective-permute-start.16) | collective-permute-done | bytes 352288 | tf_op jit(solution)/shard_map/ppermute | solution.py:184
  27.9 1.3 collective-permute-start.17
  29.2 0.1 collective-permute-start.21
  29.4 0.2 compare_convert_fusion.place_ref
  29.5 1.5 all-to-all-done
  31.0 4.6 %collective-permute-done.1.refs_0_ = bf16[688,256]{1,0:T(8,128)(2,1)} collective-permute-done((bf16[688,256]{1,0:T(8,128)(2,1)S(1)}, bf16[688,256]{1,0:T(8,128)(2,1)}, u32[]{:S(2)}, u32[]{:S(2)}) %collective-permute-start.1) | collective-permute-done | bytes 352288 | tf_op jit(solution)/shard_map/ppermute | solution.py:184
  35.6 1.3 collective-permute-start.3
  36.9 0.1 collective-permute-start.7
  37.0 6.1 %collective-permute-done.17.refs_0_ = bf16[688,256]{1,0:T(8,128)(2,1)} collective-permute-done((bf16[688,256]{1,0:T(8,128)(2,1)}, bf16[688,256]{1,0:T(8,128)(2,1)}, u32[]{:S(2)}, u32[]{:S(2)}) %collective-permute-start.17) | collective-permute-done | bytes 352288 | tf_op jit(solution)/shard_map/ppermute | solution.py:184
  43.1 1.3 collective-permute-start.18
  44.5 0.1 collective-permute-start.23
  44.6 6.0 %collective-permute-done.3.refs_0_ = bf16[688,256]{1,0:T(8,128)(2,1)S(1)} collective-permute-done((bf16[688,256]{1,0:T(8,128)(2,1)}, bf16[688,256]{1,0:T(8,128)(2,1)S(1)}, u32[]{:S(2)}, u32[]{:S(2)}) %collective-permute-start.3) | collective-permute-done | bytes 352288 | tf_op jit(solution)/shard_map/ppermute | solution.py:184
  50.6 1.3 collective-permute-start.4
  51.9 0.1 collective-permute-start.9
  52.0 3.4 %copy-done = bf16[384,11008]{1,0:T(8,128)(2,1)S(1)} copy-done((bf16[384,11008]{1,0:T(8,128)(2,1)S(1)}, bf16[384,11008]{1,0:T(8,128)(2,1)}, u32[]{:S(2)}) %copy-start) | copy-done | bytes 8454168
  55.4 3.1 %shard_map.58 = (f32[2,384,256]{2,1,0:T(8,128)S(1)}, f32[2,384,256]{2,1,0:T(8,128)S(1)}) custom-call(bf16[384,11008]{1,0:T(8,128)(2,1)S(1)} %copy-done, bf16[384,11008]{1,0:T(8,128)(2,1)} %collective-permute-done.2.other_hbm, bf16[688,256]{1,0:T(8,128)(2,1)S(1)} %get-tuple-element.149.refs_0_, bf16[688,256]{1,0:T(8,128)(2,1)S(1)} %get-tuple-element.146.refs_1_), custom_call_target="tpu_custom_call" | custom-call | flops 704643072 | bytes 2752512 | tf_op jit(solution)/shard_map/pallas_call | solution.py:105
  58.5 3.2 %shard_map.59 = (f32[2,384,256]{2,1,0:T(8,128)S(1)}, f32[2,384,256]{2,1,0:T(8,128)S(1)}) custom-call(bf16[384,11008]{1,0:T(8,128)(2,1)S(1)} %copy-done, bf16[384,11008]{1,0:T(8,128)(2,1)} %collective-permute-done.2.other_hbm, bf16[688,256]{1,0:T(8,128)(2,1)S(1)} %collective-permute-done.15.refs_0_, ...), custom_call_target="tpu_custom_call", output_to_operand_aliasing={{0}: (4, {}), {1}: (5, {})} | custom-call | flops 704643072 | bytes 2752512 | tf_op jit(solution)/shard_map/pallas_call | solution.py:105
  61.7 4.2 %shard_map.60 = (f32[2,384,256]{2,1,0:T(8,128)S(1)}, f32[2,384,256]{2,1,0:T(8,128)S(1)}) custom-call(bf16[384,11008]{1,0:T(8,128)(2,1)S(1)} %copy-done, bf16[384,11008]{1,0:T(8,128)(2,1)} %collective-permute-done.2.other_hbm, bf16[688,256]{1,0:T(8,128)(2,1)} %collective-permute-done.16.refs_0_, ...), custom_call_target="tpu_custom_call", output_to_operand_aliasing={{0}: (4, {}), {1}: (5, {})} | custom-call | flops 704643072 | bytes 2752512 | tf_op jit(solution)/shard_map/pallas_call | solution.py:105
  66.0 4.2 %shard_map.61 = (f32[2,384,256]{2,1,0:T(8,128)S(1)}, f32[2,384,256]{2,1,0:T(8,128)S(1)}) custom-call(bf16[384,11008]{1,0:T(8,128)(2,1)S(1)} %copy-done, bf16[384,11008]{1,0:T(8,128)(2,1)} %collective-permute-done.2.other_hbm, bf16[688,256]{1,0:T(8,128)(2,1)} %collective-permute-done.17.refs_0_, ...), custom_call_target="tpu_custom_call", output_to_operand_aliasing={{0}: (4, {}), {1}: (5, {})} | custom-call | flops 704643072 | bytes 2752512 | tf_op jit(solution)/shard_map/pallas_call | solution.py:105
  70.2 1.4 collective-permute-start.22
  71.8 3.1 %shard_map.50 = (f32[2,384,256]{2,1,0:T(8,128)S(1)}, f32[2,384,256]{2,1,0:T(8,128)S(1)}) custom-call(bf16[384,11008]{1,0:T(8,128)(2,1)S(1)} %copy-done, bf16[384,11008]{1,0:T(8,128)(2,1)} %collective-permute-done.2.other_hbm, bf16[688,256]{1,0:T(8,128)(2,1)S(1)} %get-tuple-element.148.refs_0_, bf16[688,256]{1,0:T(8,128)(2,1)S(1)} %get-tuple-element.147.refs_1_), custom_call_target="tpu_custom_call" | custom-call | flops 704643072 | bytes 2752512 | tf_op jit(solution)/shard_map/pallas_call | solution.py:105
  74.9 3.2 %shard_map.51 = (f32[2,384,256]{2,1,0:T(8,128)S(1)}, f32[2,384,256]{2,1,0:T(8,128)S(1)}) custom-call(bf16[384,11008]{1,0:T(8,128)(2,1)S(1)} %copy-done, bf16[384,11008]{1,0:T(8,128)(2,1)} %collective-permute-done.2.other_hbm, bf16[688,256]{1,0:T(8,128)(2,1)S(1)} %collective-permute-done.refs_0_, ...), custom_call_target="tpu_custom_call", output_to_operand_aliasing={{0}: (4, {}), {1}: (5, {})} | custom-call | flops 704643072 | bytes 2752512 | tf_op jit(solution)/shard_map/pallas_call | solution.py:105
  78.1 4.2 %shard_map.52 = (f32[2,384,256]{2,1,0:T(8,128)S(1)}, f32[2,384,256]{2,1,0:T(8,128)S(1)}) custom-call(bf16[384,11008]{1,0:T(8,128)(2,1)S(1)} %copy-done, bf16[384,11008]{1,0:T(8,128)(2,1)} %collective-permute-done.2.other_hbm, bf16[688,256]{1,0:T(8,128)(2,1)} %collective-permute-done.1.refs_0_, ...), custom_call_target="tpu_custom_call", output_to_operand_aliasing={{0}: (4, {}), {1}: (5, {})} | custom-call | flops 704643072 | bytes 2752512 | tf_op jit(solution)/shard_map/pallas_call | solution.py:105
  82.3 3.2 %shard_map.53 = (f32[2,384,256]{2,1,0:T(8,128)S(1)}, f32[2,384,256]{2,1,0:T(8,128)S(1)}) custom-call(bf16[384,11008]{1,0:T(8,128)(2,1)S(1)} %copy-done, bf16[384,11008]{1,0:T(8,128)(2,1)} %collective-permute-done.2.other_hbm, bf16[688,256]{1,0:T(8,128)(2,1)S(1)} %collective-permute-done.3.refs_0_, ...), custom_call_target="tpu_custom_call", output_to_operand_aliasing={{0}: (4, {}), {1}: (5, {})} | custom-call | flops 704643072 | bytes 2752512 | tf_op jit(solution)/shard_map/pallas_call | solution.py:105
  85.5 1.4 collective-permute-start.8
  87.0 3.1 %shard_map.62 = (f32[2,384,256]{2,1,0:T(8,128)S(1)}, f32[2,384,256]{2,1,0:T(8,128)S(1)}) custom-call(bf16[384,11008]{1,0:T(8,128)(2,1)S(1)} %copy-done, bf16[384,11008]{1,0:T(8,128)(2,1)} %collective-permute-done.2.other_hbm, bf16[688,256]{1,0:T(8,128)(2,1)S(1)} %collective-permute-done.18.refs_0_, ...), custom_call_target="tpu_custom_call", output_to_operand_aliasing={{0}: (4, {}), {1}: (5, {})} | custom-call | flops 704643072 | bytes 2752512 | tf_op jit(solution)/shard_map/pallas_call | solution.py:105
  90.2 1.4 collective-permute-start.24
  91.7 3.1 %shard_map.54 = (f32[2,384,256]{2,1,0:T(8,128)S(1)}, f32[2,384,256]{2,1,0:T(8,128)S(1)}) custom-call(bf16[384,11008]{1,0:T(8,128)(2,1)S(1)} %copy-done, bf16[384,11008]{1,0:T(8,128)(2,1)} %collective-permute-done.2.other_hbm, bf16[688,256]{1,0:T(8,128)(2,1)S(1)} %collective-permute-done.4.refs_0_, ...), custom_call_target="tpu_custom_call", output_to_operand_aliasing={{0}: (4, {}), {1}: (5, {})} | custom-call | flops 704643072 | bytes 2752512 | tf_op jit(solution)/shard_map/pallas_call | solution.py:105
  94.9 1.4 collective-permute-start.10
  96.4 3.1 %shard_map.63 = (f32[2,384,256]{2,1,0:T(8,128)S(1)}, f32[2,384,256]{2,1,0:T(8,128)S(1)}) custom-call(bf16[384,11008]{1,0:T(8,128)(2,1)S(1)} %copy-done, bf16[384,11008]{1,0:T(8,128)(2,1)} %collective-permute-done.2.other_hbm, bf16[688,256]{1,0:T(8,128)(2,1)S(1)} %collective-permute-done.22.refs_0_, ...), custom_call_target="tpu_custom_call", output_to_operand_aliasing={{0}: (4, {}), {1}: (5, {})} | custom-call | flops 704643072 | bytes 2752512 | tf_op jit(solution)/shard_map/pallas_call | solution.py:105
  99.5 1.0 collective-permute-done.24.refs_0_
  100.6 1.3 collective-permute-done.27.refs_1_
  102.0 1.3 collective-permute-start.26
  103.4 3.1 %shard_map.55 = (f32[2,384,256]{2,1,0:T(8,128)S(1)}, f32[2,384,256]{2,1,0:T(8,128)S(1)}) custom-call(bf16[384,11008]{1,0:T(8,128)(2,1)S(1)} %copy-done, bf16[384,11008]{1,0:T(8,128)(2,1)} %collective-permute-done.2.other_hbm, bf16[688,256]{1,0:T(8,128)(2,1)S(1)} %collective-permute-done.8.refs_0_, ...), custom_call_target="tpu_custom_call", output_to_operand_aliasing={{0}: (4, {}), {1}: (5, {})} | custom-call | flops 704643072 | bytes 2752512 | tf_op jit(solution)/shard_map/pallas_call | solution.py:105
  106.5 1.6 collective-permute-done.10.refs_0_
  108.1 1.3 collective-permute-done.13.refs_1_
  109.6 1.3 collective-permute-start.12
  110.9 3.1 %shard_map.64 = (f32[2,384,256]{2,1,0:T(8,128)S(1)}, f32[2,384,256]{2,1,0:T(8,128)S(1)}) custom-call(bf16[384,11008]{1,0:T(8,128)(2,1)S(1)} %copy-done, bf16[384,11008]{1,0:T(8,128)(2,1)} %collective-permute-done.2.other_hbm, bf16[688,256]{1,0:T(8,128)(2,1)S(1)} %collective-permute-done.24.refs_0_, ...), custom_call_target="tpu_custom_call", output_to_operand_aliasing={{0}: (4, {}), {1}: (5, {})} | custom-call | flops 704643072 | bytes 2752512 | tf_op jit(solution)/shard_map/pallas_call | solution.py:105
  114.1 3.2 %shard_map.56 = (f32[2,384,256]{2,1,0:T(8,128)S(1)}, f32[2,384,256]{2,1,0:T(8,128)S(1)}) custom-call(bf16[384,11008]{1,0:T(8,128)(2,1)S(1)} %copy-done, bf16[384,11008]{1,0:T(8,128)(2,1)} %collective-permute-done.2.other_hbm, bf16[688,256]{1,0:T(8,128)(2,1)S(1)} %collective-permute-done.10.refs_0_, ...), custom_call_target="tpu_custom_call", output_to_operand_aliasing={{0}: (4, {}), {1}: (5, {})} | custom-call | flops 704643072 | bytes 2752512 | tf_op jit(solution)/shard_map/pallas_call | solution.py:105
  117.3 3.2 %shard_map.65 = (f32[2,384,256]{2,1,0:T(8,128)S(1)}, f32[2,384,256]{2,1,0:T(8,128)S(1)}) custom-call(bf16[384,11008]{1,0:T(8,128)(2,1)S(1)} %copy-done, bf16[384,11008]{1,0:T(8,128)(2,1)} %collective-permute-done.2.other_hbm, bf16[688,256]{1,0:T(8,128)(2,1)S(1)} %collective-permute-done.26.refs_0_, ...), custom_call_target="tpu_custom_call", output_to_operand_aliasing={{0}: (4, {}), {1}: (5, {})} | custom-call | flops 704643072 | bytes 2752512 | tf_op jit(solution)/shard_map/pallas_call | solution.py:105
  120.5 6.6 %collective-permute-start.30 = (f32[2,384,256]{2,1,0:T(8,128)S(1)}, f32[2,384,256]{2,1,0:T(8,128)S(1)}, u32[]{:S(2)}, u32[]{:S(2)}) collective-permute-start(f32[2,384,256]{2,1,0:T(8,128)S(1)} %get-tuple-element.142), channel_id=1, source_target_pairs={{0,1},{1,0},{2,3},{3,2},{4,5},{5,4},{6,7},{7,6},{8,9},{9,8},{10,11... | collective-permute-start | bytes 2359304 | tf_op jit(solution)/shard_map/ppermute | solution.py:187
  127.1 3.1 %shard_map.57 = (f32[2,384,256]{2,1,0:T(8,128)S(1)}, f32[2,384,256]{2,1,0:T(8,128)S(1)}) custom-call(bf16[384,11008]{1,0:T(8,128)(2,1)S(1)} %copy-done, bf16[384,11008]{1,0:T(8,128)(2,1)} %collective-permute-done.2.other_hbm, bf16[688,256]{1,0:T(8,128)(2,1)S(1)} %collective-permute-done.12.refs_0_, ...), custom_call_target="tpu_custom_call", output_to_operand_aliasing={{0}: (4, {}), {1}: (5, {})} | custom-call | flops 704643072 | bytes 2752512 | tf_op jit(solution)/shard_map/pallas_call | solution.py:105
  130.3 0.7 collective-permute-start.29
  131.0 1.9 %collective-permute-done.29.refs_2_ = f32[2,384,256]{2,1,0:T(8,128)S(1)} collective-permute-done((f32[2,384,256]{2,1,0:T(8,128)S(1)}, f32[2,384,256]{2,1,0:T(8,128)S(1)}, u32[]{:S(2)}, u32[]{:S(2)}) %collective-permute-start.29) | collective-permute-done | bytes 786464 | tf_op jit(solution)/shard_map/ppermute | solution.py:187
  132.9 2.1 %shard_map.66 = bf16[16,6,16,512]{3,2,1,0:T(8,128)(2,1)} custom-call(bf16[768,384]{1,0:T(8,128)(2,1)S(1)} %compare_convert_fusion.place_ref, f32[2,384,256]{2,1,0:T(8,128)S(1)} %get-tuple-element.107.refs_0_, f32[2,384,256]{2,1,0:T(8,128)S(1)} %get-tuple-element.140.refs_1_, f32[2,384,256]{2,1,0:T(8,128)S(1)} %collective-permute-done.29.refs_2_, ...), custom_call_target="tpu_custom_call" | custom-call | flops 603979776 | bytes 1572864 | tf_op jit(solution)/shard_map/pallas_call | solution.py:141
  135.0 5.2 %all-to-all-start.1 = ((bf16[16,6,16,512]{3,2,1,0:T(8,128)(2,1)}), bf16[16,6,16,512]{3,2,1,0:T(8,128)(2,1)S(1)}, u32[]{:S(2)}, u32[]{:S(2)}) async-start(bf16[16,6,16,512]{3,2,1,0:T(8,128)(2,1)} %shard_map.66), calls=%async_computation.1 | async-start | bytes 3145728 | tf_op jit(solution)/shard_map/all_to_all | solution.py:212
  140.2 36.2 %all-to-all-done.1 = bf16[16,6,16,512]{3,2,1,0:T(8,128)(2,1)S(1)} async-done(((bf16[16,6,16,512]{3,2,1,0:T(8,128)(2,1)}), bf16[16,6,16,512]{3,2,1,0:T(8,128)(2,1)S(1)}, u32[]{:S(2)}, u32[]{:S(2)}) %all-to-all-start.1) | async-done | bytes 1572896 | tf_op jit(solution)/shard_map/all_to_all | solution.py:212
  176.4 1.1 copy.63
  177.5 0.6 copy.64
  (36 shorter events, 1.0 us)
Async XLA Ops:
  0.6 5.1 %copy-start.1 = (s32[128,1]{0,1:T(1,128)S(1)}, s32[128,1]{0,1:T(1,128)}, u32[]{:S(2)}) copy-start(s32[128,1]{0,1:T(1,128)} %param.5) | copy-start | bytes 1540
  0.6 51.4 %collective-permute-start.2 = (bf16[384,11008]{1,0:T(8,128)(2,1)}, bf16[384,11008]{1,0:T(8,128)(2,1)}, u32[]{:S(2)}, u32[]{:S(2)}) collective-permute-start(bf16[384,11008]{1,0:T(8,128)(2,1)} %own_hbm.31), channel_id=1, source_target_pairs={{0,1},{1,0},{2,3},{3,2},{4,5},{5,4},{6,7},{7,6},{8,9},{9,8},{10,11... | collective-permute-start | bytes 25362440 | tf_op jit(solution)/shard_map/ppermute | solution.py:160
  2.8 9.9 %collective-permute-start.15 = (bf16[688,256]{1,0:T(8,128)(2,1)S(1)}, bf16[688,256]{1,0:T(8,128)(2,1)S(1)}, u32[]{:S(2)}, u32[]{:S(2)}) collective-permute-start(bf16[688,256]{1,0:T(8,128)(2,1)S(1)} %get-tuple-element.149.refs_0_), channel_id=1, source_target_pairs={{0,2},{1,3},{2,6},{3,7},{6,10},{7,11},{10,14},{11,15},{14,12},{15,... | collective-permute-start | bytes 1056776 | tf_op jit(solution)/shard_map/ppermute | solution.py:184
  4.1 9.9 %collective-permute-start.19 = (bf16[688,256]{1,0:T(8,128)(2,1)S(1)}, bf16[688,256]{1,0:T(8,128)(2,1)S(1)}, u32[]{:S(2)}, u32[]{:S(2)}) collective-permute-start(bf16[688,256]{1,0:T(8,128)(2,1)S(1)} %get-tuple-element.146.refs_1_), channel_id=1, source_target_pairs={{0,4},{1,5},{2,0},{3,1},{6,2},{7,3},{10,6},{11,7},{14,10},{15,11},... | collective-permute-start | bytes 1056776 | tf_op jit(solution)/shard_map/ppermute | solution.py:184
  4.3 18.5 %collective-permute-start = (bf16[688,256]{1,0:T(8,128)(2,1)S(1)}, bf16[688,256]{1,0:T(8,128)(2,1)S(1)}, u32[]{:S(2)}, u32[]{:S(2)}) collective-permute-start(bf16[688,256]{1,0:T(8,128)(2,1)S(1)} %get-tuple-element.148.refs_0_), channel_id=1, source_target_pairs={{0,2},{1,3},{2,6},{3,7},{6,10},{7,11},{10,14},{11,15},{14,12},{15,... | collective-permute-start | bytes 1056776 | tf_op jit(solution)/shard_map/ppermute | solution.py:184
  5.6 18.5 %collective-permute-start.5 = (bf16[688,256]{1,0:T(8,128)(2,1)S(1)}, bf16[688,256]{1,0:T(8,128)(2,1)S(1)}, u32[]{:S(2)}, u32[]{:S(2)}) collective-permute-start(bf16[688,256]{1,0:T(8,128)(2,1)S(1)} %get-tuple-element.147.refs_1_), channel_id=1, source_target_pairs={{0,4},{1,5},{2,0},{3,1},{6,2},{7,3},{10,6},{11,7},{14,10},{15,11},... | collective-permute-start | bytes 1056776 | tf_op jit(solution)/shard_map/ppermute | solution.py:184
  12.7 15.2 %collective-permute-start.16 = (bf16[688,256]{1,0:T(8,128)(2,1)S(1)}, bf16[688,256]{1,0:T(8,128)(2,1)}, u32[]{:S(2)}, u32[]{:S(2)}) collective-permute-start(bf16[688,256]{1,0:T(8,128)(2,1)S(1)} %collective-permute-done.15.refs_0_), channel_id=1, source_target_pairs={{0,2},{1,3},{2,6},{3,7},{6,10},{7,11},{10,14},{11,15},{14,12},{15,... | collective-permute-start | bytes 1056776 | tf_op jit(solution)/shard_map/ppermute | solution.py:184
  14.0 15.2 %collective-permute-start.20 = (bf16[688,256]{1,0:T(8,128)(2,1)S(1)}, bf16[688,256]{1,0:T(8,128)(2,1)}, u32[]{:S(2)}, u32[]{:S(2)}) collective-permute-start(bf16[688,256]{1,0:T(8,128)(2,1)S(1)} %collective-permute-done.19.refs_1_), channel_id=1, source_target_pairs={{0,4},{1,5},{2,0},{3,1},{6,2},{7,3},{10,6},{11,7},{14,10},{15,11},... | collective-permute-start | bytes 1056776 | tf_op jit(solution)/shard_map/ppermute | solution.py:184
  14.8 16.1 %all-to-all-start = ((s32[16,1,16]{2,1,0:T(1,128)}), s32[16,1,16]{2,1,0:T(1,128)S(1)}, u32[]{:S(2)}, u32[]{:S(2)}) async-start(s32[16,1,16]{2,1,0:T(1,128)} %sub.17), calls=%async_computation | async-start | bytes 16384 | tf_op jit(solution)/shard_map/all_to_all | solution.py:200
  22.8 12.7 %collective-permute-start.1 = (bf16[688,256]{1,0:T(8,128)(2,1)S(1)}, bf16[688,256]{1,0:T(8,128)(2,1)}, u32[]{:S(2)}, u32[]{:S(2)}) collective-permute-start(bf16[688,256]{1,0:T(8,128)(2,1)S(1)} %collective-permute-done.refs_0_), channel_id=1, source_target_pairs={{0,2},{1,3},{2,6},{3,7},{6,10},{7,11},{10,14},{11,15},{14,12},{15,... | collective-permute-start | bytes 1056776 | tf_op jit(solution)/shard_map/ppermute | solution.py:184
  24.1 12.8 %collective-permute-start.6 = (bf16[688,256]{1,0:T(8,128)(2,1)S(1)}, bf16[688,256]{1,0:T(8,128)(2,1)}, u32[]{:S(2)}, u32[]{:S(2)}) collective-permute-start(bf16[688,256]{1,0:T(8,128)(2,1)S(1)} %collective-permute-done.5.refs_1_), channel_id=1, source_target_pairs={{0,4},{1,5},{2,0},{3,1},{6,2},{7,3},{10,6},{11,7},{14,10},{15,11},... | collective-permute-start | bytes 1056776 | tf_op jit(solution)/shard_map/ppermute | solution.py:184
  27.9 15.2 %collective-permute-start.17 = (bf16[688,256]{1,0:T(8,128)(2,1)}, bf16[688,256]{1,0:T(8,128)(2,1)}, u32[]{:S(2)}, u32[]{:S(2)}) collective-permute-start(bf16[688,256]{1,0:T(8,128)(2,1)} %collective-permute-done.16.refs_0_), channel_id=1, source_target_pairs={{0,2},{1,3},{2,6},{3,7},{6,10},{7,11},{10,14},{11,15},{14,12},{15,... | collective-permute-start | bytes 1056776 | tf_op jit(solution)/shard_map/ppermute | solution.py:184
  29.2 15.2 %collective-permute-start.21 = (bf16[688,256]{1,0:T(8,128)(2,1)}, bf16[688,256]{1,0:T(8,128)(2,1)}, u32[]{:S(2)}, u32[]{:S(2)}) collective-permute-start(bf16[688,256]{1,0:T(8,128)(2,1)} %collective-permute-done.20.refs_1_), channel_id=1, source_target_pairs={{0,4},{1,5},{2,0},{3,1},{6,2},{7,3},{10,6},{11,7},{14,10},{15,11},... | collective-permute-start | bytes 1056776 | tf_op jit(solution)/shard_map/ppermute | solution.py:184
  35.6 15.0 %collective-permute-start.3 = (bf16[688,256]{1,0:T(8,128)(2,1)}, bf16[688,256]{1,0:T(8,128)(2,1)S(1)}, u32[]{:S(2)}, u32[]{:S(2)}) collective-permute-start(bf16[688,256]{1,0:T(8,128)(2,1)} %collective-permute-done.1.refs_0_), channel_id=1, source_target_pairs={{0,2},{1,3},{2,6},{3,7},{6,10},{7,11},{10,14},{11,15},{14,12},{15,... | collective-permute-start | bytes 1056776 | tf_op jit(solution)/shard_map/ppermute | solution.py:184
  36.9 15.0 %collective-permute-start.7 = (bf16[688,256]{1,0:T(8,128)(2,1)}, bf16[688,256]{1,0:T(8,128)(2,1)S(1)}, u32[]{:S(2)}, u32[]{:S(2)}) collective-permute-start(bf16[688,256]{1,0:T(8,128)(2,1)} %collective-permute-done.6.refs_1_), channel_id=1, source_target_pairs={{0,4},{1,5},{2,0},{3,1},{6,2},{7,3},{10,6},{11,7},{14,10},{15,11},... | collective-permute-start | bytes 1056776 | tf_op jit(solution)/shard_map/ppermute | solution.py:184
  43.1 27.1 %collective-permute-start.18 = (bf16[688,256]{1,0:T(8,128)(2,1)}, bf16[688,256]{1,0:T(8,128)(2,1)S(1)}, u32[]{:S(2)}, u32[]{:S(2)}) collective-permute-start(bf16[688,256]{1,0:T(8,128)(2,1)} %collective-permute-done.17.refs_0_), channel_id=1, source_target_pairs={{0,2},{1,3},{2,6},{3,7},{6,10},{7,11},{10,14},{11,15},{14,12},{15,... | collective-permute-start | bytes 1056776 | tf_op jit(solution)/shard_map/ppermute | solution.py:184
  44.5 25.8 %collective-permute-start.23 = (bf16[688,256]{1,0:T(8,128)(2,1)}, bf16[688,256]{1,0:T(8,128)(2,1)S(1)}, u32[]{:S(2)}, u32[]{:S(2)}) collective-permute-start(bf16[688,256]{1,0:T(8,128)(2,1)} %collective-permute-done.21.refs_1_), channel_id=1, source_target_pairs={{0,4},{1,5},{2,0},{3,1},{6,2},{7,3},{10,6},{11,7},{14,10},{15,11},... | collective-permute-start | bytes 1056776 | tf_op jit(solution)/shard_map/ppermute | solution.py:184
  50.6 34.9 %collective-permute-start.4 = (bf16[688,256]{1,0:T(8,128)(2,1)S(1)}, bf16[688,256]{1,0:T(8,128)(2,1)S(1)}, u32[]{:S(2)}, u32[]{:S(2)}) collective-permute-start(bf16[688,256]{1,0:T(8,128)(2,1)S(1)} %collective-permute-done.3.refs_0_), channel_id=1, source_target_pairs={{0,2},{1,3},{2,6},{3,7},{6,10},{7,11},{10,14},{11,15},{14,12},{15,... | collective-permute-start | bytes 1056776 | tf_op jit(solution)/shard_map/ppermute | solution.py:184
  51.9 35.0 %collective-permute-start.9 = (bf16[688,256]{1,0:T(8,128)(2,1)S(1)}, bf16[688,256]{1,0:T(8,128)(2,1)S(1)}, u32[]{:S(2)}, u32[]{:S(2)}) collective-permute-start(bf16[688,256]{1,0:T(8,128)(2,1)S(1)} %collective-permute-done.7.refs_1_), channel_id=1, source_target_pairs={{0,4},{1,5},{2,0},{3,1},{6,2},{7,3},{10,6},{11,7},{14,10},{15,11},... | collective-permute-start | bytes 1056776 | tf_op jit(solution)/shard_map/ppermute | solution.py:184
  52.0 3.4 %copy-start = (bf16[384,11008]{1,0:T(8,128)(2,1)S(1)}, bf16[384,11008]{1,0:T(8,128)(2,1)}, u32[]{:S(2)}) copy-start(bf16[384,11008]{1,0:T(8,128)(2,1)} %own_hbm.31) | copy-start | bytes 25362436
  70.2 19.9 %collective-permute-start.22 = (bf16[688,256]{1,0:T(8,128)(2,1)S(1)}, bf16[688,256]{1,0:T(8,128)(2,1)S(1)}, u32[]{:S(2)}, u32[]{:S(2)}) collective-permute-start(bf16[688,256]{1,0:T(8,128)(2,1)S(1)} %collective-permute-done.18.refs_0_), channel_id=1, source_target_pairs={{0,2},{1,3},{2,6},{3,7},{6,10},{7,11},{10,14},{11,15},{14,12},{15,... | collective-permute-start | bytes 1056776 | tf_op jit(solution)/shard_map/ppermute | solution.py:184
  71.6 20.0 %collective-permute-start.25 = (bf16[688,256]{1,0:T(8,128)(2,1)S(1)}, bf16[688,256]{1,0:T(8,128)(2,1)S(1)}, u32[]{:S(2)}, u32[]{:S(2)}) collective-permute-start(bf16[688,256]{1,0:T(8,128)(2,1)S(1)} %collective-permute-done.23.refs_1_), channel_id=1, source_target_pairs={{0,4},{1,5},{2,0},{3,1},{6,2},{7,3},{10,6},{11,7},{14,10},{15,11},... | collective-permute-start | bytes 1056776 | tf_op jit(solution)/shard_map/ppermute | solution.py:184
  85.5 9.3 %collective-permute-start.8 = (bf16[688,256]{1,0:T(8,128)(2,1)S(1)}, bf16[688,256]{1,0:T(8,128)(2,1)S(1)}, u32[]{:S(2)}, u32[]{:S(2)}) collective-permute-start(bf16[688,256]{1,0:T(8,128)(2,1)S(1)} %collective-permute-done.4.refs_0_), channel_id=1, source_target_pairs={{0,2},{1,3},{2,6},{3,7},{6,10},{7,11},{10,14},{11,15},{14,12},{15,... | collective-permute-start | bytes 1056776 | tf_op jit(solution)/shard_map/ppermute | solution.py:184
  86.9 9.4 %collective-permute-start.11 = (bf16[688,256]{1,0:T(8,128)(2,1)S(1)}, bf16[688,256]{1,0:T(8,128)(2,1)S(1)}, u32[]{:S(2)}, u32[]{:S(2)}) collective-permute-start(bf16[688,256]{1,0:T(8,128)(2,1)S(1)} %collective-permute-done.9.refs_1_), channel_id=1, source_target_pairs={{0,4},{1,5},{2,0},{3,1},{6,2},{7,3},{10,6},{11,7},{14,10},{15,11},... | collective-permute-start | bytes 1056776 | tf_op jit(solution)/shard_map/ppermute | solution.py:184
  90.2 10.4 %collective-permute-start.24 = (bf16[688,256]{1,0:T(8,128)(2,1)S(1)}, bf16[688,256]{1,0:T(8,128)(2,1)S(1)}, u32[]{:S(2)}, u32[]{:S(2)}) collective-permute-start(bf16[688,256]{1,0:T(8,128)(2,1)S(1)} %collective-permute-done.22.refs_0_), channel_id=1, source_target_pairs={{0,2},{1,3},{2,6},{3,7},{6,10},{7,11},{10,14},{11,15},{14,12},{15,... | collective-permute-start | bytes 1056776 | tf_op jit(solution)/shard_map/ppermute | solution.py:184
  91.6 10.3 %collective-permute-start.27 = (bf16[688,256]{1,0:T(8,128)(2,1)S(1)}, bf16[688,256]{1,0:T(8,128)(2,1)S(1)}, u32[]{:S(2)}, u32[]{:S(2)}) collective-permute-start(bf16[688,256]{1,0:T(8,128)(2,1)S(1)} %collective-permute-done.25.refs_1_), channel_id=1, source_target_pairs={{0,4},{1,5},{2,0},{3,1},{6,2},{7,3},{10,6},{11,7},{14,10},{15,11},... | collective-permute-start | bytes 1056776 | tf_op jit(solution)/shard_map/ppermute | solution.py:184
  94.9 13.2 %collective-permute-start.10 = (bf16[688,256]{1,0:T(8,128)(2,1)S(1)}, bf16[688,256]{1,0:T(8,128)(2,1)S(1)}, u32[]{:S(2)}, u32[]{:S(2)}) collective-permute-start(bf16[688,256]{1,0:T(8,128)(2,1)S(1)} %collective-permute-done.8.refs_0_), channel_id=1, source_target_pairs={{0,2},{1,3},{2,6},{3,7},{6,10},{7,11},{10,14},{11,15},{14,12},{15,... | collective-permute-start | bytes 1056776 | tf_op jit(solution)/shard_map/ppermute | solution.py:184
  96.3 13.2 %collective-permute-start.13 = (bf16[688,256]{1,0:T(8,128)(2,1)S(1)}, bf16[688,256]{1,0:T(8,128)(2,1)S(1)}, u32[]{:S(2)}, u32[]{:S(2)}) collective-permute-start(bf16[688,256]{1,0:T(8,128)(2,1)S(1)} %collective-permute-done.11.refs_1_), channel_id=1, source_target_pairs={{0,4},{1,5},{2,0},{3,1},{6,2},{7,3},{10,6},{11,7},{14,10},{15,11},... | collective-permute-start | bytes 1056776 | tf_op jit(solution)/shard_map/ppermute | solution.py:184
  101.9 15.4 %collective-permute-start.28 = (bf16[688,256]{1,0:T(8,128)(2,1)S(1)}, bf16[688,256]{1,0:T(8,128)(2,1)S(1)}, u32[]{:S(2)}, u32[]{:S(2)}) collective-permute-start(bf16[688,256]{1,0:T(8,128)(2,1)S(1)} %collective-permute-done.27.refs_1_), channel_id=1, source_target_pairs={{0,4},{1,5},{2,0},{3,1},{6,2},{7,3},{10,6},{11,7},{14,10},{15,11},... | collective-permute-start | bytes 1056776 | tf_op jit(solution)/shard_map/ppermute | solution.py:184
  102.0 15.2 %collective-permute-start.26 = (bf16[688,256]{1,0:T(8,128)(2,1)S(1)}, bf16[688,256]{1,0:T(8,128)(2,1)S(1)}, u32[]{:S(2)}, u32[]{:S(2)}) collective-permute-start(bf16[688,256]{1,0:T(8,128)(2,1)S(1)} %collective-permute-done.24.refs_0_), channel_id=1, source_target_pairs={{0,2},{1,3},{2,6},{3,7},{6,10},{7,11},{10,14},{11,15},{14,12},{15,... | collective-permute-start | bytes 1056776 | tf_op jit(solution)/shard_map/ppermute | solution.py:184
  109.5 17.7 %collective-permute-start.14 = (bf16[688,256]{1,0:T(8,128)(2,1)S(1)}, bf16[688,256]{1,0:T(8,128)(2,1)S(1)}, u32[]{:S(2)}, u32[]{:S(2)}) collective-permute-start(bf16[688,256]{1,0:T(8,128)(2,1)S(1)} %collective-permute-done.13.refs_1_), channel_id=1, source_target_pairs={{0,4},{1,5},{2,0},{3,1},{6,2},{7,3},{10,6},{11,7},{14,10},{15,11},... | collective-permute-start | bytes 1056776 | tf_op jit(solution)/shard_map/ppermute | solution.py:184
  109.6 17.5 %collective-permute-start.12 = (bf16[688,256]{1,0:T(8,128)(2,1)S(1)}, bf16[688,256]{1,0:T(8,128)(2,1)S(1)}, u32[]{:S(2)}, u32[]{:S(2)}) collective-permute-start(bf16[688,256]{1,0:T(8,128)(2,1)S(1)} %collective-permute-done.10.refs_0_), channel_id=1, source_target_pairs={{0,2},{1,3},{2,6},{3,7},{6,10},{7,11},{10,14},{11,15},{14,12},{15,... | collective-permute-start | bytes 1056776 | tf_op jit(solution)/shard_map/ppermute | solution.py:184
  120.5 10.5 %collective-permute-start.30 = (f32[2,384,256]{2,1,0:T(8,128)S(1)}, f32[2,384,256]{2,1,0:T(8,128)S(1)}, u32[]{:S(2)}, u32[]{:S(2)}) collective-permute-start(f32[2,384,256]{2,1,0:T(8,128)S(1)} %get-tuple-element.142), channel_id=1, source_target_pairs={{0,1},{1,0},{2,3},{3,2},{4,5},{5,4},{6,7},{7,6},{8,9},{9,8},{10,11... | collective-permute-start | bytes 2359304 | tf_op jit(solution)/shard_map/ppermute | solution.py:187
  130.3 2.6 %collective-permute-start.29 = (f32[2,384,256]{2,1,0:T(8,128)S(1)}, f32[2,384,256]{2,1,0:T(8,128)S(1)}, u32[]{:S(2)}, u32[]{:S(2)}) collective-permute-start(f32[2,384,256]{2,1,0:T(8,128)S(1)} %get-tuple-element.141), channel_id=1, source_target_pairs={{0,1},{1,0},{2,3},{3,2},{4,5},{5,4},{6,7},{7,6},{8,9},{9,8},{10,11... | collective-permute-start | bytes 2359304 | tf_op jit(solution)/shard_map/ppermute | solution.py:187
  135.0 41.4 %all-to-all-start.1 = ((bf16[16,6,16,512]{3,2,1,0:T(8,128)(2,1)}), bf16[16,6,16,512]{3,2,1,0:T(8,128)(2,1)S(1)}, u32[]{:S(2)}, u32[]{:S(2)}) async-start(bf16[16,6,16,512]{3,2,1,0:T(8,128)(2,1)} %shard_map.66), calls=%async_computation.1 | async-start | bytes 3145728 | tf_op jit(solution)/shard_map/all_to_all | solution.py:212

commit v5 on v4

--- a/solution.py
+++ b/solution.py
@@ -10,6 +10,7 @@
 
 GRID_CHIPS = 8
 HALVES = 2
+BEHIND = (0, 0, 1, 2, 4, 5, 6)
 WAYS = (1, -1)
 LANES = 128
 WINDOW = 896
@@ -54,12 +55,15 @@
     return jnp.minimum(start // LANES * LANES, nvirt - WINDOW)
 
 
-def step_kernel(t, own_hbm, other_hbm, *refs):
+def step_kernel(t, parts, own_hbm, other_hbm, *refs):
     norb = len(WAYS)
-    pieces = refs[:norb]
-    before, (mine_ref, theirs_ref, c_buf, g_buf, sems) = refs[norb:-5], refs[-5:]
+    pieces = refs[: norb * parts]
+    scratch = refs[-3:]
+    sums = refs[-3 - 2 * parts : -3]
+    before = refs[norb * parts : -3 - 2 * parts]
+    c_buf, g_buf, sems = scratch
     rows, nvirt = own_hbm.shape
-    depth = pieces[0].shape[0]
+    depth, width = pieces[0].shape
     me = lax.axis_index("wide")
     core = lax.rem(me, 2)
     here = ring_place(lax.div(me, 2))
@@ -82,44 +86,51 @@
             copy.start()
     for i in range(norb):
         g_buf[i] = jnp.zeros_like(g_buf[i])
-        g_buf[i, pl.ds(shifts[i], depth), :] = pieces[i][...]
+        for j in range(parts):
+            g_buf[i, pl.ds(shifts[i], depth), pl.ds(j * width, width)] = pieces[
+                j * norb + i
+            ][...]
     for i in range(norb):
         for copy in copies[i]:
             copy.wait()
-        term = jnp.dot(c_buf[i], g_buf[i], preferred_element_type=jnp.float32)
-        if before:
-            mine_ref[i] = before[0][i] + term[:rows]
-            theirs_ref[i] = before[1][i] + term[rows:]
-        else:
-            mine_ref[i] = term[:rows]
-            theirs_ref[i] = term[rows:]
+        for k in range(2):
+            term = jnp.dot(
+                c_buf[i, pl.ds(k * rows, rows)], g_buf[i], preferred_element_type=jnp.float32
+            )
+            for j in range(parts):
+                part = term[:, j * width : (j + 1) * width]
+                at = 2 * j + k
+                sums[at][i] = before[at][i] + part if before else part
 
 
 def add_products(t, own, other, pieces, before):
     rows, nvirt = own.shape
-    norb = len(pieces)
-    depth, width = pieces[0].shape
+    parts, norb = len(pieces), len(WAYS)
+    depth, width = pieces[0][0].shape
     sums = jax.ShapeDtypeStruct((norb, rows, width), jnp.float32)
     vmem = pl.BlockSpec(memory_space=pltpu.VMEM)
     hbm = pl.BlockSpec(memory_space=pltpu.HBM)
-    return pl.pallas_call(
-        functools.partial(step_kernel, t),
-        out_shape=(sums, sums),
-        in_specs=[hbm, hbm] + [vmem] * (norb + len(before)),
-        out_specs=(vmem, vmem),
-        input_output_aliases={2 + norb + k: k for k in range(len(before))},
+    flat = [piece for part in pieces for piece in part]
+    old = [value for pair in before for value in pair]
+    new = pl.pallas_call(
+        functools.partial(step_kernel, t, parts),
+        out_shape=[sums] * (2 * parts),
+        in_specs=[hbm, hbm] + [vmem] * (len(flat) + len(old)),
+        out_specs=[vmem] * (2 * parts),
+        input_output_aliases={2 + len(flat) + k: k for k in range(len(old))},
         scratch_shapes=[
             pltpu.VMEM((norb, 2 * rows, WINDOW), jnp.bfloat16),
-            pltpu.VMEM((norb, WINDOW, width), jnp.bfloat16),
+            pltpu.VMEM((norb, WINDOW, parts * width), jnp.bfloat16),
             pltpu.SemaphoreType.DMA((norb, 2)),
         ],
-        compiler_params=pltpu.CompilerParams(vmem_limit_bytes=16 << 20),
+        compiler_params=pltpu.CompilerParams(vmem_limit_bytes=20 << 20),
         cost_estimate=pl.CostEstimate(
-            flops=4 * norb * rows * WINDOW * width,
+            flops=4 * norb * rows * WINDOW * parts * width,
             bytes_accessed=4 * norb * rows * WINDOW,
             transcendentals=0,
         ),
-    )(own, other, *pieces, *before)
+    )(own, other, *flat, *old)
+    return [(new[2 * j], new[2 * j + 1]) for j in range(parts)]
 
 
 def finish_kernel(place_ref, *refs):
@@ -170,19 +181,30 @@
         ]
         for way in WAYS
     ]
-    sums = [()] * HALVES
+    arrived, sums, done = [], [], 0
     for t in range(GRID_CHIPS):
+        arrived.append([list(part) for part in piece])
+        if t + 1 == GRID_CHIPS:
+            break
         for j in range(HALVES):
-            arrived = list(piece[j])
-            if t + 1 < GRID_CHIPS:
-                for i in range(norb):
-                    sent = arrived[i]
-                    if t == 2 and i == j == 0:
-                        sent, early = lax.optimization_barrier((sent, early))
-                    if t >= 4:
-                        sent, sums[j] = lax.optimization_barrier((sent, sums[j]))
-                    piece[j][i] = lax.ppermute(sent, "wide", shift[i])
-            sums[j] = add_products(t, coefficients, other, arrived, sums[j])
+            if j == HALVES - 1:
+                while done < BEHIND[t]:
+                    sums = add_products(done, coefficients, other, arrived[done], sums)
+                    done += 1
+            for i in range(norb):
+                sent = piece[j][i]
+                if t == 2 and i == j == 0:
+                    sent, early = lax.optimization_barrier((sent, early))
+                if j == HALVES - 1 and BEHIND[t]:
+                    sent, sums = lax.optimization_barrier((sent, sums))
+                piece[j][i] = lax.ppermute(sent, "wide", shift[i])
+    while done < GRID_CHIPS - 1:
+        sums = add_products(done, coefficients, other, arrived[done], sums)
+        done += 1
+    sums = [
+        add_products(done, coefficients, other, [arrived[done][j]], [sums[j]])[0]
+        for j in range(HALVES)
+    ]
     mine = [sums[j][0] for j in range(HALVES)]
     theirs = [lax.ppermute(sums[j][1], "wide", swap) for j in range(HALVES)]
     return mine, theirs, early

time: 179 us -> 165 us (0.922)
  Pallas kernels: 55.8 us -> 30.4 us
  waiting for transfers between devices: 71.7 us -> 85.9 us
  starting transfers between devices: 41.8 us -> 39.7 us
    pallas_call x16 -> x9, Pallas kernels: 53.7 us -> 28.3 us  [add_products(): pl.pallas_call(functools.partial(step_kernel, t, parts), out_shape=[sums]...]
    ppermute x28, waiting for transfers between devices: 32.1 us -> 47.8 us  [ring_products(): piece[j][i] = lax.ppermute(sent, 'wide', shift[i])]
  transfers between devices with their start and end apart: 33 -> 33, of which waited for: 12 -> 15; matrix products, arithmetic and copies ran while one was open for 2% -> 2% of each run, Pallas kernels for 30% -> 17%
where the time goes in v5:
time: 165 us
  waiting for transfers between devices  85.9 us (52%)
  starting transfers between devices  39.7 us (24%)
  Pallas kernels  30.4 us (18%)
  local copies, waits for them, and re-layouts  7.52 us (5%)
    ppermute x28, waiting for transfers between devices, ring_products(): piece[j][i] = lax.ppermute(sent, 'wide', shift[i])  47.8 us
    all_to_all x1, waiting for transfers between devices, local(): lax.all_to_all(out, 'wide', split_axis=0, concat_axis=0, tiled=True)  36.2 us
    pallas_call x9, Pallas kernels, add_products(): pl.pallas_call(functools.partial(step_kernel, t, parts), out_shape=[sums]...  28.3 us
    ppermute x28, starting transfers between devices, ring_products(): piece[j][i] = lax.ppermute(sent, 'wide', shift[i])  20.7 us
    all_to_all x1, starting transfers between devices, local(): lax.all_to_all(labels, 'wide', split_axis=0, concat_axis=0, tiled=True)  7.02 us
    ppermute x2, starting transfers between devices, ring_products(): theirs = [lax.ppermute(sums[j][1], 'wide', swap) for j in range(HALVES)]  6 us
    all_to_all x1, starting transfers between devices, local(): lax.all_to_all(out, 'wide', split_axis=0, concat_axis=0, tiled=True)  5.24 us
    unnamed x6, local copies, waits for them, and re-layouts  5.15 us
  transfers between devices with their start and end apart: 33, of which 15 were waited for; matrix products, arithmetic and copies ran while one was open for 2% of the time, Pallas kernels for 17%

profile of v5, /device:TPU:13, one launch (start us, length us, event | category | flops | bytes accessed | tf_op | source)
XLA Modules:
  0.0 164.9 jit_solution(9501445420154613918)
XLA Ops:
  0.6 0.7 collective-permute-start.2
  1.4 1.4 slice_bitcast_fusion
  2.8 1.3 collective-permute-start.15
  4.1 0.2 collective-permute-start.18
  4.3 1.3 collective-permute-start
  5.6 0.2 collective-permute-start.8
  5.8 0.2 convert_reduce_fusion
  6.1 0.7 sub.17
  6.8 7.0 %all-to-all-start = ((s32[16,1,16]{2,1,0:T(1,128)}), s32[16,1,16]{2,1,0:T(1,128)S(1)}, u32[]{:S(2)}, u32[]{:S(2)}) async-start(s32[16,1,16]{2,1,0:T(1,128)} %sub.17), calls=%async_computation | async-start | bytes 16384 | tf_op jit(solution)/shard_map/all_to_all | solution.py:222
  13.9 0.2 mul.58
  14.1 6.1 %collective-permute-done.refs_0_ = bf16[688,256]{1,0:T(8,128)(2,1)S(1)} collective-permute-done((bf16[688,256]{1,0:T(8,128)(2,1)S(1)}, bf16[688,256]{1,0:T(8,128)(2,1)S(1)}, u32[]{:S(2)}, u32[]{:S(2)}) %collective-permute-start) | collective-permute-done | bytes 352288 | tf_op jit(solution)/shard_map/ppermute | solution.py:200
  20.2 1.3 collective-permute-start.1
  21.7 1.4 collective-permute-start.16
  23.3 0.2 compare_convert_fusion.place_ref
  23.4 5.8 %collective-permute-done.1.refs_0_ = bf16[688,256]{1,0:T(8,128)(2,1)} collective-permute-done((bf16[688,256]{1,0:T(8,128)(2,1)S(1)}, bf16[688,256]{1,0:T(8,128)(2,1)}, u32[]{:S(2)}, u32[]{:S(2)}) %collective-permute-start.1) | collective-permute-done | bytes 352288 | tf_op jit(solution)/shard_map/ppermute | solution.py:200
  29.2 1.3 collective-permute-start.3
  30.5 0.1 collective-permute-start.10
  30.7 3.4 %copy-done = bf16[384,11008]{1,0:T(8,128)(2,1)S(1)} copy-done((bf16[384,11008]{1,0:T(8,128)(2,1)S(1)}, bf16[384,11008]{1,0:T(8,128)(2,1)}, u32[]{:S(2)}) %copy-start) | copy-done | bytes 8454168
  34.1 3.1 %shard_map.50 = (f32[2,384,256]{2,1,0:T(8,128)S(1)}, f32[2,384,256]{2,1,0:T(8,128)S(1)}, f32[2,384,256]{2,1,0:T(8,128)S(1)}, f32[2,384,256]{2,1,0:T(8,128)S(1)}) custom-call(bf16[384,11008]{1,0:T(8,128)(2,1)S(1)} %copy-done, bf16[384,11008]{1,0:T(8,128)(2,1)} %collective-permute-done.2.other_hbm, bf16[688,256]{1,0:T(8,128)(2,1)S(1)} %get-tuple-element.176.refs_0_, ...), custom_call_target="tpu_custom_call" | custom-call | flops 1409286144 | bytes 2752512 | tf_op jit(solution)/shard_map/pallas_call | solution.py:115
  37.3 1.4 collective-permute-start.17
  38.6 0.1 collective-permute-start.21
  38.8 5.4 %collective-permute-done.3.refs_0_ = bf16[688,256]{1,0:T(8,128)(2,1)S(1)} collective-permute-done((bf16[688,256]{1,0:T(8,128)(2,1)}, bf16[688,256]{1,0:T(8,128)(2,1)S(1)}, u32[]{:S(2)}, u32[]{:S(2)}) %collective-permute-start.3) | collective-permute-done | bytes 352288 | tf_op jit(solution)/shard_map/ppermute | solution.py:200
  44.2 1.3 collective-permute-start.4
  45.5 0.1 collective-permute-start.11
  45.7 3.2 %shard_map.51 = (f32[2,384,256]{2,1,0:T(8,128)S(1)}, f32[2,384,256]{2,1,0:T(8,128)S(1)}, f32[2,384,256]{2,1,0:T(8,128)S(1)}, f32[2,384,256]{2,1,0:T(8,128)S(1)}) custom-call(bf16[384,11008]{1,0:T(8,128)(2,1)S(1)} %copy-done, ...), custom_call_target="tpu_custom_call", output_to_operand_aliasing={{0}: (6, {}), {1}: (7, {}), {2}: (8, {}), {3}: (9, {})} | custom-call | flops 1409286144 | bytes 2752512 | tf_op jit(solution)/shard_map/pallas_call | solution.py:115
  48.9 2.9 %collective-permute-done.17.refs_2_ = bf16[688,256]{1,0:T(8,128)(2,1)S(1)} collective-permute-done((bf16[688,256]{1,0:T(8,128)(2,1)}, bf16[688,256]{1,0:T(8,128)(2,1)S(1)}, u32[]{:S(2)}, u32[]{:S(2)}) %collective-permute-start.17) | collective-permute-done | bytes 352288 | tf_op jit(solution)/shard_map/ppermute | solution.py:200
  51.8 1.3 collective-permute-start.20
  53.1 0.1 collective-permute-start.23
  53.2 6.1 %collective-permute-done.4.refs_0_ = bf16[688,256]{1,0:T(8,128)(2,1)S(1)} collective-permute-done((bf16[688,256]{1,0:T(8,128)(2,1)S(1)}, bf16[688,256]{1,0:T(8,128)(2,1)S(1)}, u32[]{:S(2)}, u32[]{:S(2)}) %collective-permute-start.4) | collective-permute-done | bytes 352288 | tf_op jit(solution)/shard_map/ppermute | solution.py:200
  59.3 1.3 collective-permute-start.5
  60.6 0.1 collective-permute-start.12
  60.8 4.5 %shard_map.52 = (f32[2,384,256]{2,1,0:T(8,128)S(1)}, f32[2,384,256]{2,1,0:T(8,128)S(1)}, f32[2,384,256]{2,1,0:T(8,128)S(1)}, f32[2,384,256]{2,1,0:T(8,128)S(1)}) custom-call(bf16[384,11008]{1,0:T(8,128)(2,1)S(1)} %copy-done, ...), custom_call_target="tpu_custom_call", output_to_operand_aliasing={{0}: (6, {}), {1}: (7, {}), {2}: (8, {}), {3}: (9, {})} | custom-call | flops 1409286144 | bytes 2752512 | tf_op jit(solution)/shard_map/pallas_call | solution.py:115
  65.3 3.2 %shard_map.53 = (f32[2,384,256]{2,1,0:T(8,128)S(1)}, f32[2,384,256]{2,1,0:T(8,128)S(1)}, f32[2,384,256]{2,1,0:T(8,128)S(1)}, f32[2,384,256]{2,1,0:T(8,128)S(1)}) custom-call(bf16[384,11008]{1,0:T(8,128)(2,1)S(1)} %copy-done, ...), custom_call_target="tpu_custom_call", output_to_operand_aliasing={{0}: (6, {}), {1}: (7, {}), {2}: (8, {}), {3}: (9, {})} | custom-call | flops 1409286144 | bytes 2752512 | tf_op jit(solution)/shard_map/pallas_call | solution.py:115
  68.5 1.4 collective-permute-start.22
  69.9 0.1 collective-permute-start.25
  70.0 4.4 %collective-permute-done.5.refs_0_ = bf16[688,256]{1,0:T(8,128)(2,1)S(1)} collective-permute-done((bf16[688,256]{1,0:T(8,128)(2,1)S(1)}, bf16[688,256]{1,0:T(8,128)(2,1)S(1)}, u32[]{:S(2)}, u32[]{:S(2)}) %collective-permute-start.5) | collective-permute-done | bytes 352288 | tf_op jit(solution)/shard_map/ppermute | solution.py:200
  74.4 1.3 collective-permute-start.6
  75.7 0.1 collective-permute-start.13
  75.9 3.2 %shard_map.54 = (f32[2,384,256]{2,1,0:T(8,128)S(1)}, f32[2,384,256]{2,1,0:T(8,128)S(1)}, f32[2,384,256]{2,1,0:T(8,128)S(1)}, f32[2,384,256]{2,1,0:T(8,128)S(1)}) custom-call(bf16[384,11008]{1,0:T(8,128)(2,1)S(1)} %copy-done, ...), custom_call_target="tpu_custom_call", output_to_operand_aliasing={{0}: (6, {}), {1}: (7, {}), {2}: (8, {}), {3}: (9, {})} | custom-call | flops 1409286144 | bytes 2752512 | tf_op jit(solution)/shard_map/pallas_call | solution.py:115
  79.1 2.9 %collective-permute-done.22.refs_2_ = bf16[688,256]{1,0:T(8,128)(2,1)S(1)} collective-permute-done((bf16[688,256]{1,0:T(8,128)(2,1)S(1)}, bf16[688,256]{1,0:T(8,128)(2,1)S(1)}, u32[]{:S(2)}, u32[]{:S(2)}) %collective-permute-start.22) | collective-permute-done | bytes 352288 | tf_op jit(solution)/shard_map/ppermute | solution.py:200
  82.0 1.3 collective-permute-start.24
  83.3 0.1 collective-permute-start.26
  83.4 6.1 %collective-permute-done.6.refs_0_ = bf16[688,256]{1,0:T(8,128)(2,1)S(1)} collective-permute-done((bf16[688,256]{1,0:T(8,128)(2,1)S(1)}, bf16[688,256]{1,0:T(8,128)(2,1)S(1)}, u32[]{:S(2)}, u32[]{:S(2)}) %collective-permute-start.6) | collective-permute-done | bytes 352288 | tf_op jit(solution)/shard_map/ppermute | solution.py:200
  89.5 1.3 collective-permute-start.7
  90.8 0.1 collective-permute-start.14
  91.0 3.2 %shard_map.55 = (f32[2,384,256]{2,1,0:T(8,128)S(1)}, f32[2,384,256]{2,1,0:T(8,128)S(1)}, f32[2,384,256]{2,1,0:T(8,128)S(1)}, f32[2,384,256]{2,1,0:T(8,128)S(1)}) custom-call(bf16[384,11008]{1,0:T(8,128)(2,1)S(1)} %copy-done, ...), custom_call_target="tpu_custom_call", output_to_operand_aliasing={{0}: (6, {}), {1}: (7, {}), {2}: (8, {}), {3}: (9, {})} | custom-call | flops 1409286144 | bytes 2752512 | tf_op jit(solution)/shard_map/pallas_call | solution.py:115
  94.2 2.9 %collective-permute-done.24.refs_2_ = bf16[688,256]{1,0:T(8,128)(2,1)S(1)} collective-permute-done((bf16[688,256]{1,0:T(8,128)(2,1)S(1)}, bf16[688,256]{1,0:T(8,128)(2,1)S(1)}, u32[]{:S(2)}, u32[]{:S(2)}) %collective-permute-start.24) | collective-permute-done | bytes 352288 | tf_op jit(solution)/shard_map/ppermute | solution.py:200
  97.1 1.0 collective-permute-done.26.refs_3_
  98.1 0.1 collective-permute-start.28
  98.2 1.3 collective-permute-start.27
  99.5 3.2 %shard_map.56 = (f32[2,384,256]{2,1,0:T(8,128)S(1)}, f32[2,384,256]{2,1,0:T(8,128)S(1)}, f32[2,384,256]{2,1,0:T(8,128)S(1)}, f32[2,384,256]{2,1,0:T(8,128)S(1)}) custom-call(bf16[384,11008]{1,0:T(8,128)(2,1)S(1)} %copy-done, ...), custom_call_target="tpu_custom_call", output_to_operand_aliasing={{0}: (6, {}), {1}: (7, {}), {2}: (8, {}), {3}: (9, {})} | custom-call | flops 1409286144 | bytes 2752512 | tf_op jit(solution)/shard_map/pallas_call | solution.py:115
  102.7 1.9 %collective-permute-done.7.refs_0_ = bf16[688,256]{1,0:T(8,128)(2,1)S(1)} collective-permute-done((bf16[688,256]{1,0:T(8,128)(2,1)S(1)}, bf16[688,256]{1,0:T(8,128)(2,1)S(1)}, u32[]{:S(2)}, u32[]{:S(2)}) %collective-permute-start.7) | collective-permute-done | bytes 352288 | tf_op jit(solution)/shard_map/ppermute | solution.py:200
  104.6 1.0 collective-permute-done.14.refs_1_
  105.6 2.4 %shard_map.57 = (f32[2,384,256]{2,1,0:T(8,128)S(1)}, f32[2,384,256]{2,1,0:T(8,128)S(1)}) custom-call(bf16[384,11008]{1,0:T(8,128)(2,1)S(1)} %copy-done, bf16[384,11008]{1,0:T(8,128)(2,1)} %collective-permute-done.2.other_hbm, bf16[688,256]{1,0:T(8,128)(2,1)S(1)} %collective-permute-done.7.refs_0_, ...), custom_call_target="tpu_custom_call", output_to_operand_aliasing={{0}: (4, {}), {1}: (5, {})} | custom-call | flops 704643072 | bytes 2752512 | tf_op jit(solution)/shard_map/pallas_call | solution.py:115
  108.0 3.8 %collective-permute-start.29 = (f32[2,384,256]{2,1,0:T(8,128)S(1)}, f32[2,384,256]{2,1,0:T(8,128)S(1)}, u32[]{:S(2)}, u32[]{:S(2)}) collective-permute-start(f32[2,384,256]{2,1,0:T(8,128)S(1)} %get-tuple-element.169), channel_id=1, source_target_pairs={{0,1},{1,0},{2,3},{3,2},{4,5},{5,4},{6,7},{7,6},{8,9},{9,8},{10,11... | collective-permute-start | bytes 2359304 | tf_op jit(solution)/shard_map/ppermute | solution.py:209
  111.8 1.3 collective-permute-done.28.refs_1_
  113.2 2.4 %shard_map.58 = (f32[2,384,256]{2,1,0:T(8,128)S(1)}, f32[2,384,256]{2,1,0:T(8,128)S(1)}) custom-call(bf16[384,11008]{1,0:T(8,128)(2,1)S(1)} %copy-done, bf16[384,11008]{1,0:T(8,128)(2,1)} %collective-permute-done.2.other_hbm, bf16[688,256]{1,0:T(8,128)(2,1)S(1)} %collective-permute-done.27.refs_0_, ...), custom_call_target="tpu_custom_call", output_to_operand_aliasing={{0}: (4, {}), {1}: (5, {})} | custom-call | flops 704643072 | bytes 2752512 | tf_op jit(solution)/shard_map/pallas_call | solution.py:115
  115.5 2.2 %collective-permute-start.30 = (f32[2,384,256]{2,1,0:T(8,128)S(1)}, f32[2,384,256]{2,1,0:T(8,128)S(1)}, u32[]{:S(2)}, u32[]{:S(2)}) collective-permute-start(f32[2,384,256]{2,1,0:T(8,128)S(1)} %get-tuple-element.170), channel_id=1, source_target_pairs={{0,1},{1,0},{2,3},{3,2},{4,5},{5,4},{6,7},{7,6},{8,9},{9,8},{10,11... | collective-permute-start | bytes 2359304 | tf_op jit(solution)/shard_map/ppermute | solution.py:209
  117.7 1.9 %collective-permute-done.30.refs_3_ = f32[2,384,256]{2,1,0:T(8,128)S(1)} collective-permute-done((f32[2,384,256]{2,1,0:T(8,128)S(1)}, f32[2,384,256]{2,1,0:T(8,128)S(1)}, u32[]{:S(2)}, u32[]{:S(2)}) %collective-permute-start.30) | collective-permute-done | bytes 786464 | tf_op jit(solution)/shard_map/ppermute | solution.py:209
  119.6 2.1 %shard_map.59 = bf16[16,6,16,512]{3,2,1,0:T(8,128)(2,1)} custom-call(bf16[768,384]{1,0:T(8,128)(2,1)S(1)} %compare_convert_fusion.place_ref, f32[2,384,256]{2,1,0:T(8,128)S(1)} %get-tuple-element.163.refs_0_, f32[2,384,256]{2,1,0:T(8,128)S(1)} %get-tuple-element.168.refs_1_, f32[2,384,256]{2,1,0:T(8,128)S(1)} %collective-permute-done.29.refs_2_, ...), custom_call_target="tpu_custom_call" | custom-call | flops 603979776 | bytes 1572864 | tf_op jit(solution)/shard_map/pallas_call | solution.py:152
  121.8 5.2 %all-to-all-start.1 = ((bf16[16,6,16,512]{3,2,1,0:T(8,128)(2,1)}), bf16[16,6,16,512]{3,2,1,0:T(8,128)(2,1)S(1)}, u32[]{:S(2)}, u32[]{:S(2)}) async-start(bf16[16,6,16,512]{3,2,1,0:T(8,128)(2,1)} %shard_map.59), calls=%async_computation.1 | async-start | bytes 3145728 | tf_op jit(solution)/shard_map/all_to_all | solution.py:234
  127.0 36.2 %all-to-all-done.1 = bf16[16,6,16,512]{3,2,1,0:T(8,128)(2,1)S(1)} async-done(((bf16[16,6,16,512]{3,2,1,0:T(8,128)(2,1)}), bf16[16,6,16,512]{3,2,1,0:T(8,128)(2,1)S(1)}, u32[]{:S(2)}, u32[]{:S(2)}) %all-to-all-start.1) | async-done | bytes 1572896 | tf_op jit(solution)/shard_map/all_to_all | solution.py:234
  163.2 1.1 copy.63
  164.3 0.6 copy.64
  (29 shorter events, 0.5 us)
Async XLA Ops:
  0.6 5.1 %copy-start.1 = (s32[128,1]{0,1:T(1,128)S(1)}, s32[128,1]{0,1:T(1,128)}, u32[]{:S(2)}) copy-start(s32[128,1]{0,1:T(1,128)} %param.5) | copy-start | bytes 1540
  0.6 30.1 %collective-permute-start.2 = (bf16[384,11008]{1,0:T(8,128)(2,1)}, bf16[384,11008]{1,0:T(8,128)(2,1)}, u32[]{:S(2)}, u32[]{:S(2)}) collective-permute-start(bf16[384,11008]{1,0:T(8,128)(2,1)} %own_hbm.17), channel_id=1, source_target_pairs={{0,1},{1,0},{2,3},{3,2},{4,5},{5,4},{6,7},{7,6},{8,9},{9,8},{10,11... | collective-permute-start | bytes 25362440 | tf_op jit(solution)/shard_map/ppermute | solution.py:171
  2.8 19.0 %collective-permute-start.15 = (bf16[688,256]{1,0:T(8,128)(2,1)S(1)}, bf16[688,256]{1,0:T(8,128)(2,1)S(1)}, u32[]{:S(2)}, u32[]{:S(2)}) collective-permute-start(bf16[688,256]{1,0:T(8,128)(2,1)S(1)} %get-tuple-element.177.refs_2_), channel_id=1, source_target_pairs={{0,2},{1,3},{2,6},{3,7},{6,10},{7,11},{10,14},{11,15},{14,12},{15,... | collective-permute-start | bytes 1056776 | tf_op jit(solution)/shard_map/ppermute | solution.py:200
  4.1 19.0 %collective-permute-start.18 = (bf16[688,256]{1,0:T(8,128)(2,1)S(1)}, bf16[688,256]{1,0:T(8,128)(2,1)S(1)}, u32[]{:S(2)}, u32[]{:S(2)}) collective-permute-start(bf16[688,256]{1,0:T(8,128)(2,1)S(1)} %get-tuple-element.174.refs_3_), channel_id=1, source_target_pairs={{0,4},{1,5},{2,0},{3,1},{6,2},{7,3},{10,6},{11,7},{14,10},{15,11},... | collective-permute-start | bytes 1056776 | tf_op jit(solution)/shard_map/ppermute | solution.py:200
  4.3 15.9 %collective-permute-start = (bf16[688,256]{1,0:T(8,128)(2,1)S(1)}, bf16[688,256]{1,0:T(8,128)(2,1)S(1)}, u32[]{:S(2)}, u32[]{:S(2)}) collective-permute-start(bf16[688,256]{1,0:T(8,128)(2,1)S(1)} %get-tuple-element.176.refs_0_), channel_id=1, source_target_pairs={{0,2},{1,3},{2,6},{3,7},{6,10},{7,11},{10,14},{11,15},{14,12},{15,... | collective-permute-start | bytes 1056776 | tf_op jit(solution)/shard_map/ppermute | solution.py:200
  5.6 16.0 %collective-permute-start.8 = (bf16[688,256]{1,0:T(8,128)(2,1)S(1)}, bf16[688,256]{1,0:T(8,128)(2,1)S(1)}, u32[]{:S(2)}, u32[]{:S(2)}) collective-permute-start(bf16[688,256]{1,0:T(8,128)(2,1)S(1)} %get-tuple-element.175.refs_1_), channel_id=1, source_target_pairs={{0,4},{1,5},{2,0},{3,1},{6,2},{7,3},{10,6},{11,7},{14,10},{15,11},... | collective-permute-start | bytes 1056776 | tf_op jit(solution)/shard_map/ppermute | solution.py:200
  6.8 16.7 %all-to-all-start = ((s32[16,1,16]{2,1,0:T(1,128)}), s32[16,1,16]{2,1,0:T(1,128)S(1)}, u32[]{:S(2)}, u32[]{:S(2)}) async-start(s32[16,1,16]{2,1,0:T(1,128)} %sub.17), calls=%async_computation | async-start | bytes 16384 | tf_op jit(solution)/shard_map/all_to_all | solution.py:222
  20.2 9.0 %collective-permute-start.1 = (bf16[688,256]{1,0:T(8,128)(2,1)S(1)}, bf16[688,256]{1,0:T(8,128)(2,1)}, u32[]{:S(2)}, u32[]{:S(2)}) collective-permute-start(bf16[688,256]{1,0:T(8,128)(2,1)S(1)} %collective-permute-done.refs_0_), channel_id=1, source_target_pairs={{0,2},{1,3},{2,6},{3,7},{6,10},{7,11},{10,14},{11,15},{14,12},{15,... | collective-permute-start | bytes 1056776 | tf_op jit(solution)/shard_map/ppermute | solution.py:200
  21.6 9.0 %collective-permute-start.9 = (bf16[688,256]{1,0:T(8,128)(2,1)S(1)}, bf16[688,256]{1,0:T(8,128)(2,1)}, u32[]{:S(2)}, u32[]{:S(2)}) collective-permute-start(bf16[688,256]{1,0:T(8,128)(2,1)S(1)} %collective-permute-done.8.refs_1_), channel_id=1, source_target_pairs={{0,4},{1,5},{2,0},{3,1},{6,2},{7,3},{10,6},{11,7},{14,10},{15,11},... | collective-permute-start | bytes 1056776 | tf_op jit(solution)/shard_map/ppermute | solution.py:200
  21.7 15.5 %collective-permute-start.16 = (bf16[688,256]{1,0:T(8,128)(2,1)S(1)}, bf16[688,256]{1,0:T(8,128)(2,1)}, u32[]{:S(2)}, u32[]{:S(2)}) collective-permute-start(bf16[688,256]{1,0:T(8,128)(2,1)S(1)} %collective-permute-done.15.refs_2_), channel_id=1, source_target_pairs={{0,2},{1,3},{2,6},{3,7},{6,10},{7,11},{10,14},{11,15},{14,12},{15,... | collective-permute-start | bytes 1056776 | tf_op jit(solution)/shard_map/ppermute | solution.py:200
  23.1 15.5 %collective-permute-start.19 = (bf16[688,256]{1,0:T(8,128)(2,1)S(1)}, bf16[688,256]{1,0:T(8,128)(2,1)}, u32[]{:S(2)}, u32[]{:S(2)}) collective-permute-start(bf16[688,256]{1,0:T(8,128)(2,1)S(1)} %collective-permute-done.18.refs_3_), channel_id=1, source_target_pairs={{0,4},{1,5},{2,0},{3,1},{6,2},{7,3},{10,6},{11,7},{14,10},{15,11},... | collective-permute-start | bytes 1056776 | tf_op jit(solution)/shard_map/ppermute | solution.py:200
  29.2 15.0 %collective-permute-start.3 = (bf16[688,256]{1,0:T(8,128)(2,1)}, bf16[688,256]{1,0:T(8,128)(2,1)S(1)}, u32[]{:S(2)}, u32[]{:S(2)}) collective-permute-start(bf16[688,256]{1,0:T(8,128)(2,1)} %collective-permute-done.1.refs_0_), channel_id=1, source_target_pairs={{0,2},{1,3},{2,6},{3,7},{6,10},{7,11},{10,14},{11,15},{14,12},{15,... | collective-permute-start | bytes 1056776 | tf_op jit(solution)/shard_map/ppermute | solution.py:200
  30.5 15.0 %collective-permute-start.10 = (bf16[688,256]{1,0:T(8,128)(2,1)}, bf16[688,256]{1,0:T(8,128)(2,1)S(1)}, u32[]{:S(2)}, u32[]{:S(2)}) collective-permute-start(bf16[688,256]{1,0:T(8,128)(2,1)} %collective-permute-done.9.refs_1_), channel_id=1, source_target_pairs={{0,4},{1,5},{2,0},{3,1},{6,2},{7,3},{10,6},{11,7},{14,10},{15,11},... | collective-permute-start | bytes 1056776 | tf_op jit(solution)/shard_map/ppermute | solution.py:200
  30.7 3.4 %copy-start = (bf16[384,11008]{1,0:T(8,128)(2,1)S(1)}, bf16[384,11008]{1,0:T(8,128)(2,1)}, u32[]{:S(2)}) copy-start(bf16[384,11008]{1,0:T(8,128)(2,1)} %own_hbm.17) | copy-start | bytes 25362436
  37.3 14.5 %collective-permute-start.17 = (bf16[688,256]{1,0:T(8,128)(2,1)}, bf16[688,256]{1,0:T(8,128)(2,1)S(1)}, u32[]{:S(2)}, u32[]{:S(2)}) collective-permute-start(bf16[688,256]{1,0:T(8,128)(2,1)} %collective-permute-done.16.refs_2_), channel_id=1, source_target_pairs={{0,2},{1,3},{2,6},{3,7},{6,10},{7,11},{10,14},{11,15},{14,12},{15,... | collective-permute-start | bytes 1056776 | tf_op jit(solution)/shard_map/ppermute | solution.py:200
  38.6 14.4 %collective-permute-start.21 = (bf16[688,256]{1,0:T(8,128)(2,1)}, bf16[688,256]{1,0:T(8,128)(2,1)S(1)}, u32[]{:S(2)}, u32[]{:S(2)}) collective-permute-start(bf16[688,256]{1,0:T(8,128)(2,1)} %collective-permute-done.19.refs_3_), channel_id=1, source_target_pairs={{0,4},{1,5},{2,0},{3,1},{6,2},{7,3},{10,6},{11,7},{14,10},{15,11},... | collective-permute-start | bytes 1056776 | tf_op jit(solution)/shard_map/ppermute | solution.py:200
  44.2 15.1 %collective-permute-start.4 = (bf16[688,256]{1,0:T(8,128)(2,1)S(1)}, bf16[688,256]{1,0:T(8,128)(2,1)S(1)}, u32[]{:S(2)}, u32[]{:S(2)}) collective-permute-start(bf16[688,256]{1,0:T(8,128)(2,1)S(1)} %collective-permute-done.3.refs_0_), channel_id=1, source_target_pairs={{0,2},{1,3},{2,6},{3,7},{6,10},{7,11},{10,14},{11,15},{14,12},{15,... | collective-permute-start | bytes 1056776 | tf_op jit(solution)/shard_map/ppermute | solution.py:200
  45.5 15.1 %collective-permute-start.11 = (bf16[688,256]{1,0:T(8,128)(2,1)S(1)}, bf16[688,256]{1,0:T(8,128)(2,1)S(1)}, u32[]{:S(2)}, u32[]{:S(2)}) collective-permute-start(bf16[688,256]{1,0:T(8,128)(2,1)S(1)} %collective-permute-done.10.refs_1_), channel_id=1, source_target_pairs={{0,4},{1,5},{2,0},{3,1},{6,2},{7,3},{10,6},{11,7},{14,10},{15,11},... | collective-permute-start | bytes 1056776 | tf_op jit(solution)/shard_map/ppermute | solution.py:200
  51.8 16.8 %collective-permute-start.20 = (bf16[688,256]{1,0:T(8,128)(2,1)S(1)}, bf16[688,256]{1,0:T(8,128)(2,1)S(1)}, u32[]{:S(2)}, u32[]{:S(2)}) collective-permute-start(bf16[688,256]{1,0:T(8,128)(2,1)S(1)} %collective-permute-done.17.refs_2_), channel_id=1, source_target_pairs={{0,2},{1,3},{2,6},{3,7},{6,10},{7,11},{10,14},{11,15},{14,12},{15,... | collective-permute-start | bytes 1056776 | tf_op jit(solution)/shard_map/ppermute | solution.py:200
  53.1 16.8 %collective-permute-start.23 = (bf16[688,256]{1,0:T(8,128)(2,1)S(1)}, bf16[688,256]{1,0:T(8,128)(2,1)S(1)}, u32[]{:S(2)}, u32[]{:S(2)}) collective-permute-start(bf16[688,256]{1,0:T(8,128)(2,1)S(1)} %collective-permute-done.21.refs_3_), channel_id=1, source_target_pairs={{0,4},{1,5},{2,0},{3,1},{6,2},{7,3},{10,6},{11,7},{14,10},{15,11},... | collective-permute-start | bytes 1056776 | tf_op jit(solution)/shard_map/ppermute | solution.py:200
  59.3 15.1 %collective-permute-start.5 = (bf16[688,256]{1,0:T(8,128)(2,1)S(1)}, bf16[688,256]{1,0:T(8,128)(2,1)S(1)}, u32[]{:S(2)}, u32[]{:S(2)}) collective-permute-start(bf16[688,256]{1,0:T(8,128)(2,1)S(1)} %collective-permute-done.4.refs_0_), channel_id=1, source_target_pairs={{0,2},{1,3},{2,6},{3,7},{6,10},{7,11},{10,14},{11,15},{14,12},{15,... | collective-permute-start | bytes 1056776 | tf_op jit(solution)/shard_map/ppermute | solution.py:200
  60.6 15.1 %collective-permute-start.12 = (bf16[688,256]{1,0:T(8,128)(2,1)S(1)}, bf16[688,256]{1,0:T(8,128)(2,1)S(1)}, u32[]{:S(2)}, u32[]{:S(2)}) collective-permute-start(bf16[688,256]{1,0:T(8,128)(2,1)S(1)} %collective-permute-done.11.refs_1_), channel_id=1, source_target_pairs={{0,4},{1,5},{2,0},{3,1},{6,2},{7,3},{10,6},{11,7},{14,10},{15,11},... | collective-permute-start | bytes 1056776 | tf_op jit(solution)/shard_map/ppermute | solution.py:200
  68.5 13.4 %collective-permute-start.22 = (bf16[688,256]{1,0:T(8,128)(2,1)S(1)}, bf16[688,256]{1,0:T(8,128)(2,1)S(1)}, u32[]{:S(2)}, u32[]{:S(2)}) collective-permute-start(bf16[688,256]{1,0:T(8,128)(2,1)S(1)} %collective-permute-done.20.refs_2_), channel_id=1, source_target_pairs={{0,2},{1,3},{2,6},{3,7},{6,10},{7,11},{10,14},{11,15},{14,12},{15,... | collective-permute-start | bytes 1056776 | tf_op jit(solution)/shard_map/ppermute | solution.py:200
  69.9 13.4 %collective-permute-start.25 = (bf16[688,256]{1,0:T(8,128)(2,1)S(1)}, bf16[688,256]{1,0:T(8,128)(2,1)S(1)}, u32[]{:S(2)}, u32[]{:S(2)}) collective-permute-start(bf16[688,256]{1,0:T(8,128)(2,1)S(1)} %collective-permute-done.23.refs_3_), channel_id=1, source_target_pairs={{0,4},{1,5},{2,0},{3,1},{6,2},{7,3},{10,6},{11,7},{14,10},{15,11},... | collective-permute-start | bytes 1056776 | tf_op jit(solution)/shard_map/ppermute | solution.py:200
  74.4 15.1 %collective-permute-start.6 = (bf16[688,256]{1,0:T(8,128)(2,1)S(1)}, bf16[688,256]{1,0:T(8,128)(2,1)S(1)}, u32[]{:S(2)}, u32[]{:S(2)}) collective-permute-start(bf16[688,256]{1,0:T(8,128)(2,1)S(1)} %collective-permute-done.5.refs_0_), channel_id=1, source_target_pairs={{0,2},{1,3},{2,6},{3,7},{6,10},{7,11},{10,14},{11,15},{14,12},{15,... | collective-permute-start | bytes 1056776 | tf_op jit(solution)/shard_map/ppermute | solution.py:200
  75.7 15.1 %collective-permute-start.13 = (bf16[688,256]{1,0:T(8,128)(2,1)S(1)}, bf16[688,256]{1,0:T(8,128)(2,1)S(1)}, u32[]{:S(2)}, u32[]{:S(2)}) collective-permute-start(bf16[688,256]{1,0:T(8,128)(2,1)S(1)} %collective-permute-done.12.refs_1_), channel_id=1, source_target_pairs={{0,4},{1,5},{2,0},{3,1},{6,2},{7,3},{10,6},{11,7},{14,10},{15,11},... | collective-permute-start | bytes 1056776 | tf_op jit(solution)/shard_map/ppermute | solution.py:200
  82.0 15.1 %collective-permute-start.24 = (bf16[688,256]{1,0:T(8,128)(2,1)S(1)}, bf16[688,256]{1,0:T(8,128)(2,1)S(1)}, u32[]{:S(2)}, u32[]{:S(2)}) collective-permute-start(bf16[688,256]{1,0:T(8,128)(2,1)S(1)} %collective-permute-done.22.refs_2_), channel_id=1, source_target_pairs={{0,2},{1,3},{2,6},{3,7},{6,10},{7,11},{10,14},{11,15},{14,12},{15,... | collective-permute-start | bytes 1056776 | tf_op jit(solution)/shard_map/ppermute | solution.py:200
  83.3 14.8 %collective-permute-start.26 = (bf16[688,256]{1,0:T(8,128)(2,1)S(1)}, bf16[688,256]{1,0:T(8,128)(2,1)S(1)}, u32[]{:S(2)}, u32[]{:S(2)}) collective-permute-start(bf16[688,256]{1,0:T(8,128)(2,1)S(1)} %collective-permute-done.25.refs_3_), channel_id=1, source_target_pairs={{0,4},{1,5},{2,0},{3,1},{6,2},{7,3},{10,6},{11,7},{14,10},{15,11},... | collective-permute-start | bytes 1056776 | tf_op jit(solution)/shard_map/ppermute | solution.py:200
  89.5 15.1 %collective-permute-start.7 = (bf16[688,256]{1,0:T(8,128)(2,1)S(1)}, bf16[688,256]{1,0:T(8,128)(2,1)S(1)}, u32[]{:S(2)}, u32[]{:S(2)}) collective-permute-start(bf16[688,256]{1,0:T(8,128)(2,1)S(1)} %collective-permute-done.6.refs_0_), channel_id=1, source_target_pairs={{0,2},{1,3},{2,6},{3,7},{6,10},{7,11},{10,14},{11,15},{14,12},{15,... | collective-permute-start | bytes 1056776 | tf_op jit(solution)/shard_map/ppermute | solution.py:200
  90.8 14.8 %collective-permute-start.14 = (bf16[688,256]{1,0:T(8,128)(2,1)S(1)}, bf16[688,256]{1,0:T(8,128)(2,1)S(1)}, u32[]{:S(2)}, u32[]{:S(2)}) collective-permute-start(bf16[688,256]{1,0:T(8,128)(2,1)S(1)} %collective-permute-done.13.refs_1_), channel_id=1, source_target_pairs={{0,4},{1,5},{2,0},{3,1},{6,2},{7,3},{10,6},{11,7},{14,10},{15,11},... | collective-permute-start | bytes 1056776 | tf_op jit(solution)/shard_map/ppermute | solution.py:200
  98.1 15.1 %collective-permute-start.28 = (bf16[688,256]{1,0:T(8,128)(2,1)S(1)}, bf16[688,256]{1,0:T(8,128)(2,1)S(1)}, u32[]{:S(2)}, u32[]{:S(2)}) collective-permute-start(bf16[688,256]{1,0:T(8,128)(2,1)S(1)} %collective-permute-done.26.refs_3_), channel_id=1, source_target_pairs={{0,4},{1,5},{2,0},{3,1},{6,2},{7,3},{10,6},{11,7},{14,10},{15,11},... | collective-permute-start | bytes 1056776 | tf_op jit(solution)/shard_map/ppermute | solution.py:200
  98.2 15.0 %collective-permute-start.27 = (bf16[688,256]{1,0:T(8,128)(2,1)S(1)}, bf16[688,256]{1,0:T(8,128)(2,1)S(1)}, u32[]{:S(2)}, u32[]{:S(2)}) collective-permute-start(bf16[688,256]{1,0:T(8,128)(2,1)S(1)} %collective-permute-done.24.refs_2_), channel_id=1, source_target_pairs={{0,2},{1,3},{2,6},{3,7},{6,10},{7,11},{10,14},{11,15},{14,12},{15,... | collective-permute-start | bytes 1056776 | tf_op jit(solution)/shard_map/ppermute | solution.py:200
  108.0 9.7 %collective-permute-start.29 = (f32[2,384,256]{2,1,0:T(8,128)S(1)}, f32[2,384,256]{2,1,0:T(8,128)S(1)}, u32[]{:S(2)}, u32[]{:S(2)}) collective-permute-start(f32[2,384,256]{2,1,0:T(8,128)S(1)} %get-tuple-element.169), channel_id=1, source_target_pairs={{0,1},{1,0},{2,3},{3,2},{4,5},{5,4},{6,7},{7,6},{8,9},{9,8},{10,11... | collective-permute-start | bytes 2359304 | tf_op jit(solution)/shard_map/ppermute | solution.py:209
  115.5 4.1 %collective-permute-start.30 = (f32[2,384,256]{2,1,0:T(8,128)S(1)}, f32[2,384,256]{2,1,0:T(8,128)S(1)}, u32[]{:S(2)}, u32[]{:S(2)}) collective-permute-start(f32[2,384,256]{2,1,0:T(8,128)S(1)} %get-tuple-element.170), channel_id=1, source_target_pairs={{0,1},{1,0},{2,3},{3,2},{4,5},{5,4},{6,7},{7,6},{8,9},{9,8},{10,11... | collective-permute-start | bytes 2359304 | tf_op jit(solution)/shard_map/ppermute | solution.py:209
  121.8 41.4 %all-to-all-start.1 = ((bf16[16,6,16,512]{3,2,1,0:T(8,128)(2,1)}), bf16[16,6,16,512]{3,2,1,0:T(8,128)(2,1)S(1)}, u32[]{:S(2)}, u32[]{:S(2)}) async-start(bf16[16,6,16,512]{3,2,1,0:T(8,128)(2,1)} %shard_map.59), calls=%async_computation.1 | async-start | bytes 3145728 | tf_op jit(solution)/shard_map/all_to_all | solution.py:234

commit v6 on v5

--- a/solution.py
+++ b/solution.py
@@ -10,7 +10,7 @@
 
 GRID_CHIPS = 8
 HALVES = 2
-BEHIND = (0, 0, 1, 2, 4, 5, 6)
+BEHIND = (0, 0, 0, 2, 3, 4, 5)
 WAYS = (1, -1)
 LANES = 128
 WINDOW = 896
@@ -55,13 +55,13 @@
     return jnp.minimum(start // LANES * LANES, nvirt - WINDOW)
 
 
-def step_kernel(t, parts, own_hbm, other_hbm, *refs):
+def step_kernel(t, parts, sides, own_hbm, other_hbm, *refs):
     norb = len(WAYS)
     pieces = refs[: norb * parts]
-    scratch = refs[-3:]
-    sums = refs[-3 - 2 * parts : -3]
-    before = refs[norb * parts : -3 - 2 * parts]
-    c_buf, g_buf, sems = scratch
+    c_buf, g_buf, sems = refs[-3:]
+    results = parts * len(sides)
+    sums = refs[-3 - results : -3]
+    before = refs[norb * parts : -3 - results]
     rows, nvirt = own_hbm.shape
     depth, width = pieces[0].shape
     me = lax.axis_index("wide")
@@ -77,9 +77,11 @@
         copies.append(
             [
                 pltpu.make_async_copy(
-                    source.at[:, columns], c_buf.at[i, pl.ds(k * rows, rows)], sems.at[i, k]
+                    (own_hbm, other_hbm)[side].at[:, columns],
+                    c_buf.at[i, pl.ds(k * rows, rows)],
+                    sems.at[i, k],
                 )
-                for k, source in enumerate((own_hbm, other_hbm))
+                for k, side in enumerate(sides)
             ]
         )
         for copy in copies[i]:
@@ -93,17 +95,17 @@
     for i in range(norb):
         for copy in copies[i]:
             copy.wait()
-        for k in range(2):
+        for k in range(len(sides)):
             term = jnp.dot(
                 c_buf[i, pl.ds(k * rows, rows)], g_buf[i], preferred_element_type=jnp.float32
             )
             for j in range(parts):
                 part = term[:, j * width : (j + 1) * width]
-                at = 2 * j + k
+                at = len(sides) * j + k
                 sums[at][i] = before[at][i] + part if before else part
 
 
-def add_products(t, own, other, pieces, before):
+def add_products(t, own, other, pieces, before, sides=(0, 1)):
     rows, nvirt = own.shape
     parts, norb = len(pieces), len(WAYS)
     depth, width = pieces[0][0].shape
@@ -111,59 +113,60 @@
     vmem = pl.BlockSpec(memory_space=pltpu.VMEM)
     hbm = pl.BlockSpec(memory_space=pltpu.HBM)
     flat = [piece for part in pieces for piece in part]
-    old = [value for pair in before for value in pair]
+    old = [value for some in before for value in some]
+    results = parts * len(sides)
     new = pl.pallas_call(
-        functools.partial(step_kernel, t, parts),
-        out_shape=[sums] * (2 * parts),
+        functools.partial(step_kernel, t, parts, sides),
+        out_shape=[sums] * results,
         in_specs=[hbm, hbm] + [vmem] * (len(flat) + len(old)),
-        out_specs=[vmem] * (2 * parts),
+        out_specs=[vmem] * results,
         input_output_aliases={2 + len(flat) + k: k for k in range(len(old))},
         scratch_shapes=[
-            pltpu.VMEM((norb, 2 * rows, WINDOW), jnp.bfloat16),
+            pltpu.VMEM((norb, len(sides) * rows, WINDOW), jnp.bfloat16),
             pltpu.VMEM((norb, WINDOW, parts * width), jnp.bfloat16),
-            pltpu.SemaphoreType.DMA((norb, 2)),
+            pltpu.SemaphoreType.DMA((norb, len(sides))),
         ],
         compiler_params=pltpu.CompilerParams(vmem_limit_bytes=20 << 20),
         cost_estimate=pl.CostEstimate(
-            flops=4 * norb * rows * WINDOW * parts * width,
-            bytes_accessed=4 * norb * rows * WINDOW,
+            flops=2 * len(sides) * norb * rows * WINDOW * parts * width,
+            bytes_accessed=2 * len(sides) * norb * rows * WINDOW,
             transcendentals=0,
         ),
     )(own, other, *flat, *old)
-    return [(new[2 * j], new[2 * j + 1]) for j in range(parts)]
-
-
-def finish_kernel(place_ref, *refs):
+    return [tuple(new[len(sides) * j : len(sides) * (j + 1)]) for j in range(parts)]
+
+
+def finish_kernel(place_ref, mine_ref, theirs_ref, *refs):
     out_ref = refs[-1]
-    mine, theirs = refs[:HALVES], refs[HALVES:-1]
+    norb, _, width = mine_ref.shape
     count, planes, slots, naux = out_ref.shape
-    norb, _, width = mine[0].shape
-    for i in range(norb):
-        for j in range(HALVES):
-            back = (mine[j][i] + theirs[j][i]).astype(jnp.bfloat16)
-            out = jnp.dot(place_ref[...], back, preferred_element_type=jnp.float32)
-            out = out.astype(jnp.bfloat16).reshape(count, planes // norb, slots, width)
-            out_ref[
-                :, pl.ds(i * (planes // norb), planes // norb), :, pl.ds(j * width, width)
-            ] = out
-
-
-def finish(place, mine, theirs, shape):
+    for before in refs[:-1]:
+        out_ref[:, :, :, : naux - width] = before[...]
+    for i in range(norb):
+        back = (mine_ref[i] + theirs_ref[i]).astype(jnp.bfloat16)
+        out = jnp.dot(place_ref[...], back, preferred_element_type=jnp.float32)
+        out = out.astype(jnp.bfloat16).reshape(count, planes // norb, slots, width)
+        plane = pl.ds(i * (planes // norb), planes // norb)
+        out_ref[:, plane, :, pl.ds(naux - width, width)] = out
+
+
+def finish(place, mine, theirs, before, shape):
+    vmem = pl.BlockSpec(memory_space=pltpu.VMEM)
     return pl.pallas_call(
         finish_kernel,
         out_shape=jax.ShapeDtypeStruct(shape, jnp.bfloat16),
-        in_specs=[pl.BlockSpec(memory_space=pltpu.VMEM)] * (1 + len(mine) + len(theirs)),
-        out_specs=pl.BlockSpec(memory_space=pltpu.VMEM),
+        in_specs=[vmem] * (3 + len(before)),
+        out_specs=vmem,
         compiler_params=pltpu.CompilerParams(vmem_limit_bytes=20 << 20),
         cost_estimate=pl.CostEstimate(
             flops=2 * math.prod(shape) * place.shape[1],
             bytes_accessed=2 * math.prod(shape),
             transcendentals=0,
         ),
-    )(place, *mine, *theirs)
-
-
-def ring_products(gamma, coefficients, early):
+    )(place, mine, theirs, *before)
+
+
+def ring_products(gamma, coefficients, ids, place, shape):
     count = lax.axis_size("wide")
     norb, depth, naux = gamma.shape
     width = naux // HALVES
@@ -187,27 +190,29 @@
         if t + 1 == GRID_CHIPS:
             break
         for j in range(HALVES):
-            if j == HALVES - 1:
+            if j == 0:
                 while done < BEHIND[t]:
                     sums = add_products(done, coefficients, other, arrived[done], sums)
                     done += 1
             for i in range(norb):
                 sent = piece[j][i]
                 if t == 2 and i == j == 0:
-                    sent, early = lax.optimization_barrier((sent, early))
-                if j == HALVES - 1 and BEHIND[t]:
+                    sent, ids, place = lax.optimization_barrier((sent, ids, place))
+                if j == 0 and BEHIND[t]:
                     sent, sums = lax.optimization_barrier((sent, sums))
                 piece[j][i] = lax.ppermute(sent, "wide", shift[i])
     while done < GRID_CHIPS - 1:
         sums = add_products(done, coefficients, other, arrived[done], sums)
         done += 1
-    sums = [
-        add_products(done, coefficients, other, [arrived[done][j]], [sums[j]])[0]
-        for j in range(HALVES)
-    ]
-    mine = [sums[j][0] for j in range(HALVES)]
-    theirs = [lax.ppermute(sums[j][1], "wide", swap) for j in range(HALVES)]
-    return mine, theirs, early
+    out = []
+    for j in range(HALVES):
+        last, out = lax.optimization_barrier(([arrived[done][j]], out))
+        mine, theirs = sums[j]
+        ((theirs,),) = add_products(done, coefficients, other, last, [(theirs,)], (1,))
+        theirs = lax.ppermute(theirs, "wide", swap)
+        ((mine,),) = add_products(done, coefficients, other, last, [(mine,)], (0,))
+        out = [finish(place, mine, theirs, out, shape[:3] + ((j + 1) * width,))]
+    return ids, out[0]
 
 
 def local(gamma, coefficients, owners):
@@ -221,8 +226,7 @@
     labels, place = routing(owners, count, slots, block_rows)
     ids = lax.all_to_all(labels, "wide", split_axis=0, concat_axis=0, tiled=True)
     if count == 2 * GRID_CHIPS and norb == len(WAYS):
-        mine, theirs, (ids, place) = ring_products(gamma, coefficients, (ids, place))
-        out = finish(place, mine, theirs, shape)
+        ids, out = ring_products(gamma, coefficients, ids, place, shape)
     else:
         gathered = lax.all_gather(gamma, "wide", axis=1, tiled=True)
         back = jnp.einsum(

time: 165 us -> 171 us (1.036)
  Pallas kernels: 30.4 us -> 33.3 us
  starting transfers between devices: 39.7 us -> 42.3 us
    pallas_call x9 -> x11, Pallas kernels: 28.3 us -> 31 us  [add_products(): pl.pallas_call(functools.partial(step_kernel, t, parts, sides), out_shape...]
    ppermute x28, starting transfers between devices: 20.7 us -> 23.1 us  [ring_products(): piece[j][i] = lax.ppermute(sent, 'wide', shift[i])]
    ppermute x28, waiting for transfers between devices: 47.8 us -> 49.5 us  [ring_products(): piece[j][i] = lax.ppermute(sent, 'wide', shift[i])]
    unnamed x6 -> x12, local copies, waits for them, and re-layouts: 5.15 us -> 5.16 us
  transfers between devices with their start and end apart: 33 -> 33, of which waited for: 15 -> 14; matrix products, arithmetic and copies ran while one was open for 2% -> 2% of each run, Pallas kernels for 17% -> 16%
where the time goes in v6:
time: 171 us
  waiting for transfers between devices  86.2 us (50%)
  starting transfers between devices  42.3 us (25%)
  Pallas kernels  33.3 us (19%)
  local copies, waits for them, and re-layouts  7.53 us (4%)
    ppermute x28, waiting for transfers between devices, ring_products(): piece[j][i] = lax.ppermute(sent, 'wide', shift[i])  49.5 us
    all_to_all x1, waiting for transfers between devices, local(): lax.all_to_all(out, 'wide', split_axis=0, concat_axis=0, tiled=True)  36.2 us
    pallas_call x11, Pallas kernels, add_products(): pl.pallas_call(functools.partial(step_kernel, t, parts, sides), out_shape...  31 us
    ppermute x28, starting transfers between devices, ring_products(): piece[j][i] = lax.ppermute(sent, 'wide', shift[i])  23.1 us
    all_to_all x1, starting transfers between devices, local(): lax.all_to_all(labels, 'wide', split_axis=0, concat_axis=0, tiled=True)  7.04 us
    all_to_all x1, starting transfers between devices, local(): lax.all_to_all(out, 'wide', split_axis=0, concat_axis=0, tiled=True)  6.13 us
    ppermute x2, starting transfers between devices, ring_products(): theirs = lax.ppermute(theirs, 'wide', swap)  5.29 us
    unnamed x12, local copies, waits for them, and re-layouts  5.16 us
  transfers between devices with their start and end apart: 33, of which 14 were waited for; matrix products, arithmetic and copies ran while one was open for 2% of the time, Pallas kernels for 16%

profile of v6, /device:TPU:13, one launch (start us, length us, event | category | flops | bytes accessed | tf_op | source)
XLA Modules:
  0.0 170.8 jit_solution(13722453475085756658)
XLA Ops:
  0.6 0.7 collective-permute-start.2
  1.4 1.4 slice_bitcast_fusion
  2.8 1.3 collective-permute-start
  4.5 1.3 collective-permute-start.3
  6.1 0.7 sub.17
  6.8 7.0 %all-to-all-start = ((s32[16,1,16]{2,1,0:T(1,128)}), s32[16,1,16]{2,1,0:T(1,128)S(1)}, u32[]{:S(2)}, u32[]{:S(2)}) async-start(s32[16,1,16]{2,1,0:T(1,128)} %sub.17), calls=%async_computation | async-start | bytes 16384 | tf_op jit(solution)/shard_map/all_to_all | solution.py:227
  13.9 0.2 mul.58
  14.1 1.2 collective-permute-start.1
  15.4 5.9 %collective-permute-done.18.refs_1_ = bf16[688,256]{1,0:T(8,128)(2,1)S(1)} collective-permute-done((bf16[688,256]{1,0:T(8,128)(2,1)S(1)}, bf16[688,256]{1,0:T(8,128)(2,1)S(1)}, u32[]{:S(2)}, u32[]{:S(2)}) %collective-permute-start.18) | collective-permute-done | bytes 352288 | tf_op jit(solution)/shard_map/ppermute | solution.py:203
  21.5 0.2 collective-permute-start.11
  21.7 1.3 collective-permute-start.4
  23.0 0.2 compare_convert_fusion.place_ref
  23.2 4.8 %collective-permute-done.1.refs_0_ = bf16[688,256]{1,0:T(8,128)(2,1)} collective-permute-done((bf16[688,256]{1,0:T(8,128)(2,1)S(1)}, bf16[688,256]{1,0:T(8,128)(2,1)}, u32[]{:S(2)}, u32[]{:S(2)}) %collective-permute-start.1) | collective-permute-done | bytes 352288 | tf_op jit(solution)/shard_map/ppermute | solution.py:203
  28.0 1.3 collective-permute-start.17
  29.4 0.7 collective-permute-done.20.refs_1_
  30.0 0.2 collective-permute-start.21
  30.3 7.3 %collective-permute-done.11.refs_3_ = bf16[688,256]{1,0:T(8,128)(2,1)} collective-permute-done((bf16[688,256]{1,0:T(8,128)(2,1)S(1)}, bf16[688,256]{1,0:T(8,128)(2,1)}, u32[]{:S(2)}, u32[]{:S(2)}) %collective-permute-start.11) | collective-permute-done | bytes 352288 | tf_op jit(solution)/shard_map/ppermute | solution.py:203
  37.6 0.2 collective-permute-start.12
  37.8 1.2 collective-permute-start.5
  39.1 3.4 %copy-done = bf16[384,11008]{1,0:T(8,128)(2,1)S(1)} copy-done((bf16[384,11008]{1,0:T(8,128)(2,1)S(1)}, bf16[384,11008]{1,0:T(8,128)(2,1)}, u32[]{:S(2)}) %copy-start) | copy-done | bytes 8454168
  42.5 3.1 %shard_map.50 = (f32[2,384,256]{2,1,0:T(8,128)S(1)}, f32[2,384,256]{2,1,0:T(8,128)S(1)}, f32[2,384,256]{2,1,0:T(8,128)S(1)}, f32[2,384,256]{2,1,0:T(8,128)S(1)}) custom-call(bf16[384,11008]{1,0:T(8,128)(2,1)S(1)} %copy-done, bf16[384,11008]{1,0:T(8,128)(2,1)} %collective-permute-done.2.other_hbm, bf16[688,256]{1,0:T(8,128)(2,1)S(1)} %get-tuple-element.158.refs_0_, ...), custom_call_target="tpu_custom_call" | custom-call | flops 1409286144 | bytes 2752512 | tf_op jit(solution)/shard_map/pallas_call | solution.py:118
  45.6 3.2 %shard_map.51 = (f32[2,384,256]{2,1,0:T(8,128)S(1)}, f32[2,384,256]{2,1,0:T(8,128)S(1)}, f32[2,384,256]{2,1,0:T(8,128)S(1)}, f32[2,384,256]{2,1,0:T(8,128)S(1)}) custom-call(bf16[384,11008]{1,0:T(8,128)(2,1)S(1)} %copy-done, ...), custom_call_target="tpu_custom_call", output_to_operand_aliasing={{0}: (6, {}), {1}: (7, {}), {2}: (8, {}), {3}: (9, {})} | custom-call | flops 1409286144 | bytes 2752512 | tf_op jit(solution)/shard_map/pallas_call | solution.py:118
  48.9 1.1 collective-permute-start.19
  50.0 0.4 collective-permute-start.23
  50.4 2.2 %collective-permute-done.12.refs_3_ = bf16[688,256]{1,0:T(8,128)(2,1)S(1)} collective-permute-done((bf16[688,256]{1,0:T(8,128)(2,1)}, bf16[688,256]{1,0:T(8,128)(2,1)S(1)}, u32[]{:S(2)}, u32[]{:S(2)}) %collective-permute-start.12) | collective-permute-done | bytes 352288 | tf_op jit(solution)/shard_map/ppermute | solution.py:203
  52.6 0.2 collective-permute-start.13
  52.8 1.2 collective-permute-start.6
  54.1 4.5 %shard_map.52 = (f32[2,384,256]{2,1,0:T(8,128)S(1)}, f32[2,384,256]{2,1,0:T(8,128)S(1)}, f32[2,384,256]{2,1,0:T(8,128)S(1)}, f32[2,384,256]{2,1,0:T(8,128)S(1)}) custom-call(bf16[384,11008]{1,0:T(8,128)(2,1)S(1)} %copy-done, ...), custom_call_target="tpu_custom_call", output_to_operand_aliasing={{0}: (6, {}), {1}: (7, {}), {2}: (8, {}), {3}: (9, {})} | custom-call | flops 1409286144 | bytes 2752512 | tf_op jit(solution)/shard_map/pallas_call | solution.py:118
  58.6 1.1 collective-permute-start.22
  59.7 0.4 collective-permute-start.25
  60.1 5.5 %collective-permute-done.13.refs_3_ = bf16[688,256]{1,0:T(8,128)(2,1)S(1)} collective-permute-done((bf16[688,256]{1,0:T(8,128)(2,1)S(1)}, bf16[688,256]{1,0:T(8,128)(2,1)S(1)}, u32[]{:S(2)}, u32[]{:S(2)}) %collective-permute-start.13) | collective-permute-done | bytes 352288 | tf_op jit(solution)/shard_map/ppermute | solution.py:203
  65.6 0.2 collective-permute-start.14
  65.8 1.9 %collective-permute-start.7 = (bf16[688,256]{1,0:T(8,128)(2,1)S(1)}, bf16[688,256]{1,0:T(8,128)(2,1)S(1)}, u32[]{:S(2)}, u32[]{:S(2)}) collective-permute-start(bf16[688,256]{1,0:T(8,128)(2,1)S(1)} %collective-permute-done.6.refs_2_), channel_id=1, source_target_pairs={{0,2},{1,3},{2,6},{3,7},{6,10},{7,11},{10,14},{11,15},{14,12},{15,... | collective-permute-start | bytes 1056776 | tf_op jit(solution)/shard_map/ppermute | solution.py:203
  67.7 3.2 %shard_map.53 = (f32[2,384,256]{2,1,0:T(8,128)S(1)}, f32[2,384,256]{2,1,0:T(8,128)S(1)}, f32[2,384,256]{2,1,0:T(8,128)S(1)}, f32[2,384,256]{2,1,0:T(8,128)S(1)}) custom-call(bf16[384,11008]{1,0:T(8,128)(2,1)S(1)} %copy-done, ...), custom_call_target="tpu_custom_call", output_to_operand_aliasing={{0}: (6, {}), {1}: (7, {}), {2}: (8, {}), {3}: (9, {})} | custom-call | flops 1409286144 | bytes 2752512 | tf_op jit(solution)/shard_map/pallas_call | solution.py:118
  70.9 1.5 collective-permute-start.24
  72.4 0.7 collective-permute-done.25.refs_1_
  73.1 0.2 collective-permute-start.27
  73.3 7.3 %collective-permute-done.14.refs_3_ = bf16[688,256]{1,0:T(8,128)(2,1)S(1)} collective-permute-done((bf16[688,256]{1,0:T(8,128)(2,1)S(1)}, bf16[688,256]{1,0:T(8,128)(2,1)S(1)}, u32[]{:S(2)}, u32[]{:S(2)}) %collective-permute-start.14) | collective-permute-done | bytes 352288 | tf_op jit(solution)/shard_map/ppermute | solution.py:203
  80.7 0.2 collective-permute-start.15
  80.9 1.9 %collective-permute-start.8 = (bf16[688,256]{1,0:T(8,128)(2,1)S(1)}, bf16[688,256]{1,0:T(8,128)(2,1)S(1)}, u32[]{:S(2)}, u32[]{:S(2)}) collective-permute-start(bf16[688,256]{1,0:T(8,128)(2,1)S(1)} %collective-permute-done.7.refs_2_), channel_id=1, source_target_pairs={{0,2},{1,3},{2,6},{3,7},{6,10},{7,11},{10,14},{11,15},{14,12},{15,... | collective-permute-start | bytes 1056776 | tf_op jit(solution)/shard_map/ppermute | solution.py:203
  82.8 3.2 %shard_map.54 = (f32[2,384,256]{2,1,0:T(8,128)S(1)}, f32[2,384,256]{2,1,0:T(8,128)S(1)}, f32[2,384,256]{2,1,0:T(8,128)S(1)}, f32[2,384,256]{2,1,0:T(8,128)S(1)}) custom-call(bf16[384,11008]{1,0:T(8,128)(2,1)S(1)} %copy-done, ...), custom_call_target="tpu_custom_call", output_to_operand_aliasing={{0}: (6, {}), {1}: (7, {}), {2}: (8, {}), {3}: (9, {})} | custom-call | flops 1409286144 | bytes 2752512 | tf_op jit(solution)/shard_map/pallas_call | solution.py:118
  86.0 2.2 %collective-permute-done.27.refs_1_ = bf16[688,256]{1,0:T(8,128)(2,1)S(1)} collective-permute-done((bf16[688,256]{1,0:T(8,128)(2,1)S(1)}, bf16[688,256]{1,0:T(8,128)(2,1)S(1)}, u32[]{:S(2)}, u32[]{:S(2)}) %collective-permute-start.27) | collective-permute-done | bytes 352288 | tf_op jit(solution)/shard_map/ppermute | solution.py:203
  88.2 0.2 collective-permute-start.28
  88.4 1.9 %collective-permute-start.26 = (bf16[688,256]{1,0:T(8,128)(2,1)S(1)}, bf16[688,256]{1,0:T(8,128)(2,1)S(1)}, u32[]{:S(2)}, u32[]{:S(2)}) collective-permute-start(bf16[688,256]{1,0:T(8,128)(2,1)S(1)} %collective-permute-done.24.refs_0_), channel_id=1, source_target_pairs={{0,2},{1,3},{2,6},{3,7},{6,10},{7,11},{10,14},{11,15},{14,12},{15,... | collective-permute-start | bytes 1056776 | tf_op jit(solution)/shard_map/ppermute | solution.py:203
  90.4 3.2 %shard_map.55 = (f32[2,384,256]{2,1,0:T(8,128)S(1)}, f32[2,384,256]{2,1,0:T(8,128)S(1)}, f32[2,384,256]{2,1,0:T(8,128)S(1)}, f32[2,384,256]{2,1,0:T(8,128)S(1)}) custom-call(bf16[384,11008]{1,0:T(8,128)(2,1)S(1)} %copy-done, ...), custom_call_target="tpu_custom_call", output_to_operand_aliasing={{0}: (6, {}), {1}: (7, {}), {2}: (8, {}), {3}: (9, {})} | custom-call | flops 1409286144 | bytes 2752512 | tf_op jit(solution)/shard_map/pallas_call | solution.py:118
  93.5 2.2 %collective-permute-done.15.refs_3_ = bf16[688,256]{1,0:T(8,128)(2,1)S(1)} collective-permute-done((bf16[688,256]{1,0:T(8,128)(2,1)S(1)}, bf16[688,256]{1,0:T(8,128)(2,1)S(1)}, u32[]{:S(2)}, u32[]{:S(2)}) %collective-permute-start.15) | collective-permute-done | bytes 352288 | tf_op jit(solution)/shard_map/ppermute | solution.py:203
  95.8 3.2 %shard_map.56 = (f32[2,384,256]{2,1,0:T(8,128)S(1)}, f32[2,384,256]{2,1,0:T(8,128)S(1)}, f32[2,384,256]{2,1,0:T(8,128)S(1)}, f32[2,384,256]{2,1,0:T(8,128)S(1)}) custom-call(bf16[384,11008]{1,0:T(8,128)(2,1)S(1)} %copy-done, ...), custom_call_target="tpu_custom_call", output_to_operand_aliasing={{0}: (6, {}), {1}: (7, {}), {2}: (8, {}), {3}: (9, {})} | custom-call | flops 1409286144 | bytes 2752512 | tf_op jit(solution)/shard_map/pallas_call | solution.py:118
  98.9 4.4 %collective-permute-done.28.refs_1_ = bf16[688,256]{1,0:T(8,128)(2,1)S(1)} collective-permute-done((bf16[688,256]{1,0:T(8,128)(2,1)S(1)}, bf16[688,256]{1,0:T(8,128)(2,1)S(1)}, u32[]{:S(2)}, u32[]{:S(2)}) %collective-permute-start.28) | collective-permute-done | bytes 352288 | tf_op jit(solution)/shard_map/ppermute | solution.py:203
  103.3 2.3 %shard_map.58 = f32[2,384,256]{2,1,0:T(8,128)S(1)} custom-call(bf16[384,11008]{1,0:T(8,128)(2,1)S(1)} %copy-done, bf16[384,11008]{1,0:T(8,128)(2,1)} %collective-permute-done.2.other_hbm, bf16[688,256]{1,0:T(8,128)(2,1)S(1)} %collective-permute-done.26.refs_0_, bf16[688,256]{1,0:T(8,128)(2,1)S(1)} %collective-permute-done.28.refs_1_, ...), custom_call_target="tpu_custom_call", output_to_operand_aliasing={{}: (4, {})} | custom-call | flops 352321536 | bytes 1376256 | tf_op jit(solution)/shard_map/pallas_call | solution.py:118
  105.6 4.2 %collective-permute-start.29 = (f32[2,384,256]{2,1,0:T(8,128)S(1)}, f32[2,384,256]{2,1,0:T(8,128)S(1)}, u32[]{:S(2)}, u32[]{:S(2)}) collective-permute-start(f32[2,384,256]{2,1,0:T(8,128)S(1)} %shard_map.58), channel_id=1, source_target_pairs={{0,1},{1,0},{2,3},{3,2},{4,5},{5,4},{6,7},{7,6},{8,9},{9,8},{10,11... | collective-permute-start | bytes 2359304 | tf_op jit(solution)/shard_map/ppermute | solution.py:212
  109.8 0.2 collective-permute-start.16
  110.0 1.3 collective-permute-start.9
  111.3 1.4 shard_map.57.mine_ref
  112.7 0.6 shard_map.59.refs_0_
  113.3 6.3 %collective-permute-done.16.refs_1_ = bf16[688,256]{1,0:T(8,128)(2,1)S(1)} collective-permute-done((bf16[688,256]{1,0:T(8,128)(2,1)S(1)}, bf16[688,256]{1,0:T(8,128)(2,1)S(1)}, u32[]{:S(2)}, u32[]{:S(2)}) %collective-permute-start.16) | collective-permute-done | bytes 352288 | tf_op jit(solution)/shard_map/ppermute | solution.py:203
  119.7 2.3 %shard_map.61 = f32[2,384,256]{2,1,0:T(8,128)S(1)} custom-call(bf16[384,11008]{1,0:T(8,128)(2,1)S(1)} %bitcast.17, bf16[384,11008]{1,0:T(8,128)(2,1)} %collective-permute-done.2.other_hbm, bf16[688,256]{1,0:T(8,128)(2,1)S(1)} %collective-permute-done.9.refs_0_, bf16[688,256]{1,0:T(8,128)(2,1)S(1)} %collective-permute-done.16.refs_1_, ...), custom_call_target="tpu_custom_call", output_to_operand_aliasing={{}: (4, {})} | custom-call | flops 352321536 | bytes 1376256 | tf_op jit(solution)/shard_map/pallas_call | solution.py:118
  122.0 1.1 collective-permute-start.30
  123.1 1.4 shard_map.60.mine_ref
  124.5 0.5 collective-permute-done.30.theirs_ref
  125.0 1.7 %shard_map.62 = bf16[16,6,16,512]{3,2,1,0:T(8,128)(2,1)} custom-call(bf16[768,384]{1,0:T(8,128)(2,1)S(1)} %compare_convert_fusion.place_ref, f32[2,384,256]{2,1,0:T(8,128)S(1)} %shard_map.60.mine_ref, f32[2,384,256]{2,1,0:T(8,128)S(1)} %collective-permute-done.30.theirs_ref, bf16[16,6,16,256]{3,2,1,0:T(8,128)(2,1)S(1)} %shard_map.59.refs_0_), custom_call_target="tpu_custom_call" | custom-call | flops 603979776 | bytes 1572864 | tf_op jit(solution)/shard_map/pallas_call | solution.py:155
  126.7 6.1 %all-to-all-start.1 = ((bf16[16,6,16,512]{3,2,1,0:T(8,128)(2,1)}), bf16[16,6,16,512]{3,2,1,0:T(8,128)(2,1)S(1)}, u32[]{:S(2)}, u32[]{:S(2)}) async-start(bf16[16,6,16,512]{3,2,1,0:T(8,128)(2,1)} %shard_map.62), calls=%async_computation.1 | async-start | bytes 3145728 | tf_op jit(solution)/shard_map/all_to_all | solution.py:238
  132.8 36.2 %all-to-all-done.1 = bf16[16,6,16,512]{3,2,1,0:T(8,128)(2,1)S(1)} async-done(((bf16[16,6,16,512]{3,2,1,0:T(8,128)(2,1)}), bf16[16,6,16,512]{3,2,1,0:T(8,128)(2,1)S(1)}, u32[]{:S(2)}, u32[]{:S(2)}) %all-to-all-start.1) | async-done | bytes 1572896 | tf_op jit(solution)/shard_map/all_to_all | solution.py:238
  169.0 1.1 copy.63
  170.2 0.6 copy.64
  (39 shorter events, 1.0 us)
Async XLA Ops:
  0.6 5.1 %copy-start.1 = (s32[128,1]{0,1:T(1,128)S(1)}, s32[128,1]{0,1:T(1,128)}, u32[]{:S(2)}) copy-start(s32[128,1]{0,1:T(1,128)} %param.5) | copy-start | bytes 1540
  0.6 38.4 %collective-permute-start.2 = (bf16[384,11008]{1,0:T(8,128)(2,1)}, bf16[384,11008]{1,0:T(8,128)(2,1)}, u32[]{:S(2)}, u32[]{:S(2)}) collective-permute-start(bf16[384,11008]{1,0:T(8,128)(2,1)} %own_hbm.21), channel_id=1, source_target_pairs={{0,1},{1,0},{2,3},{3,2},{4,5},{5,4},{6,7},{7,6},{8,9},{9,8},{10,11... | collective-permute-start | bytes 25362440 | tf_op jit(solution)/shard_map/ppermute | solution.py:174
  2.8 11.3 %collective-permute-start = (bf16[688,256]{1,0:T(8,128)(2,1)S(1)}, bf16[688,256]{1,0:T(8,128)(2,1)S(1)}, u32[]{:S(2)}, u32[]{:S(2)}) collective-permute-start(bf16[688,256]{1,0:T(8,128)(2,1)S(1)} %get-tuple-element.158.refs_0_), channel_id=1, source_target_pairs={{0,2},{1,3},{2,6},{3,7},{6,10},{7,11},{10,14},{11,15},{14,12},{15,... | collective-permute-start | bytes 1056776 | tf_op jit(solution)/shard_map/ppermute | solution.py:203
  4.1 17.3 %collective-permute-start.10 = (bf16[688,256]{1,0:T(8,128)(2,1)S(1)}, bf16[688,256]{1,0:T(8,128)(2,1)S(1)}, u32[]{:S(2)}, u32[]{:S(2)}) collective-permute-start(bf16[688,256]{1,0:T(8,128)(2,1)S(1)} %get-tuple-element.159.refs_3_), channel_id=1, source_target_pairs={{0,4},{1,5},{2,0},{3,1},{6,2},{7,3},{10,6},{11,7},{14,10},{15,11},... | collective-permute-start | bytes 1056776 | tf_op jit(solution)/shard_map/ppermute | solution.py:203
  4.3 17.0 %collective-permute-start.18 = (bf16[688,256]{1,0:T(8,128)(2,1)S(1)}, bf16[688,256]{1,0:T(8,128)(2,1)S(1)}, u32[]{:S(2)}, u32[]{:S(2)}) collective-permute-start(bf16[688,256]{1,0:T(8,128)(2,1)S(1)} %get-tuple-element.156.refs_1_), channel_id=1, source_target_pairs={{0,4},{1,5},{2,0},{3,1},{6,2},{7,3},{10,6},{11,7},{14,10},{15,11},... | collective-permute-start | bytes 1056776 | tf_op jit(solution)/shard_map/ppermute | solution.py:203
  4.5 17.3 %collective-permute-start.3 = (bf16[688,256]{1,0:T(8,128)(2,1)S(1)}, bf16[688,256]{1,0:T(8,128)(2,1)S(1)}, u32[]{:S(2)}, u32[]{:S(2)}) collective-permute-start(bf16[688,256]{1,0:T(8,128)(2,1)S(1)} %get-tuple-element.157.refs_2_), channel_id=1, source_target_pairs={{0,2},{1,3},{2,6},{3,7},{6,10},{7,11},{10,14},{11,15},{14,12},{15,... | collective-permute-start | bytes 1056776 | tf_op jit(solution)/shard_map/ppermute | solution.py:203
  6.8 16.4 %all-to-all-start = ((s32[16,1,16]{2,1,0:T(1,128)}), s32[16,1,16]{2,1,0:T(1,128)S(1)}, u32[]{:S(2)}, u32[]{:S(2)}) async-start(s32[16,1,16]{2,1,0:T(1,128)} %sub.17), calls=%async_computation | async-start | bytes 16384 | tf_op jit(solution)/shard_map/all_to_all | solution.py:227
  14.1 13.9 %collective-permute-start.1 = (bf16[688,256]{1,0:T(8,128)(2,1)S(1)}, bf16[688,256]{1,0:T(8,128)(2,1)}, u32[]{:S(2)}, u32[]{:S(2)}) collective-permute-start(bf16[688,256]{1,0:T(8,128)(2,1)S(1)} %collective-permute-done.refs_0_), channel_id=1, source_target_pairs={{0,2},{1,3},{2,6},{3,7},{6,10},{7,11},{10,14},{11,15},{14,12},{15,... | collective-permute-start | bytes 1056776 | tf_op jit(solution)/shard_map/ppermute | solution.py:203
  21.3 8.8 %collective-permute-start.20 = (bf16[688,256]{1,0:T(8,128)(2,1)S(1)}, bf16[688,256]{1,0:T(8,128)(2,1)}, u32[]{:S(2)}, u32[]{:S(2)}) collective-permute-start(bf16[688,256]{1,0:T(8,128)(2,1)S(1)} %collective-permute-done.18.refs_1_), channel_id=1, source_target_pairs={{0,4},{1,5},{2,0},{3,1},{6,2},{7,3},{10,6},{11,7},{14,10},{15,11},... | collective-permute-start | bytes 1056776 | tf_op jit(solution)/shard_map/ppermute | solution.py:203
  21.5 16.1 %collective-permute-start.11 = (bf16[688,256]{1,0:T(8,128)(2,1)S(1)}, bf16[688,256]{1,0:T(8,128)(2,1)}, u32[]{:S(2)}, u32[]{:S(2)}) collective-permute-start(bf16[688,256]{1,0:T(8,128)(2,1)S(1)} %collective-permute-done.10.refs_3_), channel_id=1, source_target_pairs={{0,4},{1,5},{2,0},{3,1},{6,2},{7,3},{10,6},{11,7},{14,10},{15,11},... | collective-permute-start | bytes 1056776 | tf_op jit(solution)/shard_map/ppermute | solution.py:203
  21.7 16.1 %collective-permute-start.4 = (bf16[688,256]{1,0:T(8,128)(2,1)S(1)}, bf16[688,256]{1,0:T(8,128)(2,1)}, u32[]{:S(2)}, u32[]{:S(2)}) collective-permute-start(bf16[688,256]{1,0:T(8,128)(2,1)S(1)} %collective-permute-done.3.refs_2_), channel_id=1, source_target_pairs={{0,2},{1,3},{2,6},{3,7},{6,10},{7,11},{10,14},{11,15},{14,12},{15,... | collective-permute-start | bytes 1056776 | tf_op jit(solution)/shard_map/ppermute | solution.py:203
  28.0 20.9 %collective-permute-start.17 = (bf16[688,256]{1,0:T(8,128)(2,1)}, bf16[688,256]{1,0:T(8,128)(2,1)S(1)}, u32[]{:S(2)}, u32[]{:S(2)}) collective-permute-start(bf16[688,256]{1,0:T(8,128)(2,1)} %collective-permute-done.1.refs_0_), channel_id=1, source_target_pairs={{0,2},{1,3},{2,6},{3,7},{6,10},{7,11},{10,14},{11,15},{14,12},{15,... | collective-permute-start | bytes 1056776 | tf_op jit(solution)/shard_map/ppermute | solution.py:203
  30.0 20.0 %collective-permute-start.21 = (bf16[688,256]{1,0:T(8,128)(2,1)}, bf16[688,256]{1,0:T(8,128)(2,1)S(1)}, u32[]{:S(2)}, u32[]{:S(2)}) collective-permute-start(bf16[688,256]{1,0:T(8,128)(2,1)} %collective-permute-done.20.refs_1_), channel_id=1, source_target_pairs={{0,4},{1,5},{2,0},{3,1},{6,2},{7,3},{10,6},{11,7},{14,10},{15,11},... | collective-permute-start | bytes 1056776 | tf_op jit(solution)/shard_map/ppermute | solution.py:203
  37.6 15.0 %collective-permute-start.12 = (bf16[688,256]{1,0:T(8,128)(2,1)}, bf16[688,256]{1,0:T(8,128)(2,1)S(1)}, u32[]{:S(2)}, u32[]{:S(2)}) collective-permute-start(bf16[688,256]{1,0:T(8,128)(2,1)} %collective-permute-done.11.refs_3_), channel_id=1, source_target_pairs={{0,4},{1,5},{2,0},{3,1},{6,2},{7,3},{10,6},{11,7},{14,10},{15,11},... | collective-permute-start | bytes 1056776 | tf_op jit(solution)/shard_map/ppermute | solution.py:203
  37.8 15.0 %collective-permute-start.5 = (bf16[688,256]{1,0:T(8,128)(2,1)}, bf16[688,256]{1,0:T(8,128)(2,1)S(1)}, u32[]{:S(2)}, u32[]{:S(2)}) collective-permute-start(bf16[688,256]{1,0:T(8,128)(2,1)} %collective-permute-done.4.refs_2_), channel_id=1, source_target_pairs={{0,2},{1,3},{2,6},{3,7},{6,10},{7,11},{10,14},{11,15},{14,12},{15,... | collective-permute-start | bytes 1056776 | tf_op jit(solution)/shard_map/ppermute | solution.py:203
  39.1 3.4 %copy-start = (bf16[384,11008]{1,0:T(8,128)(2,1)S(1)}, bf16[384,11008]{1,0:T(8,128)(2,1)}, u32[]{:S(2)}) copy-start(bf16[384,11008]{1,0:T(8,128)(2,1)} %own_hbm.21) | copy-start | bytes 25362436
  48.9 9.7 %collective-permute-start.19 = (bf16[688,256]{1,0:T(8,128)(2,1)S(1)}, bf16[688,256]{1,0:T(8,128)(2,1)S(1)}, u32[]{:S(2)}, u32[]{:S(2)}) collective-permute-start(bf16[688,256]{1,0:T(8,128)(2,1)S(1)} %collective-permute-done.17.refs_0_), channel_id=1, source_target_pairs={{0,2},{1,3},{2,6},{3,7},{6,10},{7,11},{10,14},{11,15},{14,12},{15,... | collective-permute-start | bytes 1056776 | tf_op jit(solution)/shard_map/ppermute | solution.py:203
  50.0 9.7 %collective-permute-start.23 = (bf16[688,256]{1,0:T(8,128)(2,1)S(1)}, bf16[688,256]{1,0:T(8,128)(2,1)S(1)}, u32[]{:S(2)}, u32[]{:S(2)}) collective-permute-start(bf16[688,256]{1,0:T(8,128)(2,1)S(1)} %collective-permute-done.21.refs_1_), channel_id=1, source_target_pairs={{0,4},{1,5},{2,0},{3,1},{6,2},{7,3},{10,6},{11,7},{14,10},{15,11},... | collective-permute-start | bytes 1056776 | tf_op jit(solution)/shard_map/ppermute | solution.py:203
  52.6 13.0 %collective-permute-start.13 = (bf16[688,256]{1,0:T(8,128)(2,1)S(1)}, bf16[688,256]{1,0:T(8,128)(2,1)S(1)}, u32[]{:S(2)}, u32[]{:S(2)}) collective-permute-start(bf16[688,256]{1,0:T(8,128)(2,1)S(1)} %collective-permute-done.12.refs_3_), channel_id=1, source_target_pairs={{0,4},{1,5},{2,0},{3,1},{6,2},{7,3},{10,6},{11,7},{14,10},{15,11},... | collective-permute-start | bytes 1056776 | tf_op jit(solution)/shard_map/ppermute | solution.py:203
  52.8 13.0 %collective-permute-start.6 = (bf16[688,256]{1,0:T(8,128)(2,1)S(1)}, bf16[688,256]{1,0:T(8,128)(2,1)S(1)}, u32[]{:S(2)}, u32[]{:S(2)}) collective-permute-start(bf16[688,256]{1,0:T(8,128)(2,1)S(1)} %collective-permute-done.5.refs_2_), channel_id=1, source_target_pairs={{0,2},{1,3},{2,6},{3,7},{6,10},{7,11},{10,14},{11,15},{14,12},{15,... | collective-permute-start | bytes 1056776 | tf_op jit(solution)/shard_map/ppermute | solution.py:203
  58.6 12.3 %collective-permute-start.22 = (bf16[688,256]{1,0:T(8,128)(2,1)S(1)}, bf16[688,256]{1,0:T(8,128)(2,1)S(1)}, u32[]{:S(2)}, u32[]{:S(2)}) collective-permute-start(bf16[688,256]{1,0:T(8,128)(2,1)S(1)} %collective-permute-done.19.refs_0_), channel_id=1, source_target_pairs={{0,2},{1,3},{2,6},{3,7},{6,10},{7,11},{10,14},{11,15},{14,12},{15,... | collective-permute-start | bytes 1056776 | tf_op jit(solution)/shard_map/ppermute | solution.py:203
  59.7 13.4 %collective-permute-start.25 = (bf16[688,256]{1,0:T(8,128)(2,1)S(1)}, bf16[688,256]{1,0:T(8,128)(2,1)S(1)}, u32[]{:S(2)}, u32[]{:S(2)}) collective-permute-start(bf16[688,256]{1,0:T(8,128)(2,1)S(1)} %collective-permute-done.23.refs_1_), channel_id=1, source_target_pairs={{0,4},{1,5},{2,0},{3,1},{6,2},{7,3},{10,6},{11,7},{14,10},{15,11},... | collective-permute-start | bytes 1056776 | tf_op jit(solution)/shard_map/ppermute | solution.py:203
  65.6 15.1 %collective-permute-start.14 = (bf16[688,256]{1,0:T(8,128)(2,1)S(1)}, bf16[688,256]{1,0:T(8,128)(2,1)S(1)}, u32[]{:S(2)}, u32[]{:S(2)}) collective-permute-start(bf16[688,256]{1,0:T(8,128)(2,1)S(1)} %collective-permute-done.13.refs_3_), channel_id=1, source_target_pairs={{0,4},{1,5},{2,0},{3,1},{6,2},{7,3},{10,6},{11,7},{14,10},{15,11},... | collective-permute-start | bytes 1056776 | tf_op jit(solution)/shard_map/ppermute | solution.py:203
  65.8 15.1 %collective-permute-start.7 = (bf16[688,256]{1,0:T(8,128)(2,1)S(1)}, bf16[688,256]{1,0:T(8,128)(2,1)S(1)}, u32[]{:S(2)}, u32[]{:S(2)}) collective-permute-start(bf16[688,256]{1,0:T(8,128)(2,1)S(1)} %collective-permute-done.6.refs_2_), channel_id=1, source_target_pairs={{0,2},{1,3},{2,6},{3,7},{6,10},{7,11},{10,14},{11,15},{14,12},{15,... | collective-permute-start | bytes 1056776 | tf_op jit(solution)/shard_map/ppermute | solution.py:203
  70.9 15.1 %collective-permute-start.24 = (bf16[688,256]{1,0:T(8,128)(2,1)S(1)}, bf16[688,256]{1,0:T(8,128)(2,1)S(1)}, u32[]{:S(2)}, u32[]{:S(2)}) collective-permute-start(bf16[688,256]{1,0:T(8,128)(2,1)S(1)} %collective-permute-done.22.refs_0_), channel_id=1, source_target_pairs={{0,2},{1,3},{2,6},{3,7},{6,10},{7,11},{10,14},{11,15},{14,12},{15,... | collective-permute-start | bytes 1056776 | tf_op jit(solution)/shard_map/ppermute | solution.py:203
  73.1 15.1 %collective-permute-start.27 = (bf16[688,256]{1,0:T(8,128)(2,1)S(1)}, bf16[688,256]{1,0:T(8,128)(2,1)S(1)}, u32[]{:S(2)}, u32[]{:S(2)}) collective-permute-start(bf16[688,256]{1,0:T(8,128)(2,1)S(1)} %collective-permute-done.25.refs_1_), channel_id=1, source_target_pairs={{0,4},{1,5},{2,0},{3,1},{6,2},{7,3},{10,6},{11,7},{14,10},{15,11},... | collective-permute-start | bytes 1056776 | tf_op jit(solution)/shard_map/ppermute | solution.py:203
  80.7 15.1 %collective-permute-start.15 = (bf16[688,256]{1,0:T(8,128)(2,1)S(1)}, bf16[688,256]{1,0:T(8,128)(2,1)S(1)}, u32[]{:S(2)}, u32[]{:S(2)}) collective-permute-start(bf16[688,256]{1,0:T(8,128)(2,1)S(1)} %collective-permute-done.14.refs_3_), channel_id=1, source_target_pairs={{0,4},{1,5},{2,0},{3,1},{6,2},{7,3},{10,6},{11,7},{14,10},{15,11},... | collective-permute-start | bytes 1056776 | tf_op jit(solution)/shard_map/ppermute | solution.py:203
  80.9 14.9 %collective-permute-start.8 = (bf16[688,256]{1,0:T(8,128)(2,1)S(1)}, bf16[688,256]{1,0:T(8,128)(2,1)S(1)}, u32[]{:S(2)}, u32[]{:S(2)}) collective-permute-start(bf16[688,256]{1,0:T(8,128)(2,1)S(1)} %collective-permute-done.7.refs_2_), channel_id=1, source_target_pairs={{0,2},{1,3},{2,6},{3,7},{6,10},{7,11},{10,14},{11,15},{14,12},{15,... | collective-permute-start | bytes 1056776 | tf_op jit(solution)/shard_map/ppermute | solution.py:203
  88.2 15.1 %collective-permute-start.28 = (bf16[688,256]{1,0:T(8,128)(2,1)S(1)}, bf16[688,256]{1,0:T(8,128)(2,1)S(1)}, u32[]{:S(2)}, u32[]{:S(2)}) collective-permute-start(bf16[688,256]{1,0:T(8,128)(2,1)S(1)} %collective-permute-done.27.refs_1_), channel_id=1, source_target_pairs={{0,4},{1,5},{2,0},{3,1},{6,2},{7,3},{10,6},{11,7},{14,10},{15,11},... | collective-permute-start | bytes 1056776 | tf_op jit(solution)/shard_map/ppermute | solution.py:203
  88.4 14.9 %collective-permute-start.26 = (bf16[688,256]{1,0:T(8,128)(2,1)S(1)}, bf16[688,256]{1,0:T(8,128)(2,1)S(1)}, u32[]{:S(2)}, u32[]{:S(2)}) collective-permute-start(bf16[688,256]{1,0:T(8,128)(2,1)S(1)} %collective-permute-done.24.refs_0_), channel_id=1, source_target_pairs={{0,2},{1,3},{2,6},{3,7},{6,10},{7,11},{10,14},{11,15},{14,12},{15,... | collective-permute-start | bytes 1056776 | tf_op jit(solution)/shard_map/ppermute | solution.py:203
  105.6 7.1 %collective-permute-start.29 = (f32[2,384,256]{2,1,0:T(8,128)S(1)}, f32[2,384,256]{2,1,0:T(8,128)S(1)}, u32[]{:S(2)}, u32[]{:S(2)}) collective-permute-start(f32[2,384,256]{2,1,0:T(8,128)S(1)} %shard_map.58), channel_id=1, source_target_pairs={{0,1},{1,0},{2,3},{3,2},{4,5},{5,4},{6,7},{7,6},{8,9},{9,8},{10,11... | collective-permute-start | bytes 2359304 | tf_op jit(solution)/shard_map/ppermute | solution.py:212
  109.8 9.8 %collective-permute-start.16 = (bf16[688,256]{1,0:T(8,128)(2,1)S(1)}, bf16[688,256]{1,0:T(8,128)(2,1)S(1)}, u32[]{:S(2)}, u32[]{:S(2)}) collective-permute-start(bf16[688,256]{1,0:T(8,128)(2,1)S(1)} %collective-permute-done.15.refs_3_), channel_id=1, source_target_pairs={{0,4},{1,5},{2,0},{3,1},{6,2},{7,3},{10,6},{11,7},{14,10},{15,11},... | collective-permute-start | bytes 1056776 | tf_op jit(solution)/shard_map/ppermute | solution.py:203
  110.0 9.6 %collective-permute-start.9 = (bf16[688,256]{1,0:T(8,128)(2,1)S(1)}, bf16[688,256]{1,0:T(8,128)(2,1)S(1)}, u32[]{:S(2)}, u32[]{:S(2)}) collective-permute-start(bf16[688,256]{1,0:T(8,128)(2,1)S(1)} %collective-permute-done.8.refs_2_), channel_id=1, source_target_pairs={{0,2},{1,3},{2,6},{3,7},{6,10},{7,11},{10,14},{11,15},{14,12},{15,... | collective-permute-start | bytes 1056776 | tf_op jit(solution)/shard_map/ppermute | solution.py:203
  111.3 8.3 %slice-start = ((s8[8454144]{0:T(1024)(128)(4,1)}), s8[4194304]{0:T(1024)(128)(4,1)S(1)}, s32[]{:S(2)}) async-start(s8[8454144]{0:T(1024)(128)(4,1)} %bitcast.16), calls=%async_computation.2 | async-start | bytes 8388608
  111.3 8.3 %slice-start.1 = ((s8[8454144]{0:T(1024)(128)(4,1)}), s8[4194304]{0:T(1024)(128)(4,1)S(1)}, s32[]{:S(2)}) async-start(s8[8454144]{0:T(1024)(128)(4,1)} %bitcast.16), calls=%async_computation.3 | async-start | bytes 8388608
  111.3 8.3 %slice-start.2 = ((s8[8454144]{0:T(1024)(128)(4,1)}), s8[65536]{0:T(1024)(128)(4,1)S(1)}, s32[]{:S(2)}) async-start(s8[8454144]{0:T(1024)(128)(4,1)} %bitcast.16), calls=%async_computation.4 | async-start | bytes 131072
  122.0 3.0 %collective-permute-start.30 = (f32[2,384,256]{2,1,0:T(8,128)S(1)}, f32[2,384,256]{2,1,0:T(8,128)S(1)}, u32[]{:S(2)}, u32[]{:S(2)}) collective-permute-start(f32[2,384,256]{2,1,0:T(8,128)S(1)} %shard_map.61), channel_id=1, source_target_pairs={{0,1},{1,0},{2,3},{3,2},{4,5},{5,4},{6,7},{7,6},{8,9},{9,8},{10,11... | collective-permute-start | bytes 2359304 | tf_op jit(solution)/shard_map/ppermute | solution.py:212
  126.7 42.3 %all-to-all-start.1 = ((bf16[16,6,16,512]{3,2,1,0:T(8,128)(2,1)}), bf16[16,6,16,512]{3,2,1,0:T(8,128)(2,1)S(1)}, u32[]{:S(2)}, u32[]{:S(2)}) async-start(bf16[16,6,16,512]{3,2,1,0:T(8,128)(2,1)} %shard_map.62), calls=%async_computation.1 | async-start | bytes 3145728 | tf_op jit(solution)/shard_map/all_to_all | solution.py:238

commit v7 on v5

--- a/solution.py
+++ b/solution.py
@@ -10,7 +10,7 @@
 
 GRID_CHIPS = 8
 HALVES = 2
-BEHIND = (0, 0, 1, 2, 4, 5, 6)
+BEHIND = ((0, 0), (0, 0), (0, 1), (1, 2), (2, 4), (4, 5), (5, 6))
 WAYS = (1, -1)
 LANES = 128
 WINDOW = 896
@@ -58,10 +58,9 @@
 def step_kernel(t, parts, own_hbm, other_hbm, *refs):
     norb = len(WAYS)
     pieces = refs[: norb * parts]
-    scratch = refs[-3:]
+    c_buf, g_buf, sems = refs[-3:]
     sums = refs[-3 - 2 * parts : -3]
     before = refs[norb * parts : -3 - 2 * parts]
-    c_buf, g_buf, sems = scratch
     rows, nvirt = own_hbm.shape
     depth, width = pieces[0].shape
     me = lax.axis_index("wide")
@@ -103,7 +102,49 @@
                 sums[at][i] = before[at][i] + part if before else part
 
 
-def add_products(t, own, other, pieces, before):
+def last_kernel(t, c_ref, *refs):
+    norb = len(WAYS)
+    pieces, before, sums, g_buf = refs[:norb], refs[norb : norb + 2], refs[-3:-1], refs[-1]
+    rows = before[0].shape[1]
+    depth = pieces[0].shape[0]
+    nvirt = depth * 2 * GRID_CHIPS
+    me = lax.axis_index("wide")
+    for i in range(norb):
+        chip = ring_chip(ring_place(lax.div(me, 2)) - t * WAYS[i] + GRID_CHIPS)
+        start = (2 * chip + lax.rem(me, 2)) * depth
+        shift = pl.multiple_of(start - window_at(start, nvirt), 16)
+        g_buf[i] = jnp.zeros_like(g_buf[i])
+        g_buf[i, pl.ds(shift, depth), :] = pieces[i][...]
+    for i in range(norb):
+        for k in range(2):
+            term = jnp.dot(
+                c_ref[i, pl.ds(k * rows, rows)], g_buf[i], preferred_element_type=jnp.float32
+            )
+            sums[k][i] = before[k][i] + term
+
+
+def add_last_products(t, windows, pieces, before):
+    norb = len(WAYS)
+    depth, width = pieces[0].shape
+    vmem = pl.BlockSpec(memory_space=pltpu.VMEM)
+    sums = jax.ShapeDtypeStruct(before[0].shape, jnp.float32)
+    return pl.pallas_call(
+        functools.partial(last_kernel, t),
+        out_shape=[sums] * 2,
+        in_specs=[vmem] * (1 + norb + 2),
+        out_specs=[vmem] * 2,
+        input_output_aliases={1 + norb + k: k for k in range(2)},
+        scratch_shapes=[pltpu.VMEM((norb, WINDOW, width), jnp.bfloat16)],
+        compiler_params=pltpu.CompilerParams(vmem_limit_bytes=20 << 20),
+        cost_estimate=pl.CostEstimate(
+            flops=2 * windows.size * width,
+            bytes_accessed=2 * windows.size,
+            transcendentals=0,
+        ),
+    )(windows, *pieces, *before)
+
+
+def add_products(t, own, other, pieces, before, keep=False):
     rows, nvirt = own.shape
     parts, norb = len(pieces), len(WAYS)
     depth, width = pieces[0][0].shape
@@ -112,14 +153,16 @@
     hbm = pl.BlockSpec(memory_space=pltpu.HBM)
     flat = [piece for part in pieces for piece in part]
     old = [value for pair in before for value in pair]
+    windows = (norb, 2 * rows, WINDOW)
+    kept = [jax.ShapeDtypeStruct(windows, own.dtype)] * keep
     new = pl.pallas_call(
         functools.partial(step_kernel, t, parts),
-        out_shape=[sums] * (2 * parts),
+        out_shape=[sums] * (2 * parts) + kept,
         in_specs=[hbm, hbm] + [vmem] * (len(flat) + len(old)),
-        out_specs=[vmem] * (2 * parts),
+        out_specs=[vmem] * (2 * parts + keep),
         input_output_aliases={2 + len(flat) + k: k for k in range(len(old))},
-        scratch_shapes=[
-            pltpu.VMEM((norb, 2 * rows, WINDOW), jnp.bfloat16),
+        scratch_shapes=[pltpu.VMEM(windows, own.dtype)] * (not keep)
+        + [
             pltpu.VMEM((norb, WINDOW, parts * width), jnp.bfloat16),
             pltpu.SemaphoreType.DMA((norb, 2)),
         ],
@@ -130,7 +173,8 @@
             transcendentals=0,
         ),
     )(own, other, *flat, *old)
-    return [(new[2 * j], new[2 * j + 1]) for j in range(parts)]
+    pairs = [(new[2 * j], new[2 * j + 1]) for j in range(parts)]
+    return (pairs, new[-1]) if keep else pairs
 
 
 def finish_kernel(place_ref, *refs):
@@ -187,24 +231,23 @@
         if t + 1 == GRID_CHIPS:
             break
         for j in range(HALVES):
-            if j == HALVES - 1:
-                while done < BEHIND[t]:
-                    sums = add_products(done, coefficients, other, arrived[done], sums)
-                    done += 1
+            while done < BEHIND[t][j]:
+                sums = add_products(done, coefficients, other, arrived[done], sums)
+                done += 1
             for i in range(norb):
                 sent = piece[j][i]
                 if t == 2 and i == j == 0:
                     sent, early = lax.optimization_barrier((sent, early))
-                if j == HALVES - 1 and BEHIND[t]:
+                if BEHIND[t][j]:
                     sent, sums = lax.optimization_barrier((sent, sums))
                 piece[j][i] = lax.ppermute(sent, "wide", shift[i])
     while done < GRID_CHIPS - 1:
         sums = add_products(done, coefficients, other, arrived[done], sums)
         done += 1
-    sums = [
-        add_products(done, coefficients, other, [arrived[done][j]], [sums[j]])[0]
-        for j in range(HALVES)
-    ]
+    sums[:1], windows = add_products(
+        done, coefficients, other, arrived[done][:1], sums[:1], keep=True
+    )
+    sums[1] = add_last_products(done, windows, arrived[done][1], sums[1])
     mine = [sums[j][0] for j in range(HALVES)]
     theirs = [lax.ppermute(sums[j][1], "wide", swap) for j in range(HALVES)]
     return mine, theirs, early

time: 165 us -> 162 us (0.982)
    ppermute x28, waiting for transfers between devices: 47.8 us -> 44 us  [ring_products(): piece[j][i] = lax.ppermute(sent, 'wide', shift[i])]
    all_to_all x1, waiting for transfers between devices: 0.01 us -> 3.09 us  [local(): lax.all_to_all(labels, 'wide', split_axis=0, concat_axis=0, tiled=True)]
    ppermute x2, starting transfers between devices: 6 us -> 3.5 us  [ring_products(): theirs = [lax.ppermute(sums[j][1], 'wide', swap) for j in range(HALVES)]]
    pallas_call x9 -> x8, Pallas kernels: 28.3 us -> 25.9 us  [add_products(): pl.pallas_call(functools.partial(step_kernel, t, parts), out_shape=[sums]...]
  transfers between devices with their start and end apart: 33 -> 33, of which waited for: 15 -> 17; matrix products, arithmetic and copies ran while one was open for 2% -> 2% of each run, Pallas kernels for 17% -> 17%
where the time goes in v7:
time: 162 us
  waiting for transfers between devices  85.1 us (53%)
  starting transfers between devices  38.6 us (24%)
  Pallas kernels  29.2 us (18%)
  local copies, waits for them, and re-layouts  7.52 us (5%)
    ppermute x28, waiting for transfers between devices, ring_products(): piece[j][i] = lax.ppermute(sent, 'wide', shift[i])  44 us
    all_to_all x1, waiting for transfers between devices, local(): lax.all_to_all(out, 'wide', split_axis=0, concat_axis=0, tiled=True)  36.2 us
    pallas_call x8, Pallas kernels, add_products(): pl.pallas_call(functools.partial(step_kernel, t, parts), out_shape=[sums]...  25.9 us
    ppermute x28, starting transfers between devices, ring_products(): piece[j][i] = lax.ppermute(sent, 'wide', shift[i])  20.7 us
    all_to_all x1, starting transfers between devices, local(): lax.all_to_all(labels, 'wide', split_axis=0, concat_axis=0, tiled=True)  7.02 us
    all_to_all x1, starting transfers between devices, local(): lax.all_to_all(out, 'wide', split_axis=0, concat_axis=0, tiled=True)  6.59 us
    unnamed x6, local copies, waits for them, and re-layouts  5.15 us
    ppermute x2, starting transfers between devices, ring_products(): theirs = [lax.ppermute(sums[j][1], 'wide', swap) for j in range(HALVES)]  3.5 us
  transfers between devices with their start and end apart: 33, of which 17 were waited for; matrix products, arithmetic and copies ran while one was open for 2% of the time, Pallas kernels for 17%

profile of v7, /device:TPU:13, one launch (start us, length us, event | category | flops | bytes accessed | tf_op | source)
XLA Modules:
  0.0 161.7 jit_solution(14994977229485490721)
XLA Ops:
  0.6 0.7 collective-permute-start.2
  1.4 1.4 slice_bitcast_fusion
  2.8 0.2 collective-permute-start.11
  3.1 1.4 collective-permute-start
  4.5 1.3 collective-permute-start.6
  6.1 0.7 sub.17
  6.8 7.0 %all-to-all-start = ((s32[16,1,16]{2,1,0:T(1,128)}), s32[16,1,16]{2,1,0:T(1,128)S(1)}, u32[]{:S(2)}, u32[]{:S(2)}) async-start(s32[16,1,16]{2,1,0:T(1,128)} %sub.17), calls=%async_computation | async-start | bytes 16384 | tf_op jit(solution)/shard_map/all_to_all | solution.py:265
  13.9 0.2 mul.58
  14.1 0.3 collective-permute-start.12
  14.4 1.2 collective-permute-start.1
  15.6 4.6 %collective-permute-done.4.refs_3_ = bf16[688,256]{1,0:T(8,128)(2,1)S(1)} collective-permute-done((bf16[688,256]{1,0:T(8,128)(2,1)S(1)}, bf16[688,256]{1,0:T(8,128)(2,1)S(1)}, u32[]{:S(2)}, u32[]{:S(2)}) %collective-permute-start.4) | collective-permute-done | bytes 352288 | tf_op jit(solution)/shard_map/ppermute | solution.py:243
  20.2 0.2 collective-permute-start.5
  20.4 1.3 collective-permute-start.7
  21.9 3.1 %all-to-all-done = s32[16,1,16]{2,1,0:T(1,128)S(1)} async-done(((s32[16,1,16]{2,1,0:T(1,128)}), s32[16,1,16]{2,1,0:T(1,128)S(1)}, u32[]{:S(2)}, u32[]{:S(2)}) %all-to-all-start) | async-done | bytes 1056 | tf_op jit(solution)/shard_map/all_to_all | solution.py:265
  25.0 3.0 %collective-permute-done.1.refs_0_ = bf16[688,256]{1,0:T(8,128)(2,1)} collective-permute-done((bf16[688,256]{1,0:T(8,128)(2,1)S(1)}, bf16[688,256]{1,0:T(8,128)(2,1)}, u32[]{:S(2)}, u32[]{:S(2)}) %collective-permute-start.1) | collective-permute-done | bytes 352288 | tf_op jit(solution)/shard_map/ppermute | solution.py:243
  27.9 1.2 collective-permute-start.3
  29.1 0.3 collective-permute-start.13
  29.4 3.4 %copy-done = bf16[384,11008]{1,0:T(8,128)(2,1)S(1)} copy-done((bf16[384,11008]{1,0:T(8,128)(2,1)S(1)}, bf16[384,11008]{1,0:T(8,128)(2,1)}, u32[]{:S(2)}) %copy-start) | copy-done | bytes 8454168
  32.8 3.1 %shard_map.50 = (f32[2,384,256]{2,1,0:T(8,128)S(1)}, f32[2,384,256]{2,1,0:T(8,128)S(1)}, f32[2,384,256]{2,1,0:T(8,128)S(1)}, f32[2,384,256]{2,1,0:T(8,128)S(1)}) custom-call(bf16[384,11008]{1,0:T(8,128)(2,1)S(1)} %copy-done, bf16[384,11008]{1,0:T(8,128)(2,1)} %collective-permute-done.2.other_hbm, bf16[688,256]{1,0:T(8,128)(2,1)S(1)} %get-tuple-element.258.refs_0_, ...), custom_call_target="tpu_custom_call" | custom-call | flops 1409286144 | bytes 2752512 | tf_op jit(solution)/shard_map/pallas_call | solution.py:158
  36.0 1.2 collective-permute-start.10
  37.2 0.3 collective-permute-start.9
  37.5 5.4 %collective-permute-done.3.refs_0_ = bf16[688,256]{1,0:T(8,128)(2,1)S(1)} collective-permute-done((bf16[688,256]{1,0:T(8,128)(2,1)}, bf16[688,256]{1,0:T(8,128)(2,1)S(1)}, u32[]{:S(2)}, u32[]{:S(2)}) %collective-permute-start.3) | collective-permute-done | bytes 352288 | tf_op jit(solution)/shard_map/ppermute | solution.py:243
  42.9 1.2 collective-permute-start.8
  44.1 0.3 collective-permute-start.17
  44.4 3.2 %shard_map.51 = (f32[2,384,256]{2,1,0:T(8,128)S(1)}, f32[2,384,256]{2,1,0:T(8,128)S(1)}, f32[2,384,256]{2,1,0:T(8,128)S(1)}, f32[2,384,256]{2,1,0:T(8,128)S(1)}) custom-call(bf16[384,11008]{1,0:T(8,128)(2,1)S(1)} %copy-done, ...), custom_call_target="tpu_custom_call", output_to_operand_aliasing={{0}: (6, {}), {1}: (7, {}), {2}: (8, {}), {3}: (9, {})} | custom-call | flops 1409286144 | bytes 2752512 | tf_op jit(solution)/shard_map/pallas_call | solution.py:158
  47.6 2.9 %collective-permute-done.10.refs_2_ = bf16[688,256]{1,0:T(8,128)(2,1)S(1)} collective-permute-done((bf16[688,256]{1,0:T(8,128)(2,1)}, bf16[688,256]{1,0:T(8,128)(2,1)S(1)}, u32[]{:S(2)}, u32[]{:S(2)}) %collective-permute-start.10) | collective-permute-done | bytes 352288 | tf_op jit(solution)/shard_map/ppermute | solution.py:243
  50.5 1.2 collective-permute-start.16
  51.6 0.3 collective-permute-start.15
  51.9 6.1 %collective-permute-done.8.refs_0_ = bf16[688,256]{1,0:T(8,128)(2,1)S(1)} collective-permute-done((bf16[688,256]{1,0:T(8,128)(2,1)S(1)}, bf16[688,256]{1,0:T(8,128)(2,1)S(1)}, u32[]{:S(2)}, u32[]{:S(2)}) %collective-permute-start.8) | collective-permute-done | bytes 352288 | tf_op jit(solution)/shard_map/ppermute | solution.py:243
  58.1 1.0 collective-permute-start.21
  59.1 0.5 collective-permute-start.14
  59.6 4.5 %shard_map.52 = (f32[2,384,256]{2,1,0:T(8,128)S(1)}, f32[2,384,256]{2,1,0:T(8,128)S(1)}, f32[2,384,256]{2,1,0:T(8,128)S(1)}, f32[2,384,256]{2,1,0:T(8,128)S(1)}) custom-call(bf16[384,11008]{1,0:T(8,128)(2,1)S(1)} %copy-done, ...), custom_call_target="tpu_custom_call", output_to_operand_aliasing={{0}: (6, {}), {1}: (7, {}), {2}: (8, {}), {3}: (9, {})} | custom-call | flops 1409286144 | bytes 2752512 | tf_op jit(solution)/shard_map/pallas_call | solution.py:158
  64.1 3.2 %shard_map.53 = (f32[2,384,256]{2,1,0:T(8,128)S(1)}, f32[2,384,256]{2,1,0:T(8,128)S(1)}, f32[2,384,256]{2,1,0:T(8,128)S(1)}, f32[2,384,256]{2,1,0:T(8,128)S(1)}) custom-call(bf16[384,11008]{1,0:T(8,128)(2,1)S(1)} %copy-done, ...), custom_call_target="tpu_custom_call", output_to_operand_aliasing={{0}: (6, {}), {1}: (7, {}), {2}: (8, {}), {3}: (9, {})} | custom-call | flops 1409286144 | bytes 2752512 | tf_op jit(solution)/shard_map/pallas_call | solution.py:158
  67.4 1.3 collective-permute-start.20
  68.7 0.2 collective-permute-start.19
  68.9 4.2 %collective-permute-done.14.refs_0_ = bf16[688,256]{1,0:T(8,128)(2,1)S(1)} collective-permute-done((bf16[688,256]{1,0:T(8,128)(2,1)S(1)}, bf16[688,256]{1,0:T(8,128)(2,1)S(1)}, u32[]{:S(2)}, u32[]{:S(2)}) %collective-permute-start.14) | collective-permute-done | bytes 352288 | tf_op jit(solution)/shard_map/ppermute | solution.py:243
  73.1 1.2 collective-permute-start.18
  74.3 0.3 collective-permute-start.23
  74.6 3.2 %shard_map.54 = (f32[2,384,256]{2,1,0:T(8,128)S(1)}, f32[2,384,256]{2,1,0:T(8,128)S(1)}, f32[2,384,256]{2,1,0:T(8,128)S(1)}, f32[2,384,256]{2,1,0:T(8,128)S(1)}) custom-call(bf16[384,11008]{1,0:T(8,128)(2,1)S(1)} %copy-done, ...), custom_call_target="tpu_custom_call", output_to_operand_aliasing={{0}: (6, {}), {1}: (7, {}), {2}: (8, {}), {3}: (9, {})} | custom-call | flops 1409286144 | bytes 2752512 | tf_op jit(solution)/shard_map/pallas_call | solution.py:158
  77.8 2.9 %collective-permute-done.20.refs_2_ = bf16[688,256]{1,0:T(8,128)(2,1)S(1)} collective-permute-done((bf16[688,256]{1,0:T(8,128)(2,1)S(1)}, bf16[688,256]{1,0:T(8,128)(2,1)S(1)}, u32[]{:S(2)}, u32[]{:S(2)}) %collective-permute-start.20) | collective-permute-done | bytes 352288 | tf_op jit(solution)/shard_map/ppermute | solution.py:243
  80.7 1.2 collective-permute-start.25
  81.8 0.3 collective-permute-start.26
  82.1 6.1 %collective-permute-done.18.refs_0_ = bf16[688,256]{1,0:T(8,128)(2,1)S(1)} collective-permute-done((bf16[688,256]{1,0:T(8,128)(2,1)S(1)}, bf16[688,256]{1,0:T(8,128)(2,1)S(1)}, u32[]{:S(2)}, u32[]{:S(2)}) %collective-permute-start.18) | collective-permute-done | bytes 352288 | tf_op jit(solution)/shard_map/ppermute | solution.py:243
  88.2 1.1 collective-permute-start.24
  89.3 0.4 collective-permute-start.22
  89.7 3.2 %shard_map.55 = (f32[2,384,256]{2,1,0:T(8,128)S(1)}, f32[2,384,256]{2,1,0:T(8,128)S(1)}, f32[2,384,256]{2,1,0:T(8,128)S(1)}, f32[2,384,256]{2,1,0:T(8,128)S(1)}) custom-call(bf16[384,11008]{1,0:T(8,128)(2,1)S(1)} %copy-done, ...), custom_call_target="tpu_custom_call", output_to_operand_aliasing={{0}: (6, {}), {1}: (7, {}), {2}: (8, {}), {3}: (9, {})} | custom-call | flops 1409286144 | bytes 2752512 | tf_op jit(solution)/shard_map/pallas_call | solution.py:158
  92.9 2.9 %collective-permute-done.25.refs_2_ = bf16[688,256]{1,0:T(8,128)(2,1)S(1)} collective-permute-done((bf16[688,256]{1,0:T(8,128)(2,1)S(1)}, bf16[688,256]{1,0:T(8,128)(2,1)S(1)}, u32[]{:S(2)}, u32[]{:S(2)}) %collective-permute-start.25) | collective-permute-done | bytes 352288 | tf_op jit(solution)/shard_map/ppermute | solution.py:243
  95.8 1.1 collective-permute-start.28
  96.9 0.4 collective-permute-start.27
  97.2 3.2 %shard_map.56 = (f32[2,384,256]{2,1,0:T(8,128)S(1)}, f32[2,384,256]{2,1,0:T(8,128)S(1)}, f32[2,384,256]{2,1,0:T(8,128)S(1)}, f32[2,384,256]{2,1,0:T(8,128)S(1)}) custom-call(bf16[384,11008]{1,0:T(8,128)(2,1)S(1)} %copy-done, ...), custom_call_target="tpu_custom_call", output_to_operand_aliasing={{0}: (6, {}), {1}: (7, {}), {2}: (8, {}), {3}: (9, {})} | custom-call | flops 1409286144 | bytes 2752512 | tf_op jit(solution)/shard_map/pallas_call | solution.py:158
  100.4 2.1 %collective-permute-done.24.refs_1_ = bf16[688,256]{1,0:T(8,128)(2,1)S(1)} collective-permute-done((bf16[688,256]{1,0:T(8,128)(2,1)S(1)}, bf16[688,256]{1,0:T(8,128)(2,1)S(1)}, u32[]{:S(2)}, u32[]{:S(2)}) %collective-permute-start.24) | collective-permute-done | bytes 352288 | tf_op jit(solution)/shard_map/ppermute | solution.py:243
  102.5 0.8 collective-permute-done.22.refs_0_
  103.3 2.4 %shard_map.57 = (f32[2,384,256]{2,1,0:T(8,128)S(1)}, f32[2,384,256]{2,1,0:T(8,128)S(1)}, bf16[2,768,896]{2,1,0:T(8,128)(2,1)S(1)}) custom-call(bf16[384,11008]{1,0:T(8,128)(2,1)S(1)} %copy-done, bf16[384,11008]{1,0:T(8,128)(2,1)} %collective-permute-done.2.other_hbm, ...), custom_call_target="tpu_custom_call", output_to_operand_aliasing={{0}: (4, {}), {1}: (5, {})} | custom-call | flops 704643072 | bytes 2752512 | tf_op jit(solution)/shard_map/pallas_call | solution.py:158
  105.7 2.3 %collective-permute-start.29 = (f32[2,384,256]{2,1,0:T(8,128)S(1)}, f32[2,384,256]{2,1,0:T(8,128)S(1)}, u32[]{:S(2)}, u32[]{:S(2)}) collective-permute-start(f32[2,384,256]{2,1,0:T(8,128)S(1)} %get-tuple-element.251), channel_id=1, source_target_pairs={{0,1},{1,0},{2,3},{3,2},{4,5},{5,4},{6,7},{7,6},{8,9},{9,8},{10,11... | collective-permute-start | bytes 2359304 | tf_op jit(solution)/shard_map/ppermute | solution.py:252
  108.0 2.1 %collective-permute-done.28.refs_1_ = bf16[688,256]{1,0:T(8,128)(2,1)S(1)} collective-permute-done((bf16[688,256]{1,0:T(8,128)(2,1)S(1)}, bf16[688,256]{1,0:T(8,128)(2,1)S(1)}, u32[]{:S(2)}, u32[]{:S(2)}) %collective-permute-start.28) | collective-permute-done | bytes 352288 | tf_op jit(solution)/shard_map/ppermute | solution.py:243
  110.1 0.8 collective-permute-done.27.refs_0_
  110.9 1.1 shard_map.58
  112.0 1.2 collective-permute-start.30
  113.2 1.9 %collective-permute-done.30.refs_3_ = f32[2,384,256]{2,1,0:T(8,128)S(1)} collective-permute-done((f32[2,384,256]{2,1,0:T(8,128)S(1)}, f32[2,384,256]{2,1,0:T(8,128)S(1)}, u32[]{:S(2)}, u32[]{:S(2)}) %collective-permute-start.30) | collective-permute-done | bytes 786464 | tf_op jit(solution)/shard_map/ppermute | solution.py:252
  115.1 2.1 %shard_map.59 = bf16[16,6,16,512]{3,2,1,0:T(8,128)(2,1)} custom-call(bf16[768,384]{1,0:T(8,128)(2,1)S(1)} %compare_convert_fusion.place_ref, f32[2,384,256]{2,1,0:T(8,128)S(1)} %get-tuple-element.244.refs_0_, f32[2,384,256]{2,1,0:T(8,128)S(1)} %get-tuple-element.250.refs_1_, f32[2,384,256]{2,1,0:T(8,128)S(1)} %collective-permute-done.29.refs_2_, ...), custom_call_target="tpu_custom_call" | custom-call | flops 603979776 | bytes 1572864 | tf_op jit(solution)/shard_map/pallas_call | solution.py:196
  117.2 6.6 %all-to-all-start.1 = ((bf16[16,6,16,512]{3,2,1,0:T(8,128)(2,1)}), bf16[16,6,16,512]{3,2,1,0:T(8,128)(2,1)S(1)}, u32[]{:S(2)}, u32[]{:S(2)}) async-start(bf16[16,6,16,512]{3,2,1,0:T(8,128)(2,1)} %shard_map.59), calls=%async_computation.1 | async-start | bytes 3145728 | tf_op jit(solution)/shard_map/all_to_all | solution.py:277
  123.8 36.2 %all-to-all-done.1 = bf16[16,6,16,512]{3,2,1,0:T(8,128)(2,1)S(1)} async-done(((bf16[16,6,16,512]{3,2,1,0:T(8,128)(2,1)}), bf16[16,6,16,512]{3,2,1,0:T(8,128)(2,1)S(1)}, u32[]{:S(2)}, u32[]{:S(2)}) %all-to-all-start.1) | async-done | bytes 1572896 | tf_op jit(solution)/shard_map/all_to_all | solution.py:277
  160.0 1.1 copy.63
  161.1 0.6 copy.64
  (29 shorter events, 0.8 us)
Async XLA Ops:
  0.6 5.1 %copy-start.1 = (s32[128,1]{0,1:T(1,128)S(1)}, s32[128,1]{0,1:T(1,128)}, u32[]{:S(2)}) copy-start(s32[128,1]{0,1:T(1,128)} %param.5) | copy-start | bytes 1540
  0.6 28.8 %collective-permute-start.2 = (bf16[384,11008]{1,0:T(8,128)(2,1)}, bf16[384,11008]{1,0:T(8,128)(2,1)}, u32[]{:S(2)}, u32[]{:S(2)}) collective-permute-start(bf16[384,11008]{1,0:T(8,128)(2,1)} %own_hbm.15), channel_id=1, source_target_pairs={{0,1},{1,0},{2,3},{3,2},{4,5},{5,4},{6,7},{7,6},{8,9},{9,8},{10,11... | collective-permute-start | bytes 25362440 | tf_op jit(solution)/shard_map/ppermute | solution.py:215
  2.8 11.3 %collective-permute-start.11 = (bf16[688,256]{1,0:T(8,128)(2,1)S(1)}, bf16[688,256]{1,0:T(8,128)(2,1)S(1)}, u32[]{:S(2)}, u32[]{:S(2)}) collective-permute-start(bf16[688,256]{1,0:T(8,128)(2,1)S(1)} %get-tuple-element.256.refs_1_), channel_id=1, source_target_pairs={{0,4},{1,5},{2,0},{3,1},{6,2},{7,3},{10,6},{11,7},{14,10},{15,11},... | collective-permute-start | bytes 1056776 | tf_op jit(solution)/shard_map/ppermute | solution.py:243
  3.0 17.2 %collective-permute-start.4 = (bf16[688,256]{1,0:T(8,128)(2,1)S(1)}, bf16[688,256]{1,0:T(8,128)(2,1)S(1)}, u32[]{:S(2)}, u32[]{:S(2)}) collective-permute-start(bf16[688,256]{1,0:T(8,128)(2,1)S(1)} %get-tuple-element.257.refs_3_), channel_id=1, source_target_pairs={{0,4},{1,5},{2,0},{3,1},{6,2},{7,3},{10,6},{11,7},{14,10},{15,11},... | collective-permute-start | bytes 1056776 | tf_op jit(solution)/shard_map/ppermute | solution.py:243
  3.1 11.4 %collective-permute-start = (bf16[688,256]{1,0:T(8,128)(2,1)S(1)}, bf16[688,256]{1,0:T(8,128)(2,1)S(1)}, u32[]{:S(2)}, u32[]{:S(2)}) collective-permute-start(bf16[688,256]{1,0:T(8,128)(2,1)S(1)} %get-tuple-element.258.refs_0_), channel_id=1, source_target_pairs={{0,2},{1,3},{2,6},{3,7},{6,10},{7,11},{10,14},{11,15},{14,12},{15,... | collective-permute-start | bytes 1056776 | tf_op jit(solution)/shard_map/ppermute | solution.py:243
  4.5 15.9 %collective-permute-start.6 = (bf16[688,256]{1,0:T(8,128)(2,1)S(1)}, bf16[688,256]{1,0:T(8,128)(2,1)S(1)}, u32[]{:S(2)}, u32[]{:S(2)}) collective-permute-start(bf16[688,256]{1,0:T(8,128)(2,1)S(1)} %get-tuple-element.259.refs_2_), channel_id=1, source_target_pairs={{0,2},{1,3},{2,6},{3,7},{6,10},{7,11},{10,14},{11,15},{14,12},{15,... | collective-permute-start | bytes 1056776 | tf_op jit(solution)/shard_map/ppermute | solution.py:243
  6.8 18.2 %all-to-all-start = ((s32[16,1,16]{2,1,0:T(1,128)}), s32[16,1,16]{2,1,0:T(1,128)S(1)}, u32[]{:S(2)}, u32[]{:S(2)}) async-start(s32[16,1,16]{2,1,0:T(1,128)} %sub.17), calls=%async_computation | async-start | bytes 16384 | tf_op jit(solution)/shard_map/all_to_all | solution.py:265
  14.1 15.0 %collective-permute-start.12 = (bf16[688,256]{1,0:T(8,128)(2,1)S(1)}, bf16[688,256]{1,0:T(8,128)(2,1)}, u32[]{:S(2)}, u32[]{:S(2)}) collective-permute-start(bf16[688,256]{1,0:T(8,128)(2,1)S(1)} %collective-permute-done.11.refs_1_), channel_id=1, source_target_pairs={{0,4},{1,5},{2,0},{3,1},{6,2},{7,3},{10,6},{11,7},{14,10},{15,11},... | collective-permute-start | bytes 1056776 | tf_op jit(solution)/shard_map/ppermute | solution.py:243
  14.4 13.5 %collective-permute-start.1 = (bf16[688,256]{1,0:T(8,128)(2,1)S(1)}, bf16[688,256]{1,0:T(8,128)(2,1)}, u32[]{:S(2)}, u32[]{:S(2)}) collective-permute-start(bf16[688,256]{1,0:T(8,128)(2,1)S(1)} %collective-permute-done.refs_0_), channel_id=1, source_target_pairs={{0,2},{1,3},{2,6},{3,7},{6,10},{7,11},{10,14},{11,15},{14,12},{15,... | collective-permute-start | bytes 1056776 | tf_op jit(solution)/shard_map/ppermute | solution.py:243
  20.2 16.9 %collective-permute-start.5 = (bf16[688,256]{1,0:T(8,128)(2,1)S(1)}, bf16[688,256]{1,0:T(8,128)(2,1)}, u32[]{:S(2)}, u32[]{:S(2)}) collective-permute-start(bf16[688,256]{1,0:T(8,128)(2,1)S(1)} %collective-permute-done.4.refs_3_), channel_id=1, source_target_pairs={{0,4},{1,5},{2,0},{3,1},{6,2},{7,3},{10,6},{11,7},{14,10},{15,11},... | collective-permute-start | bytes 1056776 | tf_op jit(solution)/shard_map/ppermute | solution.py:243
  20.4 15.5 %collective-permute-start.7 = (bf16[688,256]{1,0:T(8,128)(2,1)S(1)}, bf16[688,256]{1,0:T(8,128)(2,1)}, u32[]{:S(2)}, u32[]{:S(2)}) collective-permute-start(bf16[688,256]{1,0:T(8,128)(2,1)S(1)} %collective-permute-done.6.refs_2_), channel_id=1, source_target_pairs={{0,2},{1,3},{2,6},{3,7},{6,10},{7,11},{10,14},{11,15},{14,12},{15,... | collective-permute-start | bytes 1056776 | tf_op jit(solution)/shard_map/ppermute | solution.py:243
  27.9 15.0 %collective-permute-start.3 = (bf16[688,256]{1,0:T(8,128)(2,1)}, bf16[688,256]{1,0:T(8,128)(2,1)S(1)}, u32[]{:S(2)}, u32[]{:S(2)}) collective-permute-start(bf16[688,256]{1,0:T(8,128)(2,1)} %collective-permute-done.1.refs_0_), channel_id=1, source_target_pairs={{0,2},{1,3},{2,6},{3,7},{6,10},{7,11},{10,14},{11,15},{14,12},{15,... | collective-permute-start | bytes 1056776 | tf_op jit(solution)/shard_map/ppermute | solution.py:243
  29.1 15.0 %collective-permute-start.13 = (bf16[688,256]{1,0:T(8,128)(2,1)}, bf16[688,256]{1,0:T(8,128)(2,1)S(1)}, u32[]{:S(2)}, u32[]{:S(2)}) collective-permute-start(bf16[688,256]{1,0:T(8,128)(2,1)} %collective-permute-done.12.refs_1_), channel_id=1, source_target_pairs={{0,4},{1,5},{2,0},{3,1},{6,2},{7,3},{10,6},{11,7},{14,10},{15,11},... | collective-permute-start | bytes 1056776 | tf_op jit(solution)/shard_map/ppermute | solution.py:243
  29.4 3.4 %copy-start = (bf16[384,11008]{1,0:T(8,128)(2,1)S(1)}, bf16[384,11008]{1,0:T(8,128)(2,1)}, u32[]{:S(2)}) copy-start(bf16[384,11008]{1,0:T(8,128)(2,1)} %own_hbm.15) | copy-start | bytes 25362436
  36.0 14.5 %collective-permute-start.10 = (bf16[688,256]{1,0:T(8,128)(2,1)}, bf16[688,256]{1,0:T(8,128)(2,1)S(1)}, u32[]{:S(2)}, u32[]{:S(2)}) collective-permute-start(bf16[688,256]{1,0:T(8,128)(2,1)} %collective-permute-done.7.refs_2_), channel_id=1, source_target_pairs={{0,2},{1,3},{2,6},{3,7},{6,10},{7,11},{10,14},{11,15},{14,12},{15,... | collective-permute-start | bytes 1056776 | tf_op jit(solution)/shard_map/ppermute | solution.py:243
  37.2 14.4 %collective-permute-start.9 = (bf16[688,256]{1,0:T(8,128)(2,1)}, bf16[688,256]{1,0:T(8,128)(2,1)S(1)}, u32[]{:S(2)}, u32[]{:S(2)}) collective-permute-start(bf16[688,256]{1,0:T(8,128)(2,1)} %collective-permute-done.5.refs_3_), channel_id=1, source_target_pairs={{0,4},{1,5},{2,0},{3,1},{6,2},{7,3},{10,6},{11,7},{14,10},{15,11},... | collective-permute-start | bytes 1056776 | tf_op jit(solution)/shard_map/ppermute | solution.py:243
  42.9 15.1 %collective-permute-start.8 = (bf16[688,256]{1,0:T(8,128)(2,1)S(1)}, bf16[688,256]{1,0:T(8,128)(2,1)S(1)}, u32[]{:S(2)}, u32[]{:S(2)}) collective-permute-start(bf16[688,256]{1,0:T(8,128)(2,1)S(1)} %collective-permute-done.3.refs_0_), channel_id=1, source_target_pairs={{0,2},{1,3},{2,6},{3,7},{6,10},{7,11},{10,14},{11,15},{14,12},{15,... | collective-permute-start | bytes 1056776 | tf_op jit(solution)/shard_map/ppermute | solution.py:243
  44.1 14.1 %collective-permute-start.17 = (bf16[688,256]{1,0:T(8,128)(2,1)S(1)}, bf16[688,256]{1,0:T(8,128)(2,1)S(1)}, u32[]{:S(2)}, u32[]{:S(2)}) collective-permute-start(bf16[688,256]{1,0:T(8,128)(2,1)S(1)} %collective-permute-done.13.refs_1_), channel_id=1, source_target_pairs={{0,4},{1,5},{2,0},{3,1},{6,2},{7,3},{10,6},{11,7},{14,10},{15,11},... | collective-permute-start | bytes 1056776 | tf_op jit(solution)/shard_map/ppermute | solution.py:243
  50.5 16.9 %collective-permute-start.16 = (bf16[688,256]{1,0:T(8,128)(2,1)S(1)}, bf16[688,256]{1,0:T(8,128)(2,1)S(1)}, u32[]{:S(2)}, u32[]{:S(2)}) collective-permute-start(bf16[688,256]{1,0:T(8,128)(2,1)S(1)} %collective-permute-done.10.refs_2_), channel_id=1, source_target_pairs={{0,2},{1,3},{2,6},{3,7},{6,10},{7,11},{10,14},{11,15},{14,12},{15,... | collective-permute-start | bytes 1056776 | tf_op jit(solution)/shard_map/ppermute | solution.py:243
  51.6 17.0 %collective-permute-start.15 = (bf16[688,256]{1,0:T(8,128)(2,1)S(1)}, bf16[688,256]{1,0:T(8,128)(2,1)S(1)}, u32[]{:S(2)}, u32[]{:S(2)}) collective-permute-start(bf16[688,256]{1,0:T(8,128)(2,1)S(1)} %collective-permute-done.9.refs_3_), channel_id=1, source_target_pairs={{0,4},{1,5},{2,0},{3,1},{6,2},{7,3},{10,6},{11,7},{14,10},{15,11},... | collective-permute-start | bytes 1056776 | tf_op jit(solution)/shard_map/ppermute | solution.py:243
  58.1 16.1 %collective-permute-start.21 = (bf16[688,256]{1,0:T(8,128)(2,1)S(1)}, bf16[688,256]{1,0:T(8,128)(2,1)S(1)}, u32[]{:S(2)}, u32[]{:S(2)}) collective-permute-start(bf16[688,256]{1,0:T(8,128)(2,1)S(1)} %collective-permute-done.17.refs_1_), channel_id=1, source_target_pairs={{0,4},{1,5},{2,0},{3,1},{6,2},{7,3},{10,6},{11,7},{14,10},{15,11},... | collective-permute-start | bytes 1056776 | tf_op jit(solution)/shard_map/ppermute | solution.py:243
  59.1 14.0 %collective-permute-start.14 = (bf16[688,256]{1,0:T(8,128)(2,1)S(1)}, bf16[688,256]{1,0:T(8,128)(2,1)S(1)}, u32[]{:S(2)}, u32[]{:S(2)}) collective-permute-start(bf16[688,256]{1,0:T(8,128)(2,1)S(1)} %collective-permute-done.8.refs_0_), channel_id=1, source_target_pairs={{0,2},{1,3},{2,6},{3,7},{6,10},{7,11},{10,14},{11,15},{14,12},{15,... | collective-permute-start | bytes 1056776 | tf_op jit(solution)/shard_map/ppermute | solution.py:243
  67.4 13.3 %collective-permute-start.20 = (bf16[688,256]{1,0:T(8,128)(2,1)S(1)}, bf16[688,256]{1,0:T(8,128)(2,1)S(1)}, u32[]{:S(2)}, u32[]{:S(2)}) collective-permute-start(bf16[688,256]{1,0:T(8,128)(2,1)S(1)} %collective-permute-done.16.refs_2_), channel_id=1, source_target_pairs={{0,2},{1,3},{2,6},{3,7},{6,10},{7,11},{10,14},{11,15},{14,12},{15,... | collective-permute-start | bytes 1056776 | tf_op jit(solution)/shard_map/ppermute | solution.py:243
  68.7 13.2 %collective-permute-start.19 = (bf16[688,256]{1,0:T(8,128)(2,1)S(1)}, bf16[688,256]{1,0:T(8,128)(2,1)S(1)}, u32[]{:S(2)}, u32[]{:S(2)}) collective-permute-start(bf16[688,256]{1,0:T(8,128)(2,1)S(1)} %collective-permute-done.15.refs_3_), channel_id=1, source_target_pairs={{0,4},{1,5},{2,0},{3,1},{6,2},{7,3},{10,6},{11,7},{14,10},{15,11},... | collective-permute-start | bytes 1056776 | tf_op jit(solution)/shard_map/ppermute | solution.py:243
  73.1 15.1 %collective-permute-start.18 = (bf16[688,256]{1,0:T(8,128)(2,1)S(1)}, bf16[688,256]{1,0:T(8,128)(2,1)S(1)}, u32[]{:S(2)}, u32[]{:S(2)}) collective-permute-start(bf16[688,256]{1,0:T(8,128)(2,1)S(1)} %collective-permute-done.14.refs_0_), channel_id=1, source_target_pairs={{0,2},{1,3},{2,6},{3,7},{6,10},{7,11},{10,14},{11,15},{14,12},{15,... | collective-permute-start | bytes 1056776 | tf_op jit(solution)/shard_map/ppermute | solution.py:243
  74.3 13.9 %collective-permute-start.23 = (bf16[688,256]{1,0:T(8,128)(2,1)S(1)}, bf16[688,256]{1,0:T(8,128)(2,1)S(1)}, u32[]{:S(2)}, u32[]{:S(2)}) collective-permute-start(bf16[688,256]{1,0:T(8,128)(2,1)S(1)} %collective-permute-done.21.refs_1_), channel_id=1, source_target_pairs={{0,4},{1,5},{2,0},{3,1},{6,2},{7,3},{10,6},{11,7},{14,10},{15,11},... | collective-permute-start | bytes 1056776 | tf_op jit(solution)/shard_map/ppermute | solution.py:243
  80.7 15.1 %collective-permute-start.25 = (bf16[688,256]{1,0:T(8,128)(2,1)S(1)}, bf16[688,256]{1,0:T(8,128)(2,1)S(1)}, u32[]{:S(2)}, u32[]{:S(2)}) collective-permute-start(bf16[688,256]{1,0:T(8,128)(2,1)S(1)} %collective-permute-done.20.refs_2_), channel_id=1, source_target_pairs={{0,2},{1,3},{2,6},{3,7},{6,10},{7,11},{10,14},{11,15},{14,12},{15,... | collective-permute-start | bytes 1056776 | tf_op jit(solution)/shard_map/ppermute | solution.py:243
  81.8 13.9 %collective-permute-start.26 = (bf16[688,256]{1,0:T(8,128)(2,1)S(1)}, bf16[688,256]{1,0:T(8,128)(2,1)S(1)}, u32[]{:S(2)}, u32[]{:S(2)}) collective-permute-start(bf16[688,256]{1,0:T(8,128)(2,1)S(1)} %collective-permute-done.19.refs_3_), channel_id=1, source_target_pairs={{0,4},{1,5},{2,0},{3,1},{6,2},{7,3},{10,6},{11,7},{14,10},{15,11},... | collective-permute-start | bytes 1056776 | tf_op jit(solution)/shard_map/ppermute | solution.py:243
  88.2 14.3 %collective-permute-start.24 = (bf16[688,256]{1,0:T(8,128)(2,1)S(1)}, bf16[688,256]{1,0:T(8,128)(2,1)S(1)}, u32[]{:S(2)}, u32[]{:S(2)}) collective-permute-start(bf16[688,256]{1,0:T(8,128)(2,1)S(1)} %collective-permute-done.23.refs_1_), channel_id=1, source_target_pairs={{0,4},{1,5},{2,0},{3,1},{6,2},{7,3},{10,6},{11,7},{14,10},{15,11},... | collective-permute-start | bytes 1056776 | tf_op jit(solution)/shard_map/ppermute | solution.py:243
  89.3 14.0 %collective-permute-start.22 = (bf16[688,256]{1,0:T(8,128)(2,1)S(1)}, bf16[688,256]{1,0:T(8,128)(2,1)S(1)}, u32[]{:S(2)}, u32[]{:S(2)}) collective-permute-start(bf16[688,256]{1,0:T(8,128)(2,1)S(1)} %collective-permute-done.18.refs_0_), channel_id=1, source_target_pairs={{0,2},{1,3},{2,6},{3,7},{6,10},{7,11},{10,14},{11,15},{14,12},{15,... | collective-permute-start | bytes 1056776 | tf_op jit(solution)/shard_map/ppermute | solution.py:243
  95.8 14.3 %collective-permute-start.28 = (bf16[688,256]{1,0:T(8,128)(2,1)S(1)}, bf16[688,256]{1,0:T(8,128)(2,1)S(1)}, u32[]{:S(2)}, u32[]{:S(2)}) collective-permute-start(bf16[688,256]{1,0:T(8,128)(2,1)S(1)} %collective-permute-done.26.refs_3_), channel_id=1, source_target_pairs={{0,4},{1,5},{2,0},{3,1},{6,2},{7,3},{10,6},{11,7},{14,10},{15,11},... | collective-permute-start | bytes 1056776 | tf_op jit(solution)/shard_map/ppermute | solution.py:243
  96.9 14.0 %collective-permute-start.27 = (bf16[688,256]{1,0:T(8,128)(2,1)S(1)}, bf16[688,256]{1,0:T(8,128)(2,1)S(1)}, u32[]{:S(2)}, u32[]{:S(2)}) collective-permute-start(bf16[688,256]{1,0:T(8,128)(2,1)S(1)} %collective-permute-done.25.refs_2_), channel_id=1, source_target_pairs={{0,2},{1,3},{2,6},{3,7},{6,10},{7,11},{10,14},{11,15},{14,12},{15,... | collective-permute-start | bytes 1056776 | tf_op jit(solution)/shard_map/ppermute | solution.py:243
  105.7 7.5 %collective-permute-start.29 = (f32[2,384,256]{2,1,0:T(8,128)S(1)}, f32[2,384,256]{2,1,0:T(8,128)S(1)}, u32[]{:S(2)}, u32[]{:S(2)}) collective-permute-start(f32[2,384,256]{2,1,0:T(8,128)S(1)} %get-tuple-element.251), channel_id=1, source_target_pairs={{0,1},{1,0},{2,3},{3,2},{4,5},{5,4},{6,7},{7,6},{8,9},{9,8},{10,11... | collective-permute-start | bytes 2359304 | tf_op jit(solution)/shard_map/ppermute | solution.py:252
  112.0 3.1 %collective-permute-start.30 = (f32[2,384,256]{2,1,0:T(8,128)S(1)}, f32[2,384,256]{2,1,0:T(8,128)S(1)}, u32[]{:S(2)}, u32[]{:S(2)}) collective-permute-start(f32[2,384,256]{2,1,0:T(8,128)S(1)} %get-tuple-element.252), channel_id=1, source_target_pairs={{0,1},{1,0},{2,3},{3,2},{4,5},{5,4},{6,7},{7,6},{8,9},{9,8},{10,11... | collective-permute-start | bytes 2359304 | tf_op jit(solution)/shard_map/ppermute | solution.py:252
  117.2 42.8 %all-to-all-start.1 = ((bf16[16,6,16,512]{3,2,1,0:T(8,128)(2,1)}), bf16[16,6,16,512]{3,2,1,0:T(8,128)(2,1)S(1)}, u32[]{:S(2)}, u32[]{:S(2)}) async-start(bf16[16,6,16,512]{3,2,1,0:T(8,128)(2,1)} %shard_map.59), calls=%async_computation.1 | async-start | bytes 3145728 | tf_op jit(solution)/shard_map/all_to_all | solution.py:277

commit v8 on v7

--- a/solution.py
+++ b/solution.py
@@ -30,7 +30,7 @@
     return jnp.where(y == 1, 1 + z, (GRID_CHIPS - z) % GRID_CHIPS)
 
 
-def routing(owners, count, slots, block_rows):
+def routing(owners, count, slots, block_rows, mask):
     blocks_here = owners.shape[0]
     rows = blocks_here * block_rows
     owner_col = owners[:, 0]
@@ -44,9 +44,8 @@
     row_at = jnp.arange(rows, dtype=jnp.int32)
     out_at = jnp.arange(count * block_rows * slots, dtype=jnp.int32)
     row_key = jnp.repeat(target, block_rows) * block_rows + row_at % block_rows
-    out_key = (
-        out_at // (block_rows * slots) * slots + out_at % slots
-    ) * block_rows + out_at // slots % block_rows
+    owner_at = out_at // (block_rows * slots) ^ mask
+    out_key = (owner_at * slots + out_at % slots) * block_rows + out_at // slots % block_rows
     place = (out_key[:, None] == row_key[None, :]).astype(jnp.bfloat16)
     return labels.reshape(count, slots), place
 
@@ -177,37 +176,67 @@
     return (pairs, new[-1]) if keep else pairs
 
 
-def finish_kernel(place_ref, *refs):
-    out_ref = refs[-1]
-    mine, theirs = refs[:HALVES], refs[HALVES:-1]
-    count, planes, slots, naux = out_ref.shape
-    norb, _, width = mine[0].shape
-    for i in range(norb):
-        for j in range(HALVES):
-            back = (mine[j][i] + theirs[j][i]).astype(jnp.bfloat16)
-            out = jnp.dot(place_ref[...], back, preferred_element_type=jnp.float32)
-            out = out.astype(jnp.bfloat16).reshape(count, planes // norb, slots, width)
-            out_ref[
-                :, pl.ds(i * (planes // norb), planes // norb), :, pl.ds(j * width, width)
-            ] = out
+def finish_kernel(place_ref, mine_ref, theirs_ref, *out_refs):
+    norb, _, width = mine_ref.shape
+    planes, slots, _ = out_refs[0].shape
+    for i in range(norb):
+        back = (mine_ref[i] + theirs_ref[i]).astype(jnp.bfloat16)
+        out = jnp.dot(place_ref[...], back, preferred_element_type=jnp.float32)
+        out = out.astype(jnp.bfloat16).reshape(-1, planes // norb, slots, width)
+        for m, out_ref in enumerate(out_refs):
+            out_ref[pl.ds(i * (planes // norb), planes // norb)] = out[m]
 
 
 def finish(place, mine, theirs, shape):
+    vmem = pl.BlockSpec(memory_space=pltpu.VMEM)
+    count, planes, slots, _ = shape
+    part = jax.ShapeDtypeStruct((planes, slots, mine.shape[2]), jnp.bfloat16)
     return pl.pallas_call(
         finish_kernel,
-        out_shape=jax.ShapeDtypeStruct(shape, jnp.bfloat16),
-        in_specs=[pl.BlockSpec(memory_space=pltpu.VMEM)] * (1 + len(mine) + len(theirs)),
-        out_specs=pl.BlockSpec(memory_space=pltpu.VMEM),
+        out_shape=[part] * count,
+        in_specs=[vmem] * 3,
+        out_specs=[vmem] * count,
         compiler_params=pltpu.CompilerParams(vmem_limit_bytes=20 << 20),
         cost_estimate=pl.CostEstimate(
-            flops=2 * math.prod(shape) * place.shape[1],
-            bytes_accessed=2 * math.prod(shape),
+            flops=2 * count * part.size * place.shape[1],
+            bytes_accessed=2 * count * part.size,
             transcendentals=0,
         ),
-    )(place, *mine, *theirs)
-
-
-def ring_products(gamma, coefficients, early):
+    )(place, mine, theirs)
+
+
+def exchange_order(count):
+    far = list(range(count // 2, count))
+    near = list(range(count // 2))
+    return [m for pair in zip(far, near) for m in pair]
+
+
+def settle_kernel(*refs):
+    out_ref = refs[-1]
+    count, _, _, naux = out_ref.shape
+    width = naux // HALVES
+    me = lax.axis_index("wide")
+    for j in range(HALVES):
+        for k, m in enumerate(exchange_order(count)):
+            out_ref[me ^ m, :, :, pl.ds(j * width, width)] = refs[j * count + k][...]
+
+
+def settle(arrived, shape):
+    vmem = pl.BlockSpec(memory_space=pltpu.VMEM)
+    flat = [value for part in arrived for value in part]
+    return pl.pallas_call(
+        settle_kernel,
+        out_shape=jax.ShapeDtypeStruct(shape, jnp.bfloat16),
+        in_specs=[vmem] * len(flat),
+        out_specs=vmem,
+        compiler_params=pltpu.CompilerParams(vmem_limit_bytes=20 << 20),
+        cost_estimate=pl.CostEstimate(
+            flops=0, bytes_accessed=4 * math.prod(shape), transcendentals=0
+        ),
+    )(*flat)
+
+
+def ring_products(gamma, coefficients, ids, place, shape):
     count = lax.axis_size("wide")
     norb, depth, naux = gamma.shape
     width = naux // HALVES
@@ -237,7 +266,7 @@
             for i in range(norb):
                 sent = piece[j][i]
                 if t == 2 and i == j == 0:
-                    sent, early = lax.optimization_barrier((sent, early))
+                    sent, ids, place = lax.optimization_barrier((sent, ids, place))
                 if BEHIND[t][j]:
                     sent, sums = lax.optimization_barrier((sent, sums))
                 piece[j][i] = lax.ppermute(sent, "wide", shift[i])
@@ -248,9 +277,19 @@
         done, coefficients, other, arrived[done][:1], sums[:1], keep=True
     )
     sums[1] = add_last_products(done, windows, arrived[done][1], sums[1])
-    mine = [sums[j][0] for j in range(HALVES)]
-    theirs = [lax.ppermute(sums[j][1], "wide", swap) for j in range(HALVES)]
-    return mine, theirs, early
+    landed = []
+    for j in range(HALVES):
+        theirs = lax.ppermute(sums[j][1], "wide", swap)
+        parts = finish(place, sums[j][0], theirs, shape)
+        landed.append(
+            [
+                lax.ppermute(parts[m], "wide", [(d, d ^ m) for d in range(count)])
+                if m
+                else parts[m]
+                for m in exchange_order(count)
+            ]
+        )
+    return ids, settle(landed, shape)
 
 
 def local(gamma, coefficients, owners):
@@ -261,11 +300,12 @@
     norb, depth, naux = gamma.shape
     shape = (count, norb * block_rows, slots, naux)
 
-    labels, place = routing(owners, count, slots, block_rows)
+    ring = count == 2 * GRID_CHIPS and norb == len(WAYS)
+    mask = lax.axis_index("wide") if ring else 0
+    labels, place = routing(owners, count, slots, block_rows, mask)
     ids = lax.all_to_all(labels, "wide", split_axis=0, concat_axis=0, tiled=True)
-    if count == 2 * GRID_CHIPS and norb == len(WAYS):
-        mine, theirs, (ids, place) = ring_products(gamma, coefficients, (ids, place))
-        out = finish(place, mine, theirs, shape)
+    if ring:
+        ids, placed = ring_products(gamma, coefficients, ids, place, shape)
     else:
         gathered = lax.all_gather(gamma, "wide", axis=1, tiled=True)
         back = jnp.einsum(
@@ -274,7 +314,7 @@
         out = jnp.einsum("tr,irn->itn", place, back, preferred_element_type=jnp.float32)
         out = out.astype(jnp.bfloat16).reshape(norb, count, block_rows, slots, naux)
         out = out.transpose(1, 0, 2, 3, 4).reshape(shape)
-    placed = lax.all_to_all(out, "wide", split_axis=0, concat_axis=0, tiled=True)
+        placed = lax.all_to_all(out, "wide", split_axis=0, concat_axis=0, tiled=True)
     return placed.transpose(0, 2, 1, 3)[None], ids[None]
 
 

time: 162 us -> 168 us (1.037); the launches traced: 162 us -> 165 us
  starting transfers between devices: 38.6 us -> 76.7 us
  waiting for transfers between devices: 85.1 us -> 51.5 us
    ppermute x2 -> x32, starting transfers between devices: 3.5 us -> 48.2 us  [the longest x30 44.7 us: ring_products(): lax.ppermute(parts[m], 'wide', [(d, d ^ m) for d in range(count)])]
    all_to_all x1 -> x0, waiting for transfers between devices: 36.2 us -> none  [local(): lax.all_to_all(out, 'wide', split_axis=0, concat_axis=0, tiled=True)]
    all_to_all x1 -> x0, starting transfers between devices: 6.59 us -> none  [local(): lax.all_to_all(out, 'wide', split_axis=0, concat_axis=0, tiled=True)]
    ppermute x2 -> x32, waiting for transfers between devices: 1.91 us -> 4.43 us  [the longest x30 4.43 us: ring_products(): lax.ppermute(parts[m], 'wide', [(d, d ^ m) for d in range(count)])]
    unnamed x6 -> x5, local copies, waits for them, and re-layouts: 5.15 us -> 4 us
  transfers between devices with their start and end apart: 33 -> 62, of which waited for: 17 -> 19; matrix products, arithmetic and copies ran while one was open for 2% -> 2% of each run, Pallas kernels for 17% -> 17%
where the time goes in v8:
time: 168 us; the launch traced here: 165 us
  starting transfers between devices  76.7 us (46%)
  waiting for transfers between devices  51.5 us (31%)
  Pallas kernels  29.5 us (18%)
  local copies, waits for them, and re-layouts  6.38 us (4%)
    ppermute x30, starting transfers between devices, ring_products(): lax.ppermute(parts[m], 'wide', [(d, d ^ m) for d in range(count)])  44.7 us
    ppermute x28, waiting for transfers between devices, ring_products(): piece[j][i] = lax.ppermute(sent, 'wide', shift[i])  44 us
    pallas_call x8, Pallas kernels, add_products(): pl.pallas_call(functools.partial(step_kernel, t, parts), out_shape=[sums]...  25.9 us
    ppermute x28, starting transfers between devices, ring_products(): piece[j][i] = lax.ppermute(sent, 'wide', shift[i])  20.7 us
    all_to_all x1, starting transfers between devices, local(): lax.all_to_all(labels, 'wide', split_axis=0, concat_axis=0, tiled=True)  7.02 us
    ppermute x30, waiting for transfers between devices, ring_products(): lax.ppermute(parts[m], 'wide', [(d, d ^ m) for d in range(count)])  4.43 us
    unnamed x5, local copies, waits for them, and re-layouts  4 us
    ppermute x2, starting transfers between devices, ring_products(): theirs = lax.ppermute(sums[j][1], 'wide', swap)  3.5 us
  transfers between devices with their start and end apart: 62, of which 19 were waited for; matrix products, arithmetic and copies ran while one was open for 2% of the time, Pallas kernels for 17%

profile of v8, /device:TPU:13, one launch (start us, length us, event | category | flops | bytes accessed | tf_op | source)
XLA Modules:
  0.0 165.4 jit_solution(5446911205481496200)
XLA Ops:
  0.6 0.7 collective-permute-start.2
  1.4 1.4 slice_bitcast_fusion
  3.1 1.4 collective-permute-start
  4.5 1.3 collective-permute-start.6
  6.8 7.0 %all-to-all-start = ((s32[16,1,16]{2,1,0:T(1,128)}), s32[16,1,16]{2,1,0:T(1,128)S(1)}, u32[]{:S(2)}, u32[]{:S(2)}) async-start(s32[16,1,16]{2,1,0:T(1,128)} %sub.17), calls=%async_computation | async-start | bytes 16384 | tf_op jit(solution)/shard_map/all_to_all | solution.py:306
  14.4 1.2 collective-permute-start.1
  15.6 4.6 %collective-permute-done.4.refs_3_ = bf16[688,256]{1,0:T(8,128)(2,1)S(1)} collective-permute-done((bf16[688,256]{1,0:T(8,128)(2,1)S(1)}, bf16[688,256]{1,0:T(8,128)(2,1)S(1)}, u32[]{:S(2)}, u32[]{:S(2)}) %collective-permute-start.4) | collective-permute-done | bytes 352288 | tf_op jit(solution)/shard_map/ppermute | solution.py:272
  20.4 1.3 collective-permute-start.7
  21.9 3.1 %all-to-all-done = s32[16,1,16]{2,1,0:T(1,128)S(1)} async-done(((s32[16,1,16]{2,1,0:T(1,128)}), s32[16,1,16]{2,1,0:T(1,128)S(1)}, u32[]{:S(2)}, u32[]{:S(2)}) %all-to-all-start) | async-done | bytes 1056 | tf_op jit(solution)/shard_map/all_to_all | solution.py:306
  25.0 3.0 %collective-permute-done.1.refs_0_ = bf16[688,256]{1,0:T(8,128)(2,1)} collective-permute-done((bf16[688,256]{1,0:T(8,128)(2,1)S(1)}, bf16[688,256]{1,0:T(8,128)(2,1)}, u32[]{:S(2)}, u32[]{:S(2)}) %collective-permute-start.1) | collective-permute-done | bytes 352288 | tf_op jit(solution)/shard_map/ppermute | solution.py:272
  27.9 1.2 collective-permute-start.3
  29.4 3.4 %copy-done = bf16[384,11008]{1,0:T(8,128)(2,1)S(1)} copy-done((bf16[384,11008]{1,0:T(8,128)(2,1)S(1)}, bf16[384,11008]{1,0:T(8,128)(2,1)}, u32[]{:S(2)}) %copy-start) | copy-done | bytes 8454168
  32.8 3.1 %shard_map.50 = (f32[2,384,256]{2,1,0:T(8,128)S(1)}, f32[2,384,256]{2,1,0:T(8,128)S(1)}, f32[2,384,256]{2,1,0:T(8,128)S(1)}, f32[2,384,256]{2,1,0:T(8,128)S(1)}) custom-call(bf16[384,11008]{1,0:T(8,128)(2,1)S(1)} %copy-done, bf16[384,11008]{1,0:T(8,128)(2,1)} %collective-permute-done.2.other_hbm, bf16[688,256]{1,0:T(8,128)(2,1)S(1)} %get-tuple-element.322.refs_0_, ...), custom_call_target="tpu_custom_call" | custom-call | flops 1409286144 | bytes 2752512 | tf_op jit(solution)/shard_map/pallas_call | solution.py:157
  36.0 1.2 collective-permute-start.10
  37.5 5.4 %collective-permute-done.3.refs_0_ = bf16[688,256]{1,0:T(8,128)(2,1)S(1)} collective-permute-done((bf16[688,256]{1,0:T(8,128)(2,1)}, bf16[688,256]{1,0:T(8,128)(2,1)S(1)}, u32[]{:S(2)}, u32[]{:S(2)}) %collective-permute-start.3) | collective-permute-done | bytes 352288 | tf_op jit(solution)/shard_map/ppermute | solution.py:272
  42.9 1.2 collective-permute-start.8
  44.4 3.2 %shard_map.51 = (f32[2,384,256]{2,1,0:T(8,128)S(1)}, f32[2,384,256]{2,1,0:T(8,128)S(1)}, f32[2,384,256]{2,1,0:T(8,128)S(1)}, f32[2,384,256]{2,1,0:T(8,128)S(1)}) custom-call(bf16[384,11008]{1,0:T(8,128)(2,1)S(1)} %copy-done, ...), custom_call_target="tpu_custom_call", output_to_operand_aliasing={{0}: (6, {}), {1}: (7, {}), {2}: (8, {}), {3}: (9, {})} | custom-call | flops 1409286144 | bytes 2752512 | tf_op jit(solution)/shard_map/pallas_call | solution.py:157
  47.6 2.9 %collective-permute-done.10.refs_2_ = bf16[688,256]{1,0:T(8,128)(2,1)S(1)} collective-permute-done((bf16[688,256]{1,0:T(8,128)(2,1)}, bf16[688,256]{1,0:T(8,128)(2,1)S(1)}, u32[]{:S(2)}, u32[]{:S(2)}) %collective-permute-start.10) | collective-permute-done | bytes 352288 | tf_op jit(solution)/shard_map/ppermute | solution.py:272
  50.5 1.2 collective-permute-start.16
  51.9 6.1 %collective-permute-done.8.refs_0_ = bf16[688,256]{1,0:T(8,128)(2,1)S(1)} collective-permute-done((bf16[688,256]{1,0:T(8,128)(2,1)S(1)}, bf16[688,256]{1,0:T(8,128)(2,1)S(1)}, u32[]{:S(2)}, u32[]{:S(2)}) %collective-permute-start.8) | collective-permute-done | bytes 352288 | tf_op jit(solution)/shard_map/ppermute | solution.py:272
  58.1 1.0 collective-permute-start.21
  59.6 4.5 %shard_map.52 = (f32[2,384,256]{2,1,0:T(8,128)S(1)}, f32[2,384,256]{2,1,0:T(8,128)S(1)}, f32[2,384,256]{2,1,0:T(8,128)S(1)}, f32[2,384,256]{2,1,0:T(8,128)S(1)}) custom-call(bf16[384,11008]{1,0:T(8,128)(2,1)S(1)} %copy-done, ...), custom_call_target="tpu_custom_call", output_to_operand_aliasing={{0}: (6, {}), {1}: (7, {}), {2}: (8, {}), {3}: (9, {})} | custom-call | flops 1409286144 | bytes 2752512 | tf_op jit(solution)/shard_map/pallas_call | solution.py:157
  64.1 3.2 %shard_map.53 = (f32[2,384,256]{2,1,0:T(8,128)S(1)}, f32[2,384,256]{2,1,0:T(8,128)S(1)}, f32[2,384,256]{2,1,0:T(8,128)S(1)}, f32[2,384,256]{2,1,0:T(8,128)S(1)}) custom-call(bf16[384,11008]{1,0:T(8,128)(2,1)S(1)} %copy-done, ...), custom_call_target="tpu_custom_call", output_to_operand_aliasing={{0}: (6, {}), {1}: (7, {}), {2}: (8, {}), {3}: (9, {})} | custom-call | flops 1409286144 | bytes 2752512 | tf_op jit(solution)/shard_map/pallas_call | solution.py:157
  67.4 1.3 collective-permute-start.20
  68.9 4.2 %collective-permute-done.14.refs_0_ = bf16[688,256]{1,0:T(8,128)(2,1)S(1)} collective-permute-done((bf16[688,256]{1,0:T(8,128)(2,1)S(1)}, bf16[688,256]{1,0:T(8,128)(2,1)S(1)}, u32[]{:S(2)}, u32[]{:S(2)}) %collective-permute-start.14) | collective-permute-done | bytes 352288 | tf_op jit(solution)/shard_map/ppermute | solution.py:272
  73.1 1.2 collective-permute-start.18
  74.6 3.2 %shard_map.54 = (f32[2,384,256]{2,1,0:T(8,128)S(1)}, f32[2,384,256]{2,1,0:T(8,128)S(1)}, f32[2,384,256]{2,1,0:T(8,128)S(1)}, f32[2,384,256]{2,1,0:T(8,128)S(1)}) custom-call(bf16[384,11008]{1,0:T(8,128)(2,1)S(1)} %copy-done, ...), custom_call_target="tpu_custom_call", output_to_operand_aliasing={{0}: (6, {}), {1}: (7, {}), {2}: (8, {}), {3}: (9, {})} | custom-call | flops 1409286144 | bytes 2752512 | tf_op jit(solution)/shard_map/pallas_call | solution.py:157
  77.8 2.9 %collective-permute-done.20.refs_2_ = bf16[688,256]{1,0:T(8,128)(2,1)S(1)} collective-permute-done((bf16[688,256]{1,0:T(8,128)(2,1)S(1)}, bf16[688,256]{1,0:T(8,128)(2,1)S(1)}, u32[]{:S(2)}, u32[]{:S(2)}) %collective-permute-start.20) | collective-permute-done | bytes 352288 | tf_op jit(solution)/shard_map/ppermute | solution.py:272
  80.7 1.2 collective-permute-start.25
  82.1 6.1 %collective-permute-done.18.refs_0_ = bf16[688,256]{1,0:T(8,128)(2,1)S(1)} collective-permute-done((bf16[688,256]{1,0:T(8,128)(2,1)S(1)}, bf16[688,256]{1,0:T(8,128)(2,1)S(1)}, u32[]{:S(2)}, u32[]{:S(2)}) %collective-permute-start.18) | collective-permute-done | bytes 352288 | tf_op jit(solution)/shard_map/ppermute | solution.py:272
  88.2 1.1 collective-permute-start.24
  89.7 3.2 %shard_map.55 = (f32[2,384,256]{2,1,0:T(8,128)S(1)}, f32[2,384,256]{2,1,0:T(8,128)S(1)}, f32[2,384,256]{2,1,0:T(8,128)S(1)}, f32[2,384,256]{2,1,0:T(8,128)S(1)}) custom-call(bf16[384,11008]{1,0:T(8,128)(2,1)S(1)} %copy-done, ...), custom_call_target="tpu_custom_call", output_to_operand_aliasing={{0}: (6, {}), {1}: (7, {}), {2}: (8, {}), {3}: (9, {})} | custom-call | flops 1409286144 | bytes 2752512 | tf_op jit(solution)/shard_map/pallas_call | solution.py:157
  92.9 2.9 %collective-permute-done.25.refs_2_ = bf16[688,256]{1,0:T(8,128)(2,1)S(1)} collective-permute-done((bf16[688,256]{1,0:T(8,128)(2,1)S(1)}, bf16[688,256]{1,0:T(8,128)(2,1)S(1)}, u32[]{:S(2)}, u32[]{:S(2)}) %collective-permute-start.25) | collective-permute-done | bytes 352288 | tf_op jit(solution)/shard_map/ppermute | solution.py:272
  95.8 1.1 collective-permute-start.44
  97.2 3.2 %shard_map.56 = (f32[2,384,256]{2,1,0:T(8,128)S(1)}, f32[2,384,256]{2,1,0:T(8,128)S(1)}, f32[2,384,256]{2,1,0:T(8,128)S(1)}, f32[2,384,256]{2,1,0:T(8,128)S(1)}) custom-call(bf16[384,11008]{1,0:T(8,128)(2,1)S(1)} %copy-done, ...), custom_call_target="tpu_custom_call", output_to_operand_aliasing={{0}: (6, {}), {1}: (7, {}), {2}: (8, {}), {3}: (9, {})} | custom-call | flops 1409286144 | bytes 2752512 | tf_op jit(solution)/shard_map/pallas_call | solution.py:157
  100.4 2.1 %collective-permute-done.24.refs_1_ = bf16[688,256]{1,0:T(8,128)(2,1)S(1)} collective-permute-done((bf16[688,256]{1,0:T(8,128)(2,1)S(1)}, bf16[688,256]{1,0:T(8,128)(2,1)S(1)}, u32[]{:S(2)}, u32[]{:S(2)}) %collective-permute-start.24) | collective-permute-done | bytes 352288 | tf_op jit(solution)/shard_map/ppermute | solution.py:272
  102.5 0.8 collective-permute-done.22.refs_0_
  103.3 2.4 %shard_map.57 = (f32[2,384,256]{2,1,0:T(8,128)S(1)}, f32[2,384,256]{2,1,0:T(8,128)S(1)}, bf16[2,768,896]{2,1,0:T(8,128)(2,1)S(1)}) custom-call(bf16[384,11008]{1,0:T(8,128)(2,1)S(1)} %copy-done, bf16[384,11008]{1,0:T(8,128)(2,1)} %collective-permute-done.2.other_hbm, ...), custom_call_target="tpu_custom_call", output_to_operand_aliasing={{0}: (4, {}), {1}: (5, {})} | custom-call | flops 704643072 | bytes 2752512 | tf_op jit(solution)/shard_map/pallas_call | solution.py:157
  105.7 2.3 %collective-permute-start.27 = (f32[2,384,256]{2,1,0:T(8,128)S(1)}, f32[2,384,256]{2,1,0:T(8,128)S(1)}, u32[]{:S(2)}, u32[]{:S(2)}) collective-permute-start(f32[2,384,256]{2,1,0:T(8,128)S(1)} %get-tuple-element.277), channel_id=1, source_target_pairs={{0,1},{1,0},{2,3},{3,2},{4,5},{5,4},{6,7},{7,6},{8,9},{9,8},{10,11... | collective-permute-start | bytes 2359304 | tf_op jit(solution)/shard_map/ppermute | solution.py:282
  108.0 2.1 %collective-permute-done.44.refs_1_ = bf16[688,256]{1,0:T(8,128)(2,1)S(1)} collective-permute-done((bf16[688,256]{1,0:T(8,128)(2,1)S(1)}, bf16[688,256]{1,0:T(8,128)(2,1)S(1)}, u32[]{:S(2)}, u32[]{:S(2)}) %collective-permute-start.44) | collective-permute-done | bytes 352288 | tf_op jit(solution)/shard_map/ppermute | solution.py:272
  110.1 0.8 collective-permute-done.43.refs_0_
  110.9 1.1 shard_map.59
  112.0 1.2 collective-permute-start.45
  113.8 2.5 %collective-permute-start.28 = (bf16[6,16,256]{2,1,0:T(8,128)(2,1)S(1)}, bf16[6,16,256]{2,1,0:T(8,128)(2,1)S(1)}, u32[]{:S(2)}, u32[]{:S(2)}) collective-permute-start(bf16[6,16,256]{2,1,0:T(8,128)(2,1)S(1)} %get-tuple-element.278), channel_id=1, source_target_pairs={{0,8},{1,9},{2,10},{3,11},{4,12},{5,13},{6,14},{7,15},{8,0},{9,1},... | collective-permute-start | bytes 147464 | tf_op jit(solution)/shard_map/ppermute | solution.py:286
  116.7 3.3 %collective-permute-start.31 = (bf16[6,16,256]{2,1,0:T(8,128)(2,1)S(1)}, bf16[6,16,256]{2,1,0:T(8,128)(2,1)S(1)}, u32[]{:S(2)}, u32[]{:S(2)}) collective-permute-start(bf16[6,16,256]{2,1,0:T(8,128)(2,1)S(1)} %get-tuple-element.282), channel_id=1, source_target_pairs={{0,10},{1,11},{2,8},{3,9},{4,14},{5,15},{6,12},{7,13},{8,2},{9,3},... | collective-permute-start | bytes 147464 | tf_op jit(solution)/shard_map/ppermute | solution.py:286
  120.9 5.4 %collective-permute-start.33 = (bf16[6,16,256]{2,1,0:T(8,128)(2,1)S(1)}, bf16[6,16,256]{2,1,0:T(8,128)(2,1)S(1)}, u32[]{:S(2)}, u32[]{:S(2)}) collective-permute-start(bf16[6,16,256]{2,1,0:T(8,128)(2,1)S(1)} %get-tuple-element.284), channel_id=1, source_target_pairs={{0,11},{1,10},{2,9},{3,8},{4,15},{5,14},{6,13},{7,12},{8,3},{9,2},... | collective-permute-start | bytes 147464 | tf_op jit(solution)/shard_map/ppermute | solution.py:286
  126.9 1.4 collective-permute-start.36
  128.3 1.4 collective-permute-start.37
  130.2 2.0 %collective-permute-start.38 = (bf16[6,16,256]{2,1,0:T(8,128)(2,1)S(1)}, bf16[6,16,256]{2,1,0:T(8,128)(2,1)S(1)}, u32[]{:S(2)}, u32[]{:S(2)}) collective-permute-start(bf16[6,16,256]{2,1,0:T(8,128)(2,1)S(1)} %get-tuple-element.289), channel_id=1, source_target_pairs={{0,5},{1,4},{2,7},{3,6},{4,1},{5,0},{6,3},{7,2},{8,13},{9,12},{10,... | collective-permute-start | bytes 147464 | tf_op jit(solution)/shard_map/ppermute | solution.py:286
  132.2 1.4 collective-permute-start.39
  134.1 3.2 %collective-permute-start.41 = (bf16[6,16,256]{2,1,0:T(8,128)(2,1)S(1)}, bf16[6,16,256]{2,1,0:T(8,128)(2,1)S(1)}, u32[]{:S(2)}, u32[]{:S(2)}) collective-permute-start(bf16[6,16,256]{2,1,0:T(8,128)(2,1)S(1)} %get-tuple-element.292), channel_id=1, source_target_pairs={{0,15},{1,14},{2,13},{3,12},{4,11},{5,10},{6,9},{7,8},{8,7},{9,6},... | collective-permute-start | bytes 147464 | tf_op jit(solution)/shard_map/ppermute | solution.py:286
  137.2 1.7 %collective-permute-start.42 = (bf16[6,16,256]{2,1,0:T(8,128)(2,1)S(1)}, bf16[6,16,256]{2,1,0:T(8,128)(2,1)S(1)}, u32[]{:S(2)}, u32[]{:S(2)}) collective-permute-start(bf16[6,16,256]{2,1,0:T(8,128)(2,1)S(1)} %get-tuple-element.293), channel_id=1, source_target_pairs={{0,7},{1,6},{2,5},{3,4},{4,3},{5,2},{6,1},{7,0},{8,15},{9,14},{10,... | collective-permute-start | bytes 147464 | tf_op jit(solution)/shard_map/ppermute | solution.py:286
  139.6 2.7 %collective-permute-start.47 = (bf16[6,16,256]{2,1,0:T(8,128)(2,1)S(1)}, bf16[6,16,256]{2,1,0:T(8,128)(2,1)S(1)}, u32[]{:S(2)}, u32[]{:S(2)}) collective-permute-start(bf16[6,16,256]{2,1,0:T(8,128)(2,1)S(1)} %get-tuple-element.303), channel_id=1, source_target_pairs={{0,9},{1,8},{2,11},{3,10},{4,13},{5,12},{6,15},{7,14},{8,1},{9,0},... | collective-permute-start | bytes 147464 | tf_op jit(solution)/shard_map/ppermute | solution.py:286
  142.4 1.9 %collective-permute-start.49 = (bf16[6,16,256]{2,1,0:T(8,128)(2,1)S(1)}, bf16[6,16,256]{2,1,0:T(8,128)(2,1)S(1)}, u32[]{:S(2)}, u32[]{:S(2)}) collective-permute-start(bf16[6,16,256]{2,1,0:T(8,128)(2,1)S(1)} %get-tuple-element.305), channel_id=1, source_target_pairs={{0,10},{1,11},{2,8},{3,9},{4,14},{5,15},{6,12},{7,13},{8,2},{9,3},... | collective-permute-start | bytes 147464 | tf_op jit(solution)/shard_map/ppermute | solution.py:286
  144.6 3.1 %collective-permute-start.51 = (bf16[6,16,256]{2,1,0:T(8,128)(2,1)S(1)}, bf16[6,16,256]{2,1,0:T(8,128)(2,1)S(1)}, u32[]{:S(2)}, u32[]{:S(2)}) collective-permute-start(bf16[6,16,256]{2,1,0:T(8,128)(2,1)S(1)} %get-tuple-element.307), channel_id=1, source_target_pairs={{0,11},{1,10},{2,9},{3,8},{4,15},{5,14},{6,13},{7,12},{8,3},{9,2},... | collective-permute-start | bytes 147464 | tf_op jit(solution)/shard_map/ppermute | solution.py:286
  148.3 3.2 %collective-permute-start.54 = (bf16[6,16,256]{2,1,0:T(8,128)(2,1)S(1)}, bf16[6,16,256]{2,1,0:T(8,128)(2,1)S(1)}, u32[]{:S(2)}, u32[]{:S(2)}) collective-permute-start(bf16[6,16,256]{2,1,0:T(8,128)(2,1)S(1)} %get-tuple-element.310), channel_id=1, source_target_pairs={{0,4},{1,5},{2,6},{3,7},{4,0},{5,1},{6,2},{7,3},{8,12},{9,13},{10,... | collective-permute-start | bytes 147464 | tf_op jit(solution)/shard_map/ppermute | solution.py:286
  151.5 1.7 %collective-permute-start.55 = (bf16[6,16,256]{2,1,0:T(8,128)(2,1)S(1)}, bf16[6,16,256]{2,1,0:T(8,128)(2,1)S(1)}, u32[]{:S(2)}, u32[]{:S(2)}) collective-permute-start(bf16[6,16,256]{2,1,0:T(8,128)(2,1)S(1)} %get-tuple-element.311), channel_id=1, source_target_pairs={{0,13},{1,12},{2,15},{3,14},{4,9},{5,8},{6,11},{7,10},{8,5},{9,4},... | collective-permute-start | bytes 147464 | tf_op jit(solution)/shard_map/ppermute | solution.py:286
  153.8 0.8 collective-permute-start.57
  154.7 1.9 %collective-permute-start.58 = (bf16[6,16,256]{2,1,0:T(8,128)(2,1)S(1)}, bf16[6,16,256]{2,1,0:T(8,128)(2,1)S(1)}, u32[]{:S(2)}, u32[]{:S(2)}) collective-permute-start(bf16[6,16,256]{2,1,0:T(8,128)(2,1)S(1)} %get-tuple-element.314), channel_id=1, source_target_pairs={{0,6},{1,7},{2,4},{3,5},{4,2},{5,3},{6,0},{7,1},{8,14},{9,15},{10,... | collective-permute-start | bytes 147464 | tf_op jit(solution)/shard_map/ppermute | solution.py:286
  156.6 1.9 %collective-permute-start.59 = (bf16[6,16,256]{2,1,0:T(8,128)(2,1)S(1)}, bf16[6,16,256]{2,1,0:T(8,128)(2,1)S(1)}, u32[]{:S(2)}, u32[]{:S(2)}) collective-permute-start(bf16[6,16,256]{2,1,0:T(8,128)(2,1)S(1)} %get-tuple-element.315), channel_id=1, source_target_pairs={{0,15},{1,14},{2,13},{3,12},{4,11},{5,10},{6,9},{7,8},{8,7},{9,6},... | collective-permute-start | bytes 147464 | tf_op jit(solution)/shard_map/ppermute | solution.py:286
  158.5 1.3 collective-permute-start.60
  159.8 1.2 collective-permute-done.59.refs_30_
  161.0 2.5 %collective-permute-done.60.refs_31_ = bf16[6,16,256]{2,1,0:T(8,128)(2,1)S(1)} collective-permute-done((bf16[6,16,256]{2,1,0:T(8,128)(2,1)S(1)}, bf16[6,16,256]{2,1,0:T(8,128)(2,1)S(1)}, u32[]{:S(2)}, u32[]{:S(2)}) %collective-permute-start.60) | collective-permute-done | bytes 49184 | tf_op jit(solution)/shard_map/ppermute | solution.py:286
  163.5 1.3 shard_map.61
  (88 shorter events, 12.1 us)
Async XLA Ops:
  0.6 5.1 %copy-start.1 = (s32[128,1]{0,1:T(1,128)S(1)}, s32[128,1]{0,1:T(1,128)}, u32[]{:S(2)}) copy-start(s32[128,1]{0,1:T(1,128)} %param.5) | copy-start | bytes 1540
  0.6 28.8 %collective-permute-start.2 = (bf16[384,11008]{1,0:T(8,128)(2,1)}, bf16[384,11008]{1,0:T(8,128)(2,1)}, u32[]{:S(2)}, u32[]{:S(2)}) collective-permute-start(bf16[384,11008]{1,0:T(8,128)(2,1)} %own_hbm.15), channel_id=1, source_target_pairs={{0,1},{1,0},{2,3},{3,2},{4,5},{5,4},{6,7},{7,6},{8,9},{9,8},{10,11... | collective-permute-start | bytes 25362440 | tf_op jit(solution)/shard_map/ppermute | solution.py:244
  2.8 11.3 %collective-permute-start.11 = (bf16[688,256]{1,0:T(8,128)(2,1)S(1)}, bf16[688,256]{1,0:T(8,128)(2,1)S(1)}, u32[]{:S(2)}, u32[]{:S(2)}) collective-permute-start(bf16[688,256]{1,0:T(8,128)(2,1)S(1)} %get-tuple-element.320.refs_1_), channel_id=1, source_target_pairs={{0,4},{1,5},{2,0},{3,1},{6,2},{7,3},{10,6},{11,7},{14,10},{15,11},... | collective-permute-start | bytes 1056776 | tf_op jit(solution)/shard_map/ppermute | solution.py:272
  3.0 17.2 %collective-permute-start.4 = (bf16[688,256]{1,0:T(8,128)(2,1)S(1)}, bf16[688,256]{1,0:T(8,128)(2,1)S(1)}, u32[]{:S(2)}, u32[]{:S(2)}) collective-permute-start(bf16[688,256]{1,0:T(8,128)(2,1)S(1)} %get-tuple-element.321.refs_3_), channel_id=1, source_target_pairs={{0,4},{1,5},{2,0},{3,1},{6,2},{7,3},{10,6},{11,7},{14,10},{15,11},... | collective-permute-start | bytes 1056776 | tf_op jit(solution)/shard_map/ppermute | solution.py:272
  3.1 11.4 %collective-permute-start = (bf16[688,256]{1,0:T(8,128)(2,1)S(1)}, bf16[688,256]{1,0:T(8,128)(2,1)S(1)}, u32[]{:S(2)}, u32[]{:S(2)}) collective-permute-start(bf16[688,256]{1,0:T(8,128)(2,1)S(1)} %get-tuple-element.322.refs_0_), channel_id=1, source_target_pairs={{0,2},{1,3},{2,6},{3,7},{6,10},{7,11},{10,14},{11,15},{14,12},{15,... | collective-permute-start | bytes 1056776 | tf_op jit(solution)/shard_map/ppermute | solution.py:272
  4.5 15.9 %collective-permute-start.6 = (bf16[688,256]{1,0:T(8,128)(2,1)S(1)}, bf16[688,256]{1,0:T(8,128)(2,1)S(1)}, u32[]{:S(2)}, u32[]{:S(2)}) collective-permute-start(bf16[688,256]{1,0:T(8,128)(2,1)S(1)} %get-tuple-element.323.refs_2_), channel_id=1, source_target_pairs={{0,2},{1,3},{2,6},{3,7},{6,10},{7,11},{10,14},{11,15},{14,12},{15,... | collective-permute-start | bytes 1056776 | tf_op jit(solution)/shard_map/ppermute | solution.py:272
  6.8 18.2 %all-to-all-start = ((s32[16,1,16]{2,1,0:T(1,128)}), s32[16,1,16]{2,1,0:T(1,128)S(1)}, u32[]{:S(2)}, u32[]{:S(2)}) async-start(s32[16,1,16]{2,1,0:T(1,128)} %sub.17), calls=%async_computation | async-start | bytes 16384 | tf_op jit(solution)/shard_map/all_to_all | solution.py:306
  14.1 15.0 %collective-permute-start.12 = (bf16[688,256]{1,0:T(8,128)(2,1)S(1)}, bf16[688,256]{1,0:T(8,128)(2,1)}, u32[]{:S(2)}, u32[]{:S(2)}) collective-permute-start(bf16[688,256]{1,0:T(8,128)(2,1)S(1)} %collective-permute-done.11.refs_1_), channel_id=1, source_target_pairs={{0,4},{1,5},{2,0},{3,1},{6,2},{7,3},{10,6},{11,7},{14,10},{15,11},... | collective-permute-start | bytes 1056776 | tf_op jit(solution)/shard_map/ppermute | solution.py:272
  14.4 13.5 %collective-permute-start.1 = (bf16[688,256]{1,0:T(8,128)(2,1)S(1)}, bf16[688,256]{1,0:T(8,128)(2,1)}, u32[]{:S(2)}, u32[]{:S(2)}) collective-permute-start(bf16[688,256]{1,0:T(8,128)(2,1)S(1)} %collective-permute-done.refs_0_), channel_id=1, source_target_pairs={{0,2},{1,3},{2,6},{3,7},{6,10},{7,11},{10,14},{11,15},{14,12},{15,... | collective-permute-start | bytes 1056776 | tf_op jit(solution)/shard_map/ppermute | solution.py:272
  20.2 16.9 %collective-permute-start.5 = (bf16[688,256]{1,0:T(8,128)(2,1)S(1)}, bf16[688,256]{1,0:T(8,128)(2,1)}, u32[]{:S(2)}, u32[]{:S(2)}) collective-permute-start(bf16[688,256]{1,0:T(8,128)(2,1)S(1)} %collective-permute-done.4.refs_3_), channel_id=1, source_target_pairs={{0,4},{1,5},{2,0},{3,1},{6,2},{7,3},{10,6},{11,7},{14,10},{15,11},... | collective-permute-start | bytes 1056776 | tf_op jit(solution)/shard_map/ppermute | solution.py:272
  20.4 15.5 %collective-permute-start.7 = (bf16[688,256]{1,0:T(8,128)(2,1)S(1)}, bf16[688,256]{1,0:T(8,128)(2,1)}, u32[]{:S(2)}, u32[]{:S(2)}) collective-permute-start(bf16[688,256]{1,0:T(8,128)(2,1)S(1)} %collective-permute-done.6.refs_2_), channel_id=1, source_target_pairs={{0,2},{1,3},{2,6},{3,7},{6,10},{7,11},{10,14},{11,15},{14,12},{15,... | collective-permute-start | bytes 1056776 | tf_op jit(solution)/shard_map/ppermute | solution.py:272
  27.9 15.0 %collective-permute-start.3 = (bf16[688,256]{1,0:T(8,128)(2,1)}, bf16[688,256]{1,0:T(8,128)(2,1)S(1)}, u32[]{:S(2)}, u32[]{:S(2)}) collective-permute-start(bf16[688,256]{1,0:T(8,128)(2,1)} %collective-permute-done.1.refs_0_), channel_id=1, source_target_pairs={{0,2},{1,3},{2,6},{3,7},{6,10},{7,11},{10,14},{11,15},{14,12},{15,... | collective-permute-start | bytes 1056776 | tf_op jit(solution)/shard_map/ppermute | solution.py:272
  29.1 15.0 %collective-permute-start.13 = (bf16[688,256]{1,0:T(8,128)(2,1)}, bf16[688,256]{1,0:T(8,128)(2,1)S(1)}, u32[]{:S(2)}, u32[]{:S(2)}) collective-permute-start(bf16[688,256]{1,0:T(8,128)(2,1)} %collective-permute-done.12.refs_1_), channel_id=1, source_target_pairs={{0,4},{1,5},{2,0},{3,1},{6,2},{7,3},{10,6},{11,7},{14,10},{15,11},... | collective-permute-start | bytes 1056776 | tf_op jit(solution)/shard_map/ppermute | solution.py:272
  29.4 3.4 %copy-start = (bf16[384,11008]{1,0:T(8,128)(2,1)S(1)}, bf16[384,11008]{1,0:T(8,128)(2,1)}, u32[]{:S(2)}) copy-start(bf16[384,11008]{1,0:T(8,128)(2,1)} %own_hbm.15) | copy-start | bytes 25362436
  36.0 14.5 %collective-permute-start.10 = (bf16[688,256]{1,0:T(8,128)(2,1)}, bf16[688,256]{1,0:T(8,128)(2,1)S(1)}, u32[]{:S(2)}, u32[]{:S(2)}) collective-permute-start(bf16[688,256]{1,0:T(8,128)(2,1)} %collective-permute-done.7.refs_2_), channel_id=1, source_target_pairs={{0,2},{1,3},{2,6},{3,7},{6,10},{7,11},{10,14},{11,15},{14,12},{15,... | collective-permute-start | bytes 1056776 | tf_op jit(solution)/shard_map/ppermute | solution.py:272
  37.2 14.4 %collective-permute-start.9 = (bf16[688,256]{1,0:T(8,128)(2,1)}, bf16[688,256]{1,0:T(8,128)(2,1)S(1)}, u32[]{:S(2)}, u32[]{:S(2)}) collective-permute-start(bf16[688,256]{1,0:T(8,128)(2,1)} %collective-permute-done.5.refs_3_), channel_id=1, source_target_pairs={{0,4},{1,5},{2,0},{3,1},{6,2},{7,3},{10,6},{11,7},{14,10},{15,11},... | collective-permute-start | bytes 1056776 | tf_op jit(solution)/shard_map/ppermute | solution.py:272
  42.9 15.1 %collective-permute-start.8 = (bf16[688,256]{1,0:T(8,128)(2,1)S(1)}, bf16[688,256]{1,0:T(8,128)(2,1)S(1)}, u32[]{:S(2)}, u32[]{:S(2)}) collective-permute-start(bf16[688,256]{1,0:T(8,128)(2,1)S(1)} %collective-permute-done.3.refs_0_), channel_id=1, source_target_pairs={{0,2},{1,3},{2,6},{3,7},{6,10},{7,11},{10,14},{11,15},{14,12},{15,... | collective-permute-start | bytes 1056776 | tf_op jit(solution)/shard_map/ppermute | solution.py:272
  44.1 14.1 %collective-permute-start.17 = (bf16[688,256]{1,0:T(8,128)(2,1)S(1)}, bf16[688,256]{1,0:T(8,128)(2,1)S(1)}, u32[]{:S(2)}, u32[]{:S(2)}) collective-permute-start(bf16[688,256]{1,0:T(8,128)(2,1)S(1)} %collective-permute-done.13.refs_1_), channel_id=1, source_target_pairs={{0,4},{1,5},{2,0},{3,1},{6,2},{7,3},{10,6},{11,7},{14,10},{15,11},... | collective-permute-start | bytes 1056776 | tf_op jit(solution)/shard_map/ppermute | solution.py:272
  50.5 16.9 %collective-permute-start.16 = (bf16[688,256]{1,0:T(8,128)(2,1)S(1)}, bf16[688,256]{1,0:T(8,128)(2,1)S(1)}, u32[]{:S(2)}, u32[]{:S(2)}) collective-permute-start(bf16[688,256]{1,0:T(8,128)(2,1)S(1)} %collective-permute-done.10.refs_2_), channel_id=1, source_target_pairs={{0,2},{1,3},{2,6},{3,7},{6,10},{7,11},{10,14},{11,15},{14,12},{15,... | collective-permute-start | bytes 1056776 | tf_op jit(solution)/shard_map/ppermute | solution.py:272
  51.6 17.0 %collective-permute-start.15 = (bf16[688,256]{1,0:T(8,128)(2,1)S(1)}, bf16[688,256]{1,0:T(8,128)(2,1)S(1)}, u32[]{:S(2)}, u32[]{:S(2)}) collective-permute-start(bf16[688,256]{1,0:T(8,128)(2,1)S(1)} %collective-permute-done.9.refs_3_), channel_id=1, source_target_pairs={{0,4},{1,5},{2,0},{3,1},{6,2},{7,3},{10,6},{11,7},{14,10},{15,11},... | collective-permute-start | bytes 1056776 | tf_op jit(solution)/shard_map/ppermute | solution.py:272
  58.1 16.1 %collective-permute-start.21 = (bf16[688,256]{1,0:T(8,128)(2,1)S(1)}, bf16[688,256]{1,0:T(8,128)(2,1)S(1)}, u32[]{:S(2)}, u32[]{:S(2)}) collective-permute-start(bf16[688,256]{1,0:T(8,128)(2,1)S(1)} %collective-permute-done.17.refs_1_), channel_id=1, source_target_pairs={{0,4},{1,5},{2,0},{3,1},{6,2},{7,3},{10,6},{11,7},{14,10},{15,11},... | collective-permute-start | bytes 1056776 | tf_op jit(solution)/shard_map/ppermute | solution.py:272
  59.1 14.0 %collective-permute-start.14 = (bf16[688,256]{1,0:T(8,128)(2,1)S(1)}, bf16[688,256]{1,0:T(8,128)(2,1)S(1)}, u32[]{:S(2)}, u32[]{:S(2)}) collective-permute-start(bf16[688,256]{1,0:T(8,128)(2,1)S(1)} %collective-permute-done.8.refs_0_), channel_id=1, source_target_pairs={{0,2},{1,3},{2,6},{3,7},{6,10},{7,11},{10,14},{11,15},{14,12},{15,... | collective-permute-start | bytes 1056776 | tf_op jit(solution)/shard_map/ppermute | solution.py:272
  67.4 13.3 %collective-permute-start.20 = (bf16[688,256]{1,0:T(8,128)(2,1)S(1)}, bf16[688,256]{1,0:T(8,128)(2,1)S(1)}, u32[]{:S(2)}, u32[]{:S(2)}) collective-permute-start(bf16[688,256]{1,0:T(8,128)(2,1)S(1)} %collective-permute-done.16.refs_2_), channel_id=1, source_target_pairs={{0,2},{1,3},{2,6},{3,7},{6,10},{7,11},{10,14},{11,15},{14,12},{15,... | collective-permute-start | bytes 1056776 | tf_op jit(solution)/shard_map/ppermute | solution.py:272
  68.7 13.2 %collective-permute-start.19 = (bf16[688,256]{1,0:T(8,128)(2,1)S(1)}, bf16[688,256]{1,0:T(8,128)(2,1)S(1)}, u32[]{:S(2)}, u32[]{:S(2)}) collective-permute-start(bf16[688,256]{1,0:T(8,128)(2,1)S(1)} %collective-permute-done.15.refs_3_), channel_id=1, source_target_pairs={{0,4},{1,5},{2,0},{3,1},{6,2},{7,3},{10,6},{11,7},{14,10},{15,11},... | collective-permute-start | bytes 1056776 | tf_op jit(solution)/shard_map/ppermute | solution.py:272
  73.1 15.1 %collective-permute-start.18 = (bf16[688,256]{1,0:T(8,128)(2,1)S(1)}, bf16[688,256]{1,0:T(8,128)(2,1)S(1)}, u32[]{:S(2)}, u32[]{:S(2)}) collective-permute-start(bf16[688,256]{1,0:T(8,128)(2,1)S(1)} %collective-permute-done.14.refs_0_), channel_id=1, source_target_pairs={{0,2},{1,3},{2,6},{3,7},{6,10},{7,11},{10,14},{11,15},{14,12},{15,... | collective-permute-start | bytes 1056776 | tf_op jit(solution)/shard_map/ppermute | solution.py:272
  74.3 13.9 %collective-permute-start.23 = (bf16[688,256]{1,0:T(8,128)(2,1)S(1)}, bf16[688,256]{1,0:T(8,128)(2,1)S(1)}, u32[]{:S(2)}, u32[]{:S(2)}) collective-permute-start(bf16[688,256]{1,0:T(8,128)(2,1)S(1)} %collective-permute-done.21.refs_1_), channel_id=1, source_target_pairs={{0,4},{1,5},{2,0},{3,1},{6,2},{7,3},{10,6},{11,7},{14,10},{15,11},... | collective-permute-start | bytes 1056776 | tf_op jit(solution)/shard_map/ppermute | solution.py:272
  80.7 15.1 %collective-permute-start.25 = (bf16[688,256]{1,0:T(8,128)(2,1)S(1)}, bf16[688,256]{1,0:T(8,128)(2,1)S(1)}, u32[]{:S(2)}, u32[]{:S(2)}) collective-permute-start(bf16[688,256]{1,0:T(8,128)(2,1)S(1)} %collective-permute-done.20.refs_2_), channel_id=1, source_target_pairs={{0,2},{1,3},{2,6},{3,7},{6,10},{7,11},{10,14},{11,15},{14,12},{15,... | collective-permute-start | bytes 1056776 | tf_op jit(solution)/shard_map/ppermute | solution.py:272
  81.8 13.9 %collective-permute-start.26 = (bf16[688,256]{1,0:T(8,128)(2,1)S(1)}, bf16[688,256]{1,0:T(8,128)(2,1)S(1)}, u32[]{:S(2)}, u32[]{:S(2)}) collective-permute-start(bf16[688,256]{1,0:T(8,128)(2,1)S(1)} %collective-permute-done.19.refs_3_), channel_id=1, source_target_pairs={{0,4},{1,5},{2,0},{3,1},{6,2},{7,3},{10,6},{11,7},{14,10},{15,11},... | collective-permute-start | bytes 1056776 | tf_op jit(solution)/shard_map/ppermute | solution.py:272
  88.2 14.3 %collective-permute-start.24 = (bf16[688,256]{1,0:T(8,128)(2,1)S(1)}, bf16[688,256]{1,0:T(8,128)(2,1)S(1)}, u32[]{:S(2)}, u32[]{:S(2)}) collective-permute-start(bf16[688,256]{1,0:T(8,128)(2,1)S(1)} %collective-permute-done.23.refs_1_), channel_id=1, source_target_pairs={{0,4},{1,5},{2,0},{3,1},{6,2},{7,3},{10,6},{11,7},{14,10},{15,11},... | collective-permute-start | bytes 1056776 | tf_op jit(solution)/shard_map/ppermute | solution.py:272
  89.3 14.0 %collective-permute-start.22 = (bf16[688,256]{1,0:T(8,128)(2,1)S(1)}, bf16[688,256]{1,0:T(8,128)(2,1)S(1)}, u32[]{:S(2)}, u32[]{:S(2)}) collective-permute-start(bf16[688,256]{1,0:T(8,128)(2,1)S(1)} %collective-permute-done.18.refs_0_), channel_id=1, source_target_pairs={{0,2},{1,3},{2,6},{3,7},{6,10},{7,11},{10,14},{11,15},{14,12},{15,... | collective-permute-start | bytes 1056776 | tf_op jit(solution)/shard_map/ppermute | solution.py:272
  95.8 14.3 %collective-permute-start.44 = (bf16[688,256]{1,0:T(8,128)(2,1)S(1)}, bf16[688,256]{1,0:T(8,128)(2,1)S(1)}, u32[]{:S(2)}, u32[]{:S(2)}) collective-permute-start(bf16[688,256]{1,0:T(8,128)(2,1)S(1)} %collective-permute-done.26.refs_3_), channel_id=1, source_target_pairs={{0,4},{1,5},{2,0},{3,1},{6,2},{7,3},{10,6},{11,7},{14,10},{15,11},... | collective-permute-start | bytes 1056776 | tf_op jit(solution)/shard_map/ppermute | solution.py:272
  96.9 14.0 %collective-permute-start.43 = (bf16[688,256]{1,0:T(8,128)(2,1)S(1)}, bf16[688,256]{1,0:T(8,128)(2,1)S(1)}, u32[]{:S(2)}, u32[]{:S(2)}) collective-permute-start(bf16[688,256]{1,0:T(8,128)(2,1)S(1)} %collective-permute-done.25.refs_2_), channel_id=1, source_target_pairs={{0,2},{1,3},{2,6},{3,7},{6,10},{7,11},{10,14},{11,15},{14,12},{15,... | collective-permute-start | bytes 1056776 | tf_op jit(solution)/shard_map/ppermute | solution.py:272
  105.7 7.5 %collective-permute-start.27 = (f32[2,384,256]{2,1,0:T(8,128)S(1)}, f32[2,384,256]{2,1,0:T(8,128)S(1)}, u32[]{:S(2)}, u32[]{:S(2)}) collective-permute-start(f32[2,384,256]{2,1,0:T(8,128)S(1)} %get-tuple-element.277), channel_id=1, source_target_pairs={{0,1},{1,0},{2,3},{3,2},{4,5},{5,4},{6,7},{7,6},{8,9},{9,8},{10,11... | collective-permute-start | bytes 2359304 | tf_op jit(solution)/shard_map/ppermute | solution.py:282
  112.0 25.3 %collective-permute-start.45 = (f32[2,384,256]{2,1,0:T(8,128)S(1)}, f32[2,384,256]{2,1,0:T(8,128)S(1)}, u32[]{:S(2)}, u32[]{:S(2)}) collective-permute-start(f32[2,384,256]{2,1,0:T(8,128)S(1)} %get-tuple-element.300), channel_id=1, source_target_pairs={{0,1},{1,0},{2,3},{3,2},{4,5},{5,4},{6,7},{7,6},{8,9},{9,8},{10,11... | collective-permute-start | bytes 2359304 | tf_op jit(solution)/shard_map/ppermute | solution.py:282
  113.8 6.2 %collective-permute-start.28 = (bf16[6,16,256]{2,1,0:T(8,128)(2,1)S(1)}, bf16[6,16,256]{2,1,0:T(8,128)(2,1)S(1)}, u32[]{:S(2)}, u32[]{:S(2)}) collective-permute-start(bf16[6,16,256]{2,1,0:T(8,128)(2,1)S(1)} %get-tuple-element.278), channel_id=1, source_target_pairs={{0,8},{1,9},{2,10},{3,11},{4,12},{5,13},{6,14},{7,15},{8,0},{9,1},... | collective-permute-start | bytes 147464 | tf_op jit(solution)/shard_map/ppermute | solution.py:286
  116.2 4.7 %collective-permute-start.29 = (bf16[6,16,256]{2,1,0:T(8,128)(2,1)S(1)}, bf16[6,16,256]{2,1,0:T(8,128)(2,1)S(1)}, u32[]{:S(2)}, u32[]{:S(2)}) collective-permute-start(bf16[6,16,256]{2,1,0:T(8,128)(2,1)S(1)} %get-tuple-element.280), channel_id=1, source_target_pairs={{0,9},{1,8},{2,11},{3,10},{4,13},{5,12},{6,15},{7,14},{8,1},{9,0},... | collective-permute-start | bytes 147464 | tf_op jit(solution)/shard_map/ppermute | solution.py:286
  116.4 10.0 %collective-permute-start.30 = (bf16[6,16,256]{2,1,0:T(8,128)(2,1)S(1)}, bf16[6,16,256]{2,1,0:T(8,128)(2,1)S(1)}, u32[]{:S(2)}, u32[]{:S(2)}) collective-permute-start(bf16[6,16,256]{2,1,0:T(8,128)(2,1)S(1)} %get-tuple-element.281), channel_id=1, source_target_pairs={{0,1},{1,0},{2,3},{3,2},{4,5},{5,4},{6,7},{7,6},{8,9},{9,8},{10,11... | collective-permute-start | bytes 147464 | tf_op jit(solution)/shard_map/ppermute | solution.py:286
  116.7 9.6 %collective-permute-start.31 = (bf16[6,16,256]{2,1,0:T(8,128)(2,1)S(1)}, bf16[6,16,256]{2,1,0:T(8,128)(2,1)S(1)}, u32[]{:S(2)}, u32[]{:S(2)}) collective-permute-start(bf16[6,16,256]{2,1,0:T(8,128)(2,1)S(1)} %get-tuple-element.282), channel_id=1, source_target_pairs={{0,10},{1,11},{2,8},{3,9},{4,14},{5,15},{6,12},{7,13},{8,2},{9,3},... | collective-permute-start | bytes 147464 | tf_op jit(solution)/shard_map/ppermute | solution.py:286
  120.0 6.9 %collective-permute-start.32 = (bf16[6,16,256]{2,1,0:T(8,128)(2,1)S(1)}, bf16[6,16,256]{2,1,0:T(8,128)(2,1)S(1)}, u32[]{:S(2)}, u32[]{:S(2)}) collective-permute-start(bf16[6,16,256]{2,1,0:T(8,128)(2,1)S(1)} %get-tuple-element.283), channel_id=1, source_target_pairs={{0,2},{1,3},{2,0},{3,1},{4,6},{5,7},{6,4},{7,5},{8,10},{9,11},{10,... | collective-permute-start | bytes 147464 | tf_op jit(solution)/shard_map/ppermute | solution.py:286
  120.9 7.4 %collective-permute-start.33 = (bf16[6,16,256]{2,1,0:T(8,128)(2,1)S(1)}, bf16[6,16,256]{2,1,0:T(8,128)(2,1)S(1)}, u32[]{:S(2)}, u32[]{:S(2)}) collective-permute-start(bf16[6,16,256]{2,1,0:T(8,128)(2,1)S(1)} %get-tuple-element.284), channel_id=1, source_target_pairs={{0,11},{1,10},{2,9},{3,8},{4,15},{5,14},{6,13},{7,12},{8,3},{9,2},... | collective-permute-start | bytes 147464 | tf_op jit(solution)/shard_map/ppermute | solution.py:286
  126.3 3.8 %collective-permute-start.34 = (bf16[6,16,256]{2,1,0:T(8,128)(2,1)S(1)}, bf16[6,16,256]{2,1,0:T(8,128)(2,1)S(1)}, u32[]{:S(2)}, u32[]{:S(2)}) collective-permute-start(bf16[6,16,256]{2,1,0:T(8,128)(2,1)S(1)} %get-tuple-element.285), channel_id=1, source_target_pairs={{0,3},{1,2},{2,1},{3,0},{4,7},{5,6},{6,5},{7,4},{8,11},{9,10},{10,... | collective-permute-start | bytes 147464 | tf_op jit(solution)/shard_map/ppermute | solution.py:286
  126.4 5.8 %collective-permute-start.35 = (bf16[6,16,256]{2,1,0:T(8,128)(2,1)S(1)}, bf16[6,16,256]{2,1,0:T(8,128)(2,1)S(1)}, u32[]{:S(2)}, u32[]{:S(2)}) collective-permute-start(bf16[6,16,256]{2,1,0:T(8,128)(2,1)S(1)} %get-tuple-element.286), channel_id=1, source_target_pairs={{0,12},{1,13},{2,14},{3,15},{4,8},{5,9},{6,10},{7,11},{8,4},{9,5},... | collective-permute-start | bytes 147464 | tf_op jit(solution)/shard_map/ppermute | solution.py:286
  126.9 6.7 %collective-permute-start.36 = (bf16[6,16,256]{2,1,0:T(8,128)(2,1)S(1)}, bf16[6,16,256]{2,1,0:T(8,128)(2,1)S(1)}, u32[]{:S(2)}, u32[]{:S(2)}) collective-permute-start(bf16[6,16,256]{2,1,0:T(8,128)(2,1)S(1)} %get-tuple-element.287), channel_id=1, source_target_pairs={{0,4},{1,5},{2,6},{3,7},{4,0},{5,1},{6,2},{7,3},{8,12},{9,13},{10,... | collective-permute-start | bytes 147464 | tf_op jit(solution)/shard_map/ppermute | solution.py:286
  128.3 5.8 %collective-permute-start.37 = (bf16[6,16,256]{2,1,0:T(8,128)(2,1)S(1)}, bf16[6,16,256]{2,1,0:T(8,128)(2,1)S(1)}, u32[]{:S(2)}, u32[]{:S(2)}) collective-permute-start(bf16[6,16,256]{2,1,0:T(8,128)(2,1)S(1)} %get-tuple-element.288), channel_id=1, source_target_pairs={{0,13},{1,12},{2,15},{3,14},{4,9},{5,8},{6,11},{7,10},{8,5},{9,4},... | collective-permute-start | bytes 147464 | tf_op jit(solution)/shard_map/ppermute | solution.py:286
  130.2 9.3 %collective-permute-start.38 = (bf16[6,16,256]{2,1,0:T(8,128)(2,1)S(1)}, bf16[6,16,256]{2,1,0:T(8,128)(2,1)S(1)}, u32[]{:S(2)}, u32[]{:S(2)}) collective-permute-start(bf16[6,16,256]{2,1,0:T(8,128)(2,1)S(1)} %get-tuple-element.289), channel_id=1, source_target_pairs={{0,5},{1,4},{2,7},{3,6},{4,1},{5,0},{6,3},{7,2},{8,13},{9,12},{10,... | collective-permute-start | bytes 147464 | tf_op jit(solution)/shard_map/ppermute | solution.py:286
  132.2 7.4 %collective-permute-start.39 = (bf16[6,16,256]{2,1,0:T(8,128)(2,1)S(1)}, bf16[6,16,256]{2,1,0:T(8,128)(2,1)S(1)}, u32[]{:S(2)}, u32[]{:S(2)}) collective-permute-start(bf16[6,16,256]{2,1,0:T(8,128)(2,1)S(1)} %get-tuple-element.290), channel_id=1, source_target_pairs={{0,14},{1,15},{2,12},{3,13},{4,10},{5,11},{6,8},{7,9},{8,6},{9,7},... | collective-permute-start | bytes 147464 | tf_op jit(solution)/shard_map/ppermute | solution.py:286
  133.6 8.7 %collective-permute-start.40 = (bf16[6,16,256]{2,1,0:T(8,128)(2,1)S(1)}, bf16[6,16,256]{2,1,0:T(8,128)(2,1)S(1)}, u32[]{:S(2)}, u32[]{:S(2)}) collective-permute-start(bf16[6,16,256]{2,1,0:T(8,128)(2,1)S(1)} %get-tuple-element.291), channel_id=1, source_target_pairs={{0,6},{1,7},{2,4},{3,5},{4,2},{5,3},{6,0},{7,1},{8,14},{9,15},{10,... | collective-permute-start | bytes 147464 | tf_op jit(solution)/shard_map/ppermute | solution.py:286
  134.1 8.3 %collective-permute-start.41 = (bf16[6,16,256]{2,1,0:T(8,128)(2,1)S(1)}, bf16[6,16,256]{2,1,0:T(8,128)(2,1)S(1)}, u32[]{:S(2)}, u32[]{:S(2)}) collective-permute-start(bf16[6,16,256]{2,1,0:T(8,128)(2,1)S(1)} %get-tuple-element.292), channel_id=1, source_target_pairs={{0,15},{1,14},{2,13},{3,12},{4,11},{5,10},{6,9},{7,8},{8,7},{9,6},... | collective-permute-start | bytes 147464 | tf_op jit(solution)/shard_map/ppermute | solution.py:286
  137.2 7.1 %collective-permute-start.42 = (bf16[6,16,256]{2,1,0:T(8,128)(2,1)S(1)}, bf16[6,16,256]{2,1,0:T(8,128)(2,1)S(1)}, u32[]{:S(2)}, u32[]{:S(2)}) collective-permute-start(bf16[6,16,256]{2,1,0:T(8,128)(2,1)S(1)} %get-tuple-element.293), channel_id=1, source_target_pairs={{0,7},{1,6},{2,5},{3,4},{4,3},{5,2},{6,1},{7,0},{8,15},{9,14},{10,... | collective-permute-start | bytes 147464 | tf_op jit(solution)/shard_map/ppermute | solution.py:286
  139.5 5.1 %collective-permute-start.46 = (bf16[6,16,256]{2,1,0:T(8,128)(2,1)S(1)}, bf16[6,16,256]{2,1,0:T(8,128)(2,1)S(1)}, u32[]{:S(2)}, u32[]{:S(2)}) collective-permute-start(bf16[6,16,256]{2,1,0:T(8,128)(2,1)S(1)} %get-tuple-element.301), channel_id=1, source_target_pairs={{0,8},{1,9},{2,10},{3,11},{4,12},{5,13},{6,14},{7,15},{8,0},{9,1},... | collective-permute-start | bytes 147464 | tf_op jit(solution)/shard_map/ppermute | solution.py:286
  139.6 8.1 %collective-permute-start.47 = (bf16[6,16,256]{2,1,0:T(8,128)(2,1)S(1)}, bf16[6,16,256]{2,1,0:T(8,128)(2,1)S(1)}, u32[]{:S(2)}, u32[]{:S(2)}) collective-permute-start(bf16[6,16,256]{2,1,0:T(8,128)(2,1)S(1)} %get-tuple-element.303), channel_id=1, source_target_pairs={{0,9},{1,8},{2,11},{3,10},{4,13},{5,12},{6,15},{7,14},{8,1},{9,0},... | collective-permute-start | bytes 147464 | tf_op jit(solution)/shard_map/ppermute | solution.py:286
  142.3 5.4 %collective-permute-start.48 = (bf16[6,16,256]{2,1,0:T(8,128)(2,1)S(1)}, bf16[6,16,256]{2,1,0:T(8,128)(2,1)S(1)}, u32[]{:S(2)}, u32[]{:S(2)}) collective-permute-start(bf16[6,16,256]{2,1,0:T(8,128)(2,1)S(1)} %get-tuple-element.304), channel_id=1, source_target_pairs={{0,1},{1,0},{2,3},{3,2},{4,5},{5,4},{6,7},{7,6},{8,9},{9,8},{10,11... | collective-permute-start | bytes 147464 | tf_op jit(solution)/shard_map/ppermute | solution.py:286
  142.4 5.9 %collective-permute-start.49 = (bf16[6,16,256]{2,1,0:T(8,128)(2,1)S(1)}, bf16[6,16,256]{2,1,0:T(8,128)(2,1)S(1)}, u32[]{:S(2)}, u32[]{:S(2)}) collective-permute-start(bf16[6,16,256]{2,1,0:T(8,128)(2,1)S(1)} %get-tuple-element.305), channel_id=1, source_target_pairs={{0,10},{1,11},{2,8},{3,9},{4,14},{5,15},{6,12},{7,13},{8,2},{9,3},... | collective-permute-start | bytes 147464 | tf_op jit(solution)/shard_map/ppermute | solution.py:286
  144.3 7.2 %collective-permute-start.50 = (bf16[6,16,256]{2,1,0:T(8,128)(2,1)S(1)}, bf16[6,16,256]{2,1,0:T(8,128)(2,1)S(1)}, u32[]{:S(2)}, u32[]{:S(2)}) collective-permute-start(bf16[6,16,256]{2,1,0:T(8,128)(2,1)S(1)} %get-tuple-element.306), channel_id=1, source_target_pairs={{0,2},{1,3},{2,0},{3,1},{4,6},{5,7},{6,4},{7,5},{8,10},{9,11},{10,... | collective-permute-start | bytes 147464 | tf_op jit(solution)/shard_map/ppermute | solution.py:286
  144.6 8.6 %collective-permute-start.51 = (bf16[6,16,256]{2,1,0:T(8,128)(2,1)S(1)}, bf16[6,16,256]{2,1,0:T(8,128)(2,1)S(1)}, u32[]{:S(2)}, u32[]{:S(2)}) collective-permute-start(bf16[6,16,256]{2,1,0:T(8,128)(2,1)S(1)} %get-tuple-element.307), channel_id=1, source_target_pairs={{0,11},{1,10},{2,9},{3,8},{4,15},{5,14},{6,13},{7,12},{8,3},{9,2},... | collective-permute-start | bytes 147464 | tf_op jit(solution)/shard_map/ppermute | solution.py:286
  147.7 6.1 %collective-permute-start.52 = (bf16[6,16,256]{2,1,0:T(8,128)(2,1)S(1)}, bf16[6,16,256]{2,1,0:T(8,128)(2,1)S(1)}, u32[]{:S(2)}, u32[]{:S(2)}) collective-permute-start(bf16[6,16,256]{2,1,0:T(8,128)(2,1)S(1)} %get-tuple-element.308), channel_id=1, source_target_pairs={{0,3},{1,2},{2,1},{3,0},{4,7},{5,6},{6,5},{7,4},{8,11},{9,10},{10,... | collective-permute-start | bytes 147464 | tf_op jit(solution)/shard_map/ppermute | solution.py:286
  147.7 6.9 %collective-permute-start.53 = (bf16[6,16,256]{2,1,0:T(8,128)(2,1)S(1)}, bf16[6,16,256]{2,1,0:T(8,128)(2,1)S(1)}, u32[]{:S(2)}, u32[]{:S(2)}) collective-permute-start(bf16[6,16,256]{2,1,0:T(8,128)(2,1)S(1)} %get-tuple-element.309), channel_id=1, source_target_pairs={{0,12},{1,13},{2,14},{3,15},{4,8},{5,9},{6,10},{7,11},{8,4},{9,5},... | collective-permute-start | bytes 147464 | tf_op jit(solution)/shard_map/ppermute | solution.py:286
  148.3 8.3 %collective-permute-start.54 = (bf16[6,16,256]{2,1,0:T(8,128)(2,1)S(1)}, bf16[6,16,256]{2,1,0:T(8,128)(2,1)S(1)}, u32[]{:S(2)}, u32[]{:S(2)}) collective-permute-start(bf16[6,16,256]{2,1,0:T(8,128)(2,1)S(1)} %get-tuple-element.310), channel_id=1, source_target_pairs={{0,4},{1,5},{2,6},{3,7},{4,0},{5,1},{6,2},{7,3},{8,12},{9,13},{10,... | collective-permute-start | bytes 147464 | tf_op jit(solution)/shard_map/ppermute | solution.py:286
  151.5 7.0 %collective-permute-start.55 = (bf16[6,16,256]{2,1,0:T(8,128)(2,1)S(1)}, bf16[6,16,256]{2,1,0:T(8,128)(2,1)S(1)}, u32[]{:S(2)}, u32[]{:S(2)}) collective-permute-start(bf16[6,16,256]{2,1,0:T(8,128)(2,1)S(1)} %get-tuple-element.311), channel_id=1, source_target_pairs={{0,13},{1,12},{2,15},{3,14},{4,9},{5,8},{6,11},{7,10},{8,5},{9,4},... | collective-permute-start | bytes 147464 | tf_op jit(solution)/shard_map/ppermute | solution.py:286
  153.2 6.6 %collective-permute-start.56 = (bf16[6,16,256]{2,1,0:T(8,128)(2,1)S(1)}, bf16[6,16,256]{2,1,0:T(8,128)(2,1)S(1)}, u32[]{:S(2)}, u32[]{:S(2)}) collective-permute-start(bf16[6,16,256]{2,1,0:T(8,128)(2,1)S(1)} %get-tuple-element.312), channel_id=1, source_target_pairs={{0,5},{1,4},{2,7},{3,6},{4,1},{5,0},{6,3},{7,2},{8,13},{9,12},{10,... | collective-permute-start | bytes 147464 | tf_op jit(solution)/shard_map/ppermute | solution.py:286
  153.8 5.9 %collective-permute-start.57 = (bf16[6,16,256]{2,1,0:T(8,128)(2,1)S(1)}, bf16[6,16,256]{2,1,0:T(8,128)(2,1)S(1)}, u32[]{:S(2)}, u32[]{:S(2)}) collective-permute-start(bf16[6,16,256]{2,1,0:T(8,128)(2,1)S(1)} %get-tuple-element.313), channel_id=1, source_target_pairs={{0,14},{1,15},{2,12},{3,13},{4,10},{5,11},{6,8},{7,9},{8,6},{9,7},... | collective-permute-start | bytes 147464 | tf_op jit(solution)/shard_map/ppermute | solution.py:286
  154.7 5.1 %collective-permute-start.58 = (bf16[6,16,256]{2,1,0:T(8,128)(2,1)S(1)}, bf16[6,16,256]{2,1,0:T(8,128)(2,1)S(1)}, u32[]{:S(2)}, u32[]{:S(2)}) collective-permute-start(bf16[6,16,256]{2,1,0:T(8,128)(2,1)S(1)} %get-tuple-element.314), channel_id=1, source_target_pairs={{0,6},{1,7},{2,4},{3,5},{4,2},{5,3},{6,0},{7,1},{8,14},{9,15},{10,... | collective-permute-start | bytes 147464 | tf_op jit(solution)/shard_map/ppermute | solution.py:286
  156.6 4.4 %collective-permute-start.59 = (bf16[6,16,256]{2,1,0:T(8,128)(2,1)S(1)}, bf16[6,16,256]{2,1,0:T(8,128)(2,1)S(1)}, u32[]{:S(2)}, u32[]{:S(2)}) collective-permute-start(bf16[6,16,256]{2,1,0:T(8,128)(2,1)S(1)} %get-tuple-element.315), channel_id=1, source_target_pairs={{0,15},{1,14},{2,13},{3,12},{4,11},{5,10},{6,9},{7,8},{8,7},{9,6},... | collective-permute-start | bytes 147464 | tf_op jit(solution)/shard_map/ppermute | solution.py:286
  158.5 5.1 %collective-permute-start.60 = (bf16[6,16,256]{2,1,0:T(8,128)(2,1)S(1)}, bf16[6,16,256]{2,1,0:T(8,128)(2,1)S(1)}, u32[]{:S(2)}, u32[]{:S(2)}) collective-permute-start(bf16[6,16,256]{2,1,0:T(8,128)(2,1)S(1)} %get-tuple-element.316), channel_id=1, source_target_pairs={{0,7},{1,6},{2,5},{3,4},{4,3},{5,2},{6,1},{7,0},{8,15},{9,14},{10,... | collective-permute-start | bytes 147464 | tf_op jit(solution)/shard_map/ppermute | solution.py:286

commit v9 on v7

--- a/solution.py
+++ b/solution.py
@@ -177,37 +177,67 @@
     return (pairs, new[-1]) if keep else pairs
 
 
-def finish_kernel(place_ref, *refs):
-    out_ref = refs[-1]
-    mine, theirs = refs[:HALVES], refs[HALVES:-1]
-    count, planes, slots, naux = out_ref.shape
-    norb, _, width = mine[0].shape
-    for i in range(norb):
-        for j in range(HALVES):
-            back = (mine[j][i] + theirs[j][i]).astype(jnp.bfloat16)
-            out = jnp.dot(place_ref[...], back, preferred_element_type=jnp.float32)
-            out = out.astype(jnp.bfloat16).reshape(count, planes // norb, slots, width)
-            out_ref[
-                :, pl.ds(i * (planes // norb), planes // norb), :, pl.ds(j * width, width)
-            ] = out
-
-
-def finish(place, mine, theirs, shape):
+def finish_kernel(half, place_ref, mine_ref, theirs_ref, *refs):
+    out_hbm, buf, sems = refs[-3:]
+    norb, _, width = mine_ref.shape
+    _, planes, slots, _ = out_hbm.shape
+    columns = pl.ds(half * width, width)
+    copies = []
+    for i in range(norb):
+        back = (mine_ref[i] + theirs_ref[i]).astype(jnp.bfloat16)
+        out = jnp.dot(place_ref[...], back, preferred_element_type=jnp.float32)
+        plane = pl.ds(i * (planes // norb), planes // norb)
+        buf[:, plane] = out.astype(jnp.bfloat16).reshape(-1, planes // norb, slots, width)
+        copies.append(
+            pltpu.make_async_copy(
+                buf.at[:, plane], out_hbm.at[:, plane, :, columns], sems.at[i]
+            )
+        )
+        copies[i].start()
+    for copy in copies:
+        copy.wait()
+
+
+def finish(half, place, mine, theirs, before, shape):
+    vmem = pl.BlockSpec(memory_space=pltpu.VMEM)
+    hbm = pl.BlockSpec(memory_space=pltpu.HBM)
+    norb, _, width = mine.shape
     return pl.pallas_call(
-        finish_kernel,
+        functools.partial(finish_kernel, half),
         out_shape=jax.ShapeDtypeStruct(shape, jnp.bfloat16),
-        in_specs=[pl.BlockSpec(memory_space=pltpu.VMEM)] * (1 + len(mine) + len(theirs)),
-        out_specs=pl.BlockSpec(memory_space=pltpu.VMEM),
+        in_specs=[vmem] * 3 + [hbm] * len(before),
+        out_specs=hbm,
+        input_output_aliases={3: 0} if before else {},
+        scratch_shapes=[
+            pltpu.VMEM(shape[:3] + (width,), jnp.bfloat16),
+            pltpu.SemaphoreType.DMA((norb,)),
+        ],
         compiler_params=pltpu.CompilerParams(vmem_limit_bytes=20 << 20),
         cost_estimate=pl.CostEstimate(
-            flops=2 * math.prod(shape) * place.shape[1],
+            flops=math.prod(shape) * place.shape[1],
             bytes_accessed=2 * math.prod(shape),
             transcendentals=0,
         ),
-    )(place, *mine, *theirs)
-
-
-def ring_products(gamma, coefficients, early):
+    )(place, mine, theirs, *before)
+
+
+def store_kernel(value_ref, out_hbm, sem):
+    copy = pltpu.make_async_copy(value_ref, out_hbm, sem)
+    copy.start()
+    copy.wait()
+
+
+def store(value):
+    return pl.pallas_call(
+        store_kernel,
+        out_shape=jax.ShapeDtypeStruct(value.shape, value.dtype),
+        in_specs=[pl.BlockSpec(memory_space=pltpu.VMEM)],
+        out_specs=pl.BlockSpec(memory_space=pltpu.HBM),
+        scratch_shapes=[pltpu.SemaphoreType.DMA],
+    )(value)
+
+
+def ring_products(gamma, coefficients, ids, place, shape):
     count = lax.axis_size("wide")
     norb, depth, naux = gamma.shape
     width = naux // HALVES
@@ -237,7 +267,7 @@
             for i in range(norb):
                 sent = piece[j][i]
                 if t == 2 and i == j == 0:
-                    sent, early = lax.optimization_barrier((sent, early))
+                    sent, ids, place = lax.optimization_barrier((sent, ids, place))
                 if BEHIND[t][j]:
                     sent, sums = lax.optimization_barrier((sent, sums))
                 piece[j][i] = lax.ppermute(sent, "wide", shift[i])
@@ -248,9 +278,11 @@
         done, coefficients, other, arrived[done][:1], sums[:1], keep=True
     )
     sums[1] = add_last_products(done, windows, arrived[done][1], sums[1])
-    mine = [sums[j][0] for j in range(HALVES)]
     theirs = [lax.ppermute(sums[j][1], "wide", swap) for j in range(HALVES)]
-    return mine, theirs, early
+    out = []
+    for j in range(HALVES):
+        out = [finish(j, place, sums[j][0], theirs[j], out, shape)]
+    return store(ids), out[0]
 
 
 def local(gamma, coefficients, owners):
@@ -264,8 +296,7 @@
     labels, place = routing(owners, count, slots, block_rows)
     ids = lax.all_to_all(labels, "wide", split_axis=0, concat_axis=0, tiled=True)
     if count == 2 * GRID_CHIPS and norb == len(WAYS):
-        mine, theirs, (ids, place) = ring_products(gamma, coefficients, (ids, place))
-        out = finish(place, mine, theirs, shape)
+        ids, out = ring_products(gamma, coefficients, ids, place, shape)
     else:
         gathered = lax.all_gather(gamma, "wide", axis=1, tiled=True)
         back = jnp.einsum(

time: 162 us -> 161 us (level)
  waiting for transfers between devices: 85.1 us -> 81.9 us
  Pallas kernels: 29.2 us -> 32.1 us
    pallas_call x1 -> x3, Pallas kernels: 2.14 us -> 5.05 us  [the longest x2 3.75 us: finish(): pl.pallas_call(functools.partial(finish_kernel, half), out_shape=jax.Shap...]
    ppermute x2, waiting for transfers between devices: 1.91 us -> 0.03 us  [ring_products(): theirs = [lax.ppermute(sums[j][1], 'wide', swap) for j in range(HALVES)]]
    unnamed x6 -> x7, local copies, waits for them, and re-layouts: 5.15 us -> 4.55 us
  transfers between devices with their start and end apart: 33 -> 33, of which waited for: 17 -> 16; matrix products, arithmetic and copies ran while one was open for 2% -> 2% of each run, Pallas kernels for 17% -> 19%
where the time goes in v9:
time: 161 us
  waiting for transfers between devices  81.9 us (51%)
  starting transfers between devices  38.6 us (24%)
  Pallas kernels  32.1 us (20%)
  local copies, waits for them, and re-layouts  6.92 us (4%)
    ppermute x28, waiting for transfers between devices, ring_products(): piece[j][i] = lax.ppermute(sent, 'wide', shift[i])  43.9 us
    all_to_all x1, waiting for transfers between devices, local(): lax.all_to_all(out, 'wide', split_axis=0, concat_axis=0, tiled=True)  34.9 us
    pallas_call x8, Pallas kernels, add_products(): pl.pallas_call(functools.partial(step_kernel, t, parts), out_shape=[sums]...  25.9 us
    ppermute x28, starting transfers between devices, ring_products(): piece[j][i] = lax.ppermute(sent, 'wide', shift[i])  20.7 us
    all_to_all x1, starting transfers between devices, local(): lax.all_to_all(labels, 'wide', split_axis=0, concat_axis=0, tiled=True)  7.02 us
    all_to_all x1, starting transfers between devices, local(): lax.all_to_all(out, 'wide', split_axis=0, concat_axis=0, tiled=True)  6.59 us
    unnamed x7, local copies, waits for them, and re-layouts  4.55 us
    pallas_call x2, Pallas kernels, finish(): pl.pallas_call(functools.partial(finish_kernel, half), out_shape=jax.Shap...  3.75 us
  transfers between devices with their start and end apart: 33, of which 16 were waited for; matrix products, arithmetic and copies ran while one was open for 2% of the time, Pallas kernels for 19%

profile of v9, /device:TPU:13, one launch (start us, length us, event | category | flops | bytes accessed | tf_op | source)
XLA Modules:
  0.0 160.9 jit_solution(6643162968026984466)
XLA Ops:
  0.6 0.7 collective-permute-start.2
  1.4 1.4 slice_bitcast_fusion
  2.8 0.2 collective-permute-start.11
  3.1 1.4 collective-permute-start
  4.5 1.3 collective-permute-start.6
  6.1 0.7 sub.17
  6.8 7.0 %all-to-all-start = ((s32[16,1,16]{2,1,0:T(1,128)}), s32[16,1,16]{2,1,0:T(1,128)S(1)}, u32[]{:S(2)}, u32[]{:S(2)}) async-start(s32[16,1,16]{2,1,0:T(1,128)} %sub.17), calls=%async_computation | async-start | bytes 16384 | tf_op jit(solution)/shard_map/all_to_all | solution.py:297
  13.9 0.2 mul.58
  14.1 0.3 collective-permute-start.12
  14.4 1.2 collective-permute-start.1
  15.6 4.6 %collective-permute-done.4.refs_3_ = bf16[688,256]{1,0:T(8,128)(2,1)S(1)} collective-permute-done((bf16[688,256]{1,0:T(8,128)(2,1)S(1)}, bf16[688,256]{1,0:T(8,128)(2,1)S(1)}, u32[]{:S(2)}, u32[]{:S(2)}) %collective-permute-start.4) | collective-permute-done | bytes 352288 | tf_op jit(solution)/shard_map/ppermute | solution.py:273
  20.2 0.2 collective-permute-start.5
  20.4 1.3 collective-permute-start.7
  21.9 3.1 %all-to-all-done = s32[16,1,16]{2,1,0:T(1,128)S(1)} async-done(((s32[16,1,16]{2,1,0:T(1,128)}), s32[16,1,16]{2,1,0:T(1,128)S(1)}, u32[]{:S(2)}, u32[]{:S(2)}) %all-to-all-start) | async-done | bytes 1056 | tf_op jit(solution)/shard_map/all_to_all | solution.py:297
  25.0 3.0 %collective-permute-done.1.refs_0_ = bf16[688,256]{1,0:T(8,128)(2,1)} collective-permute-done((bf16[688,256]{1,0:T(8,128)(2,1)S(1)}, bf16[688,256]{1,0:T(8,128)(2,1)}, u32[]{:S(2)}, u32[]{:S(2)}) %collective-permute-start.1) | collective-permute-done | bytes 352288 | tf_op jit(solution)/shard_map/ppermute | solution.py:273
  27.9 1.2 collective-permute-start.3
  29.1 0.3 collective-permute-start.13
  29.4 3.4 %copy-done = bf16[384,11008]{1,0:T(8,128)(2,1)S(1)} copy-done((bf16[384,11008]{1,0:T(8,128)(2,1)S(1)}, bf16[384,11008]{1,0:T(8,128)(2,1)}, u32[]{:S(2)}) %copy-start) | copy-done | bytes 8454168
  32.8 3.1 %shard_map.50 = (f32[2,384,256]{2,1,0:T(8,128)S(1)}, f32[2,384,256]{2,1,0:T(8,128)S(1)}, f32[2,384,256]{2,1,0:T(8,128)S(1)}, f32[2,384,256]{2,1,0:T(8,128)S(1)}) custom-call(bf16[384,11008]{1,0:T(8,128)(2,1)S(1)} %copy-done, bf16[384,11008]{1,0:T(8,128)(2,1)} %collective-permute-done.2.other_hbm, bf16[688,256]{1,0:T(8,128)(2,1)S(1)} %get-tuple-element.258.refs_0_, ...), custom_call_target="tpu_custom_call" | custom-call | flops 1409286144 | bytes 2752512 | tf_op jit(solution)/shard_map/pallas_call | solution.py:158
  36.0 1.2 collective-permute-start.10
  37.2 0.3 collective-permute-start.9
  37.5 5.4 %collective-permute-done.3.refs_0_ = bf16[688,256]{1,0:T(8,128)(2,1)S(1)} collective-permute-done((bf16[688,256]{1,0:T(8,128)(2,1)}, bf16[688,256]{1,0:T(8,128)(2,1)S(1)}, u32[]{:S(2)}, u32[]{:S(2)}) %collective-permute-start.3) | collective-permute-done | bytes 352288 | tf_op jit(solution)/shard_map/ppermute | solution.py:273
  42.9 1.2 collective-permute-start.8
  44.1 0.3 collective-permute-start.17
  44.4 3.2 %shard_map.51 = (f32[2,384,256]{2,1,0:T(8,128)S(1)}, f32[2,384,256]{2,1,0:T(8,128)S(1)}, f32[2,384,256]{2,1,0:T(8,128)S(1)}, f32[2,384,256]{2,1,0:T(8,128)S(1)}) custom-call(bf16[384,11008]{1,0:T(8,128)(2,1)S(1)} %copy-done, ...), custom_call_target="tpu_custom_call", output_to_operand_aliasing={{0}: (6, {}), {1}: (7, {}), {2}: (8, {}), {3}: (9, {})} | custom-call | flops 1409286144 | bytes 2752512 | tf_op jit(solution)/shard_map/pallas_call | solution.py:158
  47.6 2.9 %collective-permute-done.10.refs_2_ = bf16[688,256]{1,0:T(8,128)(2,1)S(1)} collective-permute-done((bf16[688,256]{1,0:T(8,128)(2,1)}, bf16[688,256]{1,0:T(8,128)(2,1)S(1)}, u32[]{:S(2)}, u32[]{:S(2)}) %collective-permute-start.10) | collective-permute-done | bytes 352288 | tf_op jit(solution)/shard_map/ppermute | solution.py:273
  50.5 1.2 collective-permute-start.16
  51.6 0.3 collective-permute-start.15
  51.9 6.1 %collective-permute-done.8.refs_0_ = bf16[688,256]{1,0:T(8,128)(2,1)S(1)} collective-permute-done((bf16[688,256]{1,0:T(8,128)(2,1)S(1)}, bf16[688,256]{1,0:T(8,128)(2,1)S(1)}, u32[]{:S(2)}, u32[]{:S(2)}) %collective-permute-start.8) | collective-permute-done | bytes 352288 | tf_op jit(solution)/shard_map/ppermute | solution.py:273
  58.1 1.0 collective-permute-start.21
  59.1 0.4 collective-permute-start.14
  59.5 4.5 %shard_map.52 = (f32[2,384,256]{2,1,0:T(8,128)S(1)}, f32[2,384,256]{2,1,0:T(8,128)S(1)}, f32[2,384,256]{2,1,0:T(8,128)S(1)}, f32[2,384,256]{2,1,0:T(8,128)S(1)}) custom-call(bf16[384,11008]{1,0:T(8,128)(2,1)S(1)} %copy-done, ...), custom_call_target="tpu_custom_call", output_to_operand_aliasing={{0}: (6, {}), {1}: (7, {}), {2}: (8, {}), {3}: (9, {})} | custom-call | flops 1409286144 | bytes 2752512 | tf_op jit(solution)/shard_map/pallas_call | solution.py:158
  64.0 3.2 %shard_map.53 = (f32[2,384,256]{2,1,0:T(8,128)S(1)}, f32[2,384,256]{2,1,0:T(8,128)S(1)}, f32[2,384,256]{2,1,0:T(8,128)S(1)}, f32[2,384,256]{2,1,0:T(8,128)S(1)}) custom-call(bf16[384,11008]{1,0:T(8,128)(2,1)S(1)} %copy-done, ...), custom_call_target="tpu_custom_call", output_to_operand_aliasing={{0}: (6, {}), {1}: (7, {}), {2}: (8, {}), {3}: (9, {})} | custom-call | flops 1409286144 | bytes 2752512 | tf_op jit(solution)/shard_map/pallas_call | solution.py:158
  67.3 1.3 collective-permute-start.20
  68.6 0.2 collective-permute-start.19
  68.8 4.3 %collective-permute-done.14.refs_0_ = bf16[688,256]{1,0:T(8,128)(2,1)S(1)} collective-permute-done((bf16[688,256]{1,0:T(8,128)(2,1)S(1)}, bf16[688,256]{1,0:T(8,128)(2,1)S(1)}, u32[]{:S(2)}, u32[]{:S(2)}) %collective-permute-start.14) | collective-permute-done | bytes 352288 | tf_op jit(solution)/shard_map/ppermute | solution.py:273
  73.1 1.2 collective-permute-start.18
  74.3 0.3 collective-permute-start.23
  74.6 3.2 %shard_map.54 = (f32[2,384,256]{2,1,0:T(8,128)S(1)}, f32[2,384,256]{2,1,0:T(8,128)S(1)}, f32[2,384,256]{2,1,0:T(8,128)S(1)}, f32[2,384,256]{2,1,0:T(8,128)S(1)}) custom-call(bf16[384,11008]{1,0:T(8,128)(2,1)S(1)} %copy-done, ...), custom_call_target="tpu_custom_call", output_to_operand_aliasing={{0}: (6, {}), {1}: (7, {}), {2}: (8, {}), {3}: (9, {})} | custom-call | flops 1409286144 | bytes 2752512 | tf_op jit(solution)/shard_map/pallas_call | solution.py:158
  77.8 2.9 %collective-permute-done.20.refs_2_ = bf16[688,256]{1,0:T(8,128)(2,1)S(1)} collective-permute-done((bf16[688,256]{1,0:T(8,128)(2,1)S(1)}, bf16[688,256]{1,0:T(8,128)(2,1)S(1)}, u32[]{:S(2)}, u32[]{:S(2)}) %collective-permute-start.20) | collective-permute-done | bytes 352288 | tf_op jit(solution)/shard_map/ppermute | solution.py:273
  80.7 1.2 collective-permute-start.25
  81.8 0.3 collective-permute-start.26
  82.1 6.1 %collective-permute-done.18.refs_0_ = bf16[688,256]{1,0:T(8,128)(2,1)S(1)} collective-permute-done((bf16[688,256]{1,0:T(8,128)(2,1)S(1)}, bf16[688,256]{1,0:T(8,128)(2,1)S(1)}, u32[]{:S(2)}, u32[]{:S(2)}) %collective-permute-start.18) | collective-permute-done | bytes 352288 | tf_op jit(solution)/shard_map/ppermute | solution.py:273
  88.2 1.1 collective-permute-start.24
  89.3 0.4 collective-permute-start.22
  89.7 3.2 %shard_map.55 = (f32[2,384,256]{2,1,0:T(8,128)S(1)}, f32[2,384,256]{2,1,0:T(8,128)S(1)}, f32[2,384,256]{2,1,0:T(8,128)S(1)}, f32[2,384,256]{2,1,0:T(8,128)S(1)}) custom-call(bf16[384,11008]{1,0:T(8,128)(2,1)S(1)} %copy-done, ...), custom_call_target="tpu_custom_call", output_to_operand_aliasing={{0}: (6, {}), {1}: (7, {}), {2}: (8, {}), {3}: (9, {})} | custom-call | flops 1409286144 | bytes 2752512 | tf_op jit(solution)/shard_map/pallas_call | solution.py:158
  92.9 2.9 %collective-permute-done.25.refs_2_ = bf16[688,256]{1,0:T(8,128)(2,1)S(1)} collective-permute-done((bf16[688,256]{1,0:T(8,128)(2,1)S(1)}, bf16[688,256]{1,0:T(8,128)(2,1)S(1)}, u32[]{:S(2)}, u32[]{:S(2)}) %collective-permute-start.25) | collective-permute-done | bytes 352288 | tf_op jit(solution)/shard_map/ppermute | solution.py:273
  95.8 1.1 collective-permute-start.28
  96.9 0.4 collective-permute-start.27
  97.2 3.2 %shard_map.56 = (f32[2,384,256]{2,1,0:T(8,128)S(1)}, f32[2,384,256]{2,1,0:T(8,128)S(1)}, f32[2,384,256]{2,1,0:T(8,128)S(1)}, f32[2,384,256]{2,1,0:T(8,128)S(1)}) custom-call(bf16[384,11008]{1,0:T(8,128)(2,1)S(1)} %copy-done, ...), custom_call_target="tpu_custom_call", output_to_operand_aliasing={{0}: (6, {}), {1}: (7, {}), {2}: (8, {}), {3}: (9, {})} | custom-call | flops 1409286144 | bytes 2752512 | tf_op jit(solution)/shard_map/pallas_call | solution.py:158
  100.4 2.1 %collective-permute-done.24.refs_1_ = bf16[688,256]{1,0:T(8,128)(2,1)S(1)} collective-permute-done((bf16[688,256]{1,0:T(8,128)(2,1)S(1)}, bf16[688,256]{1,0:T(8,128)(2,1)S(1)}, u32[]{:S(2)}, u32[]{:S(2)}) %collective-permute-start.24) | collective-permute-done | bytes 352288 | tf_op jit(solution)/shard_map/ppermute | solution.py:273
  102.5 0.8 collective-permute-done.22.refs_0_
  103.3 2.4 %shard_map.57 = (f32[2,384,256]{2,1,0:T(8,128)S(1)}, f32[2,384,256]{2,1,0:T(8,128)S(1)}, bf16[2,768,896]{2,1,0:T(8,128)(2,1)S(1)}) custom-call(bf16[384,11008]{1,0:T(8,128)(2,1)S(1)} %copy-done, bf16[384,11008]{1,0:T(8,128)(2,1)} %collective-permute-done.2.other_hbm, ...), custom_call_target="tpu_custom_call", output_to_operand_aliasing={{0}: (4, {}), {1}: (5, {})} | custom-call | flops 704643072 | bytes 2752512 | tf_op jit(solution)/shard_map/pallas_call | solution.py:158
  105.7 2.3 %collective-permute-start.30 = (f32[2,384,256]{2,1,0:T(8,128)S(1)}, f32[2,384,256]{2,1,0:T(8,128)S(1)}, u32[]{:S(2)}, u32[]{:S(2)}) collective-permute-start(f32[2,384,256]{2,1,0:T(8,128)S(1)} %get-tuple-element.252), channel_id=1, source_target_pairs={{0,1},{1,0},{2,3},{3,2},{4,5},{5,4},{6,7},{7,6},{8,9},{9,8},{10,11... | collective-permute-start | bytes 2359304 | tf_op jit(solution)/shard_map/ppermute | solution.py:281
  108.0 2.1 %collective-permute-done.28.refs_1_ = bf16[688,256]{1,0:T(8,128)(2,1)S(1)} collective-permute-done((bf16[688,256]{1,0:T(8,128)(2,1)S(1)}, bf16[688,256]{1,0:T(8,128)(2,1)S(1)}, u32[]{:S(2)}, u32[]{:S(2)}) %collective-permute-start.28) | collective-permute-done | bytes 352288 | tf_op jit(solution)/shard_map/ppermute | solution.py:273
  110.1 0.8 collective-permute-done.27.refs_0_
  110.9 1.1 shard_map.58
  112.0 1.2 collective-permute-start.29
  113.2 1.9 %shard_map.59.refs_0_ = bf16[16,6,16,512]{3,2,1,0:T(8,128)(2,1)} custom-call(bf16[768,384]{1,0:T(8,128)(2,1)S(1)} %compare_convert_fusion.place_ref, f32[2,384,256]{2,1,0:T(8,128)S(1)} %get-tuple-element.251.mine_ref, f32[2,384,256]{2,1,0:T(8,128)S(1)} %collective-permute-done.30.theirs_ref), custom_call_target="tpu_custom_call" | custom-call | flops 301989888 | bytes 1572864 | tf_op jit(solution)/shard_map/pallas_call | solution.py:205
  115.1 1.9 %shard_map.60 = bf16[16,6,16,512]{3,2,1,0:T(8,128)(2,1)} custom-call(bf16[768,384]{1,0:T(8,128)(2,1)S(1)} %compare_convert_fusion.place_ref, f32[2,384,256]{2,1,0:T(8,128)S(1)} %get-tuple-element.249.mine_ref, f32[2,384,256]{2,1,0:T(8,128)S(1)} %collective-permute-done.29.theirs_ref, ...), custom_call_target="tpu_custom_call", output_to_operand_aliasing={{}: (3, {})} | custom-call | flops 301989888 | bytes 1572864 | tf_op jit(solution)/shard_map/pallas_call | solution.py:205
  117.0 6.6 %all-to-all-start.1 = ((bf16[16,6,16,512]{3,2,1,0:T(8,128)(2,1)}), bf16[16,6,16,512]{3,2,1,0:T(8,128)(2,1)S(1)}, u32[]{:S(2)}, u32[]{:S(2)}) async-start(bf16[16,6,16,512]{3,2,1,0:T(8,128)(2,1)} %shard_map.60), calls=%async_computation.1 | async-start | bytes 3145728 | tf_op jit(solution)/shard_map/all_to_all | solution.py:308
  123.6 1.3 shard_map.61
  124.9 34.9 %all-to-all-done.1 = bf16[16,6,16,512]{3,2,1,0:T(8,128)(2,1)S(1)} async-done(((bf16[16,6,16,512]{3,2,1,0:T(8,128)(2,1)}), bf16[16,6,16,512]{3,2,1,0:T(8,128)(2,1)S(1)}, u32[]{:S(2)}, u32[]{:S(2)}) %all-to-all-start.1) | async-done | bytes 1572896 | tf_op jit(solution)/shard_map/all_to_all | solution.py:308
  159.7 1.1 copy.64
  (32 shorter events, 0.8 us)
Async XLA Ops:
  0.6 5.1 %copy-start.2 = (s32[128,1]{0,1:T(1,128)S(1)}, s32[128,1]{0,1:T(1,128)}, u32[]{:S(2)}) copy-start(s32[128,1]{0,1:T(1,128)} %param.5) | copy-start | bytes 1540
  0.6 28.8 %collective-permute-start.2 = (bf16[384,11008]{1,0:T(8,128)(2,1)}, bf16[384,11008]{1,0:T(8,128)(2,1)}, u32[]{:S(2)}, u32[]{:S(2)}) collective-permute-start(bf16[384,11008]{1,0:T(8,128)(2,1)} %own_hbm.15), channel_id=1, source_target_pairs={{0,1},{1,0},{2,3},{3,2},{4,5},{5,4},{6,7},{7,6},{8,9},{9,8},{10,11... | collective-permute-start | bytes 25362440 | tf_op jit(solution)/shard_map/ppermute | solution.py:245
  2.8 11.3 %collective-permute-start.11 = (bf16[688,256]{1,0:T(8,128)(2,1)S(1)}, bf16[688,256]{1,0:T(8,128)(2,1)S(1)}, u32[]{:S(2)}, u32[]{:S(2)}) collective-permute-start(bf16[688,256]{1,0:T(8,128)(2,1)S(1)} %get-tuple-element.256.refs_1_), channel_id=1, source_target_pairs={{0,4},{1,5},{2,0},{3,1},{6,2},{7,3},{10,6},{11,7},{14,10},{15,11},... | collective-permute-start | bytes 1056776 | tf_op jit(solution)/shard_map/ppermute | solution.py:273
  3.0 17.2 %collective-permute-start.4 = (bf16[688,256]{1,0:T(8,128)(2,1)S(1)}, bf16[688,256]{1,0:T(8,128)(2,1)S(1)}, u32[]{:S(2)}, u32[]{:S(2)}) collective-permute-start(bf16[688,256]{1,0:T(8,128)(2,1)S(1)} %get-tuple-element.257.refs_3_), channel_id=1, source_target_pairs={{0,4},{1,5},{2,0},{3,1},{6,2},{7,3},{10,6},{11,7},{14,10},{15,11},... | collective-permute-start | bytes 1056776 | tf_op jit(solution)/shard_map/ppermute | solution.py:273
  3.1 11.4 %collective-permute-start = (bf16[688,256]{1,0:T(8,128)(2,1)S(1)}, bf16[688,256]{1,0:T(8,128)(2,1)S(1)}, u32[]{:S(2)}, u32[]{:S(2)}) collective-permute-start(bf16[688,256]{1,0:T(8,128)(2,1)S(1)} %get-tuple-element.258.refs_0_), channel_id=1, source_target_pairs={{0,2},{1,3},{2,6},{3,7},{6,10},{7,11},{10,14},{11,15},{14,12},{15,... | collective-permute-start | bytes 1056776 | tf_op jit(solution)/shard_map/ppermute | solution.py:273
  4.5 15.9 %collective-permute-start.6 = (bf16[688,256]{1,0:T(8,128)(2,1)S(1)}, bf16[688,256]{1,0:T(8,128)(2,1)S(1)}, u32[]{:S(2)}, u32[]{:S(2)}) collective-permute-start(bf16[688,256]{1,0:T(8,128)(2,1)S(1)} %get-tuple-element.259.refs_2_), channel_id=1, source_target_pairs={{0,2},{1,3},{2,6},{3,7},{6,10},{7,11},{10,14},{11,15},{14,12},{15,... | collective-permute-start | bytes 1056776 | tf_op jit(solution)/shard_map/ppermute | solution.py:273
  6.8 18.2 %all-to-all-start = ((s32[16,1,16]{2,1,0:T(1,128)}), s32[16,1,16]{2,1,0:T(1,128)S(1)}, u32[]{:S(2)}, u32[]{:S(2)}) async-start(s32[16,1,16]{2,1,0:T(1,128)} %sub.17), calls=%async_computation | async-start | bytes 16384 | tf_op jit(solution)/shard_map/all_to_all | solution.py:297
  14.1 15.0 %collective-permute-start.12 = (bf16[688,256]{1,0:T(8,128)(2,1)S(1)}, bf16[688,256]{1,0:T(8,128)(2,1)}, u32[]{:S(2)}, u32[]{:S(2)}) collective-permute-start(bf16[688,256]{1,0:T(8,128)(2,1)S(1)} %collective-permute-done.11.refs_1_), channel_id=1, source_target_pairs={{0,4},{1,5},{2,0},{3,1},{6,2},{7,3},{10,6},{11,7},{14,10},{15,11},... | collective-permute-start | bytes 1056776 | tf_op jit(solution)/shard_map/ppermute | solution.py:273
  14.4 13.5 %collective-permute-start.1 = (bf16[688,256]{1,0:T(8,128)(2,1)S(1)}, bf16[688,256]{1,0:T(8,128)(2,1)}, u32[]{:S(2)}, u32[]{:S(2)}) collective-permute-start(bf16[688,256]{1,0:T(8,128)(2,1)S(1)} %collective-permute-done.refs_0_), channel_id=1, source_target_pairs={{0,2},{1,3},{2,6},{3,7},{6,10},{7,11},{10,14},{11,15},{14,12},{15,... | collective-permute-start | bytes 1056776 | tf_op jit(solution)/shard_map/ppermute | solution.py:273
  20.2 17.0 %collective-permute-start.5 = (bf16[688,256]{1,0:T(8,128)(2,1)S(1)}, bf16[688,256]{1,0:T(8,128)(2,1)}, u32[]{:S(2)}, u32[]{:S(2)}) collective-permute-start(bf16[688,256]{1,0:T(8,128)(2,1)S(1)} %collective-permute-done.4.refs_3_), channel_id=1, source_target_pairs={{0,4},{1,5},{2,0},{3,1},{6,2},{7,3},{10,6},{11,7},{14,10},{15,11},... | collective-permute-start | bytes 1056776 | tf_op jit(solution)/shard_map/ppermute | solution.py:273
  20.4 15.5 %collective-permute-start.7 = (bf16[688,256]{1,0:T(8,128)(2,1)S(1)}, bf16[688,256]{1,0:T(8,128)(2,1)}, u32[]{:S(2)}, u32[]{:S(2)}) collective-permute-start(bf16[688,256]{1,0:T(8,128)(2,1)S(1)} %collective-permute-done.6.refs_2_), channel_id=1, source_target_pairs={{0,2},{1,3},{2,6},{3,7},{6,10},{7,11},{10,14},{11,15},{14,12},{15,... | collective-permute-start | bytes 1056776 | tf_op jit(solution)/shard_map/ppermute | solution.py:273
  25.0 11.0 %copy-start.1 = (s32[16,1,16]{2,1,0:T(1,128)}, s32[16,1,16]{2,1,0:T(1,128)S(1)}, u32[]{:S(2)}) copy-start(s32[16,1,16]{2,1,0:T(1,128)S(1)} %all-to-all-done) | copy-start | bytes 3076
  27.9 15.0 %collective-permute-start.3 = (bf16[688,256]{1,0:T(8,128)(2,1)}, bf16[688,256]{1,0:T(8,128)(2,1)S(1)}, u32[]{:S(2)}, u32[]{:S(2)}) collective-permute-start(bf16[688,256]{1,0:T(8,128)(2,1)} %collective-permute-done.1.refs_0_), channel_id=1, source_target_pairs={{0,2},{1,3},{2,6},{3,7},{6,10},{7,11},{10,14},{11,15},{14,12},{15,... | collective-permute-start | bytes 1056776 | tf_op jit(solution)/shard_map/ppermute | solution.py:273
  29.1 15.0 %collective-permute-start.13 = (bf16[688,256]{1,0:T(8,128)(2,1)}, bf16[688,256]{1,0:T(8,128)(2,1)S(1)}, u32[]{:S(2)}, u32[]{:S(2)}) collective-permute-start(bf16[688,256]{1,0:T(8,128)(2,1)} %collective-permute-done.12.refs_1_), channel_id=1, source_target_pairs={{0,4},{1,5},{2,0},{3,1},{6,2},{7,3},{10,6},{11,7},{14,10},{15,11},... | collective-permute-start | bytes 1056776 | tf_op jit(solution)/shard_map/ppermute | solution.py:273
  29.4 3.4 %copy-start = (bf16[384,11008]{1,0:T(8,128)(2,1)S(1)}, bf16[384,11008]{1,0:T(8,128)(2,1)}, u32[]{:S(2)}) copy-start(bf16[384,11008]{1,0:T(8,128)(2,1)} %own_hbm.15) | copy-start | bytes 25362436
  36.0 14.5 %collective-permute-start.10 = (bf16[688,256]{1,0:T(8,128)(2,1)}, bf16[688,256]{1,0:T(8,128)(2,1)S(1)}, u32[]{:S(2)}, u32[]{:S(2)}) collective-permute-start(bf16[688,256]{1,0:T(8,128)(2,1)} %collective-permute-done.7.refs_2_), channel_id=1, source_target_pairs={{0,2},{1,3},{2,6},{3,7},{6,10},{7,11},{10,14},{11,15},{14,12},{15,... | collective-permute-start | bytes 1056776 | tf_op jit(solution)/shard_map/ppermute | solution.py:273
  37.2 14.4 %collective-permute-start.9 = (bf16[688,256]{1,0:T(8,128)(2,1)}, bf16[688,256]{1,0:T(8,128)(2,1)S(1)}, u32[]{:S(2)}, u32[]{:S(2)}) collective-permute-start(bf16[688,256]{1,0:T(8,128)(2,1)} %collective-permute-done.5.refs_3_), channel_id=1, source_target_pairs={{0,4},{1,5},{2,0},{3,1},{6,2},{7,3},{10,6},{11,7},{14,10},{15,11},... | collective-permute-start | bytes 1056776 | tf_op jit(solution)/shard_map/ppermute | solution.py:273
  42.9 15.1 %collective-permute-start.8 = (bf16[688,256]{1,0:T(8,128)(2,1)S(1)}, bf16[688,256]{1,0:T(8,128)(2,1)S(1)}, u32[]{:S(2)}, u32[]{:S(2)}) collective-permute-start(bf16[688,256]{1,0:T(8,128)(2,1)S(1)} %collective-permute-done.3.refs_0_), channel_id=1, source_target_pairs={{0,2},{1,3},{2,6},{3,7},{6,10},{7,11},{10,14},{11,15},{14,12},{15,... | collective-permute-start | bytes 1056776 | tf_op jit(solution)/shard_map/ppermute | solution.py:273
  44.1 14.0 %collective-permute-start.17 = (bf16[688,256]{1,0:T(8,128)(2,1)S(1)}, bf16[688,256]{1,0:T(8,128)(2,1)S(1)}, u32[]{:S(2)}, u32[]{:S(2)}) collective-permute-start(bf16[688,256]{1,0:T(8,128)(2,1)S(1)} %collective-permute-done.13.refs_1_), channel_id=1, source_target_pairs={{0,4},{1,5},{2,0},{3,1},{6,2},{7,3},{10,6},{11,7},{14,10},{15,11},... | collective-permute-start | bytes 1056776 | tf_op jit(solution)/shard_map/ppermute | solution.py:273
  50.5 16.8 %collective-permute-start.16 = (bf16[688,256]{1,0:T(8,128)(2,1)S(1)}, bf16[688,256]{1,0:T(8,128)(2,1)S(1)}, u32[]{:S(2)}, u32[]{:S(2)}) collective-permute-start(bf16[688,256]{1,0:T(8,128)(2,1)S(1)} %collective-permute-done.10.refs_2_), channel_id=1, source_target_pairs={{0,2},{1,3},{2,6},{3,7},{6,10},{7,11},{10,14},{11,15},{14,12},{15,... | collective-permute-start | bytes 1056776 | tf_op jit(solution)/shard_map/ppermute | solution.py:273
  51.6 17.0 %collective-permute-start.15 = (bf16[688,256]{1,0:T(8,128)(2,1)S(1)}, bf16[688,256]{1,0:T(8,128)(2,1)S(1)}, u32[]{:S(2)}, u32[]{:S(2)}) collective-permute-start(bf16[688,256]{1,0:T(8,128)(2,1)S(1)} %collective-permute-done.9.refs_3_), channel_id=1, source_target_pairs={{0,4},{1,5},{2,0},{3,1},{6,2},{7,3},{10,6},{11,7},{14,10},{15,11},... | collective-permute-start | bytes 1056776 | tf_op jit(solution)/shard_map/ppermute | solution.py:273
  58.1 16.2 %collective-permute-start.21 = (bf16[688,256]{1,0:T(8,128)(2,1)S(1)}, bf16[688,256]{1,0:T(8,128)(2,1)S(1)}, u32[]{:S(2)}, u32[]{:S(2)}) collective-permute-start(bf16[688,256]{1,0:T(8,128)(2,1)S(1)} %collective-permute-done.17.refs_1_), channel_id=1, source_target_pairs={{0,4},{1,5},{2,0},{3,1},{6,2},{7,3},{10,6},{11,7},{14,10},{15,11},... | collective-permute-start | bytes 1056776 | tf_op jit(solution)/shard_map/ppermute | solution.py:273
  59.1 14.0 %collective-permute-start.14 = (bf16[688,256]{1,0:T(8,128)(2,1)S(1)}, bf16[688,256]{1,0:T(8,128)(2,1)S(1)}, u32[]{:S(2)}, u32[]{:S(2)}) collective-permute-start(bf16[688,256]{1,0:T(8,128)(2,1)S(1)} %collective-permute-done.8.refs_0_), channel_id=1, source_target_pairs={{0,2},{1,3},{2,6},{3,7},{6,10},{7,11},{10,14},{11,15},{14,12},{15,... | collective-permute-start | bytes 1056776 | tf_op jit(solution)/shard_map/ppermute | solution.py:273
  67.3 13.4 %collective-permute-start.20 = (bf16[688,256]{1,0:T(8,128)(2,1)S(1)}, bf16[688,256]{1,0:T(8,128)(2,1)S(1)}, u32[]{:S(2)}, u32[]{:S(2)}) collective-permute-start(bf16[688,256]{1,0:T(8,128)(2,1)S(1)} %collective-permute-done.16.refs_2_), channel_id=1, source_target_pairs={{0,2},{1,3},{2,6},{3,7},{6,10},{7,11},{10,14},{11,15},{14,12},{15,... | collective-permute-start | bytes 1056776 | tf_op jit(solution)/shard_map/ppermute | solution.py:273
  68.6 13.2 %collective-permute-start.19 = (bf16[688,256]{1,0:T(8,128)(2,1)S(1)}, bf16[688,256]{1,0:T(8,128)(2,1)S(1)}, u32[]{:S(2)}, u32[]{:S(2)}) collective-permute-start(bf16[688,256]{1,0:T(8,128)(2,1)S(1)} %collective-permute-done.15.refs_3_), channel_id=1, source_target_pairs={{0,4},{1,5},{2,0},{3,1},{6,2},{7,3},{10,6},{11,7},{14,10},{15,11},... | collective-permute-start | bytes 1056776 | tf_op jit(solution)/shard_map/ppermute | solution.py:273
  73.1 15.1 %collective-permute-start.18 = (bf16[688,256]{1,0:T(8,128)(2,1)S(1)}, bf16[688,256]{1,0:T(8,128)(2,1)S(1)}, u32[]{:S(2)}, u32[]{:S(2)}) collective-permute-start(bf16[688,256]{1,0:T(8,128)(2,1)S(1)} %collective-permute-done.14.refs_0_), channel_id=1, source_target_pairs={{0,2},{1,3},{2,6},{3,7},{6,10},{7,11},{10,14},{11,15},{14,12},{15,... | collective-permute-start | bytes 1056776 | tf_op jit(solution)/shard_map/ppermute | solution.py:273
  74.3 13.9 %collective-permute-start.23 = (bf16[688,256]{1,0:T(8,128)(2,1)S(1)}, bf16[688,256]{1,0:T(8,128)(2,1)S(1)}, u32[]{:S(2)}, u32[]{:S(2)}) collective-permute-start(bf16[688,256]{1,0:T(8,128)(2,1)S(1)} %collective-permute-done.21.refs_1_), channel_id=1, source_target_pairs={{0,4},{1,5},{2,0},{3,1},{6,2},{7,3},{10,6},{11,7},{14,10},{15,11},... | collective-permute-start | bytes 1056776 | tf_op jit(solution)/shard_map/ppermute | solution.py:273
  80.7 15.1 %collective-permute-start.25 = (bf16[688,256]{1,0:T(8,128)(2,1)S(1)}, bf16[688,256]{1,0:T(8,128)(2,1)S(1)}, u32[]{:S(2)}, u32[]{:S(2)}) collective-permute-start(bf16[688,256]{1,0:T(8,128)(2,1)S(1)} %collective-permute-done.20.refs_2_), channel_id=1, source_target_pairs={{0,2},{1,3},{2,6},{3,7},{6,10},{7,11},{10,14},{11,15},{14,12},{15,... | collective-permute-start | bytes 1056776 | tf_op jit(solution)/shard_map/ppermute | solution.py:273
  81.8 13.9 %collective-permute-start.26 = (bf16[688,256]{1,0:T(8,128)(2,1)S(1)}, bf16[688,256]{1,0:T(8,128)(2,1)S(1)}, u32[]{:S(2)}, u32[]{:S(2)}) collective-permute-start(bf16[688,256]{1,0:T(8,128)(2,1)S(1)} %collective-permute-done.19.refs_3_), channel_id=1, source_target_pairs={{0,4},{1,5},{2,0},{3,1},{6,2},{7,3},{10,6},{11,7},{14,10},{15,11},... | collective-permute-start | bytes 1056776 | tf_op jit(solution)/shard_map/ppermute | solution.py:273
  88.2 14.3 %collective-permute-start.24 = (bf16[688,256]{1,0:T(8,128)(2,1)S(1)}, bf16[688,256]{1,0:T(8,128)(2,1)S(1)}, u32[]{:S(2)}, u32[]{:S(2)}) collective-permute-start(bf16[688,256]{1,0:T(8,128)(2,1)S(1)} %collective-permute-done.23.refs_1_), channel_id=1, source_target_pairs={{0,4},{1,5},{2,0},{3,1},{6,2},{7,3},{10,6},{11,7},{14,10},{15,11},... | collective-permute-start | bytes 1056776 | tf_op jit(solution)/shard_map/ppermute | solution.py:273
  89.3 14.0 %collective-permute-start.22 = (bf16[688,256]{1,0:T(8,128)(2,1)S(1)}, bf16[688,256]{1,0:T(8,128)(2,1)S(1)}, u32[]{:S(2)}, u32[]{:S(2)}) collective-permute-start(bf16[688,256]{1,0:T(8,128)(2,1)S(1)} %collective-permute-done.18.refs_0_), channel_id=1, source_target_pairs={{0,2},{1,3},{2,6},{3,7},{6,10},{7,11},{10,14},{11,15},{14,12},{15,... | collective-permute-start | bytes 1056776 | tf_op jit(solution)/shard_map/ppermute | solution.py:273
  95.8 14.3 %collective-permute-start.28 = (bf16[688,256]{1,0:T(8,128)(2,1)S(1)}, bf16[688,256]{1,0:T(8,128)(2,1)S(1)}, u32[]{:S(2)}, u32[]{:S(2)}) collective-permute-start(bf16[688,256]{1,0:T(8,128)(2,1)S(1)} %collective-permute-done.26.refs_3_), channel_id=1, source_target_pairs={{0,4},{1,5},{2,0},{3,1},{6,2},{7,3},{10,6},{11,7},{14,10},{15,11},... | collective-permute-start | bytes 1056776 | tf_op jit(solution)/shard_map/ppermute | solution.py:273
  96.9 14.0 %collective-permute-start.27 = (bf16[688,256]{1,0:T(8,128)(2,1)S(1)}, bf16[688,256]{1,0:T(8,128)(2,1)S(1)}, u32[]{:S(2)}, u32[]{:S(2)}) collective-permute-start(bf16[688,256]{1,0:T(8,128)(2,1)S(1)} %collective-permute-done.25.refs_2_), channel_id=1, source_target_pairs={{0,2},{1,3},{2,6},{3,7},{6,10},{7,11},{10,14},{11,15},{14,12},{15,... | collective-permute-start | bytes 1056776 | tf_op jit(solution)/shard_map/ppermute | solution.py:273
  105.7 7.5 %collective-permute-start.30 = (f32[2,384,256]{2,1,0:T(8,128)S(1)}, f32[2,384,256]{2,1,0:T(8,128)S(1)}, u32[]{:S(2)}, u32[]{:S(2)}) collective-permute-start(f32[2,384,256]{2,1,0:T(8,128)S(1)} %get-tuple-element.252), channel_id=1, source_target_pairs={{0,1},{1,0},{2,3},{3,2},{4,5},{5,4},{6,7},{7,6},{8,9},{9,8},{10,11... | collective-permute-start | bytes 2359304 | tf_op jit(solution)/shard_map/ppermute | solution.py:281
  112.0 3.1 %collective-permute-start.29 = (f32[2,384,256]{2,1,0:T(8,128)S(1)}, f32[2,384,256]{2,1,0:T(8,128)S(1)}, u32[]{:S(2)}, u32[]{:S(2)}) collective-permute-start(f32[2,384,256]{2,1,0:T(8,128)S(1)} %get-tuple-element.250), channel_id=1, source_target_pairs={{0,1},{1,0},{2,3},{3,2},{4,5},{5,4},{6,7},{7,6},{8,9},{9,8},{10,11... | collective-permute-start | bytes 2359304 | tf_op jit(solution)/shard_map/ppermute | solution.py:281
  117.0 42.8 %all-to-all-start.1 = ((bf16[16,6,16,512]{3,2,1,0:T(8,128)(2,1)}), bf16[16,6,16,512]{3,2,1,0:T(8,128)(2,1)S(1)}, u32[]{:S(2)}, u32[]{:S(2)}) async-start(bf16[16,6,16,512]{3,2,1,0:T(8,128)(2,1)} %shard_map.60), calls=%async_computation.1 | async-start | bytes 3145728 | tf_op jit(solution)/shard_map/all_to_all | solution.py:308

commit v10 on v9

--- a/solution.py
+++ b/solution.py
@@ -237,16 +237,22 @@
     )(value)
 
 
-def ring_products(gamma, coefficients, ids, place, shape):
+def exchange(value):
+    return lax.all_to_all(value, "wide", split_axis=0, concat_axis=0, tiled=True)
+
+
+def ring_products(gamma, coefficients, labels, place, shape):
     count = lax.axis_size("wide")
     norb, depth, naux = gamma.shape
     width = naux // HALVES
     swap = [(d, d ^ 1) for d in range(count)]
     other = lax.ppermute(coefficients, "wide", swap)
 
-    piece = [
-        [gamma[i, :, j * width : (j + 1) * width] for i in range(norb)] for j in range(HALVES)
-    ]
+    piece = []
+    for j in range(HALVES):
+        if j:
+            gamma, place = lax.optimization_barrier((gamma, place))
+        piece.append([gamma[i, :, j * width : (j + 1) * width] for i in range(norb)])
     shift = [
         [
             (2 * ring_chip(p) + k, 2 * ring_chip(p + way) + k)
@@ -266,8 +272,11 @@
                 done += 1
             for i in range(norb):
                 sent = piece[j][i]
-                if t == 2 and i == j == 0:
-                    sent, ids, place = lax.optimization_barrier((sent, ids, place))
+                if t == 1 and i == j == HALVES - 1:
+                    sent, labels = lax.optimization_barrier((sent, labels))
+                    ids = exchange(labels)
+                if t == 3 and i == j == 0:
+                    sent, ids = lax.optimization_barrier((sent, ids))
                 if BEHIND[t][j]:
                     sent, sums = lax.optimization_barrier((sent, sums))
                 piece[j][i] = lax.ppermute(sent, "wide", shift[i])
@@ -294,9 +303,8 @@
     shape = (count, norb * block_rows, slots, naux)
 
     labels, place = routing(owners, count, slots, block_rows)
-    ids = lax.all_to_all(labels, "wide", split_axis=0, concat_axis=0, tiled=True)
     if count == 2 * GRID_CHIPS and norb == len(WAYS):
-        ids, out = ring_products(gamma, coefficients, ids, place, shape)
+        ids, out = ring_products(gamma, coefficients, labels, place, shape)
     else:
         gathered = lax.all_gather(gamma, "wide", axis=1, tiled=True)
         back = jnp.einsum(
@@ -305,7 +313,8 @@
         out = jnp.einsum("tr,irn->itn", place, back, preferred_element_type=jnp.float32)
         out = out.astype(jnp.bfloat16).reshape(norb, count, block_rows, slots, naux)
         out = out.transpose(1, 0, 2, 3, 4).reshape(shape)
-    placed = lax.all_to_all(out, "wide", split_axis=0, concat_axis=0, tiled=True)
+        ids = exchange(labels)
+    placed = exchange(out)
     return placed.transpose(0, 2, 1, 3)[None], ids[None]
 
 

time: 161 us -> 165 us (1.025)
  blocking collectives: 0 us -> 15.6 us
  waiting for transfers between devices: 81.9 us -> 73 us
  starting transfers between devices: 38.6 us -> 33.2 us
    all_to_all x0 -> x1, blocking collectives: none -> 15.6 us  [exchange(): lax.all_to_all(value, 'wide', split_axis=0, concat_axis=0, tiled=True)]
    all_to_all x2 -> x1, starting transfers between devices: 13.6 us -> 5.9 us  [exchange(): lax.all_to_all(value, 'wide', split_axis=0, concat_axis=0, tiled=True)]
    ppermute x28, waiting for transfers between devices: 43.9 us -> 38.1 us  [ring_products(): piece[j][i] = lax.ppermute(sent, 'wide', shift[i])]
    all_to_all x2 -> x1, waiting for transfers between devices: 38 us -> 34.9 us  [exchange(): lax.all_to_all(value, 'wide', split_axis=0, concat_axis=0, tiled=True)]
    ppermute x2, starting transfers between devices: 3.5 us -> 5.75 us  [ring_products(): theirs = [lax.ppermute(sums[j][1], 'wide', swap) for j in range(HALVES)]]
    unnamed x7 -> x3, local copies, waits for them, and re-layouts: 4.55 us -> 4.54 us
  transfers between devices with their start and end apart: 33 -> 32, of which waited for: 16 -> 11; matrix products, arithmetic and copies ran while one was open for 2% -> 3% of each run, Pallas kernels for 19% -> 19%
where the time goes in v10:
time: 165 us
  waiting for transfers between devices  73 us (44%)
  starting transfers between devices  33.2 us (20%)
  Pallas kernels  32.9 us (20%)
  blocking collectives  15.6 us (9%)
  local copies, waits for them, and re-layouts  7.19 us (4%)
  other arithmetic  1.87 us (1%)
    ppermute x28, waiting for transfers between devices, ring_products(): piece[j][i] = lax.ppermute(sent, 'wide', shift[i])  38.1 us
    all_to_all x1, waiting for transfers between devices, exchange(): lax.all_to_all(value, 'wide', split_axis=0, concat_axis=0, tiled=True)  34.9 us
    pallas_call x8, Pallas kernels, add_products(): pl.pallas_call(functools.partial(step_kernel, t, parts), out_shape=[sums]...  26.7 us
    ppermute x28, starting transfers between devices, ring_products(): piece[j][i] = lax.ppermute(sent, 'wide', shift[i])  20.8 us
    all_to_all x1, blocking collectives, exchange(): lax.all_to_all(value, 'wide', split_axis=0, concat_axis=0, tiled=True)  15.6 us
    all_to_all x1, starting transfers between devices, exchange(): lax.all_to_all(value, 'wide', split_axis=0, concat_axis=0, tiled=True)  5.9 us
    ppermute x2, starting transfers between devices, ring_products(): theirs = [lax.ppermute(sums[j][1], 'wide', swap) for j in range(HALVES)]  5.75 us
    unnamed x3, local copies, waits for them, and re-layouts  4.54 us
  transfers between devices with their start and end apart: 32, of which 11 were waited for; matrix products, arithmetic and copies ran while one was open for 3% of the time, Pallas kernels for 19%

profile of v10, /device:TPU:13, one launch (start us, length us, event | category | flops | bytes accessed | tf_op | source)
XLA Modules:
  0.0 164.6 jit_solution(15741127449175496469)
XLA Ops:
  0.6 0.7 collective-permute-start
  1.4 1.1 slice_bitcast_fusion
  2.5 0.2 collective-permute-start.11
  2.7 1.3 collective-permute-start.1
  4.0 0.9 convert_reduce_fusion
  4.9 0.7 broadcast_multiply_fusion
  5.7 0.2 mul.57
  5.9 0.2 compare_convert_fusion.place_ref
  6.1 1.1 slice_bitcast_fusion.1
  7.2 1.3 collective-permute-start.6
  8.6 0.2 collective-permute-start.4
  8.8 3.6 %collective-permute-done.11.refs_1_ = bf16[688,256]{1,0:T(8,128)(2,1)S(1)} collective-permute-done((bf16[688,256]{1,0:T(8,128)(2,1)S(1)}, bf16[688,256]{1,0:T(8,128)(2,1)S(1)}, u32[]{:S(2)}, u32[]{:S(2)}) %collective-permute-start.11) | collective-permute-done | bytes 352288 | tf_op jit(solution)/shard_map/ppermute | solution.py:282
  12.4 0.2 collective-permute-start.12
  12.6 1.3 collective-permute-start.2
  14.0 5.9 %collective-permute-done.6.refs_2_ = bf16[688,256]{1,0:T(8,128)(2,1)} collective-permute-done((bf16[688,256]{1,0:T(8,128)(2,1)S(1)}, bf16[688,256]{1,0:T(8,128)(2,1)}, u32[]{:S(2)}, u32[]{:S(2)}) %collective-permute-start.6) | collective-permute-done | bytes 352288 | tf_op jit(solution)/shard_map/ppermute | solution.py:282
  19.9 1.3 collective-permute-start.7
  21.3 0.2 collective-permute-start.5
  21.5 5.9 %collective-permute-done.2.refs_0_ = bf16[688,256]{1,0:T(8,128)(2,1)S(1)} collective-permute-done((bf16[688,256]{1,0:T(8,128)(2,1)S(1)}, bf16[688,256]{1,0:T(8,128)(2,1)S(1)}, u32[]{:S(2)}, u32[]{:S(2)}) %collective-permute-start.2) | collective-permute-done | bytes 352288 | tf_op jit(solution)/shard_map/ppermute | solution.py:282
  27.4 1.3 collective-permute-start.3
  28.7 0.2 collective-permute-start.13
  28.8 3.4 %copy-done = bf16[384,11008]{1,0:T(8,128)(2,1)S(1)} copy-done((bf16[384,11008]{1,0:T(8,128)(2,1)S(1)}, bf16[384,11008]{1,0:T(8,128)(2,1)}, u32[]{:S(2)}) %copy-start) | copy-done | bytes 8454168
  32.2 3.1 %shard_map.50 = (f32[2,384,256]{2,1,0:T(8,128)S(1)}, f32[2,384,256]{2,1,0:T(8,128)S(1)}, f32[2,384,256]{2,1,0:T(8,128)S(1)}, f32[2,384,256]{2,1,0:T(8,128)S(1)}) custom-call(bf16[384,11008]{1,0:T(8,128)(2,1)S(1)} %copy-done, bf16[384,11008]{1,0:T(8,128)(2,1)} %collective-permute-done.other_hbm, bf16[688,256]{1,0:T(8,128)(2,1)S(1)} %get-tuple-element.263.refs_0_, ...), custom_call_target="tpu_custom_call" | custom-call | flops 1409286144 | bytes 2752512 | tf_op jit(solution)/shard_map/pallas_call | solution.py:158
  35.4 1.4 collective-permute-start.10
  36.8 0.2 collective-permute-start.9
  36.9 15.6 %all_to_all.17 = s32[16,1,16]{2,1,0:T(1,128)} all-to-all(s32[16,1,16]{2,1,0:T(1,128)S(1)} %bitcast.19), channel_id=1, replica_groups=mesh['groups'=2,'wide'=16] {'wide'}, dimensions={0} | all-to-all | bytes 2048 | tf_op jit(solution)/shard_map/all_to_all | solution.py:241
  52.6 0.3 collective-permute-start.8
  52.9 1.2 collective-permute-start.17
  54.0 4.3 %shard_map.51 = (f32[2,384,256]{2,1,0:T(8,128)S(1)}, f32[2,384,256]{2,1,0:T(8,128)S(1)}, f32[2,384,256]{2,1,0:T(8,128)S(1)}, f32[2,384,256]{2,1,0:T(8,128)S(1)}) custom-call(bf16[384,11008]{1,0:T(8,128)(2,1)S(1)} %copy-done, ...), custom_call_target="tpu_custom_call", output_to_operand_aliasing={{0}: (6, {}), {1}: (7, {}), {2}: (8, {}), {3}: (9, {})} | custom-call | flops 1409286144 | bytes 2752512 | tf_op jit(solution)/shard_map/pallas_call | solution.py:158
  58.3 0.3 collective-permute-start.16
  58.7 1.2 collective-permute-start.15
  59.8 1.7 %collective-permute-done.8.refs_0_ = bf16[688,256]{1,0:T(8,128)(2,1)S(1)} collective-permute-done((bf16[688,256]{1,0:T(8,128)(2,1)S(1)}, bf16[688,256]{1,0:T(8,128)(2,1)S(1)}, u32[]{:S(2)}, u32[]{:S(2)}) %collective-permute-start.8) | collective-permute-done | bytes 352288 | tf_op jit(solution)/shard_map/ppermute | solution.py:282
  61.5 1.2 collective-permute-start.21
  62.7 0.3 collective-permute-start.14
  63.0 4.2 %shard_map.52 = (f32[2,384,256]{2,1,0:T(8,128)S(1)}, f32[2,384,256]{2,1,0:T(8,128)S(1)}, f32[2,384,256]{2,1,0:T(8,128)S(1)}, f32[2,384,256]{2,1,0:T(8,128)S(1)}) custom-call(bf16[384,11008]{1,0:T(8,128)(2,1)S(1)} %copy-done, ...), custom_call_target="tpu_custom_call", output_to_operand_aliasing={{0}: (6, {}), {1}: (7, {}), {2}: (8, {}), {3}: (9, {})} | custom-call | flops 1409286144 | bytes 2752512 | tf_op jit(solution)/shard_map/pallas_call | solution.py:158
  67.2 3.2 %shard_map.53 = (f32[2,384,256]{2,1,0:T(8,128)S(1)}, f32[2,384,256]{2,1,0:T(8,128)S(1)}, f32[2,384,256]{2,1,0:T(8,128)S(1)}, f32[2,384,256]{2,1,0:T(8,128)S(1)}) custom-call(bf16[384,11008]{1,0:T(8,128)(2,1)S(1)} %copy-done, ...), custom_call_target="tpu_custom_call", output_to_operand_aliasing={{0}: (6, {}), {1}: (7, {}), {2}: (8, {}), {3}: (9, {})} | custom-call | flops 1409286144 | bytes 2752512 | tf_op jit(solution)/shard_map/pallas_call | solution.py:158
  70.4 1.0 collective-permute-start.20
  71.4 0.5 collective-permute-start.19
  71.9 4.7 %collective-permute-done.14.refs_0_ = bf16[688,256]{1,0:T(8,128)(2,1)S(1)} collective-permute-done((bf16[688,256]{1,0:T(8,128)(2,1)S(1)}, bf16[688,256]{1,0:T(8,128)(2,1)S(1)}, u32[]{:S(2)}, u32[]{:S(2)}) %collective-permute-start.14) | collective-permute-done | bytes 352288 | tf_op jit(solution)/shard_map/ppermute | solution.py:282
  76.6 0.3 collective-permute-start.18
  76.9 1.2 collective-permute-start.23
  78.1 3.2 %shard_map.54 = (f32[2,384,256]{2,1,0:T(8,128)S(1)}, f32[2,384,256]{2,1,0:T(8,128)S(1)}, f32[2,384,256]{2,1,0:T(8,128)S(1)}, f32[2,384,256]{2,1,0:T(8,128)S(1)}) custom-call(bf16[384,11008]{1,0:T(8,128)(2,1)S(1)} %copy-done, ...), custom_call_target="tpu_custom_call", output_to_operand_aliasing={{0}: (6, {}), {1}: (7, {}), {2}: (8, {}), {3}: (9, {})} | custom-call | flops 1409286144 | bytes 2752512 | tf_op jit(solution)/shard_map/pallas_call | solution.py:158
  81.3 2.9 %collective-permute-done.20.refs_2_ = bf16[688,256]{1,0:T(8,128)(2,1)S(1)} collective-permute-done((bf16[688,256]{1,0:T(8,128)(2,1)S(1)}, bf16[688,256]{1,0:T(8,128)(2,1)S(1)}, u32[]{:S(2)}, u32[]{:S(2)}) %collective-permute-start.20) | collective-permute-done | bytes 352288 | tf_op jit(solution)/shard_map/ppermute | solution.py:282
  84.2 0.3 collective-permute-start.25
  84.5 1.2 collective-permute-start.26
  85.6 6.1 %collective-permute-done.18.refs_0_ = bf16[688,256]{1,0:T(8,128)(2,1)S(1)} collective-permute-done((bf16[688,256]{1,0:T(8,128)(2,1)S(1)}, bf16[688,256]{1,0:T(8,128)(2,1)S(1)}, u32[]{:S(2)}, u32[]{:S(2)}) %collective-permute-start.18) | collective-permute-done | bytes 352288 | tf_op jit(solution)/shard_map/ppermute | solution.py:282
  91.7 1.2 collective-permute-start.24
  92.9 0.3 collective-permute-start.22
  93.2 3.2 %shard_map.55 = (f32[2,384,256]{2,1,0:T(8,128)S(1)}, f32[2,384,256]{2,1,0:T(8,128)S(1)}, f32[2,384,256]{2,1,0:T(8,128)S(1)}, f32[2,384,256]{2,1,0:T(8,128)S(1)}) custom-call(bf16[384,11008]{1,0:T(8,128)(2,1)S(1)} %copy-done, ...), custom_call_target="tpu_custom_call", output_to_operand_aliasing={{0}: (6, {}), {1}: (7, {}), {2}: (8, {}), {3}: (9, {})} | custom-call | flops 1409286144 | bytes 2752512 | tf_op jit(solution)/shard_map/pallas_call | solution.py:158
  96.4 2.9 %collective-permute-done.25.refs_2_ = bf16[688,256]{1,0:T(8,128)(2,1)S(1)} collective-permute-done((bf16[688,256]{1,0:T(8,128)(2,1)S(1)}, bf16[688,256]{1,0:T(8,128)(2,1)S(1)}, u32[]{:S(2)}, u32[]{:S(2)}) %collective-permute-start.25) | collective-permute-done | bytes 352288 | tf_op jit(solution)/shard_map/ppermute | solution.py:282
  99.3 1.2 collective-permute-start.28
  100.4 0.3 collective-permute-start.27
  100.7 3.2 %shard_map.56 = (f32[2,384,256]{2,1,0:T(8,128)S(1)}, f32[2,384,256]{2,1,0:T(8,128)S(1)}, f32[2,384,256]{2,1,0:T(8,128)S(1)}, f32[2,384,256]{2,1,0:T(8,128)S(1)}) custom-call(bf16[384,11008]{1,0:T(8,128)(2,1)S(1)} %copy-done, ...), custom_call_target="tpu_custom_call", output_to_operand_aliasing={{0}: (6, {}), {1}: (7, {}), {2}: (8, {}), {3}: (9, {})} | custom-call | flops 1409286144 | bytes 2752512 | tf_op jit(solution)/shard_map/pallas_call | solution.py:158
  103.9 2.9 %collective-permute-done.24.refs_1_ = bf16[688,256]{1,0:T(8,128)(2,1)S(1)} collective-permute-done((bf16[688,256]{1,0:T(8,128)(2,1)S(1)}, bf16[688,256]{1,0:T(8,128)(2,1)S(1)}, u32[]{:S(2)}, u32[]{:S(2)}) %collective-permute-start.24) | collective-permute-done | bytes 352288 | tf_op jit(solution)/shard_map/ppermute | solution.py:282
  106.8 2.4 %shard_map.57 = (f32[2,384,256]{2,1,0:T(8,128)S(1)}, f32[2,384,256]{2,1,0:T(8,128)S(1)}, bf16[2,768,896]{2,1,0:T(8,128)(2,1)S(1)}) custom-call(bf16[384,11008]{1,0:T(8,128)(2,1)S(1)} %copy-done, bf16[384,11008]{1,0:T(8,128)(2,1)} %collective-permute-done.other_hbm, ...), custom_call_target="tpu_custom_call", output_to_operand_aliasing={{0}: (4, {}), {1}: (5, {})} | custom-call | flops 704643072 | bytes 2752512 | tf_op jit(solution)/shard_map/pallas_call | solution.py:158
  109.2 3.7 %collective-permute-start.30 = (f32[2,384,256]{2,1,0:T(8,128)S(1)}, f32[2,384,256]{2,1,0:T(8,128)S(1)}, u32[]{:S(2)}, u32[]{:S(2)}) collective-permute-start(f32[2,384,256]{2,1,0:T(8,128)S(1)} %get-tuple-element.258), channel_id=1, source_target_pairs={{0,1},{1,0},{2,3},{3,2},{4,5},{5,4},{6,7},{7,6},{8,9},{9,8},{10,11... | collective-permute-start | bytes 2359304 | tf_op jit(solution)/shard_map/ppermute | solution.py:290
  112.9 1.5 collective-permute-done.28.refs_1_
  114.4 1.1 shard_map.58
  115.5 2.1 %collective-permute-start.29 = (f32[2,384,256]{2,1,0:T(8,128)S(1)}, f32[2,384,256]{2,1,0:T(8,128)S(1)}, u32[]{:S(2)}, u32[]{:S(2)}) collective-permute-start(f32[2,384,256]{2,1,0:T(8,128)S(1)} %get-tuple-element.256), channel_id=1, source_target_pairs={{0,1},{1,0},{2,3},{3,2},{4,5},{5,4},{6,7},{7,6},{8,9},{9,8},{10,11... | collective-permute-start | bytes 2359304 | tf_op jit(solution)/shard_map/ppermute | solution.py:290
  117.6 1.9 %shard_map.59.refs_0_ = bf16[16,6,16,512]{3,2,1,0:T(8,128)(2,1)} custom-call(bf16[768,384]{1,0:T(8,128)(2,1)S(1)} %compare_convert_fusion.place_ref, f32[2,384,256]{2,1,0:T(8,128)S(1)} %get-tuple-element.257.mine_ref, f32[2,384,256]{2,1,0:T(8,128)S(1)} %collective-permute-done.30.theirs_ref), custom_call_target="tpu_custom_call" | custom-call | flops 301989888 | bytes 1572864 | tf_op jit(solution)/shard_map/pallas_call | solution.py:205
  119.5 1.9 %shard_map.60 = bf16[16,6,16,512]{3,2,1,0:T(8,128)(2,1)} custom-call(bf16[768,384]{1,0:T(8,128)(2,1)S(1)} %compare_convert_fusion.place_ref, f32[2,384,256]{2,1,0:T(8,128)S(1)} %get-tuple-element.255.mine_ref, f32[2,384,256]{2,1,0:T(8,128)S(1)} %collective-permute-done.29.theirs_ref, ...), custom_call_target="tpu_custom_call", output_to_operand_aliasing={{}: (3, {})} | custom-call | flops 301989888 | bytes 1572864 | tf_op jit(solution)/shard_map/pallas_call | solution.py:205
  121.3 5.9 %all-to-all-start.1 = ((bf16[16,6,16,512]{3,2,1,0:T(8,128)(2,1)}), bf16[16,6,16,512]{3,2,1,0:T(8,128)(2,1)S(1)}, u32[]{:S(2)}, u32[]{:S(2)}) async-start(bf16[16,6,16,512]{3,2,1,0:T(8,128)(2,1)} %shard_map.60), calls=%async_computation.1 | async-start | bytes 3145728 | tf_op jit(solution)/shard_map/all_to_all | solution.py:241
  127.2 1.3 shard_map.61
  128.6 34.9 %all-to-all-done.1 = bf16[16,6,16,512]{3,2,1,0:T(8,128)(2,1)S(1)} async-done(((bf16[16,6,16,512]{3,2,1,0:T(8,128)(2,1)}), bf16[16,6,16,512]{3,2,1,0:T(8,128)(2,1)S(1)}, u32[]{:S(2)}, u32[]{:S(2)}) %all-to-all-start.1) | async-done | bytes 1572896 | tf_op jit(solution)/shard_map/all_to_all | solution.py:241
  163.4 1.1 copy.64
  (28 shorter events, 0.4 us)
Async XLA Ops:
  0.6 28.2 %collective-permute-start = (bf16[384,11008]{1,0:T(8,128)(2,1)}, bf16[384,11008]{1,0:T(8,128)(2,1)}, u32[]{:S(2)}, u32[]{:S(2)}) collective-permute-start(bf16[384,11008]{1,0:T(8,128)(2,1)} %own_hbm.15), channel_id=1, source_target_pairs={{0,1},{1,0},{2,3},{3,2},{4,5},{5,4},{6,7},{7,6},{8,9},{9,8},{10,11... | collective-permute-start | bytes 25362440 | tf_op jit(solution)/shard_map/ppermute | solution.py:249
  2.5 9.9 %collective-permute-start.11 = (bf16[688,256]{1,0:T(8,128)(2,1)S(1)}, bf16[688,256]{1,0:T(8,128)(2,1)S(1)}, u32[]{:S(2)}, u32[]{:S(2)}) collective-permute-start(bf16[688,256]{1,0:T(8,128)(2,1)S(1)} %get-tuple-element.262.refs_1_), channel_id=1, source_target_pairs={{0,4},{1,5},{2,0},{3,1},{6,2},{7,3},{10,6},{11,7},{14,10},{15,11},... | collective-permute-start | bytes 1056776 | tf_op jit(solution)/shard_map/ppermute | solution.py:282
  2.7 9.9 %collective-permute-start.1 = (bf16[688,256]{1,0:T(8,128)(2,1)S(1)}, bf16[688,256]{1,0:T(8,128)(2,1)S(1)}, u32[]{:S(2)}, u32[]{:S(2)}) collective-permute-start(bf16[688,256]{1,0:T(8,128)(2,1)S(1)} %get-tuple-element.263.refs_0_), channel_id=1, source_target_pairs={{0,2},{1,3},{2,6},{3,7},{6,10},{7,11},{10,14},{11,15},{14,12},{15,... | collective-permute-start | bytes 1056776 | tf_op jit(solution)/shard_map/ppermute | solution.py:282
  7.2 12.7 %collective-permute-start.6 = (bf16[688,256]{1,0:T(8,128)(2,1)S(1)}, bf16[688,256]{1,0:T(8,128)(2,1)}, u32[]{:S(2)}, u32[]{:S(2)}) collective-permute-start(bf16[688,256]{1,0:T(8,128)(2,1)S(1)} %get-tuple-element.264.refs_2_), channel_id=1, source_target_pairs={{0,2},{1,3},{2,6},{3,7},{6,10},{7,11},{10,14},{11,15},{14,12},{15,... | collective-permute-start | bytes 1056776 | tf_op jit(solution)/shard_map/ppermute | solution.py:282
  8.6 12.7 %collective-permute-start.4 = (bf16[688,256]{1,0:T(8,128)(2,1)S(1)}, bf16[688,256]{1,0:T(8,128)(2,1)}, u32[]{:S(2)}, u32[]{:S(2)}) collective-permute-start(bf16[688,256]{1,0:T(8,128)(2,1)S(1)} %get-tuple-element.265.refs_3_), channel_id=1, source_target_pairs={{0,4},{1,5},{2,0},{3,1},{6,2},{7,3},{10,6},{11,7},{14,10},{15,11},... | collective-permute-start | bytes 1056776 | tf_op jit(solution)/shard_map/ppermute | solution.py:282
  12.4 16.2 %collective-permute-start.12 = (bf16[688,256]{1,0:T(8,128)(2,1)S(1)}, bf16[688,256]{1,0:T(8,128)(2,1)S(1)}, u32[]{:S(2)}, u32[]{:S(2)}) collective-permute-start(bf16[688,256]{1,0:T(8,128)(2,1)S(1)} %collective-permute-done.11.refs_1_), channel_id=1, source_target_pairs={{0,4},{1,5},{2,0},{3,1},{6,2},{7,3},{10,6},{11,7},{14,10},{15,11},... | collective-permute-start | bytes 1056776 | tf_op jit(solution)/shard_map/ppermute | solution.py:282
  12.6 14.8 %collective-permute-start.2 = (bf16[688,256]{1,0:T(8,128)(2,1)S(1)}, bf16[688,256]{1,0:T(8,128)(2,1)S(1)}, u32[]{:S(2)}, u32[]{:S(2)}) collective-permute-start(bf16[688,256]{1,0:T(8,128)(2,1)S(1)} %collective-permute-done.1.refs_0_), channel_id=1, source_target_pairs={{0,2},{1,3},{2,6},{3,7},{6,10},{7,11},{10,14},{11,15},{14,12},{15,... | collective-permute-start | bytes 1056776 | tf_op jit(solution)/shard_map/ppermute | solution.py:282
  19.9 15.5 %collective-permute-start.7 = (bf16[688,256]{1,0:T(8,128)(2,1)}, bf16[688,256]{1,0:T(8,128)(2,1)}, u32[]{:S(2)}, u32[]{:S(2)}) collective-permute-start(bf16[688,256]{1,0:T(8,128)(2,1)} %collective-permute-done.6.refs_2_), channel_id=1, source_target_pairs={{0,2},{1,3},{2,6},{3,7},{6,10},{7,11},{10,14},{11,15},{14,12},{15,... | collective-permute-start | bytes 1056776 | tf_op jit(solution)/shard_map/ppermute | solution.py:282
  21.3 15.5 %collective-permute-start.5 = (bf16[688,256]{1,0:T(8,128)(2,1)}, bf16[688,256]{1,0:T(8,128)(2,1)S(1)}, u32[]{:S(2)}, u32[]{:S(2)}) collective-permute-start(bf16[688,256]{1,0:T(8,128)(2,1)} %collective-permute-done.4.refs_3_), channel_id=1, source_target_pairs={{0,4},{1,5},{2,0},{3,1},{6,2},{7,3},{10,6},{11,7},{14,10},{15,11},... | collective-permute-start | bytes 1056776 | tf_op jit(solution)/shard_map/ppermute | solution.py:282
  27.4 25.2 %collective-permute-start.3 = (bf16[688,256]{1,0:T(8,128)(2,1)S(1)}, bf16[688,256]{1,0:T(8,128)(2,1)S(1)}, u32[]{:S(2)}, u32[]{:S(2)}) collective-permute-start(bf16[688,256]{1,0:T(8,128)(2,1)S(1)} %collective-permute-done.2.refs_0_), channel_id=1, source_target_pairs={{0,2},{1,3},{2,6},{3,7},{6,10},{7,11},{10,14},{11,15},{14,12},{15,... | collective-permute-start | bytes 1056776 | tf_op jit(solution)/shard_map/ppermute | solution.py:282
  28.7 24.2 %collective-permute-start.13 = (bf16[688,256]{1,0:T(8,128)(2,1)S(1)}, bf16[688,256]{1,0:T(8,128)(2,1)S(1)}, u32[]{:S(2)}, u32[]{:S(2)}) collective-permute-start(bf16[688,256]{1,0:T(8,128)(2,1)S(1)} %collective-permute-done.12.refs_1_), channel_id=1, source_target_pairs={{0,4},{1,5},{2,0},{3,1},{6,2},{7,3},{10,6},{11,7},{14,10},{15,11},... | collective-permute-start | bytes 1056776 | tf_op jit(solution)/shard_map/ppermute | solution.py:282
  28.8 3.4 %copy-start = (bf16[384,11008]{1,0:T(8,128)(2,1)S(1)}, bf16[384,11008]{1,0:T(8,128)(2,1)}, u32[]{:S(2)}) copy-start(bf16[384,11008]{1,0:T(8,128)(2,1)} %own_hbm.15) | copy-start | bytes 25362436
  35.4 22.9 %collective-permute-start.10 = (bf16[688,256]{1,0:T(8,128)(2,1)}, bf16[688,256]{1,0:T(8,128)(2,1)S(1)}, u32[]{:S(2)}, u32[]{:S(2)}) collective-permute-start(bf16[688,256]{1,0:T(8,128)(2,1)} %collective-permute-done.7.refs_2_), channel_id=1, source_target_pairs={{0,2},{1,3},{2,6},{3,7},{6,10},{7,11},{10,14},{11,15},{14,12},{15,... | collective-permute-start | bytes 1056776 | tf_op jit(solution)/shard_map/ppermute | solution.py:282
  36.8 21.9 %collective-permute-start.9 = (bf16[688,256]{1,0:T(8,128)(2,1)S(1)}, bf16[688,256]{1,0:T(8,128)(2,1)S(1)}, u32[]{:S(2)}, u32[]{:S(2)}) collective-permute-start(bf16[688,256]{1,0:T(8,128)(2,1)S(1)} %collective-permute-done.5.refs_3_), channel_id=1, source_target_pairs={{0,4},{1,5},{2,0},{3,1},{6,2},{7,3},{10,6},{11,7},{14,10},{15,11},... | collective-permute-start | bytes 1056776 | tf_op jit(solution)/shard_map/ppermute | solution.py:282
  52.6 9.0 %collective-permute-start.8 = (bf16[688,256]{1,0:T(8,128)(2,1)S(1)}, bf16[688,256]{1,0:T(8,128)(2,1)S(1)}, u32[]{:S(2)}, u32[]{:S(2)}) collective-permute-start(bf16[688,256]{1,0:T(8,128)(2,1)S(1)} %collective-permute-done.3.refs_0_), channel_id=1, source_target_pairs={{0,2},{1,3},{2,6},{3,7},{6,10},{7,11},{10,14},{11,15},{14,12},{15,... | collective-permute-start | bytes 1056776 | tf_op jit(solution)/shard_map/ppermute | solution.py:282
  52.9 8.7 %collective-permute-start.17 = (bf16[688,256]{1,0:T(8,128)(2,1)S(1)}, bf16[688,256]{1,0:T(8,128)(2,1)S(1)}, u32[]{:S(2)}, u32[]{:S(2)}) collective-permute-start(bf16[688,256]{1,0:T(8,128)(2,1)S(1)} %collective-permute-done.13.refs_1_), channel_id=1, source_target_pairs={{0,4},{1,5},{2,0},{3,1},{6,2},{7,3},{10,6},{11,7},{14,10},{15,11},... | collective-permute-start | bytes 1056776 | tf_op jit(solution)/shard_map/ppermute | solution.py:282
  58.3 12.1 %collective-permute-start.16 = (bf16[688,256]{1,0:T(8,128)(2,1)S(1)}, bf16[688,256]{1,0:T(8,128)(2,1)S(1)}, u32[]{:S(2)}, u32[]{:S(2)}) collective-permute-start(bf16[688,256]{1,0:T(8,128)(2,1)S(1)} %collective-permute-done.10.refs_2_), channel_id=1, source_target_pairs={{0,2},{1,3},{2,6},{3,7},{6,10},{7,11},{10,14},{11,15},{14,12},{15,... | collective-permute-start | bytes 1056776 | tf_op jit(solution)/shard_map/ppermute | solution.py:282
  58.7 12.7 %collective-permute-start.15 = (bf16[688,256]{1,0:T(8,128)(2,1)S(1)}, bf16[688,256]{1,0:T(8,128)(2,1)S(1)}, u32[]{:S(2)}, u32[]{:S(2)}) collective-permute-start(bf16[688,256]{1,0:T(8,128)(2,1)S(1)} %collective-permute-done.9.refs_3_), channel_id=1, source_target_pairs={{0,4},{1,5},{2,0},{3,1},{6,2},{7,3},{10,6},{11,7},{14,10},{15,11},... | collective-permute-start | bytes 1056776 | tf_op jit(solution)/shard_map/ppermute | solution.py:282
  61.5 15.4 %collective-permute-start.21 = (bf16[688,256]{1,0:T(8,128)(2,1)S(1)}, bf16[688,256]{1,0:T(8,128)(2,1)S(1)}, u32[]{:S(2)}, u32[]{:S(2)}) collective-permute-start(bf16[688,256]{1,0:T(8,128)(2,1)S(1)} %collective-permute-done.17.refs_1_), channel_id=1, source_target_pairs={{0,4},{1,5},{2,0},{3,1},{6,2},{7,3},{10,6},{11,7},{14,10},{15,11},... | collective-permute-start | bytes 1056776 | tf_op jit(solution)/shard_map/ppermute | solution.py:282
  62.7 13.9 %collective-permute-start.14 = (bf16[688,256]{1,0:T(8,128)(2,1)S(1)}, bf16[688,256]{1,0:T(8,128)(2,1)S(1)}, u32[]{:S(2)}, u32[]{:S(2)}) collective-permute-start(bf16[688,256]{1,0:T(8,128)(2,1)S(1)} %collective-permute-done.8.refs_0_), channel_id=1, source_target_pairs={{0,2},{1,3},{2,6},{3,7},{6,10},{7,11},{10,14},{11,15},{14,12},{15,... | collective-permute-start | bytes 1056776 | tf_op jit(solution)/shard_map/ppermute | solution.py:282
  70.4 13.8 %collective-permute-start.20 = (bf16[688,256]{1,0:T(8,128)(2,1)S(1)}, bf16[688,256]{1,0:T(8,128)(2,1)S(1)}, u32[]{:S(2)}, u32[]{:S(2)}) collective-permute-start(bf16[688,256]{1,0:T(8,128)(2,1)S(1)} %collective-permute-done.16.refs_2_), channel_id=1, source_target_pairs={{0,2},{1,3},{2,6},{3,7},{6,10},{7,11},{10,14},{11,15},{14,12},{15,... | collective-permute-start | bytes 1056776 | tf_op jit(solution)/shard_map/ppermute | solution.py:282
  71.4 13.1 %collective-permute-start.19 = (bf16[688,256]{1,0:T(8,128)(2,1)S(1)}, bf16[688,256]{1,0:T(8,128)(2,1)S(1)}, u32[]{:S(2)}, u32[]{:S(2)}) collective-permute-start(bf16[688,256]{1,0:T(8,128)(2,1)S(1)} %collective-permute-done.15.refs_3_), channel_id=1, source_target_pairs={{0,4},{1,5},{2,0},{3,1},{6,2},{7,3},{10,6},{11,7},{14,10},{15,11},... | collective-permute-start | bytes 1056776 | tf_op jit(solution)/shard_map/ppermute | solution.py:282
  76.6 15.1 %collective-permute-start.18 = (bf16[688,256]{1,0:T(8,128)(2,1)S(1)}, bf16[688,256]{1,0:T(8,128)(2,1)S(1)}, u32[]{:S(2)}, u32[]{:S(2)}) collective-permute-start(bf16[688,256]{1,0:T(8,128)(2,1)S(1)} %collective-permute-done.14.refs_0_), channel_id=1, source_target_pairs={{0,2},{1,3},{2,6},{3,7},{6,10},{7,11},{10,14},{11,15},{14,12},{15,... | collective-permute-start | bytes 1056776 | tf_op jit(solution)/shard_map/ppermute | solution.py:282
  76.9 14.8 %collective-permute-start.23 = (bf16[688,256]{1,0:T(8,128)(2,1)S(1)}, bf16[688,256]{1,0:T(8,128)(2,1)S(1)}, u32[]{:S(2)}, u32[]{:S(2)}) collective-permute-start(bf16[688,256]{1,0:T(8,128)(2,1)S(1)} %collective-permute-done.21.refs_1_), channel_id=1, source_target_pairs={{0,4},{1,5},{2,0},{3,1},{6,2},{7,3},{10,6},{11,7},{14,10},{15,11},... | collective-permute-start | bytes 1056776 | tf_op jit(solution)/shard_map/ppermute | solution.py:282
  84.2 15.1 %collective-permute-start.25 = (bf16[688,256]{1,0:T(8,128)(2,1)S(1)}, bf16[688,256]{1,0:T(8,128)(2,1)S(1)}, u32[]{:S(2)}, u32[]{:S(2)}) collective-permute-start(bf16[688,256]{1,0:T(8,128)(2,1)S(1)} %collective-permute-done.20.refs_2_), channel_id=1, source_target_pairs={{0,2},{1,3},{2,6},{3,7},{6,10},{7,11},{10,14},{11,15},{14,12},{15,... | collective-permute-start | bytes 1056776 | tf_op jit(solution)/shard_map/ppermute | solution.py:282
  84.5 14.8 %collective-permute-start.26 = (bf16[688,256]{1,0:T(8,128)(2,1)S(1)}, bf16[688,256]{1,0:T(8,128)(2,1)S(1)}, u32[]{:S(2)}, u32[]{:S(2)}) collective-permute-start(bf16[688,256]{1,0:T(8,128)(2,1)S(1)} %collective-permute-done.19.refs_3_), channel_id=1, source_target_pairs={{0,4},{1,5},{2,0},{3,1},{6,2},{7,3},{10,6},{11,7},{14,10},{15,11},... | collective-permute-start | bytes 1056776 | tf_op jit(solution)/shard_map/ppermute | solution.py:282
  91.7 15.1 %collective-permute-start.24 = (bf16[688,256]{1,0:T(8,128)(2,1)S(1)}, bf16[688,256]{1,0:T(8,128)(2,1)S(1)}, u32[]{:S(2)}, u32[]{:S(2)}) collective-permute-start(bf16[688,256]{1,0:T(8,128)(2,1)S(1)} %collective-permute-done.23.refs_1_), channel_id=1, source_target_pairs={{0,4},{1,5},{2,0},{3,1},{6,2},{7,3},{10,6},{11,7},{14,10},{15,11},... | collective-permute-start | bytes 1056776 | tf_op jit(solution)/shard_map/ppermute | solution.py:282
  92.9 13.9 %collective-permute-start.22 = (bf16[688,256]{1,0:T(8,128)(2,1)S(1)}, bf16[688,256]{1,0:T(8,128)(2,1)S(1)}, u32[]{:S(2)}, u32[]{:S(2)}) collective-permute-start(bf16[688,256]{1,0:T(8,128)(2,1)S(1)} %collective-permute-done.18.refs_0_), channel_id=1, source_target_pairs={{0,2},{1,3},{2,6},{3,7},{6,10},{7,11},{10,14},{11,15},{14,12},{15,... | collective-permute-start | bytes 1056776 | tf_op jit(solution)/shard_map/ppermute | solution.py:282
  99.3 15.1 %collective-permute-start.28 = (bf16[688,256]{1,0:T(8,128)(2,1)S(1)}, bf16[688,256]{1,0:T(8,128)(2,1)S(1)}, u32[]{:S(2)}, u32[]{:S(2)}) collective-permute-start(bf16[688,256]{1,0:T(8,128)(2,1)S(1)} %collective-permute-done.26.refs_3_), channel_id=1, source_target_pairs={{0,4},{1,5},{2,0},{3,1},{6,2},{7,3},{10,6},{11,7},{14,10},{15,11},... | collective-permute-start | bytes 1056776 | tf_op jit(solution)/shard_map/ppermute | solution.py:282
  100.4 13.9 %collective-permute-start.27 = (bf16[688,256]{1,0:T(8,128)(2,1)S(1)}, bf16[688,256]{1,0:T(8,128)(2,1)S(1)}, u32[]{:S(2)}, u32[]{:S(2)}) collective-permute-start(bf16[688,256]{1,0:T(8,128)(2,1)S(1)} %collective-permute-done.25.refs_2_), channel_id=1, source_target_pairs={{0,2},{1,3},{2,6},{3,7},{6,10},{7,11},{10,14},{11,15},{14,12},{15,... | collective-permute-start | bytes 1056776 | tf_op jit(solution)/shard_map/ppermute | solution.py:282
  109.2 8.4 %collective-permute-start.30 = (f32[2,384,256]{2,1,0:T(8,128)S(1)}, f32[2,384,256]{2,1,0:T(8,128)S(1)}, u32[]{:S(2)}, u32[]{:S(2)}) collective-permute-start(f32[2,384,256]{2,1,0:T(8,128)S(1)} %get-tuple-element.258), channel_id=1, source_target_pairs={{0,1},{1,0},{2,3},{3,2},{4,5},{5,4},{6,7},{7,6},{8,9},{9,8},{10,11... | collective-permute-start | bytes 2359304 | tf_op jit(solution)/shard_map/ppermute | solution.py:290
  115.5 4.0 %collective-permute-start.29 = (f32[2,384,256]{2,1,0:T(8,128)S(1)}, f32[2,384,256]{2,1,0:T(8,128)S(1)}, u32[]{:S(2)}, u32[]{:S(2)}) collective-permute-start(f32[2,384,256]{2,1,0:T(8,128)S(1)} %get-tuple-element.256), channel_id=1, source_target_pairs={{0,1},{1,0},{2,3},{3,2},{4,5},{5,4},{6,7},{7,6},{8,9},{9,8},{10,11... | collective-permute-start | bytes 2359304 | tf_op jit(solution)/shard_map/ppermute | solution.py:290
  121.3 42.1 %all-to-all-start.1 = ((bf16[16,6,16,512]{3,2,1,0:T(8,128)(2,1)}), bf16[16,6,16,512]{3,2,1,0:T(8,128)(2,1)S(1)}, u32[]{:S(2)}, u32[]{:S(2)}) async-start(bf16[16,6,16,512]{3,2,1,0:T(8,128)(2,1)} %shard_map.60), calls=%async_computation.1 | async-start | bytes 3145728 | tf_op jit(solution)/shard_map/all_to_all | solution.py:241

commit v11 on v10

--- a/solution.py
+++ b/solution.py
@@ -248,6 +248,7 @@
     swap = [(d, d ^ 1) for d in range(count)]
     other = lax.ppermute(coefficients, "wide", swap)
 
+    ids = exchange(labels)
     piece = []
     for j in range(HALVES):
         if j:
@@ -272,10 +273,7 @@
                 done += 1
             for i in range(norb):
                 sent = piece[j][i]
-                if t == 1 and i == j == HALVES - 1:
-                    sent, labels = lax.optimization_barrier((sent, labels))
-                    ids = exchange(labels)
-                if t == 3 and i == j == 0:
+                if t == 2 and i == j == 0:
                     sent, ids = lax.optimization_barrier((sent, ids))
                 if BEHIND[t][j]:
                     sent, sums = lax.optimization_barrier((sent, sums))

time: 165 us -> 166 us (level)
  no operation moved by 1% of the time
where the time goes in v11:
time: 166 us; the launch traced here: 165 us
  waiting for transfers between devices  72.6 us (44%)
  starting transfers between devices  33.9 us (20%)
  Pallas kernels  33 us (20%)
  blocking collectives  16.1 us (10%)
  local copies, waits for them, and re-layouts  7.2 us (4%)
  other arithmetic  1.87 us (1%)
    ppermute x28, waiting for transfers between devices, ring_products(): piece[j][i] = lax.ppermute(sent, 'wide', shift[i])  37.7 us
    all_to_all x1, waiting for transfers between devices, exchange(): lax.all_to_all(value, 'wide', split_axis=0, concat_axis=0, tiled=True)  34.9 us
    pallas_call x8, Pallas kernels, add_products(): pl.pallas_call(functools.partial(step_kernel, t, parts), out_shape=[sums]...  26.8 us
    ppermute x28, starting transfers between devices, ring_products(): piece[j][i] = lax.ppermute(sent, 'wide', shift[i])  20.7 us
    all_to_all x1, blocking collectives, exchange(): lax.all_to_all(value, 'wide', split_axis=0, concat_axis=0, tiled=True)  16.1 us
    ppermute x2, starting transfers between devices, ring_products(): theirs = [lax.ppermute(sums[j][1], 'wide', swap) for j in range(HALVES)]  6.53 us
    all_to_all x1, starting transfers between devices, exchange(): lax.all_to_all(value, 'wide', split_axis=0, concat_axis=0, tiled=True)  5.9 us
    unnamed x3, local copies, waits for them, and re-layouts  4.54 us
  transfers between devices with their start and end apart: 32, of which 11 were waited for; matrix products, arithmetic and copies ran while one was open for 3% of the time, Pallas kernels for 19%

profile of v11, /device:TPU:13, one launch (start us, length us, event | category | flops | bytes accessed | tf_op | source)
XLA Modules:
  0.0 165.5 jit_solution(18412372074773670207)
XLA Ops:
  0.6 0.7 collective-permute-start
  1.4 1.1 slice_bitcast_fusion
  2.5 0.2 collective-permute-start.11
  2.7 1.3 collective-permute-start.1
  4.0 0.9 convert_reduce_fusion
  4.9 0.7 broadcast_multiply_fusion
  5.7 0.2 mul.57
  5.9 0.2 compare_convert_fusion.place_ref
  6.1 1.1 slice_bitcast_fusion.1
  7.2 1.3 collective-permute-start.6
  8.6 0.2 collective-permute-start.4
  8.8 3.5 %collective-permute-done.1.refs_0_ = bf16[688,256]{1,0:T(8,128)(2,1)S(1)} collective-permute-done((bf16[688,256]{1,0:T(8,128)(2,1)S(1)}, bf16[688,256]{1,0:T(8,128)(2,1)S(1)}, u32[]{:S(2)}, u32[]{:S(2)}) %collective-permute-start.1) | collective-permute-done | bytes 352288 | tf_op jit(solution)/shard_map/ppermute | solution.py:280
  12.3 1.3 collective-permute-start.2
  13.6 0.2 collective-permute-start.12
  13.8 6.1 %collective-permute-done.6.refs_2_ = bf16[688,256]{1,0:T(8,128)(2,1)} collective-permute-done((bf16[688,256]{1,0:T(8,128)(2,1)S(1)}, bf16[688,256]{1,0:T(8,128)(2,1)}, u32[]{:S(2)}, u32[]{:S(2)}) %collective-permute-start.6) | collective-permute-done | bytes 352288 | tf_op jit(solution)/shard_map/ppermute | solution.py:280
  19.9 1.3 collective-permute-start.7
  21.2 0.2 collective-permute-start.5
  21.5 16.1 %all_to_all.14 = s32[16,1,16]{2,1,0:T(1,128)} all-to-all(s32[16,1,16]{2,1,0:T(1,128)S(1)} %sub.19), channel_id=1, replica_groups=mesh['groups'=2,'wide'=16] {'wide'}, dimensions={0} | all-to-all | bytes 2048 | tf_op jit(solution)/shard_map/all_to_all | solution.py:241
  37.6 0.3 collective-permute-start.3
  37.9 1.2 collective-permute-start.13
  39.1 3.4 %copy-done = bf16[384,11008]{1,0:T(8,128)(2,1)S(1)} copy-done((bf16[384,11008]{1,0:T(8,128)(2,1)S(1)}, bf16[384,11008]{1,0:T(8,128)(2,1)}, u32[]{:S(2)}) %copy-start) | copy-done | bytes 8454168
  42.5 3.1 %shard_map.50 = (f32[2,384,256]{2,1,0:T(8,128)S(1)}, f32[2,384,256]{2,1,0:T(8,128)S(1)}, f32[2,384,256]{2,1,0:T(8,128)S(1)}, f32[2,384,256]{2,1,0:T(8,128)S(1)}) custom-call(bf16[384,11008]{1,0:T(8,128)(2,1)S(1)} %copy-done, bf16[384,11008]{1,0:T(8,128)(2,1)} %collective-permute-done.other_hbm, bf16[688,256]{1,0:T(8,128)(2,1)S(1)} %get-tuple-element.259.refs_0_, ...), custom_call_target="tpu_custom_call" | custom-call | flops 1409286144 | bytes 2752512 | tf_op jit(solution)/shard_map/pallas_call | solution.py:158
  45.7 0.3 collective-permute-start.10
  46.0 1.2 collective-permute-start.9
  47.2 0.3 collective-permute-start.8
  47.5 1.2 collective-permute-start.17
  48.7 4.3 %shard_map.51 = (f32[2,384,256]{2,1,0:T(8,128)S(1)}, f32[2,384,256]{2,1,0:T(8,128)S(1)}, f32[2,384,256]{2,1,0:T(8,128)S(1)}, f32[2,384,256]{2,1,0:T(8,128)S(1)}) custom-call(bf16[384,11008]{1,0:T(8,128)(2,1)S(1)} %copy-done, ...), custom_call_target="tpu_custom_call", output_to_operand_aliasing={{0}: (6, {}), {1}: (7, {}), {2}: (8, {}), {3}: (9, {})} | custom-call | flops 1409286144 | bytes 2752512 | tf_op jit(solution)/shard_map/pallas_call | solution.py:158
  52.9 1.7 collective-permute-done.10.refs_2_
  54.6 0.3 collective-permute-start.16
  54.9 1.2 collective-permute-start.15
  56.1 6.1 %collective-permute-done.8.refs_0_ = bf16[688,256]{1,0:T(8,128)(2,1)S(1)} collective-permute-done((bf16[688,256]{1,0:T(8,128)(2,1)S(1)}, bf16[688,256]{1,0:T(8,128)(2,1)S(1)}, u32[]{:S(2)}, u32[]{:S(2)}) %collective-permute-start.8) | collective-permute-done | bytes 352288 | tf_op jit(solution)/shard_map/ppermute | solution.py:280
  62.2 1.2 collective-permute-start.21
  63.3 0.3 collective-permute-start.14
  63.6 4.3 %shard_map.52 = (f32[2,384,256]{2,1,0:T(8,128)S(1)}, f32[2,384,256]{2,1,0:T(8,128)S(1)}, f32[2,384,256]{2,1,0:T(8,128)S(1)}, f32[2,384,256]{2,1,0:T(8,128)S(1)}) custom-call(bf16[384,11008]{1,0:T(8,128)(2,1)S(1)} %copy-done, ...), custom_call_target="tpu_custom_call", output_to_operand_aliasing={{0}: (6, {}), {1}: (7, {}), {2}: (8, {}), {3}: (9, {})} | custom-call | flops 1409286144 | bytes 2752512 | tf_op jit(solution)/shard_map/pallas_call | solution.py:158
  67.9 3.2 %shard_map.53 = (f32[2,384,256]{2,1,0:T(8,128)S(1)}, f32[2,384,256]{2,1,0:T(8,128)S(1)}, f32[2,384,256]{2,1,0:T(8,128)S(1)}, f32[2,384,256]{2,1,0:T(8,128)S(1)}) custom-call(bf16[384,11008]{1,0:T(8,128)(2,1)S(1)} %copy-done, ...), custom_call_target="tpu_custom_call", output_to_operand_aliasing={{0}: (6, {}), {1}: (7, {}), {2}: (8, {}), {3}: (9, {})} | custom-call | flops 1409286144 | bytes 2752512 | tf_op jit(solution)/shard_map/pallas_call | solution.py:158
  71.2 0.6 collective-permute-start.20
  71.8 0.9 collective-permute-start.19
  72.7 4.6 %collective-permute-done.14.refs_0_ = bf16[688,256]{1,0:T(8,128)(2,1)S(1)} collective-permute-done((bf16[688,256]{1,0:T(8,128)(2,1)S(1)}, bf16[688,256]{1,0:T(8,128)(2,1)S(1)}, u32[]{:S(2)}, u32[]{:S(2)}) %collective-permute-start.14) | collective-permute-done | bytes 352288 | tf_op jit(solution)/shard_map/ppermute | solution.py:280
  77.2 0.3 collective-permute-start.18
  77.5 1.2 collective-permute-start.23
  78.7 3.2 %shard_map.54 = (f32[2,384,256]{2,1,0:T(8,128)S(1)}, f32[2,384,256]{2,1,0:T(8,128)S(1)}, f32[2,384,256]{2,1,0:T(8,128)S(1)}, f32[2,384,256]{2,1,0:T(8,128)S(1)}) custom-call(bf16[384,11008]{1,0:T(8,128)(2,1)S(1)} %copy-done, ...), custom_call_target="tpu_custom_call", output_to_operand_aliasing={{0}: (6, {}), {1}: (7, {}), {2}: (8, {}), {3}: (9, {})} | custom-call | flops 1409286144 | bytes 2752512 | tf_op jit(solution)/shard_map/pallas_call | solution.py:158
  81.9 2.9 %collective-permute-done.20.refs_2_ = bf16[688,256]{1,0:T(8,128)(2,1)S(1)} collective-permute-done((bf16[688,256]{1,0:T(8,128)(2,1)S(1)}, bf16[688,256]{1,0:T(8,128)(2,1)S(1)}, u32[]{:S(2)}, u32[]{:S(2)}) %collective-permute-start.20) | collective-permute-done | bytes 352288 | tf_op jit(solution)/shard_map/ppermute | solution.py:280
  84.8 0.3 collective-permute-start.25
  85.1 1.2 collective-permute-start.26
  86.3 6.1 %collective-permute-done.18.refs_0_ = bf16[688,256]{1,0:T(8,128)(2,1)S(1)} collective-permute-done((bf16[688,256]{1,0:T(8,128)(2,1)S(1)}, bf16[688,256]{1,0:T(8,128)(2,1)S(1)}, u32[]{:S(2)}, u32[]{:S(2)}) %collective-permute-start.18) | collective-permute-done | bytes 352288 | tf_op jit(solution)/shard_map/ppermute | solution.py:280
  92.4 1.2 collective-permute-start.24
  93.5 0.3 collective-permute-start.22
  93.8 3.2 %shard_map.55 = (f32[2,384,256]{2,1,0:T(8,128)S(1)}, f32[2,384,256]{2,1,0:T(8,128)S(1)}, f32[2,384,256]{2,1,0:T(8,128)S(1)}, f32[2,384,256]{2,1,0:T(8,128)S(1)}) custom-call(bf16[384,11008]{1,0:T(8,128)(2,1)S(1)} %copy-done, ...), custom_call_target="tpu_custom_call", output_to_operand_aliasing={{0}: (6, {}), {1}: (7, {}), {2}: (8, {}), {3}: (9, {})} | custom-call | flops 1409286144 | bytes 2752512 | tf_op jit(solution)/shard_map/pallas_call | solution.py:158
  97.0 2.9 %collective-permute-done.25.refs_2_ = bf16[688,256]{1,0:T(8,128)(2,1)S(1)} collective-permute-done((bf16[688,256]{1,0:T(8,128)(2,1)S(1)}, bf16[688,256]{1,0:T(8,128)(2,1)S(1)}, u32[]{:S(2)}, u32[]{:S(2)}) %collective-permute-start.25) | collective-permute-done | bytes 352288 | tf_op jit(solution)/shard_map/ppermute | solution.py:280
  99.9 1.2 collective-permute-start.28
  101.1 0.3 collective-permute-start.27
  101.4 3.2 %shard_map.56 = (f32[2,384,256]{2,1,0:T(8,128)S(1)}, f32[2,384,256]{2,1,0:T(8,128)S(1)}, f32[2,384,256]{2,1,0:T(8,128)S(1)}, f32[2,384,256]{2,1,0:T(8,128)S(1)}) custom-call(bf16[384,11008]{1,0:T(8,128)(2,1)S(1)} %copy-done, ...), custom_call_target="tpu_custom_call", output_to_operand_aliasing={{0}: (6, {}), {1}: (7, {}), {2}: (8, {}), {3}: (9, {})} | custom-call | flops 1409286144 | bytes 2752512 | tf_op jit(solution)/shard_map/pallas_call | solution.py:158
  104.6 2.9 %collective-permute-done.24.refs_1_ = bf16[688,256]{1,0:T(8,128)(2,1)S(1)} collective-permute-done((bf16[688,256]{1,0:T(8,128)(2,1)S(1)}, bf16[688,256]{1,0:T(8,128)(2,1)S(1)}, u32[]{:S(2)}, u32[]{:S(2)}) %collective-permute-start.24) | collective-permute-done | bytes 352288 | tf_op jit(solution)/shard_map/ppermute | solution.py:280
  107.5 2.4 %shard_map.57 = (f32[2,384,256]{2,1,0:T(8,128)S(1)}, f32[2,384,256]{2,1,0:T(8,128)S(1)}, bf16[2,768,896]{2,1,0:T(8,128)(2,1)S(1)}) custom-call(bf16[384,11008]{1,0:T(8,128)(2,1)S(1)} %copy-done, bf16[384,11008]{1,0:T(8,128)(2,1)} %collective-permute-done.other_hbm, ...), custom_call_target="tpu_custom_call", output_to_operand_aliasing={{0}: (4, {}), {1}: (5, {})} | custom-call | flops 704643072 | bytes 2752512 | tf_op jit(solution)/shard_map/pallas_call | solution.py:158
  109.8 4.2 %collective-permute-start.30 = (f32[2,384,256]{2,1,0:T(8,128)S(1)}, f32[2,384,256]{2,1,0:T(8,128)S(1)}, u32[]{:S(2)}, u32[]{:S(2)}) collective-permute-start(f32[2,384,256]{2,1,0:T(8,128)S(1)} %get-tuple-element.254), channel_id=1, source_target_pairs={{0,1},{1,0},{2,3},{3,2},{4,5},{5,4},{6,7},{7,6},{8,9},{9,8},{10,11... | collective-permute-start | bytes 2359304 | tf_op jit(solution)/shard_map/ppermute | solution.py:288
  114.0 1.0 collective-permute-done.28.refs_1_
  115.0 1.1 shard_map.58
  116.1 2.3 %collective-permute-start.29 = (f32[2,384,256]{2,1,0:T(8,128)S(1)}, f32[2,384,256]{2,1,0:T(8,128)S(1)}, u32[]{:S(2)}, u32[]{:S(2)}) collective-permute-start(f32[2,384,256]{2,1,0:T(8,128)S(1)} %get-tuple-element.252), channel_id=1, source_target_pairs={{0,1},{1,0},{2,3},{3,2},{4,5},{5,4},{6,7},{7,6},{8,9},{9,8},{10,11... | collective-permute-start | bytes 2359304 | tf_op jit(solution)/shard_map/ppermute | solution.py:288
  118.5 1.9 %shard_map.59.refs_0_ = bf16[16,6,16,512]{3,2,1,0:T(8,128)(2,1)} custom-call(bf16[768,384]{1,0:T(8,128)(2,1)S(1)} %compare_convert_fusion.place_ref, f32[2,384,256]{2,1,0:T(8,128)S(1)} %get-tuple-element.253.mine_ref, f32[2,384,256]{2,1,0:T(8,128)S(1)} %collective-permute-done.30.theirs_ref), custom_call_target="tpu_custom_call" | custom-call | flops 301989888 | bytes 1572864 | tf_op jit(solution)/shard_map/pallas_call | solution.py:205
  120.4 1.9 %shard_map.60 = bf16[16,6,16,512]{3,2,1,0:T(8,128)(2,1)} custom-call(bf16[768,384]{1,0:T(8,128)(2,1)S(1)} %compare_convert_fusion.place_ref, f32[2,384,256]{2,1,0:T(8,128)S(1)} %get-tuple-element.251.mine_ref, f32[2,384,256]{2,1,0:T(8,128)S(1)} %collective-permute-done.29.theirs_ref, ...), custom_call_target="tpu_custom_call", output_to_operand_aliasing={{}: (3, {})} | custom-call | flops 301989888 | bytes 1572864 | tf_op jit(solution)/shard_map/pallas_call | solution.py:205
  122.3 5.9 %all-to-all-start.1 = ((bf16[16,6,16,512]{3,2,1,0:T(8,128)(2,1)}), bf16[16,6,16,512]{3,2,1,0:T(8,128)(2,1)S(1)}, u32[]{:S(2)}, u32[]{:S(2)}) async-start(bf16[16,6,16,512]{3,2,1,0:T(8,128)(2,1)} %shard_map.60), calls=%async_computation.1 | async-start | bytes 3145728 | tf_op jit(solution)/shard_map/all_to_all | solution.py:241
  128.2 1.3 shard_map.61
  129.5 34.9 %all-to-all-done.1 = bf16[16,6,16,512]{3,2,1,0:T(8,128)(2,1)S(1)} async-done(((bf16[16,6,16,512]{3,2,1,0:T(8,128)(2,1)}), bf16[16,6,16,512]{3,2,1,0:T(8,128)(2,1)S(1)}, u32[]{:S(2)}, u32[]{:S(2)}) %all-to-all-start.1) | async-done | bytes 1572896 | tf_op jit(solution)/shard_map/all_to_all | solution.py:241
  164.4 1.1 copy.64
  (28 shorter events, 0.4 us)
Async XLA Ops:
  0.6 38.5 %collective-permute-start = (bf16[384,11008]{1,0:T(8,128)(2,1)}, bf16[384,11008]{1,0:T(8,128)(2,1)}, u32[]{:S(2)}, u32[]{:S(2)}) collective-permute-start(bf16[384,11008]{1,0:T(8,128)(2,1)} %own_hbm.15), channel_id=1, source_target_pairs={{0,1},{1,0},{2,3},{3,2},{4,5},{5,4},{6,7},{7,6},{8,9},{9,8},{10,11... | collective-permute-start | bytes 25362440 | tf_op jit(solution)/shard_map/ppermute | solution.py:249
  2.5 11.1 %collective-permute-start.11 = (bf16[688,256]{1,0:T(8,128)(2,1)S(1)}, bf16[688,256]{1,0:T(8,128)(2,1)S(1)}, u32[]{:S(2)}, u32[]{:S(2)}) collective-permute-start(bf16[688,256]{1,0:T(8,128)(2,1)S(1)} %get-tuple-element.258.refs_1_), channel_id=1, source_target_pairs={{0,4},{1,5},{2,0},{3,1},{6,2},{7,3},{10,6},{11,7},{14,10},{15,11},... | collective-permute-start | bytes 1056776 | tf_op jit(solution)/shard_map/ppermute | solution.py:280
  2.7 9.5 %collective-permute-start.1 = (bf16[688,256]{1,0:T(8,128)(2,1)S(1)}, bf16[688,256]{1,0:T(8,128)(2,1)S(1)}, u32[]{:S(2)}, u32[]{:S(2)}) collective-permute-start(bf16[688,256]{1,0:T(8,128)(2,1)S(1)} %get-tuple-element.259.refs_0_), channel_id=1, source_target_pairs={{0,2},{1,3},{2,6},{3,7},{6,10},{7,11},{10,14},{11,15},{14,12},{15,... | collective-permute-start | bytes 1056776 | tf_op jit(solution)/shard_map/ppermute | solution.py:280
  7.2 12.7 %collective-permute-start.6 = (bf16[688,256]{1,0:T(8,128)(2,1)S(1)}, bf16[688,256]{1,0:T(8,128)(2,1)}, u32[]{:S(2)}, u32[]{:S(2)}) collective-permute-start(bf16[688,256]{1,0:T(8,128)(2,1)S(1)} %get-tuple-element.260.refs_2_), channel_id=1, source_target_pairs={{0,2},{1,3},{2,6},{3,7},{6,10},{7,11},{10,14},{11,15},{14,12},{15,... | collective-permute-start | bytes 1056776 | tf_op jit(solution)/shard_map/ppermute | solution.py:280
  8.6 12.6 %collective-permute-start.4 = (bf16[688,256]{1,0:T(8,128)(2,1)S(1)}, bf16[688,256]{1,0:T(8,128)(2,1)}, u32[]{:S(2)}, u32[]{:S(2)}) collective-permute-start(bf16[688,256]{1,0:T(8,128)(2,1)S(1)} %get-tuple-element.261.refs_3_), channel_id=1, source_target_pairs={{0,4},{1,5},{2,0},{3,1},{6,2},{7,3},{10,6},{11,7},{14,10},{15,11},... | collective-permute-start | bytes 1056776 | tf_op jit(solution)/shard_map/ppermute | solution.py:280
  12.3 25.4 %collective-permute-start.2 = (bf16[688,256]{1,0:T(8,128)(2,1)S(1)}, bf16[688,256]{1,0:T(8,128)(2,1)S(1)}, u32[]{:S(2)}, u32[]{:S(2)}) collective-permute-start(bf16[688,256]{1,0:T(8,128)(2,1)S(1)} %collective-permute-done.1.refs_0_), channel_id=1, source_target_pairs={{0,2},{1,3},{2,6},{3,7},{6,10},{7,11},{10,14},{11,15},{14,12},{15,... | collective-permute-start | bytes 1056776 | tf_op jit(solution)/shard_map/ppermute | solution.py:280
  13.6 24.4 %collective-permute-start.12 = (bf16[688,256]{1,0:T(8,128)(2,1)S(1)}, bf16[688,256]{1,0:T(8,128)(2,1)S(1)}, u32[]{:S(2)}, u32[]{:S(2)}) collective-permute-start(bf16[688,256]{1,0:T(8,128)(2,1)S(1)} %collective-permute-done.11.refs_1_), channel_id=1, source_target_pairs={{0,4},{1,5},{2,0},{3,1},{6,2},{7,3},{10,6},{11,7},{14,10},{15,11},... | collective-permute-start | bytes 1056776 | tf_op jit(solution)/shard_map/ppermute | solution.py:280
  19.9 25.7 %collective-permute-start.7 = (bf16[688,256]{1,0:T(8,128)(2,1)}, bf16[688,256]{1,0:T(8,128)(2,1)}, u32[]{:S(2)}, u32[]{:S(2)}) collective-permute-start(bf16[688,256]{1,0:T(8,128)(2,1)} %collective-permute-done.6.refs_2_), channel_id=1, source_target_pairs={{0,2},{1,3},{2,6},{3,7},{6,10},{7,11},{10,14},{11,15},{14,12},{15,... | collective-permute-start | bytes 1056776 | tf_op jit(solution)/shard_map/ppermute | solution.py:280
  21.2 24.8 %collective-permute-start.5 = (bf16[688,256]{1,0:T(8,128)(2,1)}, bf16[688,256]{1,0:T(8,128)(2,1)}, u32[]{:S(2)}, u32[]{:S(2)}) collective-permute-start(bf16[688,256]{1,0:T(8,128)(2,1)} %collective-permute-done.4.refs_3_), channel_id=1, source_target_pairs={{0,4},{1,5},{2,0},{3,1},{6,2},{7,3},{10,6},{11,7},{14,10},{15,11},... | collective-permute-start | bytes 1056776 | tf_op jit(solution)/shard_map/ppermute | solution.py:280
  37.6 9.6 %collective-permute-start.3 = (bf16[688,256]{1,0:T(8,128)(2,1)S(1)}, bf16[688,256]{1,0:T(8,128)(2,1)S(1)}, u32[]{:S(2)}, u32[]{:S(2)}) collective-permute-start(bf16[688,256]{1,0:T(8,128)(2,1)S(1)} %collective-permute-done.2.refs_0_), channel_id=1, source_target_pairs={{0,2},{1,3},{2,6},{3,7},{6,10},{7,11},{10,14},{11,15},{14,12},{15,... | collective-permute-start | bytes 1056776 | tf_op jit(solution)/shard_map/ppermute | solution.py:280
  37.9 9.6 %collective-permute-start.13 = (bf16[688,256]{1,0:T(8,128)(2,1)S(1)}, bf16[688,256]{1,0:T(8,128)(2,1)S(1)}, u32[]{:S(2)}, u32[]{:S(2)}) collective-permute-start(bf16[688,256]{1,0:T(8,128)(2,1)S(1)} %collective-permute-done.12.refs_1_), channel_id=1, source_target_pairs={{0,4},{1,5},{2,0},{3,1},{6,2},{7,3},{10,6},{11,7},{14,10},{15,11},... | collective-permute-start | bytes 1056776 | tf_op jit(solution)/shard_map/ppermute | solution.py:280
  39.1 3.4 %copy-start = (bf16[384,11008]{1,0:T(8,128)(2,1)S(1)}, bf16[384,11008]{1,0:T(8,128)(2,1)}, u32[]{:S(2)}) copy-start(bf16[384,11008]{1,0:T(8,128)(2,1)} %own_hbm.15) | copy-start | bytes 25362436
  45.7 8.9 %collective-permute-start.10 = (bf16[688,256]{1,0:T(8,128)(2,1)}, bf16[688,256]{1,0:T(8,128)(2,1)S(1)}, u32[]{:S(2)}, u32[]{:S(2)}) collective-permute-start(bf16[688,256]{1,0:T(8,128)(2,1)} %collective-permute-done.7.refs_2_), channel_id=1, source_target_pairs={{0,2},{1,3},{2,6},{3,7},{6,10},{7,11},{10,14},{11,15},{14,12},{15,... | collective-permute-start | bytes 1056776 | tf_op jit(solution)/shard_map/ppermute | solution.py:280
  46.0 8.9 %collective-permute-start.9 = (bf16[688,256]{1,0:T(8,128)(2,1)}, bf16[688,256]{1,0:T(8,128)(2,1)S(1)}, u32[]{:S(2)}, u32[]{:S(2)}) collective-permute-start(bf16[688,256]{1,0:T(8,128)(2,1)} %collective-permute-done.5.refs_3_), channel_id=1, source_target_pairs={{0,4},{1,5},{2,0},{3,1},{6,2},{7,3},{10,6},{11,7},{14,10},{15,11},... | collective-permute-start | bytes 1056776 | tf_op jit(solution)/shard_map/ppermute | solution.py:280
  47.2 15.0 %collective-permute-start.8 = (bf16[688,256]{1,0:T(8,128)(2,1)S(1)}, bf16[688,256]{1,0:T(8,128)(2,1)S(1)}, u32[]{:S(2)}, u32[]{:S(2)}) collective-permute-start(bf16[688,256]{1,0:T(8,128)(2,1)S(1)} %collective-permute-done.3.refs_0_), channel_id=1, source_target_pairs={{0,2},{1,3},{2,6},{3,7},{6,10},{7,11},{10,14},{11,15},{14,12},{15,... | collective-permute-start | bytes 1056776 | tf_op jit(solution)/shard_map/ppermute | solution.py:280
  47.5 14.7 %collective-permute-start.17 = (bf16[688,256]{1,0:T(8,128)(2,1)S(1)}, bf16[688,256]{1,0:T(8,128)(2,1)S(1)}, u32[]{:S(2)}, u32[]{:S(2)}) collective-permute-start(bf16[688,256]{1,0:T(8,128)(2,1)S(1)} %collective-permute-done.13.refs_1_), channel_id=1, source_target_pairs={{0,4},{1,5},{2,0},{3,1},{6,2},{7,3},{10,6},{11,7},{14,10},{15,11},... | collective-permute-start | bytes 1056776 | tf_op jit(solution)/shard_map/ppermute | solution.py:280
  54.6 16.6 %collective-permute-start.16 = (bf16[688,256]{1,0:T(8,128)(2,1)S(1)}, bf16[688,256]{1,0:T(8,128)(2,1)S(1)}, u32[]{:S(2)}, u32[]{:S(2)}) collective-permute-start(bf16[688,256]{1,0:T(8,128)(2,1)S(1)} %collective-permute-done.10.refs_2_), channel_id=1, source_target_pairs={{0,2},{1,3},{2,6},{3,7},{6,10},{7,11},{10,14},{11,15},{14,12},{15,... | collective-permute-start | bytes 1056776 | tf_op jit(solution)/shard_map/ppermute | solution.py:280
  54.9 16.9 %collective-permute-start.15 = (bf16[688,256]{1,0:T(8,128)(2,1)S(1)}, bf16[688,256]{1,0:T(8,128)(2,1)S(1)}, u32[]{:S(2)}, u32[]{:S(2)}) collective-permute-start(bf16[688,256]{1,0:T(8,128)(2,1)S(1)} %collective-permute-done.9.refs_3_), channel_id=1, source_target_pairs={{0,4},{1,5},{2,0},{3,1},{6,2},{7,3},{10,6},{11,7},{14,10},{15,11},... | collective-permute-start | bytes 1056776 | tf_op jit(solution)/shard_map/ppermute | solution.py:280
  62.2 15.4 %collective-permute-start.21 = (bf16[688,256]{1,0:T(8,128)(2,1)S(1)}, bf16[688,256]{1,0:T(8,128)(2,1)S(1)}, u32[]{:S(2)}, u32[]{:S(2)}) collective-permute-start(bf16[688,256]{1,0:T(8,128)(2,1)S(1)} %collective-permute-done.17.refs_1_), channel_id=1, source_target_pairs={{0,4},{1,5},{2,0},{3,1},{6,2},{7,3},{10,6},{11,7},{14,10},{15,11},... | collective-permute-start | bytes 1056776 | tf_op jit(solution)/shard_map/ppermute | solution.py:280
  63.3 13.9 %collective-permute-start.14 = (bf16[688,256]{1,0:T(8,128)(2,1)S(1)}, bf16[688,256]{1,0:T(8,128)(2,1)S(1)}, u32[]{:S(2)}, u32[]{:S(2)}) collective-permute-start(bf16[688,256]{1,0:T(8,128)(2,1)S(1)} %collective-permute-done.8.refs_0_), channel_id=1, source_target_pairs={{0,2},{1,3},{2,6},{3,7},{6,10},{7,11},{10,14},{11,15},{14,12},{15,... | collective-permute-start | bytes 1056776 | tf_op jit(solution)/shard_map/ppermute | solution.py:280
  71.2 13.6 %collective-permute-start.20 = (bf16[688,256]{1,0:T(8,128)(2,1)S(1)}, bf16[688,256]{1,0:T(8,128)(2,1)S(1)}, u32[]{:S(2)}, u32[]{:S(2)}) collective-permute-start(bf16[688,256]{1,0:T(8,128)(2,1)S(1)} %collective-permute-done.16.refs_2_), channel_id=1, source_target_pairs={{0,2},{1,3},{2,6},{3,7},{6,10},{7,11},{10,14},{11,15},{14,12},{15,... | collective-permute-start | bytes 1056776 | tf_op jit(solution)/shard_map/ppermute | solution.py:280
  71.8 13.3 %collective-permute-start.19 = (bf16[688,256]{1,0:T(8,128)(2,1)S(1)}, bf16[688,256]{1,0:T(8,128)(2,1)S(1)}, u32[]{:S(2)}, u32[]{:S(2)}) collective-permute-start(bf16[688,256]{1,0:T(8,128)(2,1)S(1)} %collective-permute-done.15.refs_3_), channel_id=1, source_target_pairs={{0,4},{1,5},{2,0},{3,1},{6,2},{7,3},{10,6},{11,7},{14,10},{15,11},... | collective-permute-start | bytes 1056776 | tf_op jit(solution)/shard_map/ppermute | solution.py:280
  77.2 15.1 %collective-permute-start.18 = (bf16[688,256]{1,0:T(8,128)(2,1)S(1)}, bf16[688,256]{1,0:T(8,128)(2,1)S(1)}, u32[]{:S(2)}, u32[]{:S(2)}) collective-permute-start(bf16[688,256]{1,0:T(8,128)(2,1)S(1)} %collective-permute-done.14.refs_0_), channel_id=1, source_target_pairs={{0,2},{1,3},{2,6},{3,7},{6,10},{7,11},{10,14},{11,15},{14,12},{15,... | collective-permute-start | bytes 1056776 | tf_op jit(solution)/shard_map/ppermute | solution.py:280
  77.5 14.8 %collective-permute-start.23 = (bf16[688,256]{1,0:T(8,128)(2,1)S(1)}, bf16[688,256]{1,0:T(8,128)(2,1)S(1)}, u32[]{:S(2)}, u32[]{:S(2)}) collective-permute-start(bf16[688,256]{1,0:T(8,128)(2,1)S(1)} %collective-permute-done.21.refs_1_), channel_id=1, source_target_pairs={{0,4},{1,5},{2,0},{3,1},{6,2},{7,3},{10,6},{11,7},{14,10},{15,11},... | collective-permute-start | bytes 1056776 | tf_op jit(solution)/shard_map/ppermute | solution.py:280
  84.8 15.1 %collective-permute-start.25 = (bf16[688,256]{1,0:T(8,128)(2,1)S(1)}, bf16[688,256]{1,0:T(8,128)(2,1)S(1)}, u32[]{:S(2)}, u32[]{:S(2)}) collective-permute-start(bf16[688,256]{1,0:T(8,128)(2,1)S(1)} %collective-permute-done.20.refs_2_), channel_id=1, source_target_pairs={{0,2},{1,3},{2,6},{3,7},{6,10},{7,11},{10,14},{11,15},{14,12},{15,... | collective-permute-start | bytes 1056776 | tf_op jit(solution)/shard_map/ppermute | solution.py:280
  85.1 14.8 %collective-permute-start.26 = (bf16[688,256]{1,0:T(8,128)(2,1)S(1)}, bf16[688,256]{1,0:T(8,128)(2,1)S(1)}, u32[]{:S(2)}, u32[]{:S(2)}) collective-permute-start(bf16[688,256]{1,0:T(8,128)(2,1)S(1)} %collective-permute-done.19.refs_3_), channel_id=1, source_target_pairs={{0,4},{1,5},{2,0},{3,1},{6,2},{7,3},{10,6},{11,7},{14,10},{15,11},... | collective-permute-start | bytes 1056776 | tf_op jit(solution)/shard_map/ppermute | solution.py:280
  92.4 15.1 %collective-permute-start.24 = (bf16[688,256]{1,0:T(8,128)(2,1)S(1)}, bf16[688,256]{1,0:T(8,128)(2,1)S(1)}, u32[]{:S(2)}, u32[]{:S(2)}) collective-permute-start(bf16[688,256]{1,0:T(8,128)(2,1)S(1)} %collective-permute-done.23.refs_1_), channel_id=1, source_target_pairs={{0,4},{1,5},{2,0},{3,1},{6,2},{7,3},{10,6},{11,7},{14,10},{15,11},... | collective-permute-start | bytes 1056776 | tf_op jit(solution)/shard_map/ppermute | solution.py:280
  93.5 13.9 %collective-permute-start.22 = (bf16[688,256]{1,0:T(8,128)(2,1)S(1)}, bf16[688,256]{1,0:T(8,128)(2,1)S(1)}, u32[]{:S(2)}, u32[]{:S(2)}) collective-permute-start(bf16[688,256]{1,0:T(8,128)(2,1)S(1)} %collective-permute-done.18.refs_0_), channel_id=1, source_target_pairs={{0,2},{1,3},{2,6},{3,7},{6,10},{7,11},{10,14},{11,15},{14,12},{15,... | collective-permute-start | bytes 1056776 | tf_op jit(solution)/shard_map/ppermute | solution.py:280
  99.9 15.1 %collective-permute-start.28 = (bf16[688,256]{1,0:T(8,128)(2,1)S(1)}, bf16[688,256]{1,0:T(8,128)(2,1)S(1)}, u32[]{:S(2)}, u32[]{:S(2)}) collective-permute-start(bf16[688,256]{1,0:T(8,128)(2,1)S(1)} %collective-permute-done.26.refs_3_), channel_id=1, source_target_pairs={{0,4},{1,5},{2,0},{3,1},{6,2},{7,3},{10,6},{11,7},{14,10},{15,11},... | collective-permute-start | bytes 1056776 | tf_op jit(solution)/shard_map/ppermute | solution.py:280
  101.1 13.9 %collective-permute-start.27 = (bf16[688,256]{1,0:T(8,128)(2,1)S(1)}, bf16[688,256]{1,0:T(8,128)(2,1)S(1)}, u32[]{:S(2)}, u32[]{:S(2)}) collective-permute-start(bf16[688,256]{1,0:T(8,128)(2,1)S(1)} %collective-permute-done.25.refs_2_), channel_id=1, source_target_pairs={{0,2},{1,3},{2,6},{3,7},{6,10},{7,11},{10,14},{11,15},{14,12},{15,... | collective-permute-start | bytes 1056776 | tf_op jit(solution)/shard_map/ppermute | solution.py:280
  109.8 8.6 %collective-permute-start.30 = (f32[2,384,256]{2,1,0:T(8,128)S(1)}, f32[2,384,256]{2,1,0:T(8,128)S(1)}, u32[]{:S(2)}, u32[]{:S(2)}) collective-permute-start(f32[2,384,256]{2,1,0:T(8,128)S(1)} %get-tuple-element.254), channel_id=1, source_target_pairs={{0,1},{1,0},{2,3},{3,2},{4,5},{5,4},{6,7},{7,6},{8,9},{9,8},{10,11... | collective-permute-start | bytes 2359304 | tf_op jit(solution)/shard_map/ppermute | solution.py:288
  116.1 4.2 %collective-permute-start.29 = (f32[2,384,256]{2,1,0:T(8,128)S(1)}, f32[2,384,256]{2,1,0:T(8,128)S(1)}, u32[]{:S(2)}, u32[]{:S(2)}) collective-permute-start(f32[2,384,256]{2,1,0:T(8,128)S(1)} %get-tuple-element.252), channel_id=1, source_target_pairs={{0,1},{1,0},{2,3},{3,2},{4,5},{5,4},{6,7},{7,6},{8,9},{9,8},{10,11... | collective-permute-start | bytes 2359304 | tf_op jit(solution)/shard_map/ppermute | solution.py:288
  122.3 42.1 %all-to-all-start.1 = ((bf16[16,6,16,512]{3,2,1,0:T(8,128)(2,1)}), bf16[16,6,16,512]{3,2,1,0:T(8,128)(2,1)S(1)}, u32[]{:S(2)}, u32[]{:S(2)}) async-start(bf16[16,6,16,512]{3,2,1,0:T(8,128)(2,1)} %shard_map.60), calls=%async_computation.1 | async-start | bytes 3145728 | tf_op jit(solution)/shard_map/all_to_all | solution.py:241

commit v12 on v10

--- a/solution.py
+++ b/solution.py
@@ -272,11 +272,9 @@
                 done += 1
             for i in range(norb):
                 sent = piece[j][i]
-                if t == 1 and i == j == HALVES - 1:
+                if t == 1 and i == j == 0:
                     sent, labels = lax.optimization_barrier((sent, labels))
                     ids = exchange(labels)
-                if t == 3 and i == j == 0:
-                    sent, ids = lax.optimization_barrier((sent, ids))
                 if BEHIND[t][j]:
                     sent, sums = lax.optimization_barrier((sent, sums))
                 piece[j][i] = lax.ppermute(sent, "wide", shift[i])

time: 165 us -> 170 us (1.030)
  blocking collectives: 15.6 us -> 0 us
  local copies, waits for them, and re-layouts: 7.19 us -> 16.5 us
  starting transfers between devices: 33.2 us -> 39.1 us
  waiting for transfers between devices: 73 us -> 77.5 us
    all_to_all x1 -> x0, blocking collectives: 15.6 us -> none  [exchange(): lax.all_to_all(value, 'wide', split_axis=0, concat_axis=0, tiled=True)]
    unnamed x3 -> x29, local copies, waits for them, and re-layouts: 4.54 us -> 13.3 us
    all_to_all x1 -> x2, starting transfers between devices: 5.9 us -> 12.1 us  [exchange(): lax.all_to_all(value, 'wide', split_axis=0, concat_axis=0, tiled=True)]
    ppermute x28, waiting for transfers between devices: 38.1 us -> 42.6 us  [ring_products(): piece[j][i] = lax.ppermute(sent, 'wide', shift[i])]
    all_to_all x1 -> x2, waiting for transfers between devices: 34.9 us -> 34.9 us  [exchange(): lax.all_to_all(value, 'wide', split_axis=0, concat_axis=0, tiled=True)]
  transfers between devices with their start and end apart: 32 -> 33, of which waited for: 11 -> 14; matrix products, arithmetic and copies ran while one was open for 3% -> 3% of each run, Pallas kernels for 19% -> 19%
where the time goes in v12:
time: 170 us
  waiting for transfers between devices  77.5 us (46%)
  starting transfers between devices  39.1 us (23%)
  Pallas kernels  33 us (19%)
  local copies, waits for them, and re-layouts  16.5 us (10%)
  other arithmetic  2.69 us (2%)
    ppermute x28, waiting for transfers between devices, ring_products(): piece[j][i] = lax.ppermute(sent, 'wide', shift[i])  42.6 us
    all_to_all x2, waiting for transfers between devices, exchange(): lax.all_to_all(value, 'wide', split_axis=0, concat_axis=0, tiled=True)  34.9 us
    pallas_call x8, Pallas kernels, add_products(): pl.pallas_call(functools.partial(step_kernel, t, parts), out_shape=[sums]...  25.9 us
    ppermute x28, starting transfers between devices, ring_products(): piece[j][i] = lax.ppermute(sent, 'wide', shift[i])  20.7 us
    unnamed x29, local copies, waits for them, and re-layouts  13.3 us
    all_to_all x2, starting transfers between devices, exchange(): lax.all_to_all(value, 'wide', split_axis=0, concat_axis=0, tiled=True)  12.1 us
    ppermute x2, starting transfers between devices, ring_products(): theirs = [lax.ppermute(sums[j][1], 'wide', swap) for j in range(HALVES)]  5.53 us
    pallas_call x2, Pallas kernels, finish(): pl.pallas_call(functools.partial(finish_kernel, half), out_shape=jax.Shap...  4.66 us
  transfers between devices with their start and end apart: 33, of which 14 were waited for; matrix products, arithmetic and copies ran while one was open for 3% of the time, Pallas kernels for 19%

profile of v12, /device:TPU:13, one launch (start us, length us, event | category | flops | bytes accessed | tf_op | source)
XLA Modules:
  0.0 169.7 jit_solution(1867729494596943500)
XLA Ops:
  0.6 0.7 collective-permute-start
  1.4 1.1 slice_bitcast_fusion
  2.7 1.3 collective-permute-start.1
  4.0 0.9 convert_reduce_fusion
  4.9 0.7 broadcast_multiply_fusion
  5.9 1.0 compare_convert_fusion.place_ref
  6.9 1.1 slice_bitcast_fusion.1
  8.1 1.3 collective-permute-start.6
  9.4 0.7 copy-done.5
  10.3 0.7 copy-done.7
  11.2 0.7 sub.19
  11.9 0.4 collective-permute-done.1.refs_0_
  12.3 1.3 collective-permute-start.2
  13.6 0.8 copy-done.11
  14.5 0.7 copy-done.9
  15.2 4.7 %collective-permute-done.6.refs_2_ = bf16[688,256]{1,0:T(8,128)(2,1)} collective-permute-done((bf16[688,256]{1,0:T(8,128)(2,1)S(1)}, bf16[688,256]{1,0:T(8,128)(2,1)}, u32[]{:S(2)}, u32[]{:S(2)}) %collective-permute-start.6) | collective-permute-done | bytes 352288 | tf_op jit(solution)/shard_map/ppermute | solution.py:280
  19.9 1.3 collective-permute-start.7
  21.4 6.0 %collective-permute-done.2.refs_0_ = bf16[688,256]{1,0:T(8,128)(2,1)S(1)} collective-permute-done((bf16[688,256]{1,0:T(8,128)(2,1)S(1)}, bf16[688,256]{1,0:T(8,128)(2,1)S(1)}, u32[]{:S(2)}, u32[]{:S(2)}) %collective-permute-start.2) | collective-permute-done | bytes 352288 | tf_op jit(solution)/shard_map/ppermute | solution.py:280
  27.4 1.3 collective-permute-start.3
  28.8 3.4 %copy-done = bf16[384,11008]{1,0:T(8,128)(2,1)S(1)} copy-done((bf16[384,11008]{1,0:T(8,128)(2,1)S(1)}, bf16[384,11008]{1,0:T(8,128)(2,1)}, u32[]{:S(2)}) %copy-start) | copy-done | bytes 8454168
  32.3 1.0 copy-done.4
  33.2 1.0 copy-done.6
  34.2 1.0 copy-done.8
  35.2 3.3 %shard_map.50 = (f32[2,384,256]{2,1,0:T(8,128)S(1)}, f32[2,384,256]{2,1,0:T(8,128)S(1)}, f32[2,384,256]{2,1,0:T(8,128)S(1)}, f32[2,384,256]{2,1,0:T(8,128)S(1)}) custom-call(bf16[384,11008]{1,0:T(8,128)(2,1)S(1)} %copy-done, bf16[384,11008]{1,0:T(8,128)(2,1)} %collective-permute-done.other_hbm, bf16[688,256]{1,0:T(8,128)(2,1)S(1)} %copy-done.4, ...), custom_call_target="tpu_custom_call" | custom-call | flops 1409286144 | bytes 2752512 | tf_op jit(solution)/shard_map/pallas_call | solution.py:158
  38.5 1.3 collective-permute-start.10
  40.0 2.4 %collective-permute-done.3.refs_0_ = bf16[688,256]{1,0:T(8,128)(2,1)S(1)} collective-permute-done((bf16[688,256]{1,0:T(8,128)(2,1)S(1)}, bf16[688,256]{1,0:T(8,128)(2,1)S(1)}, u32[]{:S(2)}, u32[]{:S(2)}) %collective-permute-start.3) | collective-permute-done | bytes 352288 | tf_op jit(solution)/shard_map/ppermute | solution.py:280
  42.5 1.3 collective-permute-start.8
  43.9 4.3 %shard_map.51 = (f32[2,384,256]{2,1,0:T(8,128)S(1)}, f32[2,384,256]{2,1,0:T(8,128)S(1)}, f32[2,384,256]{2,1,0:T(8,128)S(1)}, f32[2,384,256]{2,1,0:T(8,128)S(1)}) custom-call(bf16[384,11008]{1,0:T(8,128)(2,1)S(1)} %copy-done, ...), custom_call_target="tpu_custom_call", output_to_operand_aliasing={{0}: (6, {}), {1}: (7, {}), {2}: (8, {}), {3}: (9, {})} | custom-call | flops 1409286144 | bytes 2752512 | tf_op jit(solution)/shard_map/pallas_call | solution.py:158
  48.2 1.5 collective-permute-done.10.refs_2_
  49.7 1.3 collective-permute-start.16
  51.2 6.1 %collective-permute-done.8.refs_0_ = bf16[688,256]{1,0:T(8,128)(2,1)S(1)} collective-permute-done((bf16[688,256]{1,0:T(8,128)(2,1)S(1)}, bf16[688,256]{1,0:T(8,128)(2,1)S(1)}, u32[]{:S(2)}, u32[]{:S(2)}) %collective-permute-start.8) | collective-permute-done | bytes 352288 | tf_op jit(solution)/shard_map/ppermute | solution.py:280
  57.6 1.1 collective-permute-start.14
  58.8 3.2 %shard_map.52 = (f32[2,384,256]{2,1,0:T(8,128)S(1)}, f32[2,384,256]{2,1,0:T(8,128)S(1)}, f32[2,384,256]{2,1,0:T(8,128)S(1)}, f32[2,384,256]{2,1,0:T(8,128)S(1)}) custom-call(bf16[384,11008]{1,0:T(8,128)(2,1)S(1)} %copy-done, ...), custom_call_target="tpu_custom_call", output_to_operand_aliasing={{0}: (6, {}), {1}: (7, {}), {2}: (8, {}), {3}: (9, {})} | custom-call | flops 1409286144 | bytes 2752512 | tf_op jit(solution)/shard_map/pallas_call | solution.py:158
  61.9 3.2 %shard_map.53 = (f32[2,384,256]{2,1,0:T(8,128)S(1)}, f32[2,384,256]{2,1,0:T(8,128)S(1)}, f32[2,384,256]{2,1,0:T(8,128)S(1)}, f32[2,384,256]{2,1,0:T(8,128)S(1)}) custom-call(bf16[384,11008]{1,0:T(8,128)(2,1)S(1)} %copy-done, ...), custom_call_target="tpu_custom_call", output_to_operand_aliasing={{0}: (6, {}), {1}: (7, {}), {2}: (8, {}), {3}: (9, {})} | custom-call | flops 1409286144 | bytes 2752512 | tf_op jit(solution)/shard_map/pallas_call | solution.py:158
  65.2 1.3 collective-permute-start.20
  66.7 5.7 %collective-permute-done.14.refs_0_ = bf16[688,256]{1,0:T(8,128)(2,1)S(1)} collective-permute-done((bf16[688,256]{1,0:T(8,128)(2,1)S(1)}, bf16[688,256]{1,0:T(8,128)(2,1)S(1)}, u32[]{:S(2)}, u32[]{:S(2)}) %collective-permute-start.14) | collective-permute-done | bytes 352288 | tf_op jit(solution)/shard_map/ppermute | solution.py:280
  72.4 1.3 collective-permute-start.18
  73.8 3.2 %shard_map.54 = (f32[2,384,256]{2,1,0:T(8,128)S(1)}, f32[2,384,256]{2,1,0:T(8,128)S(1)}, f32[2,384,256]{2,1,0:T(8,128)S(1)}, f32[2,384,256]{2,1,0:T(8,128)S(1)}) custom-call(bf16[384,11008]{1,0:T(8,128)(2,1)S(1)} %copy-done, ...), custom_call_target="tpu_custom_call", output_to_operand_aliasing={{0}: (6, {}), {1}: (7, {}), {2}: (8, {}), {3}: (9, {})} | custom-call | flops 1409286144 | bytes 2752512 | tf_op jit(solution)/shard_map/pallas_call | solution.py:158
  77.0 2.9 %collective-permute-done.20.refs_2_ = bf16[688,256]{1,0:T(8,128)(2,1)S(1)} collective-permute-done((bf16[688,256]{1,0:T(8,128)(2,1)S(1)}, bf16[688,256]{1,0:T(8,128)(2,1)S(1)}, u32[]{:S(2)}, u32[]{:S(2)}) %collective-permute-start.20) | collective-permute-done | bytes 352288 | tf_op jit(solution)/shard_map/ppermute | solution.py:280
  79.9 1.3 collective-permute-start.25
  81.4 6.1 %collective-permute-done.18.refs_0_ = bf16[688,256]{1,0:T(8,128)(2,1)S(1)} collective-permute-done((bf16[688,256]{1,0:T(8,128)(2,1)S(1)}, bf16[688,256]{1,0:T(8,128)(2,1)S(1)}, u32[]{:S(2)}, u32[]{:S(2)}) %collective-permute-start.18) | collective-permute-done | bytes 352288 | tf_op jit(solution)/shard_map/ppermute | solution.py:280
  87.5 0.3 collective-permute-start.24
  87.8 1.1 collective-permute-start.22
  88.9 3.2 %shard_map.55 = (f32[2,384,256]{2,1,0:T(8,128)S(1)}, f32[2,384,256]{2,1,0:T(8,128)S(1)}, f32[2,384,256]{2,1,0:T(8,128)S(1)}, f32[2,384,256]{2,1,0:T(8,128)S(1)}) custom-call(bf16[384,11008]{1,0:T(8,128)(2,1)S(1)} %copy-done, ...), custom_call_target="tpu_custom_call", output_to_operand_aliasing={{0}: (6, {}), {1}: (7, {}), {2}: (8, {}), {3}: (9, {})} | custom-call | flops 1409286144 | bytes 2752512 | tf_op jit(solution)/shard_map/pallas_call | solution.py:158
  92.1 2.9 %collective-permute-done.25.refs_2_ = bf16[688,256]{1,0:T(8,128)(2,1)S(1)} collective-permute-done((bf16[688,256]{1,0:T(8,128)(2,1)S(1)}, bf16[688,256]{1,0:T(8,128)(2,1)S(1)}, u32[]{:S(2)}, u32[]{:S(2)}) %collective-permute-start.25) | collective-permute-done | bytes 352288 | tf_op jit(solution)/shard_map/ppermute | solution.py:280
  95.4 1.1 collective-permute-start.27
  96.5 3.2 %shard_map.56 = (f32[2,384,256]{2,1,0:T(8,128)S(1)}, f32[2,384,256]{2,1,0:T(8,128)S(1)}, f32[2,384,256]{2,1,0:T(8,128)S(1)}, f32[2,384,256]{2,1,0:T(8,128)S(1)}) custom-call(bf16[384,11008]{1,0:T(8,128)(2,1)S(1)} %copy-done, ...), custom_call_target="tpu_custom_call", output_to_operand_aliasing={{0}: (6, {}), {1}: (7, {}), {2}: (8, {}), {3}: (9, {})} | custom-call | flops 1409286144 | bytes 2752512 | tf_op jit(solution)/shard_map/pallas_call | solution.py:158
  99.7 1.0 collective-permute-done.24.refs_1_
  100.7 1.9 %collective-permute-done.22.refs_0_ = bf16[688,256]{1,0:T(8,128)(2,1)S(1)} collective-permute-done((bf16[688,256]{1,0:T(8,128)(2,1)S(1)}, bf16[688,256]{1,0:T(8,128)(2,1)S(1)}, u32[]{:S(2)}, u32[]{:S(2)}) %collective-permute-start.22) | collective-permute-done | bytes 352288 | tf_op jit(solution)/shard_map/ppermute | solution.py:280
  102.6 2.4 %shard_map.57 = (f32[2,384,256]{2,1,0:T(8,128)S(1)}, f32[2,384,256]{2,1,0:T(8,128)S(1)}, bf16[2,768,896]{2,1,0:T(8,128)(2,1)S(1)}) custom-call(bf16[384,11008]{1,0:T(8,128)(2,1)S(1)} %copy-done, bf16[384,11008]{1,0:T(8,128)(2,1)} %collective-permute-done.other_hbm, ...), custom_call_target="tpu_custom_call", output_to_operand_aliasing={{0}: (4, {}), {1}: (5, {})} | custom-call | flops 704643072 | bytes 2752512 | tf_op jit(solution)/shard_map/pallas_call | solution.py:158
  104.9 4.1 %collective-permute-start.30 = (f32[2,384,256]{2,1,0:T(8,128)S(1)}, f32[2,384,256]{2,1,0:T(8,128)}, u32[]{:S(2)}, u32[]{:S(2)}) collective-permute-start(f32[2,384,256]{2,1,0:T(8,128)S(1)} %get-tuple-element.254), channel_id=1, source_target_pairs={{0,1},{1,0},{2,3},{3,2},{4,5},{5,4},{6,7},{7,6},{8,9},{9,8},{10,11... | collective-permute-start | bytes 2359304 | tf_op jit(solution)/shard_map/ppermute | solution.py:288
  109.0 1.1 collective-permute-done.27.refs_0_
  110.1 1.1 shard_map.58
  111.2 1.5 collective-permute-start.29
  112.7 6.1 %all-to-all-start.1 = ((s32[16,1,16]{2,1,0:T(1,128)}), s32[16,1,16]{2,1,0:T(1,128)S(1)}, u32[]{:S(2)}, u32[]{:S(2)}) async-start(s32[16,1,16]{2,1,0:T(1,128)} %bitcast.7), calls=%async_computation.1 | async-start | bytes 16384 | tf_op jit(solution)/shard_map/all_to_all | solution.py:241
  118.8 1.1 copy-done.2
  119.9 2.3 %shard_map.59.refs_0_ = bf16[16,6,16,512]{3,2,1,0:T(8,128)(2,1)S(1)} custom-call(bf16[768,384]{1,0:T(8,128)(2,1)S(1)} %copy-done.2, f32[2,384,256]{2,1,0:T(8,128)S(1)} %get-tuple-element.253.mine_ref, f32[2,384,256]{2,1,0:T(8,128)} %collective-permute-done.30.theirs_ref), custom_call_target="tpu_custom_call" | custom-call | flops 301989888 | bytes 1572864 | tf_op jit(solution)/shard_map/pallas_call | solution.py:205
  122.2 2.3 %shard_map.60 = bf16[16,6,16,512]{3,2,1,0:T(8,128)(2,1)S(1)} custom-call(bf16[768,384]{1,0:T(8,128)(2,1)S(1)} %copy-done.2, f32[2,384,256]{2,1,0:T(8,128)S(1)} %get-tuple-element.251.mine_ref, f32[2,384,256]{2,1,0:T(8,128)} %collective-permute-done.29.theirs_ref, bf16[16,6,16,512]{3,2,1,0:T(8,128)(2,1)S(1)} %shard_map.59.refs_0_), custom_call_target="tpu_custom_call", output_to_operand_aliasing={{}: (3, {})} | custom-call | flops 301989888 | bytes 1572864 | tf_op jit(solution)/shard_map/pallas_call | solution.py:205
  124.6 1.1 copy-done.1
  125.7 0.6 copy-done.13
  126.3 6.0 %all-to-all-start = ((bf16[16,6,16,512]{3,2,1,0:T(8,128)(2,1)}), bf16[16,6,16,512]{3,2,1,0:T(8,128)(2,1)S(1)}, u32[]{:S(2)}, u32[]{:S(2)}) async-start(bf16[16,6,16,512]{3,2,1,0:T(8,128)(2,1)} %copy-done.1), calls=%async_computation | async-start | bytes 3145728 | tf_op jit(solution)/shard_map/all_to_all | solution.py:241
  132.3 1.3 shard_map.61
  133.7 34.9 %all-to-all-done = bf16[16,6,16,512]{3,2,1,0:T(8,128)(2,1)S(1)} async-done(((bf16[16,6,16,512]{3,2,1,0:T(8,128)(2,1)}), bf16[16,6,16,512]{3,2,1,0:T(8,128)(2,1)S(1)}, u32[]{:S(2)}, u32[]{:S(2)}) %all-to-all-start) | async-done | bytes 1572896 | tf_op jit(solution)/shard_map/all_to_all | solution.py:241
  168.5 1.1 copy.64
  (55 shorter events, 3.1 us)
Async XLA Ops:
  0.6 28.2 %collective-permute-start = (bf16[384,11008]{1,0:T(8,128)(2,1)}, bf16[384,11008]{1,0:T(8,128)(2,1)}, u32[]{:S(2)}, u32[]{:S(2)}) collective-permute-start(bf16[384,11008]{1,0:T(8,128)(2,1)} %own_hbm.15), channel_id=1, source_target_pairs={{0,1},{1,0},{2,3},{3,2},{4,5},{5,4},{6,7},{7,6},{8,9},{9,8},{10,11... | collective-permute-start | bytes 25362440 | tf_op jit(solution)/shard_map/ppermute | solution.py:249
  2.5 26.3 %copy-start.3 = (bf16[688,256]{1,0:T(8,128)(2,1)}, bf16[688,256]{1,0:T(8,128)(2,1)S(1)}, u32[]{:S(2)}) copy-start(bf16[688,256]{1,0:T(8,128)(2,1)S(1)} %get-tuple-element.259.refs_0_) | copy-start | bytes 1056772
  2.5 11.8 %collective-permute-start.11 = (bf16[688,256]{1,0:T(8,128)(2,1)S(1)}, bf16[688,256]{1,0:T(8,128)(2,1)S(1)}, u32[]{:S(2)}, u32[]{:S(2)}) collective-permute-start(bf16[688,256]{1,0:T(8,128)(2,1)S(1)} %get-tuple-element.258.refs_1_), channel_id=1, source_target_pairs={{0,4},{1,5},{2,0},{3,1},{6,2},{7,3},{10,6},{11,7},{14,10},{15,11},... | collective-permute-start | bytes 1056776 | tf_op jit(solution)/shard_map/ppermute | solution.py:280
  2.7 9.5 %collective-permute-start.1 = (bf16[688,256]{1,0:T(8,128)(2,1)S(1)}, bf16[688,256]{1,0:T(8,128)(2,1)S(1)}, u32[]{:S(2)}, u32[]{:S(2)}) collective-permute-start(bf16[688,256]{1,0:T(8,128)(2,1)S(1)} %get-tuple-element.259.refs_0_), channel_id=1, source_target_pairs={{0,2},{1,3},{2,6},{3,7},{6,10},{7,11},{10,14},{11,15},{14,12},{15,... | collective-permute-start | bytes 1056776 | tf_op jit(solution)/shard_map/ppermute | solution.py:280
  8.1 11.9 %collective-permute-start.6 = (bf16[688,256]{1,0:T(8,128)(2,1)S(1)}, bf16[688,256]{1,0:T(8,128)(2,1)}, u32[]{:S(2)}, u32[]{:S(2)}) collective-permute-start(bf16[688,256]{1,0:T(8,128)(2,1)S(1)} %get-tuple-element.260.refs_2_), channel_id=1, source_target_pairs={{0,2},{1,3},{2,6},{3,7},{6,10},{7,11},{10,14},{11,15},{14,12},{15,... | collective-permute-start | bytes 1056776 | tf_op jit(solution)/shard_map/ppermute | solution.py:280
  9.4 0.7 copy-start.5
  10.1 11.1 %collective-permute-start.4 = (bf16[688,256]{1,0:T(8,128)(2,1)S(1)}, bf16[688,256]{1,0:T(8,128)(2,1)}, u32[]{:S(2)}, u32[]{:S(2)}) collective-permute-start(bf16[688,256]{1,0:T(8,128)(2,1)S(1)} %get-tuple-element.261.refs_3_), channel_id=1, source_target_pairs={{0,4},{1,5},{2,0},{3,1},{6,2},{7,3},{10,6},{11,7},{14,10},{15,11},... | collective-permute-start | bytes 1056776 | tf_op jit(solution)/shard_map/ppermute | solution.py:280
  10.3 0.7 copy-start.7
  12.3 15.1 %collective-permute-start.2 = (bf16[688,256]{1,0:T(8,128)(2,1)S(1)}, bf16[688,256]{1,0:T(8,128)(2,1)S(1)}, u32[]{:S(2)}, u32[]{:S(2)}) collective-permute-start(bf16[688,256]{1,0:T(8,128)(2,1)S(1)} %collective-permute-done.1.refs_0_), channel_id=1, source_target_pairs={{0,2},{1,3},{2,6},{3,7},{6,10},{7,11},{10,14},{11,15},{14,12},{15,... | collective-permute-start | bytes 1056776 | tf_op jit(solution)/shard_map/ppermute | solution.py:280
  13.6 0.8 copy-start.11
  14.3 14.3 %collective-permute-start.12 = (bf16[688,256]{1,0:T(8,128)(2,1)S(1)}, bf16[688,256]{1,0:T(8,128)(2,1)S(1)}, u32[]{:S(2)}, u32[]{:S(2)}) collective-permute-start(bf16[688,256]{1,0:T(8,128)(2,1)S(1)} %collective-permute-done.11.refs_1_), channel_id=1, source_target_pairs={{0,4},{1,5},{2,0},{3,1},{6,2},{7,3},{10,6},{11,7},{14,10},{15,11},... | collective-permute-start | bytes 1056776 | tf_op jit(solution)/shard_map/ppermute | solution.py:280
  14.5 0.7 copy-start.9
  19.9 18.6 %collective-permute-start.7 = (bf16[688,256]{1,0:T(8,128)(2,1)}, bf16[688,256]{1,0:T(8,128)(2,1)S(1)}, u32[]{:S(2)}, u32[]{:S(2)}) collective-permute-start(bf16[688,256]{1,0:T(8,128)(2,1)} %collective-permute-done.6.refs_2_), channel_id=1, source_target_pairs={{0,2},{1,3},{2,6},{3,7},{6,10},{7,11},{10,14},{11,15},{14,12},{15,... | collective-permute-start | bytes 1056776 | tf_op jit(solution)/shard_map/ppermute | solution.py:280
  21.2 18.6 %collective-permute-start.5 = (bf16[688,256]{1,0:T(8,128)(2,1)}, bf16[688,256]{1,0:T(8,128)(2,1)S(1)}, u32[]{:S(2)}, u32[]{:S(2)}) collective-permute-start(bf16[688,256]{1,0:T(8,128)(2,1)} %collective-permute-done.4.refs_3_), channel_id=1, source_target_pairs={{0,4},{1,5},{2,0},{3,1},{6,2},{7,3},{10,6},{11,7},{14,10},{15,11},... | collective-permute-start | bytes 1056776 | tf_op jit(solution)/shard_map/ppermute | solution.py:280
  27.4 15.1 %collective-permute-start.3 = (bf16[688,256]{1,0:T(8,128)(2,1)S(1)}, bf16[688,256]{1,0:T(8,128)(2,1)S(1)}, u32[]{:S(2)}, u32[]{:S(2)}) collective-permute-start(bf16[688,256]{1,0:T(8,128)(2,1)S(1)} %collective-permute-done.2.refs_0_), channel_id=1, source_target_pairs={{0,2},{1,3},{2,6},{3,7},{6,10},{7,11},{10,14},{11,15},{14,12},{15,... | collective-permute-start | bytes 1056776 | tf_op jit(solution)/shard_map/ppermute | solution.py:280
  28.7 15.1 %collective-permute-start.13 = (bf16[688,256]{1,0:T(8,128)(2,1)S(1)}, bf16[688,256]{1,0:T(8,128)(2,1)S(1)}, u32[]{:S(2)}, u32[]{:S(2)}) collective-permute-start(bf16[688,256]{1,0:T(8,128)(2,1)S(1)} %collective-permute-done.12.refs_1_), channel_id=1, source_target_pairs={{0,4},{1,5},{2,0},{3,1},{6,2},{7,3},{10,6},{11,7},{14,10},{15,11},... | collective-permute-start | bytes 1056776 | tf_op jit(solution)/shard_map/ppermute | solution.py:280
  28.8 3.4 %copy-start = (bf16[384,11008]{1,0:T(8,128)(2,1)S(1)}, bf16[384,11008]{1,0:T(8,128)(2,1)}, u32[]{:S(2)}) copy-start(bf16[384,11008]{1,0:T(8,128)(2,1)} %own_hbm.15) | copy-start | bytes 25362436
  32.2 1.0 copy-start.4
  33.2 1.0 copy-start.6
  34.2 1.0 copy-start.8
  35.2 8.7 %copy-start.10 = (bf16[688,256]{1,0:T(8,128)(2,1)S(1)}, bf16[688,256]{1,0:T(8,128)(2,1)}, u32[]{:S(2)}) copy-start(bf16[688,256]{1,0:T(8,128)(2,1)} %copy-done.9) | copy-start | bytes 1056772
  35.2 8.7 %copy-start.12 = (bf16[688,256]{1,0:T(8,128)(2,1)S(1)}, bf16[688,256]{1,0:T(8,128)(2,1)}, u32[]{:S(2)}) copy-start(bf16[688,256]{1,0:T(8,128)(2,1)} %copy-done.11) | copy-start | bytes 1056772
  38.5 11.2 %collective-permute-start.10 = (bf16[688,256]{1,0:T(8,128)(2,1)S(1)}, bf16[688,256]{1,0:T(8,128)(2,1)S(1)}, u32[]{:S(2)}, u32[]{:S(2)}) collective-permute-start(bf16[688,256]{1,0:T(8,128)(2,1)S(1)} %collective-permute-done.7.refs_2_), channel_id=1, source_target_pairs={{0,2},{1,3},{2,6},{3,7},{6,10},{7,11},{10,14},{11,15},{14,12},{15,... | collective-permute-start | bytes 1056776 | tf_op jit(solution)/shard_map/ppermute | solution.py:280
  39.9 11.2 %collective-permute-start.9 = (bf16[688,256]{1,0:T(8,128)(2,1)S(1)}, bf16[688,256]{1,0:T(8,128)(2,1)S(1)}, u32[]{:S(2)}, u32[]{:S(2)}) collective-permute-start(bf16[688,256]{1,0:T(8,128)(2,1)S(1)} %collective-permute-done.5.refs_3_), channel_id=1, source_target_pairs={{0,4},{1,5},{2,0},{3,1},{6,2},{7,3},{10,6},{11,7},{14,10},{15,11},... | collective-permute-start | bytes 1056776 | tf_op jit(solution)/shard_map/ppermute | solution.py:280
  42.5 14.8 %collective-permute-start.8 = (bf16[688,256]{1,0:T(8,128)(2,1)S(1)}, bf16[688,256]{1,0:T(8,128)(2,1)S(1)}, u32[]{:S(2)}, u32[]{:S(2)}) collective-permute-start(bf16[688,256]{1,0:T(8,128)(2,1)S(1)} %collective-permute-done.3.refs_0_), channel_id=1, source_target_pairs={{0,2},{1,3},{2,6},{3,7},{6,10},{7,11},{10,14},{11,15},{14,12},{15,... | collective-permute-start | bytes 1056776 | tf_op jit(solution)/shard_map/ppermute | solution.py:280
  43.8 13.5 %collective-permute-start.17 = (bf16[688,256]{1,0:T(8,128)(2,1)S(1)}, bf16[688,256]{1,0:T(8,128)(2,1)S(1)}, u32[]{:S(2)}, u32[]{:S(2)}) collective-permute-start(bf16[688,256]{1,0:T(8,128)(2,1)S(1)} %collective-permute-done.13.refs_1_), channel_id=1, source_target_pairs={{0,4},{1,5},{2,0},{3,1},{6,2},{7,3},{10,6},{11,7},{14,10},{15,11},... | collective-permute-start | bytes 1056776 | tf_op jit(solution)/shard_map/ppermute | solution.py:280
  49.7 15.5 %collective-permute-start.16 = (bf16[688,256]{1,0:T(8,128)(2,1)S(1)}, bf16[688,256]{1,0:T(8,128)(2,1)S(1)}, u32[]{:S(2)}, u32[]{:S(2)}) collective-permute-start(bf16[688,256]{1,0:T(8,128)(2,1)S(1)} %collective-permute-done.10.refs_2_), channel_id=1, source_target_pairs={{0,2},{1,3},{2,6},{3,7},{6,10},{7,11},{10,14},{11,15},{14,12},{15,... | collective-permute-start | bytes 1056776 | tf_op jit(solution)/shard_map/ppermute | solution.py:280
  51.0 15.5 %collective-permute-start.15 = (bf16[688,256]{1,0:T(8,128)(2,1)S(1)}, bf16[688,256]{1,0:T(8,128)(2,1)S(1)}, u32[]{:S(2)}, u32[]{:S(2)}) collective-permute-start(bf16[688,256]{1,0:T(8,128)(2,1)S(1)} %collective-permute-done.9.refs_3_), channel_id=1, source_target_pairs={{0,4},{1,5},{2,0},{3,1},{6,2},{7,3},{10,6},{11,7},{14,10},{15,11},... | collective-permute-start | bytes 1056776 | tf_op jit(solution)/shard_map/ppermute | solution.py:280
  57.3 16.4 %collective-permute-start.21 = (bf16[688,256]{1,0:T(8,128)(2,1)S(1)}, bf16[688,256]{1,0:T(8,128)(2,1)S(1)}, u32[]{:S(2)}, u32[]{:S(2)}) collective-permute-start(bf16[688,256]{1,0:T(8,128)(2,1)S(1)} %collective-permute-done.17.refs_1_), channel_id=1, source_target_pairs={{0,4},{1,5},{2,0},{3,1},{6,2},{7,3},{10,6},{11,7},{14,10},{15,11},... | collective-permute-start | bytes 1056776 | tf_op jit(solution)/shard_map/ppermute | solution.py:280
  57.6 14.7 %collective-permute-start.14 = (bf16[688,256]{1,0:T(8,128)(2,1)S(1)}, bf16[688,256]{1,0:T(8,128)(2,1)S(1)}, u32[]{:S(2)}, u32[]{:S(2)}) collective-permute-start(bf16[688,256]{1,0:T(8,128)(2,1)S(1)} %collective-permute-done.8.refs_0_), channel_id=1, source_target_pairs={{0,2},{1,3},{2,6},{3,7},{6,10},{7,11},{10,14},{11,15},{14,12},{15,... | collective-permute-start | bytes 1056776 | tf_op jit(solution)/shard_map/ppermute | solution.py:280
  65.2 14.7 %collective-permute-start.20 = (bf16[688,256]{1,0:T(8,128)(2,1)S(1)}, bf16[688,256]{1,0:T(8,128)(2,1)S(1)}, u32[]{:S(2)}, u32[]{:S(2)}) collective-permute-start(bf16[688,256]{1,0:T(8,128)(2,1)S(1)} %collective-permute-done.16.refs_2_), channel_id=1, source_target_pairs={{0,2},{1,3},{2,6},{3,7},{6,10},{7,11},{10,14},{11,15},{14,12},{15,... | collective-permute-start | bytes 1056776 | tf_op jit(solution)/shard_map/ppermute | solution.py:280
  66.5 14.7 %collective-permute-start.19 = (bf16[688,256]{1,0:T(8,128)(2,1)S(1)}, bf16[688,256]{1,0:T(8,128)(2,1)S(1)}, u32[]{:S(2)}, u32[]{:S(2)}) collective-permute-start(bf16[688,256]{1,0:T(8,128)(2,1)S(1)} %collective-permute-done.15.refs_3_), channel_id=1, source_target_pairs={{0,4},{1,5},{2,0},{3,1},{6,2},{7,3},{10,6},{11,7},{14,10},{15,11},... | collective-permute-start | bytes 1056776 | tf_op jit(solution)/shard_map/ppermute | solution.py:280
  72.4 15.1 %collective-permute-start.18 = (bf16[688,256]{1,0:T(8,128)(2,1)S(1)}, bf16[688,256]{1,0:T(8,128)(2,1)S(1)}, u32[]{:S(2)}, u32[]{:S(2)}) collective-permute-start(bf16[688,256]{1,0:T(8,128)(2,1)S(1)} %collective-permute-done.14.refs_0_), channel_id=1, source_target_pairs={{0,2},{1,3},{2,6},{3,7},{6,10},{7,11},{10,14},{11,15},{14,12},{15,... | collective-permute-start | bytes 1056776 | tf_op jit(solution)/shard_map/ppermute | solution.py:280
  73.7 13.8 %collective-permute-start.23 = (bf16[688,256]{1,0:T(8,128)(2,1)S(1)}, bf16[688,256]{1,0:T(8,128)(2,1)S(1)}, u32[]{:S(2)}, u32[]{:S(2)}) collective-permute-start(bf16[688,256]{1,0:T(8,128)(2,1)S(1)} %collective-permute-done.21.refs_1_), channel_id=1, source_target_pairs={{0,4},{1,5},{2,0},{3,1},{6,2},{7,3},{10,6},{11,7},{14,10},{15,11},... | collective-permute-start | bytes 1056776 | tf_op jit(solution)/shard_map/ppermute | solution.py:280
  79.9 15.1 %collective-permute-start.25 = (bf16[688,256]{1,0:T(8,128)(2,1)S(1)}, bf16[688,256]{1,0:T(8,128)(2,1)S(1)}, u32[]{:S(2)}, u32[]{:S(2)}) collective-permute-start(bf16[688,256]{1,0:T(8,128)(2,1)S(1)} %collective-permute-done.20.refs_2_), channel_id=1, source_target_pairs={{0,2},{1,3},{2,6},{3,7},{6,10},{7,11},{10,14},{11,15},{14,12},{15,... | collective-permute-start | bytes 1056776 | tf_op jit(solution)/shard_map/ppermute | solution.py:280
  81.2 13.8 %collective-permute-start.26 = (bf16[688,256]{1,0:T(8,128)(2,1)S(1)}, bf16[688,256]{1,0:T(8,128)(2,1)S(1)}, u32[]{:S(2)}, u32[]{:S(2)}) collective-permute-start(bf16[688,256]{1,0:T(8,128)(2,1)S(1)} %collective-permute-done.19.refs_3_), channel_id=1, source_target_pairs={{0,4},{1,5},{2,0},{3,1},{6,2},{7,3},{10,6},{11,7},{14,10},{15,11},... | collective-permute-start | bytes 1056776 | tf_op jit(solution)/shard_map/ppermute | solution.py:280
  87.5 13.2 %collective-permute-start.24 = (bf16[688,256]{1,0:T(8,128)(2,1)S(1)}, bf16[688,256]{1,0:T(8,128)(2,1)S(1)}, u32[]{:S(2)}, u32[]{:S(2)}) collective-permute-start(bf16[688,256]{1,0:T(8,128)(2,1)S(1)} %collective-permute-done.23.refs_1_), channel_id=1, source_target_pairs={{0,4},{1,5},{2,0},{3,1},{6,2},{7,3},{10,6},{11,7},{14,10},{15,11},... | collective-permute-start | bytes 1056776 | tf_op jit(solution)/shard_map/ppermute | solution.py:280
  87.8 14.7 %collective-permute-start.22 = (bf16[688,256]{1,0:T(8,128)(2,1)S(1)}, bf16[688,256]{1,0:T(8,128)(2,1)S(1)}, u32[]{:S(2)}, u32[]{:S(2)}) collective-permute-start(bf16[688,256]{1,0:T(8,128)(2,1)S(1)} %collective-permute-done.18.refs_0_), channel_id=1, source_target_pairs={{0,2},{1,3},{2,6},{3,7},{6,10},{7,11},{10,14},{11,15},{14,12},{15,... | collective-permute-start | bytes 1056776 | tf_op jit(solution)/shard_map/ppermute | solution.py:280
  95.0 14.0 %collective-permute-start.28 = (bf16[688,256]{1,0:T(8,128)(2,1)S(1)}, bf16[688,256]{1,0:T(8,128)(2,1)S(1)}, u32[]{:S(2)}, u32[]{:S(2)}) collective-permute-start(bf16[688,256]{1,0:T(8,128)(2,1)S(1)} %collective-permute-done.26.refs_3_), channel_id=1, source_target_pairs={{0,4},{1,5},{2,0},{3,1},{6,2},{7,3},{10,6},{11,7},{14,10},{15,11},... | collective-permute-start | bytes 1056776 | tf_op jit(solution)/shard_map/ppermute | solution.py:280
  95.4 14.7 %collective-permute-start.27 = (bf16[688,256]{1,0:T(8,128)(2,1)S(1)}, bf16[688,256]{1,0:T(8,128)(2,1)S(1)}, u32[]{:S(2)}, u32[]{:S(2)}) collective-permute-start(bf16[688,256]{1,0:T(8,128)(2,1)S(1)} %collective-permute-done.25.refs_2_), channel_id=1, source_target_pairs={{0,2},{1,3},{2,6},{3,7},{6,10},{7,11},{10,14},{11,15},{14,12},{15,... | collective-permute-start | bytes 1056776 | tf_op jit(solution)/shard_map/ppermute | solution.py:280
  104.9 13.9 %collective-permute-start.30 = (f32[2,384,256]{2,1,0:T(8,128)S(1)}, f32[2,384,256]{2,1,0:T(8,128)}, u32[]{:S(2)}, u32[]{:S(2)}) collective-permute-start(f32[2,384,256]{2,1,0:T(8,128)S(1)} %get-tuple-element.254), channel_id=1, source_target_pairs={{0,1},{1,0},{2,3},{3,2},{4,5},{5,4},{6,7},{7,6},{8,9},{9,8},{10,11... | collective-permute-start | bytes 2359304 | tf_op jit(solution)/shard_map/ppermute | solution.py:288
  111.2 11.0 %collective-permute-start.29 = (f32[2,384,256]{2,1,0:T(8,128)S(1)}, f32[2,384,256]{2,1,0:T(8,128)}, u32[]{:S(2)}, u32[]{:S(2)}) collective-permute-start(f32[2,384,256]{2,1,0:T(8,128)S(1)} %get-tuple-element.252), channel_id=1, source_target_pairs={{0,1},{1,0},{2,3},{3,2},{4,5},{5,4},{6,7},{7,6},{8,9},{9,8},{10,11... | collective-permute-start | bytes 2359304 | tf_op jit(solution)/shard_map/ppermute | solution.py:288
  112.7 13.0 %all-to-all-start.1 = ((s32[16,1,16]{2,1,0:T(1,128)}), s32[16,1,16]{2,1,0:T(1,128)S(1)}, u32[]{:S(2)}, u32[]{:S(2)}) async-start(s32[16,1,16]{2,1,0:T(1,128)} %bitcast.7), calls=%async_computation.1 | async-start | bytes 16384 | tf_op jit(solution)/shard_map/all_to_all | solution.py:241
  118.8 1.1 copy-start.2
  124.6 1.1 copy-start.1
  125.7 0.6 copy-start.13
  126.3 42.2 %all-to-all-start = ((bf16[16,6,16,512]{3,2,1,0:T(8,128)(2,1)}), bf16[16,6,16,512]{3,2,1,0:T(8,128)(2,1)S(1)}, u32[]{:S(2)}, u32[]{:S(2)}) async-start(bf16[16,6,16,512]{3,2,1,0:T(8,128)(2,1)} %copy-done.1), calls=%async_computation | async-start | bytes 3145728 | tf_op jit(solution)/shard_map/all_to_all | solution.py:241

commit v13 on v11

--- a/solution.py
+++ b/solution.py
@@ -248,11 +248,11 @@
     swap = [(d, d ^ 1) for d in range(count)]
     other = lax.ppermute(coefficients, "wide", swap)
 
-    ids = exchange(labels)
     piece = []
     for j in range(HALVES):
         if j:
-            gamma, place = lax.optimization_barrier((gamma, place))
+            gamma, labels, place = lax.optimization_barrier((gamma, labels, place))
+            ids = exchange(labels)
         piece.append([gamma[i, :, j * width : (j + 1) * width] for i in range(norb)])
     shift = [
         [

time: 166 us -> 166 us (level)
  waiting for transfers between devices: 72.6 us -> 75.4 us
  Pallas kernels: 33 us -> 30.8 us
    ppermute x28, waiting for transfers between devices: 37.7 us -> 40.4 us  [ring_products(): piece[j][i] = lax.ppermute(sent, 'wide', shift[i])]
    pallas_call x8, Pallas kernels: 26.8 us -> 24.6 us  [add_products(): pl.pallas_call(functools.partial(step_kernel, t, parts), out_shape=[sums]...]
    unnamed x3 -> x5, local copies, waits for them, and re-layouts: 4.54 us -> 4.55 us
  transfers between devices with their start and end apart: 32 -> 32, of which waited for: 11 -> 11; matrix products, arithmetic and copies ran while one was open for 3% -> 2% of each run, Pallas kernels for 19% -> 18%
where the time goes in v13:
time: 166 us; the launch traced here: 165 us
  waiting for transfers between devices  75.4 us (45%)
  starting transfers between devices  33.9 us (20%)
  Pallas kernels  30.8 us (19%)
  blocking collectives  16.4 us (10%)
  local copies, waits for them, and re-layouts  6.1 us (4%)
  other arithmetic  1.88 us (1%)
    ppermute x28, waiting for transfers between devices, ring_products(): piece[j][i] = lax.ppermute(sent, 'wide', shift[i])  40.4 us
    all_to_all x1, waiting for transfers between devices, exchange(): lax.all_to_all(value, 'wide', split_axis=0, concat_axis=0, tiled=True)  34.9 us
    pallas_call x8, Pallas kernels, add_products(): pl.pallas_call(functools.partial(step_kernel, t, parts), out_shape=[sums]...  24.6 us
    ppermute x28, starting transfers between devices, ring_products(): piece[j][i] = lax.ppermute(sent, 'wide', shift[i])  20.8 us
    all_to_all x1, blocking collectives, exchange(): lax.all_to_all(value, 'wide', split_axis=0, concat_axis=0, tiled=True)  16.4 us
    ppermute x2, starting transfers between devices, ring_products(): theirs = [lax.ppermute(sums[j][1], 'wide', swap) for j in range(HALVES)]  6.54 us
    all_to_all x1, starting transfers between devices, exchange(): lax.all_to_all(value, 'wide', split_axis=0, concat_axis=0, tiled=True)  5.9 us
    unnamed x5, local copies, waits for them, and re-layouts  4.55 us
  transfers between devices with their start and end apart: 32, of which 11 were waited for; matrix products, arithmetic and copies ran while one was open for 2% of the time, Pallas kernels for 18%

profile of v13, /device:TPU:13, one launch (start us, length us, event | category | flops | bytes accessed | tf_op | source)
XLA Modules:
  0.0 165.3 jit_solution(6208184691666419109)
XLA Ops:
  0.6 0.7 collective-permute-start
  1.4 1.1 slice_bitcast_fusion
  2.5 0.3 collective-permute-start.11
  2.8 1.3 collective-permute-start.1
  4.1 0.9 convert_reduce_fusion
  5.0 0.7 broadcast_multiply_fusion
  5.7 0.2 mul.58
  5.9 0.1 select_reduce_fusion
  6.1 0.2 compare_convert_fusion.place_ref
  6.4 1.3 collective-permute-start.6
  7.8 0.2 collective-permute-start.4
  7.9 4.3 %collective-permute-done.1.refs_0_ = bf16[688,256]{1,0:T(8,128)(2,1)S(1)} collective-permute-done((bf16[688,256]{1,0:T(8,128)(2,1)S(1)}, bf16[688,256]{1,0:T(8,128)(2,1)S(1)}, u32[]{:S(2)}, u32[]{:S(2)}) %collective-permute-start.1) | collective-permute-done | bytes 352288 | tf_op jit(solution)/shard_map/ppermute | solution.py:280
  12.2 1.3 collective-permute-start.2
  13.5 0.2 collective-permute-start.12
  13.7 6.1 %collective-permute-done.6.refs_2_ = bf16[688,256]{1,0:T(8,128)(2,1)S(1)} collective-permute-done((bf16[688,256]{1,0:T(8,128)(2,1)S(1)}, bf16[688,256]{1,0:T(8,128)(2,1)S(1)}, u32[]{:S(2)}, u32[]{:S(2)}) %collective-permute-start.6) | collective-permute-done | bytes 352288 | tf_op jit(solution)/shard_map/ppermute | solution.py:280
  19.8 1.3 collective-permute-start.7
  21.1 0.2 collective-permute-start.5
  21.2 16.4 %all_to_all.17 = s32[16,1,16]{2,1,0:T(1,128)} all-to-all(s32[16,1,16]{2,1,0:T(1,128)S(1)} %bitcast.19), channel_id=1, replica_groups=mesh['groups'=2,'wide'=16] {'wide'}, dimensions={0} | all-to-all | bytes 2048 | tf_op jit(solution)/shard_map/all_to_all | solution.py:241
  37.7 0.3 collective-permute-start.3
  38.0 1.2 collective-permute-start.13
  39.1 3.4 %copy-done = bf16[384,11008]{1,0:T(8,128)(2,1)S(1)} copy-done((bf16[384,11008]{1,0:T(8,128)(2,1)S(1)}, bf16[384,11008]{1,0:T(8,128)(2,1)}, u32[]{:S(2)}) %copy-start) | copy-done | bytes 8454168
  42.5 3.1 %shard_map.50 = (f32[2,384,256]{2,1,0:T(8,128)S(1)}, f32[2,384,256]{2,1,0:T(8,128)S(1)}, f32[2,384,256]{2,1,0:T(8,128)S(1)}, f32[2,384,256]{2,1,0:T(8,128)S(1)}) custom-call(bf16[384,11008]{1,0:T(8,128)(2,1)S(1)} %copy-done, bf16[384,11008]{1,0:T(8,128)(2,1)} %collective-permute-done.other_hbm, bf16[688,256]{1,0:T(8,128)(2,1)S(1)} %get-tuple-element.261.refs_0_, ...), custom_call_target="tpu_custom_call" | custom-call | flops 1409286144 | bytes 2752512 | tf_op jit(solution)/shard_map/pallas_call | solution.py:158
  45.7 0.3 collective-permute-start.10
  46.1 1.2 collective-permute-start.9
  47.2 0.3 collective-permute-start.8
  47.5 1.2 collective-permute-start.17
  48.7 3.2 %shard_map.51 = (f32[2,384,256]{2,1,0:T(8,128)S(1)}, f32[2,384,256]{2,1,0:T(8,128)S(1)}, f32[2,384,256]{2,1,0:T(8,128)S(1)}, f32[2,384,256]{2,1,0:T(8,128)S(1)}) custom-call(bf16[384,11008]{1,0:T(8,128)(2,1)S(1)} %copy-done, ...), custom_call_target="tpu_custom_call", output_to_operand_aliasing={{0}: (6, {}), {1}: (7, {}), {2}: (8, {}), {3}: (9, {})} | custom-call | flops 1409286144 | bytes 2752512 | tf_op jit(solution)/shard_map/pallas_call | solution.py:158
  51.9 2.5 %collective-permute-done.10.refs_2_ = bf16[688,256]{1,0:T(8,128)(2,1)S(1)} collective-permute-done((bf16[688,256]{1,0:T(8,128)(2,1)S(1)}, bf16[688,256]{1,0:T(8,128)(2,1)S(1)}, u32[]{:S(2)}, u32[]{:S(2)}) %collective-permute-start.10) | collective-permute-done | bytes 352288 | tf_op jit(solution)/shard_map/ppermute | solution.py:280
  54.4 0.3 collective-permute-start.16
  54.7 1.2 collective-permute-start.15
  55.9 6.1 %collective-permute-done.8.refs_0_ = bf16[688,256]{1,0:T(8,128)(2,1)S(1)} collective-permute-done((bf16[688,256]{1,0:T(8,128)(2,1)S(1)}, bf16[688,256]{1,0:T(8,128)(2,1)S(1)}, u32[]{:S(2)}, u32[]{:S(2)}) %collective-permute-start.8) | collective-permute-done | bytes 352288 | tf_op jit(solution)/shard_map/ppermute | solution.py:280
  62.0 1.2 collective-permute-start.21
  63.2 0.3 collective-permute-start.14
  63.5 3.2 %shard_map.52 = (f32[2,384,256]{2,1,0:T(8,128)S(1)}, f32[2,384,256]{2,1,0:T(8,128)S(1)}, f32[2,384,256]{2,1,0:T(8,128)S(1)}, f32[2,384,256]{2,1,0:T(8,128)S(1)}) custom-call(bf16[384,11008]{1,0:T(8,128)(2,1)S(1)} %copy-done, ...), custom_call_target="tpu_custom_call", output_to_operand_aliasing={{0}: (6, {}), {1}: (7, {}), {2}: (8, {}), {3}: (9, {})} | custom-call | flops 1409286144 | bytes 2752512 | tf_op jit(solution)/shard_map/pallas_call | solution.py:158
  66.6 3.2 %shard_map.53 = (f32[2,384,256]{2,1,0:T(8,128)S(1)}, f32[2,384,256]{2,1,0:T(8,128)S(1)}, f32[2,384,256]{2,1,0:T(8,128)S(1)}, f32[2,384,256]{2,1,0:T(8,128)S(1)}) custom-call(bf16[384,11008]{1,0:T(8,128)(2,1)S(1)} %copy-done, ...), custom_call_target="tpu_custom_call", output_to_operand_aliasing={{0}: (6, {}), {1}: (7, {}), {2}: (8, {}), {3}: (9, {})} | custom-call | flops 1409286144 | bytes 2752512 | tf_op jit(solution)/shard_map/pallas_call | solution.py:158
  69.9 0.4 collective-permute-start.20
  70.3 1.1 collective-permute-start.19
  71.4 5.7 %collective-permute-done.14.refs_0_ = bf16[688,256]{1,0:T(8,128)(2,1)S(1)} collective-permute-done((bf16[688,256]{1,0:T(8,128)(2,1)S(1)}, bf16[688,256]{1,0:T(8,128)(2,1)S(1)}, u32[]{:S(2)}, u32[]{:S(2)}) %collective-permute-start.14) | collective-permute-done | bytes 352288 | tf_op jit(solution)/shard_map/ppermute | solution.py:280
  77.1 0.3 collective-permute-start.18
  77.4 1.2 collective-permute-start.23
  78.5 3.2 %shard_map.54 = (f32[2,384,256]{2,1,0:T(8,128)S(1)}, f32[2,384,256]{2,1,0:T(8,128)S(1)}, f32[2,384,256]{2,1,0:T(8,128)S(1)}, f32[2,384,256]{2,1,0:T(8,128)S(1)}) custom-call(bf16[384,11008]{1,0:T(8,128)(2,1)S(1)} %copy-done, ...), custom_call_target="tpu_custom_call", output_to_operand_aliasing={{0}: (6, {}), {1}: (7, {}), {2}: (8, {}), {3}: (9, {})} | custom-call | flops 1409286144 | bytes 2752512 | tf_op jit(solution)/shard_map/pallas_call | solution.py:158
  81.7 2.9 %collective-permute-done.20.refs_2_ = bf16[688,256]{1,0:T(8,128)(2,1)S(1)} collective-permute-done((bf16[688,256]{1,0:T(8,128)(2,1)S(1)}, bf16[688,256]{1,0:T(8,128)(2,1)S(1)}, u32[]{:S(2)}, u32[]{:S(2)}) %collective-permute-start.20) | collective-permute-done | bytes 352288 | tf_op jit(solution)/shard_map/ppermute | solution.py:280
  84.6 0.3 collective-permute-start.25
  84.9 1.2 collective-permute-start.26
  86.1 6.1 %collective-permute-done.18.refs_0_ = bf16[688,256]{1,0:T(8,128)(2,1)S(1)} collective-permute-done((bf16[688,256]{1,0:T(8,128)(2,1)S(1)}, bf16[688,256]{1,0:T(8,128)(2,1)S(1)}, u32[]{:S(2)}, u32[]{:S(2)}) %collective-permute-start.18) | collective-permute-done | bytes 352288 | tf_op jit(solution)/shard_map/ppermute | solution.py:280
  92.2 1.2 collective-permute-start.24
  93.4 0.3 collective-permute-start.22
  93.6 3.2 %shard_map.55 = (f32[2,384,256]{2,1,0:T(8,128)S(1)}, f32[2,384,256]{2,1,0:T(8,128)S(1)}, f32[2,384,256]{2,1,0:T(8,128)S(1)}, f32[2,384,256]{2,1,0:T(8,128)S(1)}) custom-call(bf16[384,11008]{1,0:T(8,128)(2,1)S(1)} %copy-done, ...), custom_call_target="tpu_custom_call", output_to_operand_aliasing={{0}: (6, {}), {1}: (7, {}), {2}: (8, {}), {3}: (9, {})} | custom-call | flops 1409286144 | bytes 2752512 | tf_op jit(solution)/shard_map/pallas_call | solution.py:158
  96.8 2.9 %collective-permute-done.25.refs_2_ = bf16[688,256]{1,0:T(8,128)(2,1)S(1)} collective-permute-done((bf16[688,256]{1,0:T(8,128)(2,1)S(1)}, bf16[688,256]{1,0:T(8,128)(2,1)S(1)}, u32[]{:S(2)}, u32[]{:S(2)}) %collective-permute-start.25) | collective-permute-done | bytes 352288 | tf_op jit(solution)/shard_map/ppermute | solution.py:280
  99.7 1.2 collective-permute-start.28
  100.9 0.3 collective-permute-start.27
  101.2 3.2 %shard_map.56 = (f32[2,384,256]{2,1,0:T(8,128)S(1)}, f32[2,384,256]{2,1,0:T(8,128)S(1)}, f32[2,384,256]{2,1,0:T(8,128)S(1)}, f32[2,384,256]{2,1,0:T(8,128)S(1)}) custom-call(bf16[384,11008]{1,0:T(8,128)(2,1)S(1)} %copy-done, ...), custom_call_target="tpu_custom_call", output_to_operand_aliasing={{0}: (6, {}), {1}: (7, {}), {2}: (8, {}), {3}: (9, {})} | custom-call | flops 1409286144 | bytes 2752512 | tf_op jit(solution)/shard_map/pallas_call | solution.py:158
  104.4 2.9 %collective-permute-done.24.refs_1_ = bf16[688,256]{1,0:T(8,128)(2,1)S(1)} collective-permute-done((bf16[688,256]{1,0:T(8,128)(2,1)S(1)}, bf16[688,256]{1,0:T(8,128)(2,1)S(1)}, u32[]{:S(2)}, u32[]{:S(2)}) %collective-permute-start.24) | collective-permute-done | bytes 352288 | tf_op jit(solution)/shard_map/ppermute | solution.py:280
  107.3 2.4 %shard_map.57 = (f32[2,384,256]{2,1,0:T(8,128)S(1)}, f32[2,384,256]{2,1,0:T(8,128)S(1)}, bf16[2,768,896]{2,1,0:T(8,128)(2,1)S(1)}) custom-call(bf16[384,11008]{1,0:T(8,128)(2,1)S(1)} %copy-done, bf16[384,11008]{1,0:T(8,128)(2,1)} %collective-permute-done.other_hbm, ...), custom_call_target="tpu_custom_call", output_to_operand_aliasing={{0}: (4, {}), {1}: (5, {})} | custom-call | flops 704643072 | bytes 2752512 | tf_op jit(solution)/shard_map/pallas_call | solution.py:158
  109.6 4.2 %collective-permute-start.30 = (f32[2,384,256]{2,1,0:T(8,128)S(1)}, f32[2,384,256]{2,1,0:T(8,128)S(1)}, u32[]{:S(2)}, u32[]{:S(2)}) collective-permute-start(f32[2,384,256]{2,1,0:T(8,128)S(1)} %get-tuple-element.256), channel_id=1, source_target_pairs={{0,1},{1,0},{2,3},{3,2},{4,5},{5,4},{6,7},{7,6},{8,9},{9,8},{10,11... | collective-permute-start | bytes 2359304 | tf_op jit(solution)/shard_map/ppermute | solution.py:288
  113.9 1.0 collective-permute-done.28.refs_1_
  114.8 1.1 shard_map.58
  116.0 2.3 %collective-permute-start.29 = (f32[2,384,256]{2,1,0:T(8,128)S(1)}, f32[2,384,256]{2,1,0:T(8,128)S(1)}, u32[]{:S(2)}, u32[]{:S(2)}) collective-permute-start(f32[2,384,256]{2,1,0:T(8,128)S(1)} %get-tuple-element.254), channel_id=1, source_target_pairs={{0,1},{1,0},{2,3},{3,2},{4,5},{5,4},{6,7},{7,6},{8,9},{9,8},{10,11... | collective-permute-start | bytes 2359304 | tf_op jit(solution)/shard_map/ppermute | solution.py:288
  118.3 1.9 %shard_map.59.refs_0_ = bf16[16,6,16,512]{3,2,1,0:T(8,128)(2,1)} custom-call(bf16[768,384]{1,0:T(8,128)(2,1)S(1)} %compare_convert_fusion.place_ref, f32[2,384,256]{2,1,0:T(8,128)S(1)} %get-tuple-element.255.mine_ref, f32[2,384,256]{2,1,0:T(8,128)S(1)} %collective-permute-done.30.theirs_ref), custom_call_target="tpu_custom_call" | custom-call | flops 301989888 | bytes 1572864 | tf_op jit(solution)/shard_map/pallas_call | solution.py:205
  120.2 1.9 %shard_map.60 = bf16[16,6,16,512]{3,2,1,0:T(8,128)(2,1)} custom-call(bf16[768,384]{1,0:T(8,128)(2,1)S(1)} %compare_convert_fusion.place_ref, f32[2,384,256]{2,1,0:T(8,128)S(1)} %get-tuple-element.253.mine_ref, f32[2,384,256]{2,1,0:T(8,128)S(1)} %collective-permute-done.29.theirs_ref, ...), custom_call_target="tpu_custom_call", output_to_operand_aliasing={{}: (3, {})} | custom-call | flops 301989888 | bytes 1572864 | tf_op jit(solution)/shard_map/pallas_call | solution.py:205
  122.1 5.9 %all-to-all-start.1 = ((bf16[16,6,16,512]{3,2,1,0:T(8,128)(2,1)}), bf16[16,6,16,512]{3,2,1,0:T(8,128)(2,1)S(1)}, u32[]{:S(2)}, u32[]{:S(2)}) async-start(bf16[16,6,16,512]{3,2,1,0:T(8,128)(2,1)} %shard_map.60), calls=%async_computation.1 | async-start | bytes 3145728 | tf_op jit(solution)/shard_map/all_to_all | solution.py:241
  128.0 1.3 shard_map.61
  129.3 34.9 %all-to-all-done.1 = bf16[16,6,16,512]{3,2,1,0:T(8,128)(2,1)S(1)} async-done(((bf16[16,6,16,512]{3,2,1,0:T(8,128)(2,1)}), bf16[16,6,16,512]{3,2,1,0:T(8,128)(2,1)S(1)}, u32[]{:S(2)}, u32[]{:S(2)}) %all-to-all-start.1) | async-done | bytes 1572896 | tf_op jit(solution)/shard_map/all_to_all | solution.py:241
  164.2 1.1 copy.64
  (30 shorter events, 0.3 us)
Async XLA Ops:
  0.6 5.7 %copy-start.1 = (bf16[2,688,512]{2,1,0:T(8,128)(2,1)S(1)}, bf16[2,688,512]{2,1,0:T(8,128)(2,1)}, u32[]{:S(2)}) copy-start(bf16[2,688,512]{2,1,0:T(8,128)(2,1)} %param.3) | copy-start | bytes 4227076
  0.6 38.5 %collective-permute-start = (bf16[384,11008]{1,0:T(8,128)(2,1)}, bf16[384,11008]{1,0:T(8,128)(2,1)}, u32[]{:S(2)}, u32[]{:S(2)}) collective-permute-start(bf16[384,11008]{1,0:T(8,128)(2,1)} %own_hbm.15), channel_id=1, source_target_pairs={{0,1},{1,0},{2,3},{3,2},{4,5},{5,4},{6,7},{7,6},{8,9},{9,8},{10,11... | collective-permute-start | bytes 25362440 | tf_op jit(solution)/shard_map/ppermute | solution.py:249
  2.5 11.0 %collective-permute-start.11 = (bf16[688,256]{1,0:T(8,128)(2,1)S(1)}, bf16[688,256]{1,0:T(8,128)(2,1)S(1)}, u32[]{:S(2)}, u32[]{:S(2)}) collective-permute-start(bf16[688,256]{1,0:T(8,128)(2,1)S(1)} %get-tuple-element.260.refs_1_), channel_id=1, source_target_pairs={{0,4},{1,5},{2,0},{3,1},{6,2},{7,3},{10,6},{11,7},{14,10},{15,11},... | collective-permute-start | bytes 1056776 | tf_op jit(solution)/shard_map/ppermute | solution.py:280
  2.8 9.5 %collective-permute-start.1 = (bf16[688,256]{1,0:T(8,128)(2,1)S(1)}, bf16[688,256]{1,0:T(8,128)(2,1)S(1)}, u32[]{:S(2)}, u32[]{:S(2)}) collective-permute-start(bf16[688,256]{1,0:T(8,128)(2,1)S(1)} %get-tuple-element.261.refs_0_), channel_id=1, source_target_pairs={{0,2},{1,3},{2,6},{3,7},{6,10},{7,11},{10,14},{11,15},{14,12},{15,... | collective-permute-start | bytes 1056776 | tf_op jit(solution)/shard_map/ppermute | solution.py:280
  6.4 13.4 %collective-permute-start.6 = (bf16[688,256]{1,0:T(8,128)(2,1)S(1)}, bf16[688,256]{1,0:T(8,128)(2,1)S(1)}, u32[]{:S(2)}, u32[]{:S(2)}) collective-permute-start(bf16[688,256]{1,0:T(8,128)(2,1)S(1)} %get-tuple-element.262.refs_2_), channel_id=1, source_target_pairs={{0,2},{1,3},{2,6},{3,7},{6,10},{7,11},{10,14},{11,15},{14,12},{15,... | collective-permute-start | bytes 1056776 | tf_op jit(solution)/shard_map/ppermute | solution.py:280
  7.8 13.3 %collective-permute-start.4 = (bf16[688,256]{1,0:T(8,128)(2,1)S(1)}, bf16[688,256]{1,0:T(8,128)(2,1)S(1)}, u32[]{:S(2)}, u32[]{:S(2)}) collective-permute-start(bf16[688,256]{1,0:T(8,128)(2,1)S(1)} %get-tuple-element.263.refs_3_), channel_id=1, source_target_pairs={{0,4},{1,5},{2,0},{3,1},{6,2},{7,3},{10,6},{11,7},{14,10},{15,11},... | collective-permute-start | bytes 1056776 | tf_op jit(solution)/shard_map/ppermute | solution.py:280
  12.2 25.4 %collective-permute-start.2 = (bf16[688,256]{1,0:T(8,128)(2,1)S(1)}, bf16[688,256]{1,0:T(8,128)(2,1)S(1)}, u32[]{:S(2)}, u32[]{:S(2)}) collective-permute-start(bf16[688,256]{1,0:T(8,128)(2,1)S(1)} %collective-permute-done.1.refs_0_), channel_id=1, source_target_pairs={{0,2},{1,3},{2,6},{3,7},{6,10},{7,11},{10,14},{11,15},{14,12},{15,... | collective-permute-start | bytes 1056776 | tf_op jit(solution)/shard_map/ppermute | solution.py:280
  13.5 24.4 %collective-permute-start.12 = (bf16[688,256]{1,0:T(8,128)(2,1)S(1)}, bf16[688,256]{1,0:T(8,128)(2,1)S(1)}, u32[]{:S(2)}, u32[]{:S(2)}) collective-permute-start(bf16[688,256]{1,0:T(8,128)(2,1)S(1)} %collective-permute-done.11.refs_1_), channel_id=1, source_target_pairs={{0,4},{1,5},{2,0},{3,1},{6,2},{7,3},{10,6},{11,7},{14,10},{15,11},... | collective-permute-start | bytes 1056776 | tf_op jit(solution)/shard_map/ppermute | solution.py:280
  19.8 25.9 %collective-permute-start.7 = (bf16[688,256]{1,0:T(8,128)(2,1)S(1)}, bf16[688,256]{1,0:T(8,128)(2,1)S(1)}, u32[]{:S(2)}, u32[]{:S(2)}) collective-permute-start(bf16[688,256]{1,0:T(8,128)(2,1)S(1)} %collective-permute-done.6.refs_2_), channel_id=1, source_target_pairs={{0,2},{1,3},{2,6},{3,7},{6,10},{7,11},{10,14},{11,15},{14,12},{15,... | collective-permute-start | bytes 1056776 | tf_op jit(solution)/shard_map/ppermute | solution.py:280
  21.1 25.0 %collective-permute-start.5 = (bf16[688,256]{1,0:T(8,128)(2,1)S(1)}, bf16[688,256]{1,0:T(8,128)(2,1)S(1)}, u32[]{:S(2)}, u32[]{:S(2)}) collective-permute-start(bf16[688,256]{1,0:T(8,128)(2,1)S(1)} %collective-permute-done.4.refs_3_), channel_id=1, source_target_pairs={{0,4},{1,5},{2,0},{3,1},{6,2},{7,3},{10,6},{11,7},{14,10},{15,11},... | collective-permute-start | bytes 1056776 | tf_op jit(solution)/shard_map/ppermute | solution.py:280
  37.7 9.6 %collective-permute-start.3 = (bf16[688,256]{1,0:T(8,128)(2,1)S(1)}, bf16[688,256]{1,0:T(8,128)(2,1)S(1)}, u32[]{:S(2)}, u32[]{:S(2)}) collective-permute-start(bf16[688,256]{1,0:T(8,128)(2,1)S(1)} %collective-permute-done.2.refs_0_), channel_id=1, source_target_pairs={{0,2},{1,3},{2,6},{3,7},{6,10},{7,11},{10,14},{11,15},{14,12},{15,... | collective-permute-start | bytes 1056776 | tf_op jit(solution)/shard_map/ppermute | solution.py:280
  38.0 9.6 %collective-permute-start.13 = (bf16[688,256]{1,0:T(8,128)(2,1)S(1)}, bf16[688,256]{1,0:T(8,128)(2,1)S(1)}, u32[]{:S(2)}, u32[]{:S(2)}) collective-permute-start(bf16[688,256]{1,0:T(8,128)(2,1)S(1)} %collective-permute-done.12.refs_1_), channel_id=1, source_target_pairs={{0,4},{1,5},{2,0},{3,1},{6,2},{7,3},{10,6},{11,7},{14,10},{15,11},... | collective-permute-start | bytes 1056776 | tf_op jit(solution)/shard_map/ppermute | solution.py:280
  39.1 3.4 %copy-start = (bf16[384,11008]{1,0:T(8,128)(2,1)S(1)}, bf16[384,11008]{1,0:T(8,128)(2,1)}, u32[]{:S(2)}) copy-start(bf16[384,11008]{1,0:T(8,128)(2,1)} %own_hbm.15) | copy-start | bytes 25362436
  45.7 8.7 %collective-permute-start.10 = (bf16[688,256]{1,0:T(8,128)(2,1)S(1)}, bf16[688,256]{1,0:T(8,128)(2,1)S(1)}, u32[]{:S(2)}, u32[]{:S(2)}) collective-permute-start(bf16[688,256]{1,0:T(8,128)(2,1)S(1)} %collective-permute-done.7.refs_2_), channel_id=1, source_target_pairs={{0,2},{1,3},{2,6},{3,7},{6,10},{7,11},{10,14},{11,15},{14,12},{15,... | collective-permute-start | bytes 1056776 | tf_op jit(solution)/shard_map/ppermute | solution.py:280
  46.1 8.7 %collective-permute-start.9 = (bf16[688,256]{1,0:T(8,128)(2,1)S(1)}, bf16[688,256]{1,0:T(8,128)(2,1)S(1)}, u32[]{:S(2)}, u32[]{:S(2)}) collective-permute-start(bf16[688,256]{1,0:T(8,128)(2,1)S(1)} %collective-permute-done.5.refs_3_), channel_id=1, source_target_pairs={{0,4},{1,5},{2,0},{3,1},{6,2},{7,3},{10,6},{11,7},{14,10},{15,11},... | collective-permute-start | bytes 1056776 | tf_op jit(solution)/shard_map/ppermute | solution.py:280
  47.2 14.7 %collective-permute-start.8 = (bf16[688,256]{1,0:T(8,128)(2,1)S(1)}, bf16[688,256]{1,0:T(8,128)(2,1)S(1)}, u32[]{:S(2)}, u32[]{:S(2)}) collective-permute-start(bf16[688,256]{1,0:T(8,128)(2,1)S(1)} %collective-permute-done.3.refs_0_), channel_id=1, source_target_pairs={{0,2},{1,3},{2,6},{3,7},{6,10},{7,11},{10,14},{11,15},{14,12},{15,... | collective-permute-start | bytes 1056776 | tf_op jit(solution)/shard_map/ppermute | solution.py:280
  47.5 14.5 %collective-permute-start.17 = (bf16[688,256]{1,0:T(8,128)(2,1)S(1)}, bf16[688,256]{1,0:T(8,128)(2,1)S(1)}, u32[]{:S(2)}, u32[]{:S(2)}) collective-permute-start(bf16[688,256]{1,0:T(8,128)(2,1)S(1)} %collective-permute-done.13.refs_1_), channel_id=1, source_target_pairs={{0,4},{1,5},{2,0},{3,1},{6,2},{7,3},{10,6},{11,7},{14,10},{15,11},... | collective-permute-start | bytes 1056776 | tf_op jit(solution)/shard_map/ppermute | solution.py:280
  54.4 15.5 %collective-permute-start.16 = (bf16[688,256]{1,0:T(8,128)(2,1)S(1)}, bf16[688,256]{1,0:T(8,128)(2,1)S(1)}, u32[]{:S(2)}, u32[]{:S(2)}) collective-permute-start(bf16[688,256]{1,0:T(8,128)(2,1)S(1)} %collective-permute-done.10.refs_2_), channel_id=1, source_target_pairs={{0,2},{1,3},{2,6},{3,7},{6,10},{7,11},{10,14},{11,15},{14,12},{15,... | collective-permute-start | bytes 1056776 | tf_op jit(solution)/shard_map/ppermute | solution.py:280
  54.7 15.6 %collective-permute-start.15 = (bf16[688,256]{1,0:T(8,128)(2,1)S(1)}, bf16[688,256]{1,0:T(8,128)(2,1)S(1)}, u32[]{:S(2)}, u32[]{:S(2)}) collective-permute-start(bf16[688,256]{1,0:T(8,128)(2,1)S(1)} %collective-permute-done.9.refs_3_), channel_id=1, source_target_pairs={{0,4},{1,5},{2,0},{3,1},{6,2},{7,3},{10,6},{11,7},{14,10},{15,11},... | collective-permute-start | bytes 1056776 | tf_op jit(solution)/shard_map/ppermute | solution.py:280
  62.0 15.4 %collective-permute-start.21 = (bf16[688,256]{1,0:T(8,128)(2,1)S(1)}, bf16[688,256]{1,0:T(8,128)(2,1)S(1)}, u32[]{:S(2)}, u32[]{:S(2)}) collective-permute-start(bf16[688,256]{1,0:T(8,128)(2,1)S(1)} %collective-permute-done.17.refs_1_), channel_id=1, source_target_pairs={{0,4},{1,5},{2,0},{3,1},{6,2},{7,3},{10,6},{11,7},{14,10},{15,11},... | collective-permute-start | bytes 1056776 | tf_op jit(solution)/shard_map/ppermute | solution.py:280
  63.2 13.9 %collective-permute-start.14 = (bf16[688,256]{1,0:T(8,128)(2,1)S(1)}, bf16[688,256]{1,0:T(8,128)(2,1)S(1)}, u32[]{:S(2)}, u32[]{:S(2)}) collective-permute-start(bf16[688,256]{1,0:T(8,128)(2,1)S(1)} %collective-permute-done.8.refs_0_), channel_id=1, source_target_pairs={{0,2},{1,3},{2,6},{3,7},{6,10},{7,11},{10,14},{11,15},{14,12},{15,... | collective-permute-start | bytes 1056776 | tf_op jit(solution)/shard_map/ppermute | solution.py:280
  69.9 14.7 %collective-permute-start.20 = (bf16[688,256]{1,0:T(8,128)(2,1)S(1)}, bf16[688,256]{1,0:T(8,128)(2,1)S(1)}, u32[]{:S(2)}, u32[]{:S(2)}) collective-permute-start(bf16[688,256]{1,0:T(8,128)(2,1)S(1)} %collective-permute-done.16.refs_2_), channel_id=1, source_target_pairs={{0,2},{1,3},{2,6},{3,7},{6,10},{7,11},{10,14},{11,15},{14,12},{15,... | collective-permute-start | bytes 1056776 | tf_op jit(solution)/shard_map/ppermute | solution.py:280
  70.3 14.6 %collective-permute-start.19 = (bf16[688,256]{1,0:T(8,128)(2,1)S(1)}, bf16[688,256]{1,0:T(8,128)(2,1)S(1)}, u32[]{:S(2)}, u32[]{:S(2)}) collective-permute-start(bf16[688,256]{1,0:T(8,128)(2,1)S(1)} %collective-permute-done.15.refs_3_), channel_id=1, source_target_pairs={{0,4},{1,5},{2,0},{3,1},{6,2},{7,3},{10,6},{11,7},{14,10},{15,11},... | collective-permute-start | bytes 1056776 | tf_op jit(solution)/shard_map/ppermute | solution.py:280
  77.1 15.1 %collective-permute-start.18 = (bf16[688,256]{1,0:T(8,128)(2,1)S(1)}, bf16[688,256]{1,0:T(8,128)(2,1)S(1)}, u32[]{:S(2)}, u32[]{:S(2)}) collective-permute-start(bf16[688,256]{1,0:T(8,128)(2,1)S(1)} %collective-permute-done.14.refs_0_), channel_id=1, source_target_pairs={{0,2},{1,3},{2,6},{3,7},{6,10},{7,11},{10,14},{11,15},{14,12},{15,... | collective-permute-start | bytes 1056776 | tf_op jit(solution)/shard_map/ppermute | solution.py:280
  77.4 14.8 %collective-permute-start.23 = (bf16[688,256]{1,0:T(8,128)(2,1)S(1)}, bf16[688,256]{1,0:T(8,128)(2,1)S(1)}, u32[]{:S(2)}, u32[]{:S(2)}) collective-permute-start(bf16[688,256]{1,0:T(8,128)(2,1)S(1)} %collective-permute-done.21.refs_1_), channel_id=1, source_target_pairs={{0,4},{1,5},{2,0},{3,1},{6,2},{7,3},{10,6},{11,7},{14,10},{15,11},... | collective-permute-start | bytes 1056776 | tf_op jit(solution)/shard_map/ppermute | solution.py:280
  84.6 15.1 %collective-permute-start.25 = (bf16[688,256]{1,0:T(8,128)(2,1)S(1)}, bf16[688,256]{1,0:T(8,128)(2,1)S(1)}, u32[]{:S(2)}, u32[]{:S(2)}) collective-permute-start(bf16[688,256]{1,0:T(8,128)(2,1)S(1)} %collective-permute-done.20.refs_2_), channel_id=1, source_target_pairs={{0,2},{1,3},{2,6},{3,7},{6,10},{7,11},{10,14},{11,15},{14,12},{15,... | collective-permute-start | bytes 1056776 | tf_op jit(solution)/shard_map/ppermute | solution.py:280
  84.9 14.8 %collective-permute-start.26 = (bf16[688,256]{1,0:T(8,128)(2,1)S(1)}, bf16[688,256]{1,0:T(8,128)(2,1)S(1)}, u32[]{:S(2)}, u32[]{:S(2)}) collective-permute-start(bf16[688,256]{1,0:T(8,128)(2,1)S(1)} %collective-permute-done.19.refs_3_), channel_id=1, source_target_pairs={{0,4},{1,5},{2,0},{3,1},{6,2},{7,3},{10,6},{11,7},{14,10},{15,11},... | collective-permute-start | bytes 1056776 | tf_op jit(solution)/shard_map/ppermute | solution.py:280
  92.2 15.1 %collective-permute-start.24 = (bf16[688,256]{1,0:T(8,128)(2,1)S(1)}, bf16[688,256]{1,0:T(8,128)(2,1)S(1)}, u32[]{:S(2)}, u32[]{:S(2)}) collective-permute-start(bf16[688,256]{1,0:T(8,128)(2,1)S(1)} %collective-permute-done.23.refs_1_), channel_id=1, source_target_pairs={{0,4},{1,5},{2,0},{3,1},{6,2},{7,3},{10,6},{11,7},{14,10},{15,11},... | collective-permute-start | bytes 1056776 | tf_op jit(solution)/shard_map/ppermute | solution.py:280
  93.4 13.9 %collective-permute-start.22 = (bf16[688,256]{1,0:T(8,128)(2,1)S(1)}, bf16[688,256]{1,0:T(8,128)(2,1)S(1)}, u32[]{:S(2)}, u32[]{:S(2)}) collective-permute-start(bf16[688,256]{1,0:T(8,128)(2,1)S(1)} %collective-permute-done.18.refs_0_), channel_id=1, source_target_pairs={{0,2},{1,3},{2,6},{3,7},{6,10},{7,11},{10,14},{11,15},{14,12},{15,... | collective-permute-start | bytes 1056776 | tf_op jit(solution)/shard_map/ppermute | solution.py:280
  99.7 15.1 %collective-permute-start.28 = (bf16[688,256]{1,0:T(8,128)(2,1)S(1)}, bf16[688,256]{1,0:T(8,128)(2,1)S(1)}, u32[]{:S(2)}, u32[]{:S(2)}) collective-permute-start(bf16[688,256]{1,0:T(8,128)(2,1)S(1)} %collective-permute-done.26.refs_3_), channel_id=1, source_target_pairs={{0,4},{1,5},{2,0},{3,1},{6,2},{7,3},{10,6},{11,7},{14,10},{15,11},... | collective-permute-start | bytes 1056776 | tf_op jit(solution)/shard_map/ppermute | solution.py:280
  100.9 13.9 %collective-permute-start.27 = (bf16[688,256]{1,0:T(8,128)(2,1)S(1)}, bf16[688,256]{1,0:T(8,128)(2,1)S(1)}, u32[]{:S(2)}, u32[]{:S(2)}) collective-permute-start(bf16[688,256]{1,0:T(8,128)(2,1)S(1)} %collective-permute-done.25.refs_2_), channel_id=1, source_target_pairs={{0,2},{1,3},{2,6},{3,7},{6,10},{7,11},{10,14},{11,15},{14,12},{15,... | collective-permute-start | bytes 1056776 | tf_op jit(solution)/shard_map/ppermute | solution.py:280
  109.6 8.6 %collective-permute-start.30 = (f32[2,384,256]{2,1,0:T(8,128)S(1)}, f32[2,384,256]{2,1,0:T(8,128)S(1)}, u32[]{:S(2)}, u32[]{:S(2)}) collective-permute-start(f32[2,384,256]{2,1,0:T(8,128)S(1)} %get-tuple-element.256), channel_id=1, source_target_pairs={{0,1},{1,0},{2,3},{3,2},{4,5},{5,4},{6,7},{7,6},{8,9},{9,8},{10,11... | collective-permute-start | bytes 2359304 | tf_op jit(solution)/shard_map/ppermute | solution.py:288
  116.0 4.2 %collective-permute-start.29 = (f32[2,384,256]{2,1,0:T(8,128)S(1)}, f32[2,384,256]{2,1,0:T(8,128)S(1)}, u32[]{:S(2)}, u32[]{:S(2)}) collective-permute-start(f32[2,384,256]{2,1,0:T(8,128)S(1)} %get-tuple-element.254), channel_id=1, source_target_pairs={{0,1},{1,0},{2,3},{3,2},{4,5},{5,4},{6,7},{7,6},{8,9},{9,8},{10,11... | collective-permute-start | bytes 2359304 | tf_op jit(solution)/shard_map/ppermute | solution.py:288
  122.1 42.1 %all-to-all-start.1 = ((bf16[16,6,16,512]{3,2,1,0:T(8,128)(2,1)}), bf16[16,6,16,512]{3,2,1,0:T(8,128)(2,1)S(1)}, u32[]{:S(2)}, u32[]{:S(2)}) async-start(bf16[16,6,16,512]{3,2,1,0:T(8,128)(2,1)} %shard_map.60), calls=%async_computation.1 | async-start | bytes 3145728 | tf_op jit(solution)/shard_map/all_to_all | solution.py:241

commit v14 on v9

--- a/solution.py
+++ b/solution.py
@@ -180,8 +180,7 @@
 def finish_kernel(half, place_ref, mine_ref, theirs_ref, *refs):
     out_hbm, buf, sems = refs[-3:]
     norb, _, width = mine_ref.shape
-    _, planes, slots, _ = out_hbm.shape
-    columns = pl.ds(half * width, width)
+    _, _, planes, slots, _ = out_hbm.shape
     copies = []
     for i in range(norb):
         back = (mine_ref[i] + theirs_ref[i]).astype(jnp.bfloat16)
@@ -189,9 +188,7 @@
         plane = pl.ds(i * (planes // norb), planes // norb)
         buf[:, plane] = out.astype(jnp.bfloat16).reshape(-1, planes // norb, slots, width)
         copies.append(
-            pltpu.make_async_copy(
-                buf.at[:, plane], out_hbm.at[:, plane, :, columns], sems.at[i]
-            )
+            pltpu.make_async_copy(buf.at[:, plane], out_hbm.at[:, half, plane], sems.at[i])
         )
         copies[i].start()
     for copy in copies:
@@ -204,7 +201,7 @@
     norb, _, width = mine.shape
     return pl.pallas_call(
         functools.partial(finish_kernel, half),
-        out_shape=jax.ShapeDtypeStruct(shape, jnp.bfloat16),
+        out_shape=jax.ShapeDtypeStruct((shape[0], HALVES) + shape[1:3] + (width,), jnp.bfloat16),
         in_specs=[vmem] * 3 + [hbm] * len(before),
         out_specs=hbm,
         input_output_aliases={3: 0} if before else {},
@@ -306,6 +303,8 @@
         out = out.astype(jnp.bfloat16).reshape(norb, count, block_rows, slots, naux)
         out = out.transpose(1, 0, 2, 3, 4).reshape(shape)
     placed = lax.all_to_all(out, "wide", split_axis=0, concat_axis=0, tiled=True)
+    if placed.ndim > len(shape):
+        placed = placed.transpose(0, 2, 3, 1, 4).reshape(shape)
     return placed.transpose(0, 2, 1, 3)[None], ids[None]
 
 

time: 161 us -> 161 us (level)
    unnamed x7 -> x6, local copies, waits for them, and re-layouts: 4.55 us -> 3.41 us
  transfers between devices with their start and end apart: 33 -> 33, of which waited for: 16 -> 17; matrix products, arithmetic and copies ran while one was open for 2% -> 2% of each run, Pallas kernels for 19% -> 19%
where the time goes in v14:
time: 161 us
  waiting for transfers between devices  82.3 us (51%)
  starting transfers between devices  38.6 us (24%)
  Pallas kernels  31.3 us (19%)
  local copies, waits for them, and re-layouts  7.12 us (4%)
    ppermute x28, waiting for transfers between devices, ring_products(): piece[j][i] = lax.ppermute(sent, 'wide', shift[i])  43.9 us
    all_to_all x1, waiting for transfers between devices, local(): lax.all_to_all(out, 'wide', split_axis=0, concat_axis=0, tiled=True)  34.9 us
    pallas_call x8, Pallas kernels, add_products(): pl.pallas_call(functools.partial(step_kernel, t, parts), out_shape=[sums]...  25.9 us
    ppermute x28, starting transfers between devices, ring_products(): piece[j][i] = lax.ppermute(sent, 'wide', shift[i])  20.7 us
    all_to_all x1, starting transfers between devices, local(): lax.all_to_all(labels, 'wide', split_axis=0, concat_axis=0, tiled=True)  7.02 us
    all_to_all x1, starting transfers between devices, local(): lax.all_to_all(out, 'wide', split_axis=0, concat_axis=0, tiled=True)  6.6 us
    ppermute x2, starting transfers between devices, ring_products(): theirs = [lax.ppermute(sums[j][1], 'wide', swap) for j in range(HALVES)]  3.5 us
    unnamed x6, local copies, waits for them, and re-layouts  3.41 us
  transfers between devices with their start and end apart: 33, of which 17 were waited for; matrix products, arithmetic and copies ran while one was open for 2% of the time, Pallas kernels for 19%

profile of v14, /device:TPU:13, one launch (start us, length us, event | category | flops | bytes accessed | tf_op | source)
XLA Modules:
  0.0 160.7 jit_solution(7592061309642612585)
XLA Ops:
  0.6 0.7 collective-permute-start.2
  1.4 1.4 slice_bitcast_fusion
  2.8 0.2 collective-permute-start.11
  3.1 1.4 collective-permute-start
  4.5 1.3 collective-permute-start.6
  6.1 0.7 sub.17
  6.8 7.0 %all-to-all-start = ((s32[16,1,16]{2,1,0:T(1,128)}), s32[16,1,16]{2,1,0:T(1,128)S(1)}, u32[]{:S(2)}, u32[]{:S(2)}) async-start(s32[16,1,16]{2,1,0:T(1,128)} %sub.17), calls=%async_computation | async-start | bytes 16384 | tf_op jit(solution)/shard_map/all_to_all | solution.py:294
  13.9 0.2 mul.58
  14.1 0.3 collective-permute-start.12
  14.4 1.2 collective-permute-start.1
  15.6 4.6 %collective-permute-done.4.refs_3_ = bf16[688,256]{1,0:T(8,128)(2,1)S(1)} collective-permute-done((bf16[688,256]{1,0:T(8,128)(2,1)S(1)}, bf16[688,256]{1,0:T(8,128)(2,1)S(1)}, u32[]{:S(2)}, u32[]{:S(2)}) %collective-permute-start.4) | collective-permute-done | bytes 352288 | tf_op jit(solution)/shard_map/ppermute | solution.py:270
  20.4 1.3 collective-permute-start.7
  21.9 3.1 %all-to-all-done = s32[16,1,16]{2,1,0:T(1,128)S(1)} async-done(((s32[16,1,16]{2,1,0:T(1,128)}), s32[16,1,16]{2,1,0:T(1,128)S(1)}, u32[]{:S(2)}, u32[]{:S(2)}) %all-to-all-start) | async-done | bytes 1056 | tf_op jit(solution)/shard_map/all_to_all | solution.py:294
  25.0 3.0 %collective-permute-done.1.refs_0_ = bf16[688,256]{1,0:T(8,128)(2,1)} collective-permute-done((bf16[688,256]{1,0:T(8,128)(2,1)S(1)}, bf16[688,256]{1,0:T(8,128)(2,1)}, u32[]{:S(2)}, u32[]{:S(2)}) %collective-permute-start.1) | collective-permute-done | bytes 352288 | tf_op jit(solution)/shard_map/ppermute | solution.py:270
  27.9 1.2 collective-permute-start.3
  29.1 0.3 collective-permute-start.13
  29.4 3.4 %copy-done = bf16[384,11008]{1,0:T(8,128)(2,1)S(1)} copy-done((bf16[384,11008]{1,0:T(8,128)(2,1)S(1)}, bf16[384,11008]{1,0:T(8,128)(2,1)}, u32[]{:S(2)}) %copy-start) | copy-done | bytes 8454168
  32.8 3.1 %shard_map.50 = (f32[2,384,256]{2,1,0:T(8,128)S(1)}, f32[2,384,256]{2,1,0:T(8,128)S(1)}, f32[2,384,256]{2,1,0:T(8,128)S(1)}, f32[2,384,256]{2,1,0:T(8,128)S(1)}) custom-call(bf16[384,11008]{1,0:T(8,128)(2,1)S(1)} %copy-done, bf16[384,11008]{1,0:T(8,128)(2,1)} %collective-permute-done.2.other_hbm, bf16[688,256]{1,0:T(8,128)(2,1)S(1)} %get-tuple-element.258.refs_0_, ...), custom_call_target="tpu_custom_call" | custom-call | flops 1409286144 | bytes 2752512 | tf_op jit(solution)/shard_map/pallas_call | solution.py:158
  36.0 1.2 collective-permute-start.10
  37.2 0.3 collective-permute-start.9
  37.5 5.4 %collective-permute-done.3.refs_0_ = bf16[688,256]{1,0:T(8,128)(2,1)S(1)} collective-permute-done((bf16[688,256]{1,0:T(8,128)(2,1)}, bf16[688,256]{1,0:T(8,128)(2,1)S(1)}, u32[]{:S(2)}, u32[]{:S(2)}) %collective-permute-start.3) | collective-permute-done | bytes 352288 | tf_op jit(solution)/shard_map/ppermute | solution.py:270
  42.9 1.2 collective-permute-start.8
  44.1 0.3 collective-permute-start.17
  44.4 3.2 %shard_map.51 = (f32[2,384,256]{2,1,0:T(8,128)S(1)}, f32[2,384,256]{2,1,0:T(8,128)S(1)}, f32[2,384,256]{2,1,0:T(8,128)S(1)}, f32[2,384,256]{2,1,0:T(8,128)S(1)}) custom-call(bf16[384,11008]{1,0:T(8,128)(2,1)S(1)} %copy-done, ...), custom_call_target="tpu_custom_call", output_to_operand_aliasing={{0}: (6, {}), {1}: (7, {}), {2}: (8, {}), {3}: (9, {})} | custom-call | flops 1409286144 | bytes 2752512 | tf_op jit(solution)/shard_map/pallas_call | solution.py:158
  47.6 2.9 %collective-permute-done.10.refs_2_ = bf16[688,256]{1,0:T(8,128)(2,1)S(1)} collective-permute-done((bf16[688,256]{1,0:T(8,128)(2,1)}, bf16[688,256]{1,0:T(8,128)(2,1)S(1)}, u32[]{:S(2)}, u32[]{:S(2)}) %collective-permute-start.10) | collective-permute-done | bytes 352288 | tf_op jit(solution)/shard_map/ppermute | solution.py:270
  50.5 1.2 collective-permute-start.16
  51.6 0.3 collective-permute-start.15
  51.9 6.1 %collective-permute-done.8.refs_0_ = bf16[688,256]{1,0:T(8,128)(2,1)S(1)} collective-permute-done((bf16[688,256]{1,0:T(8,128)(2,1)S(1)}, bf16[688,256]{1,0:T(8,128)(2,1)S(1)}, u32[]{:S(2)}, u32[]{:S(2)}) %collective-permute-start.8) | collective-permute-done | bytes 352288 | tf_op jit(solution)/shard_map/ppermute | solution.py:270
  58.1 1.0 collective-permute-start.21
  59.1 0.4 collective-permute-start.14
  59.5 4.5 %shard_map.52 = (f32[2,384,256]{2,1,0:T(8,128)S(1)}, f32[2,384,256]{2,1,0:T(8,128)S(1)}, f32[2,384,256]{2,1,0:T(8,128)S(1)}, f32[2,384,256]{2,1,0:T(8,128)S(1)}) custom-call(bf16[384,11008]{1,0:T(8,128)(2,1)S(1)} %copy-done, ...), custom_call_target="tpu_custom_call", output_to_operand_aliasing={{0}: (6, {}), {1}: (7, {}), {2}: (8, {}), {3}: (9, {})} | custom-call | flops 1409286144 | bytes 2752512 | tf_op jit(solution)/shard_map/pallas_call | solution.py:158
  64.0 3.2 %shard_map.53 = (f32[2,384,256]{2,1,0:T(8,128)S(1)}, f32[2,384,256]{2,1,0:T(8,128)S(1)}, f32[2,384,256]{2,1,0:T(8,128)S(1)}, f32[2,384,256]{2,1,0:T(8,128)S(1)}) custom-call(bf16[384,11008]{1,0:T(8,128)(2,1)S(1)} %copy-done, ...), custom_call_target="tpu_custom_call", output_to_operand_aliasing={{0}: (6, {}), {1}: (7, {}), {2}: (8, {}), {3}: (9, {})} | custom-call | flops 1409286144 | bytes 2752512 | tf_op jit(solution)/shard_map/pallas_call | solution.py:158
  67.3 1.3 collective-permute-start.20
  68.6 0.2 collective-permute-start.19
  68.8 4.3 %collective-permute-done.14.refs_0_ = bf16[688,256]{1,0:T(8,128)(2,1)S(1)} collective-permute-done((bf16[688,256]{1,0:T(8,128)(2,1)S(1)}, bf16[688,256]{1,0:T(8,128)(2,1)S(1)}, u32[]{:S(2)}, u32[]{:S(2)}) %collective-permute-start.14) | collective-permute-done | bytes 352288 | tf_op jit(solution)/shard_map/ppermute | solution.py:270
  73.1 1.2 collective-permute-start.18
  74.3 0.3 collective-permute-start.23
  74.6 3.2 %shard_map.54 = (f32[2,384,256]{2,1,0:T(8,128)S(1)}, f32[2,384,256]{2,1,0:T(8,128)S(1)}, f32[2,384,256]{2,1,0:T(8,128)S(1)}, f32[2,384,256]{2,1,0:T(8,128)S(1)}) custom-call(bf16[384,11008]{1,0:T(8,128)(2,1)S(1)} %copy-done, ...), custom_call_target="tpu_custom_call", output_to_operand_aliasing={{0}: (6, {}), {1}: (7, {}), {2}: (8, {}), {3}: (9, {})} | custom-call | flops 1409286144 | bytes 2752512 | tf_op jit(solution)/shard_map/pallas_call | solution.py:158
  77.8 2.9 %collective-permute-done.20.refs_2_ = bf16[688,256]{1,0:T(8,128)(2,1)S(1)} collective-permute-done((bf16[688,256]{1,0:T(8,128)(2,1)S(1)}, bf16[688,256]{1,0:T(8,128)(2,1)S(1)}, u32[]{:S(2)}, u32[]{:S(2)}) %collective-permute-start.20) | collective-permute-done | bytes 352288 | tf_op jit(solution)/shard_map/ppermute | solution.py:270
  80.7 1.2 collective-permute-start.25
  81.8 0.3 collective-permute-start.26
  82.1 6.1 %collective-permute-done.18.refs_0_ = bf16[688,256]{1,0:T(8,128)(2,1)S(1)} collective-permute-done((bf16[688,256]{1,0:T(8,128)(2,1)S(1)}, bf16[688,256]{1,0:T(8,128)(2,1)S(1)}, u32[]{:S(2)}, u32[]{:S(2)}) %collective-permute-start.18) | collective-permute-done | bytes 352288 | tf_op jit(solution)/shard_map/ppermute | solution.py:270
  88.2 1.1 collective-permute-start.24
  89.3 0.4 collective-permute-start.22
  89.7 3.2 %shard_map.55 = (f32[2,384,256]{2,1,0:T(8,128)S(1)}, f32[2,384,256]{2,1,0:T(8,128)S(1)}, f32[2,384,256]{2,1,0:T(8,128)S(1)}, f32[2,384,256]{2,1,0:T(8,128)S(1)}) custom-call(bf16[384,11008]{1,0:T(8,128)(2,1)S(1)} %copy-done, ...), custom_call_target="tpu_custom_call", output_to_operand_aliasing={{0}: (6, {}), {1}: (7, {}), {2}: (8, {}), {3}: (9, {})} | custom-call | flops 1409286144 | bytes 2752512 | tf_op jit(solution)/shard_map/pallas_call | solution.py:158
  92.9 2.9 %collective-permute-done.25.refs_2_ = bf16[688,256]{1,0:T(8,128)(2,1)S(1)} collective-permute-done((bf16[688,256]{1,0:T(8,128)(2,1)S(1)}, bf16[688,256]{1,0:T(8,128)(2,1)S(1)}, u32[]{:S(2)}, u32[]{:S(2)}) %collective-permute-start.25) | collective-permute-done | bytes 352288 | tf_op jit(solution)/shard_map/ppermute | solution.py:270
  95.8 1.1 collective-permute-start.28
  96.9 0.4 collective-permute-start.27
  97.2 3.2 %shard_map.56 = (f32[2,384,256]{2,1,0:T(8,128)S(1)}, f32[2,384,256]{2,1,0:T(8,128)S(1)}, f32[2,384,256]{2,1,0:T(8,128)S(1)}, f32[2,384,256]{2,1,0:T(8,128)S(1)}) custom-call(bf16[384,11008]{1,0:T(8,128)(2,1)S(1)} %copy-done, ...), custom_call_target="tpu_custom_call", output_to_operand_aliasing={{0}: (6, {}), {1}: (7, {}), {2}: (8, {}), {3}: (9, {})} | custom-call | flops 1409286144 | bytes 2752512 | tf_op jit(solution)/shard_map/pallas_call | solution.py:158
  100.4 2.1 %collective-permute-done.24.refs_1_ = bf16[688,256]{1,0:T(8,128)(2,1)S(1)} collective-permute-done((bf16[688,256]{1,0:T(8,128)(2,1)S(1)}, bf16[688,256]{1,0:T(8,128)(2,1)S(1)}, u32[]{:S(2)}, u32[]{:S(2)}) %collective-permute-start.24) | collective-permute-done | bytes 352288 | tf_op jit(solution)/shard_map/ppermute | solution.py:270
  102.5 0.8 collective-permute-done.22.refs_0_
  103.3 2.4 %shard_map.57 = (f32[2,384,256]{2,1,0:T(8,128)S(1)}, f32[2,384,256]{2,1,0:T(8,128)S(1)}, bf16[2,768,896]{2,1,0:T(8,128)(2,1)S(1)}) custom-call(bf16[384,11008]{1,0:T(8,128)(2,1)S(1)} %copy-done, bf16[384,11008]{1,0:T(8,128)(2,1)} %collective-permute-done.2.other_hbm, ...), custom_call_target="tpu_custom_call", output_to_operand_aliasing={{0}: (4, {}), {1}: (5, {})} | custom-call | flops 704643072 | bytes 2752512 | tf_op jit(solution)/shard_map/pallas_call | solution.py:158
  105.7 2.3 %collective-permute-start.30 = (f32[2,384,256]{2,1,0:T(8,128)S(1)}, f32[2,384,256]{2,1,0:T(8,128)S(1)}, u32[]{:S(2)}, u32[]{:S(2)}) collective-permute-start(f32[2,384,256]{2,1,0:T(8,128)S(1)} %get-tuple-element.252), channel_id=1, source_target_pairs={{0,1},{1,0},{2,3},{3,2},{4,5},{5,4},{6,7},{7,6},{8,9},{9,8},{10,11... | collective-permute-start | bytes 2359304 | tf_op jit(solution)/shard_map/ppermute | solution.py:278
  108.0 2.1 %collective-permute-done.28.refs_1_ = bf16[688,256]{1,0:T(8,128)(2,1)S(1)} collective-permute-done((bf16[688,256]{1,0:T(8,128)(2,1)S(1)}, bf16[688,256]{1,0:T(8,128)(2,1)S(1)}, u32[]{:S(2)}, u32[]{:S(2)}) %collective-permute-start.28) | collective-permute-done | bytes 352288 | tf_op jit(solution)/shard_map/ppermute | solution.py:270
  110.1 0.8 collective-permute-done.27.refs_0_
  110.9 1.1 shard_map.58
  112.0 1.2 collective-permute-start.29
  113.2 1.5 shard_map.59.refs_0_
  114.7 0.4 collective-permute-done.29.theirs_ref
  115.1 1.5 shard_map.60
  116.6 6.6 %all-to-all-start.1 = ((bf16[16,2,6,16,256]{4,3,2,1,0:T(8,128)(2,1)}), bf16[16,2,6,16,256]{4,3,2,1,0:T(8,128)(2,1)S(1)}, u32[]{:S(2)}, u32[]{:S(2)}) async-start(bf16[16,2,6,16,256]{4,3,2,1,0:T(8,128)(2,1)} %shard_map.60), calls=%async_computation.1 | async-start | bytes 3145728 | tf_op jit(solution)/shard_map/all_to_all | solution.py:305
  123.2 1.3 shard_map.61
  124.5 34.9 %all-to-all-done.1 = bf16[16,2,6,16,256]{4,3,2,1,0:T(8,128)(2,1)S(1)} async-done(((bf16[16,2,6,16,256]{4,3,2,1,0:T(8,128)(2,1)}), bf16[16,2,6,16,256]{4,3,2,1,0:T(8,128)(2,1)S(1)}, u32[]{:S(2)}, u32[]{:S(2)}) %all-to-all-start.1) | async-done | bytes 1572896 | tf_op jit(solution)/shard_map/all_to_all | solution.py:305
  159.4 1.3 copy.37
  (32 shorter events, 0.9 us)
Async XLA Ops:
  0.6 5.1 %copy-start.2 = (s32[128,1]{0,1:T(1,128)S(1)}, s32[128,1]{0,1:T(1,128)}, u32[]{:S(2)}) copy-start(s32[128,1]{0,1:T(1,128)} %param.5) | copy-start | bytes 1540
  0.6 28.8 %collective-permute-start.2 = (bf16[384,11008]{1,0:T(8,128)(2,1)}, bf16[384,11008]{1,0:T(8,128)(2,1)}, u32[]{:S(2)}, u32[]{:S(2)}) collective-permute-start(bf16[384,11008]{1,0:T(8,128)(2,1)} %own_hbm.15), channel_id=1, source_target_pairs={{0,1},{1,0},{2,3},{3,2},{4,5},{5,4},{6,7},{7,6},{8,9},{9,8},{10,11... | collective-permute-start | bytes 25362440 | tf_op jit(solution)/shard_map/ppermute | solution.py:242
  2.8 11.3 %collective-permute-start.11 = (bf16[688,256]{1,0:T(8,128)(2,1)S(1)}, bf16[688,256]{1,0:T(8,128)(2,1)S(1)}, u32[]{:S(2)}, u32[]{:S(2)}) collective-permute-start(bf16[688,256]{1,0:T(8,128)(2,1)S(1)} %get-tuple-element.256.refs_1_), channel_id=1, source_target_pairs={{0,4},{1,5},{2,0},{3,1},{6,2},{7,3},{10,6},{11,7},{14,10},{15,11},... | collective-permute-start | bytes 1056776 | tf_op jit(solution)/shard_map/ppermute | solution.py:270
  3.0 17.2 %collective-permute-start.4 = (bf16[688,256]{1,0:T(8,128)(2,1)S(1)}, bf16[688,256]{1,0:T(8,128)(2,1)S(1)}, u32[]{:S(2)}, u32[]{:S(2)}) collective-permute-start(bf16[688,256]{1,0:T(8,128)(2,1)S(1)} %get-tuple-element.257.refs_3_), channel_id=1, source_target_pairs={{0,4},{1,5},{2,0},{3,1},{6,2},{7,3},{10,6},{11,7},{14,10},{15,11},... | collective-permute-start | bytes 1056776 | tf_op jit(solution)/shard_map/ppermute | solution.py:270
  3.1 11.4 %collective-permute-start = (bf16[688,256]{1,0:T(8,128)(2,1)S(1)}, bf16[688,256]{1,0:T(8,128)(2,1)S(1)}, u32[]{:S(2)}, u32[]{:S(2)}) collective-permute-start(bf16[688,256]{1,0:T(8,128)(2,1)S(1)} %get-tuple-element.258.refs_0_), channel_id=1, source_target_pairs={{0,2},{1,3},{2,6},{3,7},{6,10},{7,11},{10,14},{11,15},{14,12},{15,... | collective-permute-start | bytes 1056776 | tf_op jit(solution)/shard_map/ppermute | solution.py:270
  4.5 15.9 %collective-permute-start.6 = (bf16[688,256]{1,0:T(8,128)(2,1)S(1)}, bf16[688,256]{1,0:T(8,128)(2,1)S(1)}, u32[]{:S(2)}, u32[]{:S(2)}) collective-permute-start(bf16[688,256]{1,0:T(8,128)(2,1)S(1)} %get-tuple-element.259.refs_2_), channel_id=1, source_target_pairs={{0,2},{1,3},{2,6},{3,7},{6,10},{7,11},{10,14},{11,15},{14,12},{15,... | collective-permute-start | bytes 1056776 | tf_op jit(solution)/shard_map/ppermute | solution.py:270
  6.8 18.2 %all-to-all-start = ((s32[16,1,16]{2,1,0:T(1,128)}), s32[16,1,16]{2,1,0:T(1,128)S(1)}, u32[]{:S(2)}, u32[]{:S(2)}) async-start(s32[16,1,16]{2,1,0:T(1,128)} %sub.17), calls=%async_computation | async-start | bytes 16384 | tf_op jit(solution)/shard_map/all_to_all | solution.py:294
  14.1 15.0 %collective-permute-start.12 = (bf16[688,256]{1,0:T(8,128)(2,1)S(1)}, bf16[688,256]{1,0:T(8,128)(2,1)}, u32[]{:S(2)}, u32[]{:S(2)}) collective-permute-start(bf16[688,256]{1,0:T(8,128)(2,1)S(1)} %collective-permute-done.11.refs_1_), channel_id=1, source_target_pairs={{0,4},{1,5},{2,0},{3,1},{6,2},{7,3},{10,6},{11,7},{14,10},{15,11},... | collective-permute-start | bytes 1056776 | tf_op jit(solution)/shard_map/ppermute | solution.py:270
  14.4 13.5 %collective-permute-start.1 = (bf16[688,256]{1,0:T(8,128)(2,1)S(1)}, bf16[688,256]{1,0:T(8,128)(2,1)}, u32[]{:S(2)}, u32[]{:S(2)}) collective-permute-start(bf16[688,256]{1,0:T(8,128)(2,1)S(1)} %collective-permute-done.refs_0_), channel_id=1, source_target_pairs={{0,2},{1,3},{2,6},{3,7},{6,10},{7,11},{10,14},{11,15},{14,12},{15,... | collective-permute-start | bytes 1056776 | tf_op jit(solution)/shard_map/ppermute | solution.py:270
  20.2 17.0 %collective-permute-start.5 = (bf16[688,256]{1,0:T(8,128)(2,1)S(1)}, bf16[688,256]{1,0:T(8,128)(2,1)}, u32[]{:S(2)}, u32[]{:S(2)}) collective-permute-start(bf16[688,256]{1,0:T(8,128)(2,1)S(1)} %collective-permute-done.4.refs_3_), channel_id=1, source_target_pairs={{0,4},{1,5},{2,0},{3,1},{6,2},{7,3},{10,6},{11,7},{14,10},{15,11},... | collective-permute-start | bytes 1056776 | tf_op jit(solution)/shard_map/ppermute | solution.py:270
  20.4 15.5 %collective-permute-start.7 = (bf16[688,256]{1,0:T(8,128)(2,1)S(1)}, bf16[688,256]{1,0:T(8,128)(2,1)}, u32[]{:S(2)}, u32[]{:S(2)}) collective-permute-start(bf16[688,256]{1,0:T(8,128)(2,1)S(1)} %collective-permute-done.6.refs_2_), channel_id=1, source_target_pairs={{0,2},{1,3},{2,6},{3,7},{6,10},{7,11},{10,14},{11,15},{14,12},{15,... | collective-permute-start | bytes 1056776 | tf_op jit(solution)/shard_map/ppermute | solution.py:270
  25.0 11.0 %copy-start.1 = (s32[16,1,16]{2,1,0:T(1,128)}, s32[16,1,16]{2,1,0:T(1,128)S(1)}, u32[]{:S(2)}) copy-start(s32[16,1,16]{2,1,0:T(1,128)S(1)} %all-to-all-done) | copy-start | bytes 3076
  27.9 15.0 %collective-permute-start.3 = (bf16[688,256]{1,0:T(8,128)(2,1)}, bf16[688,256]{1,0:T(8,128)(2,1)S(1)}, u32[]{:S(2)}, u32[]{:S(2)}) collective-permute-start(bf16[688,256]{1,0:T(8,128)(2,1)} %collective-permute-done.1.refs_0_), channel_id=1, source_target_pairs={{0,2},{1,3},{2,6},{3,7},{6,10},{7,11},{10,14},{11,15},{14,12},{15,... | collective-permute-start | bytes 1056776 | tf_op jit(solution)/shard_map/ppermute | solution.py:270
  29.1 15.0 %collective-permute-start.13 = (bf16[688,256]{1,0:T(8,128)(2,1)}, bf16[688,256]{1,0:T(8,128)(2,1)S(1)}, u32[]{:S(2)}, u32[]{:S(2)}) collective-permute-start(bf16[688,256]{1,0:T(8,128)(2,1)} %collective-permute-done.12.refs_1_), channel_id=1, source_target_pairs={{0,4},{1,5},{2,0},{3,1},{6,2},{7,3},{10,6},{11,7},{14,10},{15,11},... | collective-permute-start | bytes 1056776 | tf_op jit(solution)/shard_map/ppermute | solution.py:270
  29.4 3.4 %copy-start = (bf16[384,11008]{1,0:T(8,128)(2,1)S(1)}, bf16[384,11008]{1,0:T(8,128)(2,1)}, u32[]{:S(2)}) copy-start(bf16[384,11008]{1,0:T(8,128)(2,1)} %own_hbm.15) | copy-start | bytes 25362436
  36.0 14.5 %collective-permute-start.10 = (bf16[688,256]{1,0:T(8,128)(2,1)}, bf16[688,256]{1,0:T(8,128)(2,1)S(1)}, u32[]{:S(2)}, u32[]{:S(2)}) collective-permute-start(bf16[688,256]{1,0:T(8,128)(2,1)} %collective-permute-done.7.refs_2_), channel_id=1, source_target_pairs={{0,2},{1,3},{2,6},{3,7},{6,10},{7,11},{10,14},{11,15},{14,12},{15,... | collective-permute-start | bytes 1056776 | tf_op jit(solution)/shard_map/ppermute | solution.py:270
  37.2 14.4 %collective-permute-start.9 = (bf16[688,256]{1,0:T(8,128)(2,1)}, bf16[688,256]{1,0:T(8,128)(2,1)S(1)}, u32[]{:S(2)}, u32[]{:S(2)}) collective-permute-start(bf16[688,256]{1,0:T(8,128)(2,1)} %collective-permute-done.5.refs_3_), channel_id=1, source_target_pairs={{0,4},{1,5},{2,0},{3,1},{6,2},{7,3},{10,6},{11,7},{14,10},{15,11},... | collective-permute-start | bytes 1056776 | tf_op jit(solution)/shard_map/ppermute | solution.py:270
  42.9 15.1 %collective-permute-start.8 = (bf16[688,256]{1,0:T(8,128)(2,1)S(1)}, bf16[688,256]{1,0:T(8,128)(2,1)S(1)}, u32[]{:S(2)}, u32[]{:S(2)}) collective-permute-start(bf16[688,256]{1,0:T(8,128)(2,1)S(1)} %collective-permute-done.3.refs_0_), channel_id=1, source_target_pairs={{0,2},{1,3},{2,6},{3,7},{6,10},{7,11},{10,14},{11,15},{14,12},{15,... | collective-permute-start | bytes 1056776 | tf_op jit(solution)/shard_map/ppermute | solution.py:270
  44.1 14.0 %collective-permute-start.17 = (bf16[688,256]{1,0:T(8,128)(2,1)S(1)}, bf16[688,256]{1,0:T(8,128)(2,1)S(1)}, u32[]{:S(2)}, u32[]{:S(2)}) collective-permute-start(bf16[688,256]{1,0:T(8,128)(2,1)S(1)} %collective-permute-done.13.refs_1_), channel_id=1, source_target_pairs={{0,4},{1,5},{2,0},{3,1},{6,2},{7,3},{10,6},{11,7},{14,10},{15,11},... | collective-permute-start | bytes 1056776 | tf_op jit(solution)/shard_map/ppermute | solution.py:270
  50.5 16.8 %collective-permute-start.16 = (bf16[688,256]{1,0:T(8,128)(2,1)S(1)}, bf16[688,256]{1,0:T(8,128)(2,1)S(1)}, u32[]{:S(2)}, u32[]{:S(2)}) collective-permute-start(bf16[688,256]{1,0:T(8,128)(2,1)S(1)} %collective-permute-done.10.refs_2_), channel_id=1, source_target_pairs={{0,2},{1,3},{2,6},{3,7},{6,10},{7,11},{10,14},{11,15},{14,12},{15,... | collective-permute-start | bytes 1056776 | tf_op jit(solution)/shard_map/ppermute | solution.py:270
  51.6 17.0 %collective-permute-start.15 = (bf16[688,256]{1,0:T(8,128)(2,1)S(1)}, bf16[688,256]{1,0:T(8,128)(2,1)S(1)}, u32[]{:S(2)}, u32[]{:S(2)}) collective-permute-start(bf16[688,256]{1,0:T(8,128)(2,1)S(1)} %collective-permute-done.9.refs_3_), channel_id=1, source_target_pairs={{0,4},{1,5},{2,0},{3,1},{6,2},{7,3},{10,6},{11,7},{14,10},{15,11},... | collective-permute-start | bytes 1056776 | tf_op jit(solution)/shard_map/ppermute | solution.py:270
  58.1 16.2 %collective-permute-start.21 = (bf16[688,256]{1,0:T(8,128)(2,1)S(1)}, bf16[688,256]{1,0:T(8,128)(2,1)S(1)}, u32[]{:S(2)}, u32[]{:S(2)}) collective-permute-start(bf16[688,256]{1,0:T(8,128)(2,1)S(1)} %collective-permute-done.17.refs_1_), channel_id=1, source_target_pairs={{0,4},{1,5},{2,0},{3,1},{6,2},{7,3},{10,6},{11,7},{14,10},{15,11},... | collective-permute-start | bytes 1056776 | tf_op jit(solution)/shard_map/ppermute | solution.py:270
  59.1 14.0 %collective-permute-start.14 = (bf16[688,256]{1,0:T(8,128)(2,1)S(1)}, bf16[688,256]{1,0:T(8,128)(2,1)S(1)}, u32[]{:S(2)}, u32[]{:S(2)}) collective-permute-start(bf16[688,256]{1,0:T(8,128)(2,1)S(1)} %collective-permute-done.8.refs_0_), channel_id=1, source_target_pairs={{0,2},{1,3},{2,6},{3,7},{6,10},{7,11},{10,14},{11,15},{14,12},{15,... | collective-permute-start | bytes 1056776 | tf_op jit(solution)/shard_map/ppermute | solution.py:270
  67.3 13.4 %collective-permute-start.20 = (bf16[688,256]{1,0:T(8,128)(2,1)S(1)}, bf16[688,256]{1,0:T(8,128)(2,1)S(1)}, u32[]{:S(2)}, u32[]{:S(2)}) collective-permute-start(bf16[688,256]{1,0:T(8,128)(2,1)S(1)} %collective-permute-done.16.refs_2_), channel_id=1, source_target_pairs={{0,2},{1,3},{2,6},{3,7},{6,10},{7,11},{10,14},{11,15},{14,12},{15,... | collective-permute-start | bytes 1056776 | tf_op jit(solution)/shard_map/ppermute | solution.py:270
  68.6 13.2 %collective-permute-start.19 = (bf16[688,256]{1,0:T(8,128)(2,1)S(1)}, bf16[688,256]{1,0:T(8,128)(2,1)S(1)}, u32[]{:S(2)}, u32[]{:S(2)}) collective-permute-start(bf16[688,256]{1,0:T(8,128)(2,1)S(1)} %collective-permute-done.15.refs_3_), channel_id=1, source_target_pairs={{0,4},{1,5},{2,0},{3,1},{6,2},{7,3},{10,6},{11,7},{14,10},{15,11},... | collective-permute-start | bytes 1056776 | tf_op jit(solution)/shard_map/ppermute | solution.py:270
  73.1 15.1 %collective-permute-start.18 = (bf16[688,256]{1,0:T(8,128)(2,1)S(1)}, bf16[688,256]{1,0:T(8,128)(2,1)S(1)}, u32[]{:S(2)}, u32[]{:S(2)}) collective-permute-start(bf16[688,256]{1,0:T(8,128)(2,1)S(1)} %collective-permute-done.14.refs_0_), channel_id=1, source_target_pairs={{0,2},{1,3},{2,6},{3,7},{6,10},{7,11},{10,14},{11,15},{14,12},{15,... | collective-permute-start | bytes 1056776 | tf_op jit(solution)/shard_map/ppermute | solution.py:270
  74.3 13.9 %collective-permute-start.23 = (bf16[688,256]{1,0:T(8,128)(2,1)S(1)}, bf16[688,256]{1,0:T(8,128)(2,1)S(1)}, u32[]{:S(2)}, u32[]{:S(2)}) collective-permute-start(bf16[688,256]{1,0:T(8,128)(2,1)S(1)} %collective-permute-done.21.refs_1_), channel_id=1, source_target_pairs={{0,4},{1,5},{2,0},{3,1},{6,2},{7,3},{10,6},{11,7},{14,10},{15,11},... | collective-permute-start | bytes 1056776 | tf_op jit(solution)/shard_map/ppermute | solution.py:270
  80.7 15.1 %collective-permute-start.25 = (bf16[688,256]{1,0:T(8,128)(2,1)S(1)}, bf16[688,256]{1,0:T(8,128)(2,1)S(1)}, u32[]{:S(2)}, u32[]{:S(2)}) collective-permute-start(bf16[688,256]{1,0:T(8,128)(2,1)S(1)} %collective-permute-done.20.refs_2_), channel_id=1, source_target_pairs={{0,2},{1,3},{2,6},{3,7},{6,10},{7,11},{10,14},{11,15},{14,12},{15,... | collective-permute-start | bytes 1056776 | tf_op jit(solution)/shard_map/ppermute | solution.py:270
  81.8 13.9 %collective-permute-start.26 = (bf16[688,256]{1,0:T(8,128)(2,1)S(1)}, bf16[688,256]{1,0:T(8,128)(2,1)S(1)}, u32[]{:S(2)}, u32[]{:S(2)}) collective-permute-start(bf16[688,256]{1,0:T(8,128)(2,1)S(1)} %collective-permute-done.19.refs_3_), channel_id=1, source_target_pairs={{0,4},{1,5},{2,0},{3,1},{6,2},{7,3},{10,6},{11,7},{14,10},{15,11},... | collective-permute-start | bytes 1056776 | tf_op jit(solution)/shard_map/ppermute | solution.py:270
  88.2 14.3 %collective-permute-start.24 = (bf16[688,256]{1,0:T(8,128)(2,1)S(1)}, bf16[688,256]{1,0:T(8,128)(2,1)S(1)}, u32[]{:S(2)}, u32[]{:S(2)}) collective-permute-start(bf16[688,256]{1,0:T(8,128)(2,1)S(1)} %collective-permute-done.23.refs_1_), channel_id=1, source_target_pairs={{0,4},{1,5},{2,0},{3,1},{6,2},{7,3},{10,6},{11,7},{14,10},{15,11},... | collective-permute-start | bytes 1056776 | tf_op jit(solution)/shard_map/ppermute | solution.py:270
  89.3 14.0 %collective-permute-start.22 = (bf16[688,256]{1,0:T(8,128)(2,1)S(1)}, bf16[688,256]{1,0:T(8,128)(2,1)S(1)}, u32[]{:S(2)}, u32[]{:S(2)}) collective-permute-start(bf16[688,256]{1,0:T(8,128)(2,1)S(1)} %collective-permute-done.18.refs_0_), channel_id=1, source_target_pairs={{0,2},{1,3},{2,6},{3,7},{6,10},{7,11},{10,14},{11,15},{14,12},{15,... | collective-permute-start | bytes 1056776 | tf_op jit(solution)/shard_map/ppermute | solution.py:270
  95.8 14.3 %collective-permute-start.28 = (bf16[688,256]{1,0:T(8,128)(2,1)S(1)}, bf16[688,256]{1,0:T(8,128)(2,1)S(1)}, u32[]{:S(2)}, u32[]{:S(2)}) collective-permute-start(bf16[688,256]{1,0:T(8,128)(2,1)S(1)} %collective-permute-done.26.refs_3_), channel_id=1, source_target_pairs={{0,4},{1,5},{2,0},{3,1},{6,2},{7,3},{10,6},{11,7},{14,10},{15,11},... | collective-permute-start | bytes 1056776 | tf_op jit(solution)/shard_map/ppermute | solution.py:270
  96.9 14.0 %collective-permute-start.27 = (bf16[688,256]{1,0:T(8,128)(2,1)S(1)}, bf16[688,256]{1,0:T(8,128)(2,1)S(1)}, u32[]{:S(2)}, u32[]{:S(2)}) collective-permute-start(bf16[688,256]{1,0:T(8,128)(2,1)S(1)} %collective-permute-done.25.refs_2_), channel_id=1, source_target_pairs={{0,2},{1,3},{2,6},{3,7},{6,10},{7,11},{10,14},{11,15},{14,12},{15,... | collective-permute-start | bytes 1056776 | tf_op jit(solution)/shard_map/ppermute | solution.py:270
  105.7 7.5 %collective-permute-start.30 = (f32[2,384,256]{2,1,0:T(8,128)S(1)}, f32[2,384,256]{2,1,0:T(8,128)S(1)}, u32[]{:S(2)}, u32[]{:S(2)}) collective-permute-start(f32[2,384,256]{2,1,0:T(8,128)S(1)} %get-tuple-element.252), channel_id=1, source_target_pairs={{0,1},{1,0},{2,3},{3,2},{4,5},{5,4},{6,7},{7,6},{8,9},{9,8},{10,11... | collective-permute-start | bytes 2359304 | tf_op jit(solution)/shard_map/ppermute | solution.py:278
  112.0 3.1 %collective-permute-start.29 = (f32[2,384,256]{2,1,0:T(8,128)S(1)}, f32[2,384,256]{2,1,0:T(8,128)S(1)}, u32[]{:S(2)}, u32[]{:S(2)}) collective-permute-start(f32[2,384,256]{2,1,0:T(8,128)S(1)} %get-tuple-element.250), channel_id=1, source_target_pairs={{0,1},{1,0},{2,3},{3,2},{4,5},{5,4},{6,7},{7,6},{8,9},{9,8},{10,11... | collective-permute-start | bytes 2359304 | tf_op jit(solution)/shard_map/ppermute | solution.py:278
  116.6 42.8 %all-to-all-start.1 = ((bf16[16,2,6,16,256]{4,3,2,1,0:T(8,128)(2,1)}), bf16[16,2,6,16,256]{4,3,2,1,0:T(8,128)(2,1)S(1)}, u32[]{:S(2)}, u32[]{:S(2)}) async-start(bf16[16,2,6,16,256]{4,3,2,1,0:T(8,128)(2,1)} %shard_map.60), calls=%async_computation.1 | async-start | bytes 3145728 | tf_op jit(solution)/shard_map/all_to_all | solution.py:305

commit v15 on v14

--- a/solution.py
+++ b/solution.py
@@ -11,7 +11,7 @@
 GRID_CHIPS = 8
 HALVES = 2
 BEHIND = ((0, 0), (0, 0), (0, 1), (1, 2), (2, 4), (4, 5), (5, 6))
-WAYS = (1, -1)
+WAYS = (-1, 1)
 LANES = 128
 WINDOW = 896
 

time: 161 us -> 161 us (level)
  starting transfers between devices: 38.6 us -> 36.8 us
  waiting for transfers between devices: 82.3 us -> 84.1 us
    ppermute x28, waiting for transfers between devices: 43.9 us -> 47 us  [ring_products(): piece[j][i] = lax.ppermute(sent, 'wide', shift[i])]
    all_to_all x1, starting transfers between devices: 6.6 us -> 4.24 us  [local(): lax.all_to_all(out, 'wide', split_axis=0, concat_axis=0, tiled=True)]
  transfers between devices with their start and end apart: 33 -> 33, of which waited for: 17 -> 15; matrix products, arithmetic and copies ran while one was open for 2% -> 2% of each run, Pallas kernels for 19% -> 19%
where the time goes in v15:
time: 161 us
  waiting for transfers between devices  84.1 us (52%)
  starting transfers between devices  36.8 us (23%)
  Pallas kernels  31.3 us (19%)
  local copies, waits for them, and re-layouts  7.12 us (4%)
    ppermute x28, waiting for transfers between devices, ring_products(): piece[j][i] = lax.ppermute(sent, 'wide', shift[i])  47 us
    all_to_all x1, waiting for transfers between devices, local(): lax.all_to_all(out, 'wide', split_axis=0, concat_axis=0, tiled=True)  34.9 us
    pallas_call x8, Pallas kernels, add_products(): pl.pallas_call(functools.partial(step_kernel, t, parts), out_shape=[sums]...  25.9 us
    ppermute x28, starting transfers between devices, ring_products(): piece[j][i] = lax.ppermute(sent, 'wide', shift[i])  20.8 us
    all_to_all x1, starting transfers between devices, local(): lax.all_to_all(labels, 'wide', split_axis=0, concat_axis=0, tiled=True)  7.02 us
    all_to_all x1, starting transfers between devices, local(): lax.all_to_all(out, 'wide', split_axis=0, concat_axis=0, tiled=True)  4.24 us
    ppermute x2, starting transfers between devices, ring_products(): theirs = [lax.ppermute(sums[j][1], 'wide', swap) for j in range(HALVES)]  4.06 us
    unnamed x6, local copies, waits for them, and re-layouts  3.41 us
  transfers between devices with their start and end apart: 33, of which 15 were waited for; matrix products, arithmetic and copies ran while one was open for 2% of the time, Pallas kernels for 19%

profile of v15, /device:TPU:13, one launch (start us, length us, event | category | flops | bytes accessed | tf_op | source)
XLA Modules:
  0.0 160.7 jit_solution(7640196928428292945)
XLA Ops:
  0.6 0.7 collective-permute-start.2
  1.4 1.4 slice_bitcast_fusion
  2.8 1.3 collective-permute-start.11
  4.1 1.3 collective-permute-start.4
  5.4 0.2 collective-permute-start
  5.6 0.2 collective-permute-start.6
  5.8 0.2 convert_reduce_fusion
  6.1 0.7 sub.17
  6.8 7.0 %all-to-all-start = ((s32[16,1,16]{2,1,0:T(1,128)}), s32[16,1,16]{2,1,0:T(1,128)S(1)}, u32[]{:S(2)}, u32[]{:S(2)}) async-start(s32[16,1,16]{2,1,0:T(1,128)} %sub.17), calls=%async_computation | async-start | bytes 16384 | tf_op jit(solution)/shard_map/all_to_all | solution.py:294
  13.9 0.2 mul.58
  14.1 1.2 collective-permute-start.12
  15.3 0.3 collective-permute-start.1
  15.6 4.6 %collective-permute-done.4.refs_3_ = bf16[688,256]{1,0:T(8,128)(2,1)S(1)} collective-permute-done((bf16[688,256]{1,0:T(8,128)(2,1)S(1)}, bf16[688,256]{1,0:T(8,128)(2,1)S(1)}, u32[]{:S(2)}, u32[]{:S(2)}) %collective-permute-start.4) | collective-permute-done | bytes 352288 | tf_op jit(solution)/shard_map/ppermute | solution.py:270
  20.2 1.3 collective-permute-start.5
  21.6 0.7 collective-permute-done.6.refs_2_
  22.3 0.1 collective-permute-start.7
  22.5 0.2 compare_convert_fusion.place_ref
  22.6 1.9 %all-to-all-done = s32[16,1,16]{2,1,0:T(1,128)S(1)} async-done(((s32[16,1,16]{2,1,0:T(1,128)}), s32[16,1,16]{2,1,0:T(1,128)S(1)}, u32[]{:S(2)}, u32[]{:S(2)}) %all-to-all-start) | async-done | bytes 1056 | tf_op jit(solution)/shard_map/all_to_all | solution.py:294
  24.5 5.5 %collective-permute-done.1.refs_0_ = bf16[688,256]{1,0:T(8,128)(2,1)} collective-permute-done((bf16[688,256]{1,0:T(8,128)(2,1)S(1)}, bf16[688,256]{1,0:T(8,128)(2,1)}, u32[]{:S(2)}, u32[]{:S(2)}) %collective-permute-start.1) | collective-permute-done | bytes 352288 | tf_op jit(solution)/shard_map/ppermute | solution.py:270
  30.1 1.3 collective-permute-start.13
  31.5 3.4 %copy-done = bf16[384,11008]{1,0:T(8,128)(2,1)S(1)} copy-done((bf16[384,11008]{1,0:T(8,128)(2,1)S(1)}, bf16[384,11008]{1,0:T(8,128)(2,1)}, u32[]{:S(2)}) %copy-start) | copy-done | bytes 8454168
  34.9 3.1 %shard_map.50 = (f32[2,384,256]{2,1,0:T(8,128)S(1)}, f32[2,384,256]{2,1,0:T(8,128)S(1)}, f32[2,384,256]{2,1,0:T(8,128)S(1)}, f32[2,384,256]{2,1,0:T(8,128)S(1)}) custom-call(bf16[384,11008]{1,0:T(8,128)(2,1)S(1)} %copy-done, bf16[384,11008]{1,0:T(8,128)(2,1)} %collective-permute-done.2.other_hbm, bf16[688,256]{1,0:T(8,128)(2,1)S(1)} %get-tuple-element.258.refs_0_, ...), custom_call_target="tpu_custom_call" | custom-call | flops 1409286144 | bytes 2752512 | tf_op jit(solution)/shard_map/pallas_call | solution.py:158
  38.1 0.2 collective-permute-start.10
  38.2 1.3 collective-permute-start.9
  39.6 5.4 %collective-permute-done.3.refs_0_ = bf16[688,256]{1,0:T(8,128)(2,1)S(1)} collective-permute-done((bf16[688,256]{1,0:T(8,128)(2,1)}, bf16[688,256]{1,0:T(8,128)(2,1)S(1)}, u32[]{:S(2)}, u32[]{:S(2)}) %collective-permute-start.3) | collective-permute-done | bytes 352288 | tf_op jit(solution)/shard_map/ppermute | solution.py:270
  45.1 1.3 collective-permute-start.17
  46.5 3.2 %shard_map.51 = (f32[2,384,256]{2,1,0:T(8,128)S(1)}, f32[2,384,256]{2,1,0:T(8,128)S(1)}, f32[2,384,256]{2,1,0:T(8,128)S(1)}, f32[2,384,256]{2,1,0:T(8,128)S(1)}) custom-call(bf16[384,11008]{1,0:T(8,128)(2,1)S(1)} %copy-done, ...), custom_call_target="tpu_custom_call", output_to_operand_aliasing={{0}: (6, {}), {1}: (7, {}), {2}: (8, {}), {3}: (9, {})} | custom-call | flops 1409286144 | bytes 2752512 | tf_op jit(solution)/shard_map/pallas_call | solution.py:158
  49.7 2.9 %collective-permute-done.10.refs_2_ = bf16[688,256]{1,0:T(8,128)(2,1)S(1)} collective-permute-done((bf16[688,256]{1,0:T(8,128)(2,1)}, bf16[688,256]{1,0:T(8,128)(2,1)S(1)}, u32[]{:S(2)}, u32[]{:S(2)}) %collective-permute-start.10) | collective-permute-done | bytes 352288 | tf_op jit(solution)/shard_map/ppermute | solution.py:270
  52.6 0.1 collective-permute-start.16
  52.7 1.3 collective-permute-start.15
  54.0 6.1 %collective-permute-done.8.refs_0_ = bf16[688,256]{1,0:T(8,128)(2,1)S(1)} collective-permute-done((bf16[688,256]{1,0:T(8,128)(2,1)S(1)}, bf16[688,256]{1,0:T(8,128)(2,1)S(1)}, u32[]{:S(2)}, u32[]{:S(2)}) %collective-permute-start.8) | collective-permute-done | bytes 352288 | tf_op jit(solution)/shard_map/ppermute | solution.py:270
  60.1 0.2 collective-permute-start.21
  60.3 1.3 collective-permute-start.14
  61.6 4.5 %shard_map.52 = (f32[2,384,256]{2,1,0:T(8,128)S(1)}, f32[2,384,256]{2,1,0:T(8,128)S(1)}, f32[2,384,256]{2,1,0:T(8,128)S(1)}, f32[2,384,256]{2,1,0:T(8,128)S(1)}) custom-call(bf16[384,11008]{1,0:T(8,128)(2,1)S(1)} %copy-done, ...), custom_call_target="tpu_custom_call", output_to_operand_aliasing={{0}: (6, {}), {1}: (7, {}), {2}: (8, {}), {3}: (9, {})} | custom-call | flops 1409286144 | bytes 2752512 | tf_op jit(solution)/shard_map/pallas_call | solution.py:158
  66.1 3.2 %shard_map.53 = (f32[2,384,256]{2,1,0:T(8,128)S(1)}, f32[2,384,256]{2,1,0:T(8,128)S(1)}, f32[2,384,256]{2,1,0:T(8,128)S(1)}, f32[2,384,256]{2,1,0:T(8,128)S(1)}) custom-call(bf16[384,11008]{1,0:T(8,128)(2,1)S(1)} %copy-done, ...), custom_call_target="tpu_custom_call", output_to_operand_aliasing={{0}: (6, {}), {1}: (7, {}), {2}: (8, {}), {3}: (9, {})} | custom-call | flops 1409286144 | bytes 2752512 | tf_op jit(solution)/shard_map/pallas_call | solution.py:158
  69.3 0.2 collective-permute-start.20
  69.5 1.3 collective-permute-start.19
  70.8 4.4 %collective-permute-done.14.refs_0_ = bf16[688,256]{1,0:T(8,128)(2,1)S(1)} collective-permute-done((bf16[688,256]{1,0:T(8,128)(2,1)S(1)}, bf16[688,256]{1,0:T(8,128)(2,1)S(1)}, u32[]{:S(2)}, u32[]{:S(2)}) %collective-permute-start.14) | collective-permute-done | bytes 352288 | tf_op jit(solution)/shard_map/ppermute | solution.py:270
  75.2 0.1 collective-permute-start.18
  75.3 1.3 collective-permute-start.23
  76.7 3.2 %shard_map.54 = (f32[2,384,256]{2,1,0:T(8,128)S(1)}, f32[2,384,256]{2,1,0:T(8,128)S(1)}, f32[2,384,256]{2,1,0:T(8,128)S(1)}, f32[2,384,256]{2,1,0:T(8,128)S(1)}) custom-call(bf16[384,11008]{1,0:T(8,128)(2,1)S(1)} %copy-done, ...), custom_call_target="tpu_custom_call", output_to_operand_aliasing={{0}: (6, {}), {1}: (7, {}), {2}: (8, {}), {3}: (9, {})} | custom-call | flops 1409286144 | bytes 2752512 | tf_op jit(solution)/shard_map/pallas_call | solution.py:158
  79.9 2.9 %collective-permute-done.20.refs_2_ = bf16[688,256]{1,0:T(8,128)(2,1)S(1)} collective-permute-done((bf16[688,256]{1,0:T(8,128)(2,1)S(1)}, bf16[688,256]{1,0:T(8,128)(2,1)S(1)}, u32[]{:S(2)}, u32[]{:S(2)}) %collective-permute-start.20) | collective-permute-done | bytes 352288 | tf_op jit(solution)/shard_map/ppermute | solution.py:270
  82.9 1.3 collective-permute-start.26
  84.2 6.1 %collective-permute-done.18.refs_0_ = bf16[688,256]{1,0:T(8,128)(2,1)S(1)} collective-permute-done((bf16[688,256]{1,0:T(8,128)(2,1)S(1)}, bf16[688,256]{1,0:T(8,128)(2,1)S(1)}, u32[]{:S(2)}, u32[]{:S(2)}) %collective-permute-start.18) | collective-permute-done | bytes 352288 | tf_op jit(solution)/shard_map/ppermute | solution.py:270
  90.3 0.2 collective-permute-start.24
  90.5 1.3 collective-permute-start.22
  91.8 3.2 %shard_map.55 = (f32[2,384,256]{2,1,0:T(8,128)S(1)}, f32[2,384,256]{2,1,0:T(8,128)S(1)}, f32[2,384,256]{2,1,0:T(8,128)S(1)}, f32[2,384,256]{2,1,0:T(8,128)S(1)}) custom-call(bf16[384,11008]{1,0:T(8,128)(2,1)S(1)} %copy-done, ...), custom_call_target="tpu_custom_call", output_to_operand_aliasing={{0}: (6, {}), {1}: (7, {}), {2}: (8, {}), {3}: (9, {})} | custom-call | flops 1409286144 | bytes 2752512 | tf_op jit(solution)/shard_map/pallas_call | solution.py:158
  95.0 2.9 %collective-permute-done.25.refs_2_ = bf16[688,256]{1,0:T(8,128)(2,1)S(1)} collective-permute-done((bf16[688,256]{1,0:T(8,128)(2,1)S(1)}, bf16[688,256]{1,0:T(8,128)(2,1)S(1)}, u32[]{:S(2)}, u32[]{:S(2)}) %collective-permute-start.25) | collective-permute-done | bytes 352288 | tf_op jit(solution)/shard_map/ppermute | solution.py:270
  97.8 0.2 collective-permute-start.28
  98.0 1.3 collective-permute-start.27
  99.3 3.2 %shard_map.56 = (f32[2,384,256]{2,1,0:T(8,128)S(1)}, f32[2,384,256]{2,1,0:T(8,128)S(1)}, f32[2,384,256]{2,1,0:T(8,128)S(1)}, f32[2,384,256]{2,1,0:T(8,128)S(1)}) custom-call(bf16[384,11008]{1,0:T(8,128)(2,1)S(1)} %copy-done, ...), custom_call_target="tpu_custom_call", output_to_operand_aliasing={{0}: (6, {}), {1}: (7, {}), {2}: (8, {}), {3}: (9, {})} | custom-call | flops 1409286144 | bytes 2752512 | tf_op jit(solution)/shard_map/pallas_call | solution.py:158
  102.5 2.9 %collective-permute-done.22.refs_0_ = bf16[688,256]{1,0:T(8,128)(2,1)S(1)} collective-permute-done((bf16[688,256]{1,0:T(8,128)(2,1)S(1)}, bf16[688,256]{1,0:T(8,128)(2,1)S(1)}, u32[]{:S(2)}, u32[]{:S(2)}) %collective-permute-start.22) | collective-permute-done | bytes 352288 | tf_op jit(solution)/shard_map/ppermute | solution.py:270
  105.4 2.4 %shard_map.57 = (f32[2,384,256]{2,1,0:T(8,128)S(1)}, f32[2,384,256]{2,1,0:T(8,128)S(1)}, bf16[2,768,896]{2,1,0:T(8,128)(2,1)S(1)}) custom-call(bf16[384,11008]{1,0:T(8,128)(2,1)S(1)} %copy-done, bf16[384,11008]{1,0:T(8,128)(2,1)} %collective-permute-done.2.other_hbm, ...), custom_call_target="tpu_custom_call", output_to_operand_aliasing={{0}: (4, {}), {1}: (5, {})} | custom-call | flops 704643072 | bytes 2752512 | tf_op jit(solution)/shard_map/pallas_call | solution.py:158
  107.8 2.5 %collective-permute-start.30 = (f32[2,384,256]{2,1,0:T(8,128)S(1)}, f32[2,384,256]{2,1,0:T(8,128)S(1)}, u32[]{:S(2)}, u32[]{:S(2)}) collective-permute-start(f32[2,384,256]{2,1,0:T(8,128)S(1)} %get-tuple-element.252), channel_id=1, source_target_pairs={{0,1},{1,0},{2,3},{3,2},{4,5},{5,4},{6,7},{7,6},{8,9},{9,8},{10,11... | collective-permute-start | bytes 2359304 | tf_op jit(solution)/shard_map/ppermute | solution.py:278
  110.3 2.6 %collective-permute-done.27.refs_0_ = bf16[688,256]{1,0:T(8,128)(2,1)S(1)} collective-permute-done((bf16[688,256]{1,0:T(8,128)(2,1)S(1)}, bf16[688,256]{1,0:T(8,128)(2,1)S(1)}, u32[]{:S(2)}, u32[]{:S(2)}) %collective-permute-start.27) | collective-permute-done | bytes 352288 | tf_op jit(solution)/shard_map/ppermute | solution.py:270
  112.9 1.1 shard_map.58
  114.1 1.5 collective-permute-start.29
  115.6 1.5 shard_map.59.refs_0_
  117.1 0.4 collective-permute-done.29.theirs_ref
  117.5 1.5 shard_map.60
  119.0 4.2 %all-to-all-start.1 = ((bf16[16,2,6,16,256]{4,3,2,1,0:T(8,128)(2,1)}), bf16[16,2,6,16,256]{4,3,2,1,0:T(8,128)(2,1)S(1)}, u32[]{:S(2)}, u32[]{:S(2)}) async-start(bf16[16,2,6,16,256]{4,3,2,1,0:T(8,128)(2,1)} %shard_map.60), calls=%async_computation.1 | async-start | bytes 3145728 | tf_op jit(solution)/shard_map/all_to_all | solution.py:305
  123.2 1.3 shard_map.61
  124.5 34.9 %all-to-all-done.1 = bf16[16,2,6,16,256]{4,3,2,1,0:T(8,128)(2,1)S(1)} async-done(((bf16[16,2,6,16,256]{4,3,2,1,0:T(8,128)(2,1)}), bf16[16,2,6,16,256]{4,3,2,1,0:T(8,128)(2,1)S(1)}, u32[]{:S(2)}, u32[]{:S(2)}) %all-to-all-start.1) | async-done | bytes 1572896 | tf_op jit(solution)/shard_map/all_to_all | solution.py:305
  159.4 1.3 copy.37
  (32 shorter events, 0.7 us)
Async XLA Ops:
  0.6 5.1 %copy-start.2 = (s32[128,1]{0,1:T(1,128)S(1)}, s32[128,1]{0,1:T(1,128)}, u32[]{:S(2)}) copy-start(s32[128,1]{0,1:T(1,128)} %param.5) | copy-start | bytes 1540
  0.6 30.8 %collective-permute-start.2 = (bf16[384,11008]{1,0:T(8,128)(2,1)}, bf16[384,11008]{1,0:T(8,128)(2,1)}, u32[]{:S(2)}, u32[]{:S(2)}) collective-permute-start(bf16[384,11008]{1,0:T(8,128)(2,1)} %own_hbm.15), channel_id=1, source_target_pairs={{0,1},{1,0},{2,3},{3,2},{4,5},{5,4},{6,7},{7,6},{8,9},{9,8},{10,11... | collective-permute-start | bytes 25362440 | tf_op jit(solution)/shard_map/ppermute | solution.py:242
  2.8 11.3 %collective-permute-start.11 = (bf16[688,256]{1,0:T(8,128)(2,1)S(1)}, bf16[688,256]{1,0:T(8,128)(2,1)S(1)}, u32[]{:S(2)}, u32[]{:S(2)}) collective-permute-start(bf16[688,256]{1,0:T(8,128)(2,1)S(1)} %get-tuple-element.256.refs_1_), channel_id=1, source_target_pairs={{0,2},{1,3},{2,6},{3,7},{6,10},{7,11},{10,14},{11,15},{14,12},{15,... | collective-permute-start | bytes 1056776 | tf_op jit(solution)/shard_map/ppermute | solution.py:270
  4.1 16.1 %collective-permute-start.4 = (bf16[688,256]{1,0:T(8,128)(2,1)S(1)}, bf16[688,256]{1,0:T(8,128)(2,1)S(1)}, u32[]{:S(2)}, u32[]{:S(2)}) collective-permute-start(bf16[688,256]{1,0:T(8,128)(2,1)S(1)} %get-tuple-element.257.refs_3_), channel_id=1, source_target_pairs={{0,2},{1,3},{2,6},{3,7},{6,10},{7,11},{10,14},{11,15},{14,12},{15,... | collective-permute-start | bytes 1056776 | tf_op jit(solution)/shard_map/ppermute | solution.py:270
  5.4 9.9 %collective-permute-start = (bf16[688,256]{1,0:T(8,128)(2,1)S(1)}, bf16[688,256]{1,0:T(8,128)(2,1)S(1)}, u32[]{:S(2)}, u32[]{:S(2)}) collective-permute-start(bf16[688,256]{1,0:T(8,128)(2,1)S(1)} %get-tuple-element.258.refs_0_), channel_id=1, source_target_pairs={{0,4},{1,5},{2,0},{3,1},{6,2},{7,3},{10,6},{11,7},{14,10},{15,11},... | collective-permute-start | bytes 1056776 | tf_op jit(solution)/shard_map/ppermute | solution.py:270
  5.6 16.7 %collective-permute-start.6 = (bf16[688,256]{1,0:T(8,128)(2,1)S(1)}, bf16[688,256]{1,0:T(8,128)(2,1)S(1)}, u32[]{:S(2)}, u32[]{:S(2)}) collective-permute-start(bf16[688,256]{1,0:T(8,128)(2,1)S(1)} %get-tuple-element.259.refs_2_), channel_id=1, source_target_pairs={{0,4},{1,5},{2,0},{3,1},{6,2},{7,3},{10,6},{11,7},{14,10},{15,11},... | collective-permute-start | bytes 1056776 | tf_op jit(solution)/shard_map/ppermute | solution.py:270
  6.8 17.7 %all-to-all-start = ((s32[16,1,16]{2,1,0:T(1,128)}), s32[16,1,16]{2,1,0:T(1,128)S(1)}, u32[]{:S(2)}, u32[]{:S(2)}) async-start(s32[16,1,16]{2,1,0:T(1,128)} %sub.17), calls=%async_computation | async-start | bytes 16384 | tf_op jit(solution)/shard_map/all_to_all | solution.py:294
  14.1 16.0 %collective-permute-start.12 = (bf16[688,256]{1,0:T(8,128)(2,1)S(1)}, bf16[688,256]{1,0:T(8,128)(2,1)}, u32[]{:S(2)}, u32[]{:S(2)}) collective-permute-start(bf16[688,256]{1,0:T(8,128)(2,1)S(1)} %collective-permute-done.11.refs_1_), channel_id=1, source_target_pairs={{0,2},{1,3},{2,6},{3,7},{6,10},{7,11},{10,14},{11,15},{14,12},{15,... | collective-permute-start | bytes 1056776 | tf_op jit(solution)/shard_map/ppermute | solution.py:270
  15.3 14.7 %collective-permute-start.1 = (bf16[688,256]{1,0:T(8,128)(2,1)S(1)}, bf16[688,256]{1,0:T(8,128)(2,1)}, u32[]{:S(2)}, u32[]{:S(2)}) collective-permute-start(bf16[688,256]{1,0:T(8,128)(2,1)S(1)} %collective-permute-done.refs_0_), channel_id=1, source_target_pairs={{0,4},{1,5},{2,0},{3,1},{6,2},{7,3},{10,6},{11,7},{14,10},{15,11},... | collective-permute-start | bytes 1056776 | tf_op jit(solution)/shard_map/ppermute | solution.py:270
  20.2 18.0 %collective-permute-start.5 = (bf16[688,256]{1,0:T(8,128)(2,1)S(1)}, bf16[688,256]{1,0:T(8,128)(2,1)}, u32[]{:S(2)}, u32[]{:S(2)}) collective-permute-start(bf16[688,256]{1,0:T(8,128)(2,1)S(1)} %collective-permute-done.4.refs_3_), channel_id=1, source_target_pairs={{0,2},{1,3},{2,6},{3,7},{6,10},{7,11},{10,14},{11,15},{14,12},{15,... | collective-permute-start | bytes 1056776 | tf_op jit(solution)/shard_map/ppermute | solution.py:270
  22.3 15.7 %collective-permute-start.7 = (bf16[688,256]{1,0:T(8,128)(2,1)S(1)}, bf16[688,256]{1,0:T(8,128)(2,1)}, u32[]{:S(2)}, u32[]{:S(2)}) collective-permute-start(bf16[688,256]{1,0:T(8,128)(2,1)S(1)} %collective-permute-done.6.refs_2_), channel_id=1, source_target_pairs={{0,4},{1,5},{2,0},{3,1},{6,2},{7,3},{10,6},{11,7},{14,10},{15,11},... | collective-permute-start | bytes 1056776 | tf_op jit(solution)/shard_map/ppermute | solution.py:270
  24.5 13.5 %copy-start.1 = (s32[16,1,16]{2,1,0:T(1,128)}, s32[16,1,16]{2,1,0:T(1,128)S(1)}, u32[]{:S(2)}) copy-start(s32[16,1,16]{2,1,0:T(1,128)S(1)} %all-to-all-done) | copy-start | bytes 3076
  30.0 15.0 %collective-permute-start.3 = (bf16[688,256]{1,0:T(8,128)(2,1)}, bf16[688,256]{1,0:T(8,128)(2,1)S(1)}, u32[]{:S(2)}, u32[]{:S(2)}) collective-permute-start(bf16[688,256]{1,0:T(8,128)(2,1)} %collective-permute-done.1.refs_0_), channel_id=1, source_target_pairs={{0,4},{1,5},{2,0},{3,1},{6,2},{7,3},{10,6},{11,7},{14,10},{15,11},... | collective-permute-start | bytes 1056776 | tf_op jit(solution)/shard_map/ppermute | solution.py:270
  30.1 15.0 %collective-permute-start.13 = (bf16[688,256]{1,0:T(8,128)(2,1)}, bf16[688,256]{1,0:T(8,128)(2,1)S(1)}, u32[]{:S(2)}, u32[]{:S(2)}) collective-permute-start(bf16[688,256]{1,0:T(8,128)(2,1)} %collective-permute-done.12.refs_1_), channel_id=1, source_target_pairs={{0,2},{1,3},{2,6},{3,7},{6,10},{7,11},{10,14},{11,15},{14,12},{15,... | collective-permute-start | bytes 1056776 | tf_op jit(solution)/shard_map/ppermute | solution.py:270
  31.5 3.4 %copy-start = (bf16[384,11008]{1,0:T(8,128)(2,1)S(1)}, bf16[384,11008]{1,0:T(8,128)(2,1)}, u32[]{:S(2)}) copy-start(bf16[384,11008]{1,0:T(8,128)(2,1)} %own_hbm.15) | copy-start | bytes 25362436
  38.1 14.5 %collective-permute-start.10 = (bf16[688,256]{1,0:T(8,128)(2,1)}, bf16[688,256]{1,0:T(8,128)(2,1)S(1)}, u32[]{:S(2)}, u32[]{:S(2)}) collective-permute-start(bf16[688,256]{1,0:T(8,128)(2,1)} %collective-permute-done.7.refs_2_), channel_id=1, source_target_pairs={{0,4},{1,5},{2,0},{3,1},{6,2},{7,3},{10,6},{11,7},{14,10},{15,11},... | collective-permute-start | bytes 1056776 | tf_op jit(solution)/shard_map/ppermute | solution.py:270
  38.2 14.4 %collective-permute-start.9 = (bf16[688,256]{1,0:T(8,128)(2,1)}, bf16[688,256]{1,0:T(8,128)(2,1)S(1)}, u32[]{:S(2)}, u32[]{:S(2)}) collective-permute-start(bf16[688,256]{1,0:T(8,128)(2,1)} %collective-permute-done.5.refs_3_), channel_id=1, source_target_pairs={{0,2},{1,3},{2,6},{3,7},{6,10},{7,11},{10,14},{11,15},{14,12},{15,... | collective-permute-start | bytes 1056776 | tf_op jit(solution)/shard_map/ppermute | solution.py:270
  45.0 15.1 %collective-permute-start.8 = (bf16[688,256]{1,0:T(8,128)(2,1)S(1)}, bf16[688,256]{1,0:T(8,128)(2,1)S(1)}, u32[]{:S(2)}, u32[]{:S(2)}) collective-permute-start(bf16[688,256]{1,0:T(8,128)(2,1)S(1)} %collective-permute-done.3.refs_0_), channel_id=1, source_target_pairs={{0,4},{1,5},{2,0},{3,1},{6,2},{7,3},{10,6},{11,7},{14,10},{15,11},... | collective-permute-start | bytes 1056776 | tf_op jit(solution)/shard_map/ppermute | solution.py:270
  45.1 15.0 %collective-permute-start.17 = (bf16[688,256]{1,0:T(8,128)(2,1)S(1)}, bf16[688,256]{1,0:T(8,128)(2,1)S(1)}, u32[]{:S(2)}, u32[]{:S(2)}) collective-permute-start(bf16[688,256]{1,0:T(8,128)(2,1)S(1)} %collective-permute-done.13.refs_1_), channel_id=1, source_target_pairs={{0,2},{1,3},{2,6},{3,7},{6,10},{7,11},{10,14},{11,15},{14,12},{15,... | collective-permute-start | bytes 1056776 | tf_op jit(solution)/shard_map/ppermute | solution.py:270
  52.6 16.8 %collective-permute-start.16 = (bf16[688,256]{1,0:T(8,128)(2,1)S(1)}, bf16[688,256]{1,0:T(8,128)(2,1)S(1)}, u32[]{:S(2)}, u32[]{:S(2)}) collective-permute-start(bf16[688,256]{1,0:T(8,128)(2,1)S(1)} %collective-permute-done.10.refs_2_), channel_id=1, source_target_pairs={{0,4},{1,5},{2,0},{3,1},{6,2},{7,3},{10,6},{11,7},{14,10},{15,11},... | collective-permute-start | bytes 1056776 | tf_op jit(solution)/shard_map/ppermute | solution.py:270
  52.7 16.8 %collective-permute-start.15 = (bf16[688,256]{1,0:T(8,128)(2,1)S(1)}, bf16[688,256]{1,0:T(8,128)(2,1)S(1)}, u32[]{:S(2)}, u32[]{:S(2)}) collective-permute-start(bf16[688,256]{1,0:T(8,128)(2,1)S(1)} %collective-permute-done.9.refs_3_), channel_id=1, source_target_pairs={{0,2},{1,3},{2,6},{3,7},{6,10},{7,11},{10,14},{11,15},{14,12},{15,... | collective-permute-start | bytes 1056776 | tf_op jit(solution)/shard_map/ppermute | solution.py:270
  60.1 15.2 %collective-permute-start.21 = (bf16[688,256]{1,0:T(8,128)(2,1)S(1)}, bf16[688,256]{1,0:T(8,128)(2,1)S(1)}, u32[]{:S(2)}, u32[]{:S(2)}) collective-permute-start(bf16[688,256]{1,0:T(8,128)(2,1)S(1)} %collective-permute-done.17.refs_1_), channel_id=1, source_target_pairs={{0,2},{1,3},{2,6},{3,7},{6,10},{7,11},{10,14},{11,15},{14,12},{15,... | collective-permute-start | bytes 1056776 | tf_op jit(solution)/shard_map/ppermute | solution.py:270
  60.3 14.9 %collective-permute-start.14 = (bf16[688,256]{1,0:T(8,128)(2,1)S(1)}, bf16[688,256]{1,0:T(8,128)(2,1)S(1)}, u32[]{:S(2)}, u32[]{:S(2)}) collective-permute-start(bf16[688,256]{1,0:T(8,128)(2,1)S(1)} %collective-permute-done.8.refs_0_), channel_id=1, source_target_pairs={{0,4},{1,5},{2,0},{3,1},{6,2},{7,3},{10,6},{11,7},{14,10},{15,11},... | collective-permute-start | bytes 1056776 | tf_op jit(solution)/shard_map/ppermute | solution.py:270
  69.3 13.4 %collective-permute-start.20 = (bf16[688,256]{1,0:T(8,128)(2,1)S(1)}, bf16[688,256]{1,0:T(8,128)(2,1)S(1)}, u32[]{:S(2)}, u32[]{:S(2)}) collective-permute-start(bf16[688,256]{1,0:T(8,128)(2,1)S(1)} %collective-permute-done.16.refs_2_), channel_id=1, source_target_pairs={{0,4},{1,5},{2,0},{3,1},{6,2},{7,3},{10,6},{11,7},{14,10},{15,11},... | collective-permute-start | bytes 1056776 | tf_op jit(solution)/shard_map/ppermute | solution.py:270
  69.5 13.4 %collective-permute-start.19 = (bf16[688,256]{1,0:T(8,128)(2,1)S(1)}, bf16[688,256]{1,0:T(8,128)(2,1)S(1)}, u32[]{:S(2)}, u32[]{:S(2)}) collective-permute-start(bf16[688,256]{1,0:T(8,128)(2,1)S(1)} %collective-permute-done.15.refs_3_), channel_id=1, source_target_pairs={{0,2},{1,3},{2,6},{3,7},{6,10},{7,11},{10,14},{11,15},{14,12},{15,... | collective-permute-start | bytes 1056776 | tf_op jit(solution)/shard_map/ppermute | solution.py:270
  75.2 15.1 %collective-permute-start.18 = (bf16[688,256]{1,0:T(8,128)(2,1)S(1)}, bf16[688,256]{1,0:T(8,128)(2,1)S(1)}, u32[]{:S(2)}, u32[]{:S(2)}) collective-permute-start(bf16[688,256]{1,0:T(8,128)(2,1)S(1)} %collective-permute-done.14.refs_0_), channel_id=1, source_target_pairs={{0,4},{1,5},{2,0},{3,1},{6,2},{7,3},{10,6},{11,7},{14,10},{15,11},... | collective-permute-start | bytes 1056776 | tf_op jit(solution)/shard_map/ppermute | solution.py:270
  75.3 15.0 %collective-permute-start.23 = (bf16[688,256]{1,0:T(8,128)(2,1)S(1)}, bf16[688,256]{1,0:T(8,128)(2,1)S(1)}, u32[]{:S(2)}, u32[]{:S(2)}) collective-permute-start(bf16[688,256]{1,0:T(8,128)(2,1)S(1)} %collective-permute-done.21.refs_1_), channel_id=1, source_target_pairs={{0,2},{1,3},{2,6},{3,7},{6,10},{7,11},{10,14},{11,15},{14,12},{15,... | collective-permute-start | bytes 1056776 | tf_op jit(solution)/shard_map/ppermute | solution.py:270
  82.7 15.1 %collective-permute-start.25 = (bf16[688,256]{1,0:T(8,128)(2,1)S(1)}, bf16[688,256]{1,0:T(8,128)(2,1)S(1)}, u32[]{:S(2)}, u32[]{:S(2)}) collective-permute-start(bf16[688,256]{1,0:T(8,128)(2,1)S(1)} %collective-permute-done.20.refs_2_), channel_id=1, source_target_pairs={{0,4},{1,5},{2,0},{3,1},{6,2},{7,3},{10,6},{11,7},{14,10},{15,11},... | collective-permute-start | bytes 1056776 | tf_op jit(solution)/shard_map/ppermute | solution.py:270
  82.9 15.0 %collective-permute-start.26 = (bf16[688,256]{1,0:T(8,128)(2,1)S(1)}, bf16[688,256]{1,0:T(8,128)(2,1)S(1)}, u32[]{:S(2)}, u32[]{:S(2)}) collective-permute-start(bf16[688,256]{1,0:T(8,128)(2,1)S(1)} %collective-permute-done.19.refs_3_), channel_id=1, source_target_pairs={{0,2},{1,3},{2,6},{3,7},{6,10},{7,11},{10,14},{11,15},{14,12},{15,... | collective-permute-start | bytes 1056776 | tf_op jit(solution)/shard_map/ppermute | solution.py:270
  90.3 12.2 %collective-permute-start.24 = (bf16[688,256]{1,0:T(8,128)(2,1)S(1)}, bf16[688,256]{1,0:T(8,128)(2,1)S(1)}, u32[]{:S(2)}, u32[]{:S(2)}) collective-permute-start(bf16[688,256]{1,0:T(8,128)(2,1)S(1)} %collective-permute-done.23.refs_1_), channel_id=1, source_target_pairs={{0,2},{1,3},{2,6},{3,7},{6,10},{7,11},{10,14},{11,15},{14,12},{15,... | collective-permute-start | bytes 1056776 | tf_op jit(solution)/shard_map/ppermute | solution.py:270
  90.5 14.9 %collective-permute-start.22 = (bf16[688,256]{1,0:T(8,128)(2,1)S(1)}, bf16[688,256]{1,0:T(8,128)(2,1)S(1)}, u32[]{:S(2)}, u32[]{:S(2)}) collective-permute-start(bf16[688,256]{1,0:T(8,128)(2,1)S(1)} %collective-permute-done.18.refs_0_), channel_id=1, source_target_pairs={{0,4},{1,5},{2,0},{3,1},{6,2},{7,3},{10,6},{11,7},{14,10},{15,11},... | collective-permute-start | bytes 1056776 | tf_op jit(solution)/shard_map/ppermute | solution.py:270
  97.8 12.5 %collective-permute-start.28 = (bf16[688,256]{1,0:T(8,128)(2,1)S(1)}, bf16[688,256]{1,0:T(8,128)(2,1)S(1)}, u32[]{:S(2)}, u32[]{:S(2)}) collective-permute-start(bf16[688,256]{1,0:T(8,128)(2,1)S(1)} %collective-permute-done.26.refs_3_), channel_id=1, source_target_pairs={{0,2},{1,3},{2,6},{3,7},{6,10},{7,11},{10,14},{11,15},{14,12},{15,... | collective-permute-start | bytes 1056776 | tf_op jit(solution)/shard_map/ppermute | solution.py:270
  98.0 14.9 %collective-permute-start.27 = (bf16[688,256]{1,0:T(8,128)(2,1)S(1)}, bf16[688,256]{1,0:T(8,128)(2,1)S(1)}, u32[]{:S(2)}, u32[]{:S(2)}) collective-permute-start(bf16[688,256]{1,0:T(8,128)(2,1)S(1)} %collective-permute-done.25.refs_2_), channel_id=1, source_target_pairs={{0,4},{1,5},{2,0},{3,1},{6,2},{7,3},{10,6},{11,7},{14,10},{15,11},... | collective-permute-start | bytes 1056776 | tf_op jit(solution)/shard_map/ppermute | solution.py:270
  107.8 7.8 %collective-permute-start.30 = (f32[2,384,256]{2,1,0:T(8,128)S(1)}, f32[2,384,256]{2,1,0:T(8,128)S(1)}, u32[]{:S(2)}, u32[]{:S(2)}) collective-permute-start(f32[2,384,256]{2,1,0:T(8,128)S(1)} %get-tuple-element.252), channel_id=1, source_target_pairs={{0,1},{1,0},{2,3},{3,2},{4,5},{5,4},{6,7},{7,6},{8,9},{9,8},{10,11... | collective-permute-start | bytes 2359304 | tf_op jit(solution)/shard_map/ppermute | solution.py:278
  114.1 3.4 %collective-permute-start.29 = (f32[2,384,256]{2,1,0:T(8,128)S(1)}, f32[2,384,256]{2,1,0:T(8,128)S(1)}, u32[]{:S(2)}, u32[]{:S(2)}) collective-permute-start(f32[2,384,256]{2,1,0:T(8,128)S(1)} %get-tuple-element.250), channel_id=1, source_target_pairs={{0,1},{1,0},{2,3},{3,2},{4,5},{5,4},{6,7},{7,6},{8,9},{9,8},{10,11... | collective-permute-start | bytes 2359304 | tf_op jit(solution)/shard_map/ppermute | solution.py:278
  119.0 40.4 %all-to-all-start.1 = ((bf16[16,2,6,16,256]{4,3,2,1,0:T(8,128)(2,1)}), bf16[16,2,6,16,256]{4,3,2,1,0:T(8,128)(2,1)S(1)}, u32[]{:S(2)}, u32[]{:S(2)}) async-start(bf16[16,2,6,16,256]{4,3,2,1,0:T(8,128)(2,1)} %shard_map.60), calls=%async_computation.1 | async-start | bytes 3145728 | tf_op jit(solution)/shard_map/all_to_all | solution.py:305
